TPU v7x, 32 devices: a whole 2x2x4 slice. The times are simulated.
32 devices in a mesh: depth: 2 (over core), row: 2 (over x), col: 8 (over z, y).
Axes of the slice: x: 2, y: 2, z: 4, core: 2. Of those that a mesh axis runs over, the one named last changes fastest.
Arguments:
- probe: float32 [2, 256, 256], replicated, may hold values from -6 to 6
- object_re: bfloat16 [2, 1024, 8192], P('depth', 'row', 'col'), may hold values from 0.099609375 to 1.8984375
- object_im: bfloat16 [2, 1024, 8192], P('depth', 'row', 'col'), may hold values from -1.796875 to 1.796875
- phases: float32 [256, 256], replicated, may hold values from -3.140625 to 3.140625
- centres: int32 [2, 8, 4, 2, 2], P('row', 'col'), may hold values from 0 to 1023, as said below
- occupied: int32 [2, 8, 4], P('row', 'col'), may hold values from 0 to 2, as said below
- measured: float32 [2, 8, 4, 2, 256, 256], P('row', 'col'), may hold values from 0 to 4
Outputs:
- object_grad: float32 [2, 2, 1024, 8192], P(None, 'depth', 'row', 'col')
- probe_grad: float32 [2, 256, 256], P(None, 'depth')
Inputs may be any that keep to these rules, and one draw needn't show every extreme that they name: `centres`: the 256 x 256 window around every centre, starting 256 // 2 pixels before it in both directions, lies inside the field of view. `occupied`: in every draw some tile has all 2 slots used in some micro-batch.
All inputs are finite; a program needn't handle non-finite values.
Results may differ from a plain program's by a relative error of at most 0.006.
Values may be sent and summed in bfloat16 or wider, within the bound.
No kernel may reach another device: no remote copies, remote signals or barrier semaphores. Data moves between devices by JAX's collectives and lax.ppermute only.
A program may use at most 192 MiB of HBM per device.

v0:
```python
import math

import jax
import jax.numpy as jnp
from jax import lax
from jax.sharding import PartitionSpec as P

precise = lax.Precision.HIGH


def padded_2(array, sides, width):
    for axis, dim in sides:
        size, length = (lax.axis_size(axis), array.shape[dim])
        up = [(i, (i + 1) % size) for i in range(size - 1)]
        down = [(j, i) for i, j in up]
        last = lax.slice_in_dim(array, length - width, length, axis=dim)
        first = lax.slice_in_dim(array, 0, width, axis=dim)
        before = lax.ppermute(last, axis, up)
        after = lax.ppermute(first, axis, down)
        array = jnp.concatenate([before, array, after], axis=dim)
    return array


def as_sent(array):
    return jax.tree.map(lambda a: a.astype(jnp.bfloat16) if a.dtype == jnp.float32 else a, array)


def from_behind(block, axis, distance):
    devices = range(lax.axis_size(axis))
    route = [(i - distance, i) for i in devices if i - distance in devices]
    return lax.ppermute(block, axis, route)


def tables(frame_size):
    indices = jnp.arange(frame_size, dtype=jnp.int32)
    phase_turns = indices[:, None] * indices[None, :] % frame_size
    angles = phase_turns.astype(jnp.float32) * (-2.0 * math.pi / frame_size)
    scaling = 1.0 / math.sqrt(frame_size)
    return (jnp.cos(angles) * scaling, jnp.sin(angles) * scaling)


def complex_mul(left_re, left_im, right_re, right_im):
    return (left_re * right_re - left_im * right_im, left_re * right_im + left_im * right_re)


def conj_mul(left_re, left_im, right_re, right_im):
    return (left_re * right_re + left_im * right_im, left_re * right_im - left_im * right_re)


def apply_left(mat_re, mat_im, data_re, data_im):

    def product(matrix, data):
        return jnp.einsum("jk,bkl->bjl", matrix, data, precision=precise)

    return (
        product(mat_re, data_re) - product(mat_im, data_im),
        product(mat_re, data_im) + product(mat_im, data_re),
    )


def apply_right(data_re, data_im, mat_re, mat_im):

    def product(data, matrix):
        return jnp.einsum("bjk,kl->bjl", data, matrix, precision=precise)

    return (
        product(data_re, mat_re) - product(data_im, mat_im),
        product(data_re, mat_im) + product(data_im, mat_re),
    )


def transform(data_re, data_im, cosine, sines, direction):
    signed = sines * direction
    half_re, half_im = apply_left(cosine, signed, data_re, data_im)
    return apply_right(half_re, half_im, cosine, signed)


def shards(probe, object_re, object_im, phases, centres, occupied, measured):
    frame_size = probe.shape[1]
    half_size = frame_size // 2
    sections = lax.axis_size("depth")
    my_section = lax.axis_index("depth")
    tile_rows = object_re.shape[1]
    tile_cols = object_re.shape[2]
    batches = centres.shape[2]
    slot_count = centres.shape[3]
    cosine, sines = tables(frame_size)
    kern_re = jnp.cos(phases)
    kern_im = jnp.sin(phases)
    planes = jnp.stack([object_re[0], object_im[0]])
    padded = padded_2(planes, (("row", 1), ("col", 2)), half_size)
    per_group = batches * slot_count // batches
    centre_px = centres[0, 0]
    slot_ids = jnp.arange(slot_count, dtype=jnp.int32)
    live_mask = (slot_ids[None, :] < occupied[0, 0][:, None]).astype(jnp.float32)
    frames = measured[0, 0]

    def window_at(centre):
        anchor = (jnp.zeros((), jnp.int32), centre[0], centre[1])
        return lax.dynamic_slice(padded, anchor, (2, frame_size, frame_size))

    windows = jax.vmap(jax.vmap(window_at, out_axes=1), out_axes=0)(centre_px).astype(jnp.float32)
    zero_wave = jnp.zeros((2, per_group, frame_size, frame_size), jnp.bfloat16)
    zero_field = jnp.zeros((2, per_group, frame_size, frame_size), jnp.float32)

    def propagate(data_re, data_im, direction):
        freq_re, freq_im = transform(data_re, data_im, cosine, sines, 1.0)
        kept_re, kept_im = complex_mul(freq_re, freq_im, kern_re, direction * kern_im)
        return transform(kept_re, kept_im, cosine, sines, -1.0)

    def carry_on(incoming, window, measure):
        exit_re, exit_im = complex_mul(incoming[0], incoming[1], window[0], window[1])
        out_re, out_im = propagate(exit_re, exit_im, 1.0)
        return (jnp.stack([out_re, out_im]).astype(jnp.bfloat16), zero_field)

    def detect(incoming, window, measure):
        exit_re, exit_im = complex_mul(incoming[0], incoming[1], window[0], window[1])
        freq_re, freq_im = transform(exit_re, exit_im, cosine, sines, 1.0)
        misfit = freq_re * freq_re + freq_im * freq_im - measure
        back_re, back_im = transform(misfit * freq_re, misfit * freq_im, cosine, sines, -1.0)
        return (zero_wave, jnp.stack([back_re, back_im]))

    def standby(incoming, window, measure):
        return (zero_wave, zero_field)

    launch = jnp.broadcast_to(probe[:, None], (2, per_group, frame_size, frame_size))
    steps_total = batches + sections - 1

    def forward_step(step_no, loop_state):
        received, inputs, farside = loop_state
        group_id = step_no - my_section
        active = (group_id >= 0) & (group_id < batches)
        group_at = jnp.clip(group_id, 0, batches - 1)
        target = jnp.where(active, group_at, batches)
        incoming = lax.cond(my_section == 0, lambda: launch, lambda: received.astype(jnp.float32))
        branch = jnp.where(active, jnp.where(my_section == sections - 1, 2, 1), 0)
        outgoing, far_adjoint = lax.switch(
            branch, [standby, carry_on, detect], incoming, windows[group_at], frames[group_at]
        )
        inputs = lax.dynamic_update_index_in_dim(inputs, incoming, target, 0)
        farside = lax.dynamic_update_index_in_dim(farside, far_adjoint, target, 0)
        received = jax.tree.map(
            lambda part, own: part.astype(own.dtype),
            from_behind(as_sent(outgoing), "depth", 1),
            outgoing,
        )
        return (received, inputs, farside)

    stored = jnp.zeros((batches + 1, 2, per_group, frame_size, frame_size), jnp.float32)
    _, inputs, farside = lax.fori_loop(0, steps_total, forward_step, (zero_wave, stored, stored))

    def hand_back(adjoint, window):
        pull_re, pull_im = conj_mul(window[0], window[1], adjoint[0], adjoint[1])
        out_re, out_im = propagate(pull_re, pull_im, -1.0)
        return (jnp.stack([out_re, out_im]).astype(jnp.bfloat16), jnp.stack([pull_re, pull_im]))

    def finish(adjoint, window):
        pull_re, pull_im = conj_mul(window[0], window[1], adjoint[0], adjoint[1])
        return (zero_wave, jnp.stack([pull_re, pull_im]))

    def pause(adjoint, window):
        return (zero_wave, zero_field)

    def backward_step(step_no, loop_state):
        received, gradient, probe_sum = loop_state
        group_id = step_no - (sections - 1 - my_section)
        active = (group_id >= 0) & (group_id < batches)
        group_at = jnp.clip(group_id, 0, batches - 1)
        adjoint = lax.cond(
            my_section == sections - 1,
            lambda: farside[group_at],
            lambda: received.astype(jnp.float32),
        )
        branch = jnp.where(active, jnp.where(my_section == 0, 2, 1), 0)
        outgoing, pulled = lax.switch(
            branch, [pause, hand_back, finish], adjoint, windows[group_at]
        )
        weight = live_mask[group_at] * active.astype(jnp.float32)
        incoming = inputs[group_at]
        grad_re, grad_im = conj_mul(incoming[0], incoming[1], adjoint[0], adjoint[1])
        update = jnp.stack([grad_re, grad_im]) * weight[None, :, None, None]
        places = centre_px[group_at]

        def deposit(slot_no, buffer):
            anchor = (jnp.zeros((), jnp.int32), places[slot_no, 0], places[slot_no, 1])
            current = lax.dynamic_slice(buffer, anchor, (2, frame_size, frame_size))
            addition = lax.dynamic_index_in_dim(update, slot_no, 1, False)
            return lax.dynamic_update_slice(buffer, current + addition, anchor)

        gradient = lax.fori_loop(0, per_group, deposit, gradient)
        anchor_flag = jnp.where(my_section == 0, 1.0, 0.0).astype(jnp.float32)
        probe_sum = probe_sum + jnp.sum(
            pulled * (weight * anchor_flag)[None, :, None, None], axis=1
        )
        received = jax.tree.map(
            lambda part, own: part.astype(own.dtype),
            from_behind(as_sent(outgoing), "depth", -1),
            outgoing,
        )
        return (received, gradient, probe_sum)

    gradient = jnp.zeros((2, tile_rows + 2 * half_size, tile_cols + 2 * half_size), jnp.float32)
    probe_sum = jnp.zeros((2, frame_size, frame_size), jnp.float32)
    _, gradient, probe_sum = lax.fori_loop(
        0, steps_total, backward_step, (zero_wave, gradient, probe_sum)
    )
    extended = padded_2(gradient.astype(jnp.bfloat16), (("row", 1), ("col", 2)), half_size).astype(
        gradient.dtype
    )
    rows_part = extended[:, 2 * half_size : 2 * half_size + tile_rows]
    rows_part = rows_part.at[:, :half_size].add(extended[:, :half_size])
    rows_part = rows_part.at[:, tile_rows - half_size :].add(
        extended[:, tile_rows + 3 * half_size :]
    )
    folded = rows_part[:, :, 2 * half_size : 2 * half_size + tile_cols]
    folded = folded.at[:, :, :half_size].add(rows_part[:, :, :half_size])
    folded = folded.at[:, :, tile_cols - half_size :].add(
        rows_part[:, :, tile_cols + 3 * half_size :]
    )
    tiles_summed = lax.psum(probe_sum, ("row", "col"))
    probe_share = lax.psum_scatter(
        tiles_summed.astype(jnp.bfloat16), "depth", scatter_dimension=1, tiled=True
    ).astype(jnp.float32)
    return (folded[:, None], probe_share)


def solution(mesh):
    in_specs = (
        P(),
        P("depth", "row", "col"),
        P("depth", "row", "col"),
        P(),
        P("row", "col", None, None, None),
        P("row", "col", None),
        P("row", "col", None, None, None, None),
    )
    out_specs = (P(None, "depth", "row", "col"), P(None, "depth", None))
    return jax.shard_map(shards, mesh=mesh, in_specs=in_specs, out_specs=out_specs, check_vma=False)
```

profile of v0, /device:TPU:27, one launch (start us, length us, event | category | flops | bytes accessed | tf_op | source)
XLA Modules:
  0.0 597.5 jit_solution(9488975381769385980)
XLA Ops:
  16.5 9.3 %collective-permute-done.2 = bf16[2,128,1024]{2,1,0:T(8,128)(2,1)S(1)} collective-permute-done((bf16[2,128,1024]{2,1,0:T(8,128)(2,1)}, bf16[2,128,1024]{2,1,0:T(8,128)(2,1)S(1)}, u32[]{:S(2)}, u32[]{:S(2)}) %collective-permute-start.2) | collective-permute-done | bytes 524320 | tf_op jit(solution)/shard_map/ppermute | solution.py:18
  38.5 10.7 %collective-permute-done.5 = bf16[2,768,128]{2,1,0:T(8,128)(2,1)S(1)} collective-permute-done((bf16[2,768,128]{2,1,0:T(8,128)(2,1)S(1)}, bf16[2,768,128]{2,1,0:T(8,128)(2,1)S(1)}, u32[]{:S(2)}, u32[]{:S(2)}) %collective-permute-start.5) | collective-permute-done | bytes 393248 | tf_op jit(solution)/shard_map/ppermute | solution.py:19
  52.3 30.5 %while.82 = (s32[]{:T(128)}, bf16[2,768,1280]{2,1,0:T(8,128)(2,1)}, s32[8,3]{1,0:T(8,128)S(1)}, bf16[8,2,256,256]{3,2,1,0:T(8,128)(2,1)}, s32[]{:T(128)}) while((s32[]{:T(128)}, bf16[2,768,1280]{2,1,0:T(8,128)(2,1)}, s32[8,3]{1,0:T(8,128)S(1)}, bf16[8,2,256,256]{3,2,1,0:T(8,128)(2,1)}, s32[]{:T(128)}) %tuple.318), condition=%wide.while_cond.4, body=%wide.while_body.4.sunk | while | flops 2 | bytes 525429 | solution.py:100
  98.8 132.8 %while.83 = (s32[]{:T(128)}, bf16[2,2,256,256]{3,2,1,0:T(8,128)(2,1)}, f32[5,2,2,256,256]{4,3,2,1,0:T(8,128)}, f32[5,2,2,256,256]{4,3,2,1,0:T(8,128)}, s32[]{:T(...) while((s32[]{:T(128)}, ...), condition=%wide.region_6.7_spmd.clone.clone, body=%wide.region_0.6_spmd.clone.clone.sunk | while | flops 3227648000 | bytes 48759476 | solution.py:150
  123.2 11.2 %collective-permute-done = bf16[2,2,256,256]{3,2,1,0:T(8,128)(2,1)S(1)} collective-permute-done((bf16[2,2,256,256]{3,2,1,0:T(8,128)(2,1)}, bf16[2,2,256,256]{3,2,1,0:T(8,128)(2,1)S(1)}, u32[]{:S(2)}, u32[]{:S(2)}) %collective-permute-start) | collective-permute-done | bytes 524320 | tf_op jit(solution)/shard_map/while/body/eval_jaxpr/ppermute | solution.py:31
  139.6 14.8 %conditional.17 = (bf16[2,2,256,256]{3,2,1,0:T(8,128)(2,1)}, f32[1,2,2,256,256]{4,3,2,1,0:T(8,128)}) conditional(s32[]{:T(128)} %clamp.24, () %tuple.276, (f32[2,2,256,256]{3,2,1,0:T(8,128)S(1)}, f32[2,2,256,256]{2,3,1,0:T(8,128)S(1)}, f32[256,256]{1,0:T(8,128)S(1)}, f32[256,256]{1,0:T(8,128)S(1)}, f32[256,256]{1,0:T(8,128)S(1)}, ...), branch_computations={%region_3.3_spmd, %region_4.4_spmd, %region_5.5_spmd} | conditional | flops 3225419776 | bytes 36175892 | solution.py:137
  163.7 14.8 %conditional.17 = (bf16[2,2,256,256]{3,2,1,0:T(8,128)(2,1)}, f32[1,2,2,256,256]{4,3,2,1,0:T(8,128)}) conditional(s32[]{:T(128)} %clamp.24, () %tuple.276, (f32[2,2,256,256]{3,2,1,0:T(8,128)S(1)}, f32[2,2,256,256]{2,3,1,0:T(8,128)S(1)}, f32[256,256]{1,0:T(8,128)S(1)}, f32[256,256]{1,0:T(8,128)S(1)}, f32[256,256]{1,0:T(8,128)S(1)}, ...), branch_computations={%region_3.3_spmd, %region_4.4_spmd, %region_5.5_spmd} | conditional | flops 3225419776 | bytes 36175892 | solution.py:137
  187.8 14.8 %conditional.17 = (bf16[2,2,256,256]{3,2,1,0:T(8,128)(2,1)}, f32[1,2,2,256,256]{4,3,2,1,0:T(8,128)}) conditional(s32[]{:T(128)} %clamp.24, () %tuple.276, (f32[2,2,256,256]{3,2,1,0:T(8,128)S(1)}, f32[2,2,256,256]{2,3,1,0:T(8,128)S(1)}, f32[256,256]{1,0:T(8,128)S(1)}, f32[256,256]{1,0:T(8,128)S(1)}, f32[256,256]{1,0:T(8,128)S(1)}, ...), branch_computations={%region_3.3_spmd, %region_4.4_spmd, %region_5.5_spmd} | conditional | flops 3225419776 | bytes 36175892 | solution.py:137
  211.9 14.8 %conditional.17 = (bf16[2,2,256,256]{3,2,1,0:T(8,128)(2,1)}, f32[1,2,2,256,256]{4,3,2,1,0:T(8,128)}) conditional(s32[]{:T(128)} %clamp.24, () %tuple.276, (f32[2,2,256,256]{3,2,1,0:T(8,128)S(1)}, f32[2,2,256,256]{2,3,1,0:T(8,128)S(1)}, f32[256,256]{1,0:T(8,128)S(1)}, f32[256,256]{1,0:T(8,128)S(1)}, f32[256,256]{1,0:T(8,128)S(1)}, ...), branch_computations={%region_3.3_spmd, %region_4.4_spmd, %region_5.5_spmd} | conditional | flops 3225419776 | bytes 36175892 | solution.py:137
  236.0 244.4 %while.85 = (s32[]{:T(128)}, bf16[2,2,256,256]{3,2,1,0:T(8,128)(2,1)}, f32[2,768,1280]{2,1,0:T(8,128)}, f32[2,256,256]{1,2,0:T(8,128)}, s32[]{:T(128)}, /*index=...) while((s32[]{:T(128)}, ...), condition=%wide.region_16.17_spmd.clone.clone, body=%wide.region_7.16_spmd.clone.clone.sunk | while | flops 3229155328 | bytes 60294088 | solution.py:204
  238.8 17.1 %conditional.19 = (bf16[2,2,256,256]{3,2,1,0:T(8,128)(2,1)}, f32[2,2,256,256]{2,3,1,0:T(8,128)}) conditional(s32[]{:T(128)} %clamp.25, () %tuple.283, (f32[2,2,256,256]{2,3,1,0:T(8,128)S(1)}, f32[2,2,256,256]{3,2,1,0:T(8,128)S(1)}, f32[256,256]{1,0:T(8,128)S(1)}, f32[256,256]{1,0:T(8,128)S(1)}, f32[256,256]{1,0:T(8,128)S(1)}, ...), branch_computations={%region_10.10_spmd, %region_11.11_spmd.clone, %region_12.12_spmd} | conditional | flops 3225878528 | bytes 40370220 | solution.py:175
  260.2 25.1 %while.86 = (s32[]{:T(128)}, f32[2,768,1280]{2,1,0:T(8,128)}, s32[2,2]{1,0:T(2,128)S(1)}, f32[2,2,256,256]{3,2,0,1:T(8,128)S(1)}, s32[]{:T(128)}, /*index=5*/s32[]{:T(128)}, s32[]{:T(128)}, s32[]{:T(128)}) while((s32[]{:T(128)}, f32[2,768,1280]{2,1,0:T(8,128)}, s32[2,2]{1,0:T(2,128)S(1)}, f32[2,2,256,256]{3,2,0,1:T(8,128)S(1)}, s32[]{:T(128)}, ...), condition=%wide.region_14.14_spmd, body=%wide.region_13.13_spmd.sunk | while | flops 131080 | bytes 2621637 | solution.py:190
  289.8 17.1 %conditional.19 = (bf16[2,2,256,256]{3,2,1,0:T(8,128)(2,1)}, f32[2,2,256,256]{2,3,1,0:T(8,128)}) conditional(s32[]{:T(128)} %clamp.25, () %tuple.283, (f32[2,2,256,256]{2,3,1,0:T(8,128)S(1)}, f32[2,2,256,256]{3,2,1,0:T(8,128)S(1)}, f32[256,256]{1,0:T(8,128)S(1)}, f32[256,256]{1,0:T(8,128)S(1)}, f32[256,256]{1,0:T(8,128)S(1)}, ...), branch_computations={%region_10.10_spmd, %region_11.11_spmd.clone, %region_12.12_spmd} | conditional | flops 3225878528 | bytes 40370220 | solution.py:175
  311.3 25.4 %while.86 = (s32[]{:T(128)}, f32[2,768,1280]{2,1,0:T(8,128)}, s32[2,2]{1,0:T(2,128)S(1)}, f32[2,2,256,256]{3,2,0,1:T(8,128)S(1)}, s32[]{:T(128)}, /*index=5*/s32[]{:T(128)}, s32[]{:T(128)}, s32[]{:T(128)}) while((s32[]{:T(128)}, f32[2,768,1280]{2,1,0:T(8,128)}, s32[2,2]{1,0:T(2,128)S(1)}, f32[2,2,256,256]{3,2,0,1:T(8,128)S(1)}, s32[]{:T(128)}, ...), condition=%wide.region_14.14_spmd, body=%wide.region_13.13_spmd.sunk | while | flops 131080 | bytes 2621637 | solution.py:190
  317.1 6.9 %dynamic_update_slice.35 = f32[2,768,1280]{2,1,0:T(8,128)} dynamic-update-slice(f32[2,768,1280]{2,1,0:T(8,128)} %get-tuple-element.1977, f32[2,256,256]{2,1,0:T(8,128)S(1)} %bitcast_add_fusion.2, s32[]{:T(128)} %constant.330.clone.1..sunk.2..sunk, s32[]{:T(128)S(6)} %select_n.269, s32[]{:T(128)S(6)} %select_n.270) | dynamic-update-slice | bytes 1048580 | tf_op jit(solution)/shard_map/while/body/eval_jaxpr/while/body/eval_jaxpr/dynamic_update_slice | solution.py:188
  329.8 6.8 %dynamic_update_slice.35 = f32[2,768,1280]{2,1,0:T(8,128)} dynamic-update-slice(f32[2,768,1280]{2,1,0:T(8,128)} %get-tuple-element.1977, f32[2,256,256]{2,1,0:T(8,128)S(1)} %bitcast_add_fusion.2, s32[]{:T(128)} %constant.330.clone.1..sunk.2..sunk, s32[]{:T(128)S(6)} %select_n.269, s32[]{:T(128)S(6)} %select_n.270) | dynamic-update-slice | bytes 1048580 | tf_op jit(solution)/shard_map/while/body/eval_jaxpr/while/body/eval_jaxpr/dynamic_update_slice | solution.py:188
  342.2 17.1 %conditional.19 = (bf16[2,2,256,256]{3,2,1,0:T(8,128)(2,1)}, f32[2,2,256,256]{2,3,1,0:T(8,128)}) conditional(s32[]{:T(128)} %clamp.25, () %tuple.283, (f32[2,2,256,256]{2,3,1,0:T(8,128)S(1)}, f32[2,2,256,256]{3,2,1,0:T(8,128)S(1)}, f32[256,256]{1,0:T(8,128)S(1)}, f32[256,256]{1,0:T(8,128)S(1)}, f32[256,256]{1,0:T(8,128)S(1)}, ...), branch_computations={%region_10.10_spmd, %region_11.11_spmd.clone, %region_12.12_spmd} | conditional | flops 3225878528 | bytes 40370220 | solution.py:175
  363.7 24.5 %while.86 = (s32[]{:T(128)}, f32[2,768,1280]{2,1,0:T(8,128)}, s32[2,2]{1,0:T(2,128)S(1)}, f32[2,2,256,256]{3,2,0,1:T(8,128)S(1)}, s32[]{:T(128)}, /*index=5*/s32[]{:T(128)}, s32[]{:T(128)}, s32[]{:T(128)}) while((s32[]{:T(128)}, f32[2,768,1280]{2,1,0:T(8,128)}, s32[2,2]{1,0:T(2,128)S(1)}, f32[2,2,256,256]{3,2,0,1:T(8,128)S(1)}, s32[]{:T(128)}, ...), condition=%wide.region_14.14_spmd, body=%wide.region_13.13_spmd.sunk | while | flops 131080 | bytes 2621637 | solution.py:190
  381.3 6.8 %dynamic_update_slice.35 = f32[2,768,1280]{2,1,0:T(8,128)} dynamic-update-slice(f32[2,768,1280]{2,1,0:T(8,128)} %get-tuple-element.1977, f32[2,256,256]{2,1,0:T(8,128)S(1)} %bitcast_add_fusion.2, s32[]{:T(128)} %constant.330.clone.1..sunk.2..sunk, s32[]{:T(128)S(6)} %select_n.269, s32[]{:T(128)S(6)} %select_n.270) | dynamic-update-slice | bytes 1048580 | tf_op jit(solution)/shard_map/while/body/eval_jaxpr/while/body/eval_jaxpr/dynamic_update_slice | solution.py:188
  393.7 17.1 %conditional.19 = (bf16[2,2,256,256]{3,2,1,0:T(8,128)(2,1)}, f32[2,2,256,256]{2,3,1,0:T(8,128)}) conditional(s32[]{:T(128)} %clamp.25, () %tuple.283, (f32[2,2,256,256]{2,3,1,0:T(8,128)S(1)}, f32[2,2,256,256]{3,2,1,0:T(8,128)S(1)}, f32[256,256]{1,0:T(8,128)S(1)}, f32[256,256]{1,0:T(8,128)S(1)}, f32[256,256]{1,0:T(8,128)S(1)}, ...), branch_computations={%region_10.10_spmd, %region_11.11_spmd.clone, %region_12.12_spmd} | conditional | flops 3225878528 | bytes 40370220 | solution.py:175
  415.1 25.3 %while.86 = (s32[]{:T(128)}, f32[2,768,1280]{2,1,0:T(8,128)}, s32[2,2]{1,0:T(2,128)S(1)}, f32[2,2,256,256]{3,2,0,1:T(8,128)S(1)}, s32[]{:T(128)}, /*index=5*/s32[]{:T(128)}, s32[]{:T(128)}, s32[]{:T(128)}) while((s32[]{:T(128)}, f32[2,768,1280]{2,1,0:T(8,128)}, s32[2,2]{1,0:T(2,128)S(1)}, f32[2,2,256,256]{3,2,0,1:T(8,128)S(1)}, s32[]{:T(128)}, ...), condition=%wide.region_14.14_spmd, body=%wide.region_13.13_spmd.sunk | while | flops 131080 | bytes 2621637 | solution.py:190
  452.2 25.3 %while.86 = (s32[]{:T(128)}, f32[2,768,1280]{2,1,0:T(8,128)}, s32[2,2]{1,0:T(2,128)S(1)}, f32[2,2,256,256]{3,2,0,1:T(8,128)S(1)}, s32[]{:T(128)}, /*index=5*/s32[]{:T(128)}, s32[]{:T(128)}, s32[]{:T(128)}) while((s32[]{:T(128)}, f32[2,768,1280]{2,1,0:T(8,128)}, s32[2,2]{1,0:T(2,128)S(1)}, f32[2,2,256,256]{3,2,0,1:T(8,128)S(1)}, s32[]{:T(128)}, ...), condition=%wide.region_14.14_spmd, body=%wide.region_13.13_spmd.sunk | while | flops 131080 | bytes 2621637 | solution.py:190
  458.1 6.8 %dynamic_update_slice.35 = f32[2,768,1280]{2,1,0:T(8,128)} dynamic-update-slice(f32[2,768,1280]{2,1,0:T(8,128)} %get-tuple-element.1977, f32[2,256,256]{2,1,0:T(8,128)S(1)} %bitcast_add_fusion.2, s32[]{:T(128)} %constant.330.clone.1..sunk.2..sunk, s32[]{:T(128)S(6)} %select_n.269, s32[]{:T(128)S(6)} %select_n.270) | dynamic-update-slice | bytes 1048580 | tf_op jit(solution)/shard_map/while/body/eval_jaxpr/while/body/eval_jaxpr/dynamic_update_slice | solution.py:188
  492.5 67.8 %all-reduce.1 = bf16[2,256,256]{2,1,0:T(8,128)(2,1)} all-reduce(f32[2,256,256]{2,1,0:T(8,128)S(1)} %copy.157), channel_id=1, replica_groups=mesh['depth'=2,'row'=2,'col'=8] {'row','col'}, use_global_device_ids=true, to_apply=%region_17.18 | all-reduce | flops 131072 | bytes 786432 | tf_op jit(solution)/shard_map/psum | solution.py:220
  (423 shorter events, 417.4 us)
Async XLA Ops:
  7.2 9.1 %copy-start.9 = (s32[1,1,4,2,2]{2,4,3,1,0:T(2,128)S(1)}, s32[1,1,4,2,2]{2,4,3,1,0:T(2,128)}, u32[]{:S(2)}) copy-start(s32[1,1,4,2,2]{2,4,3,1,0:T(2,128)} %param.35) | copy-start | bytes 196
  7.2 561.3 %reduce-scatter.2.cloned.1.call-start = ((), (), s32[]{:S(2)}) async-start(), calls=%async_computation.1 | async-start | bytes 393216 | tf_op jit(solution)/shard_map/reduce_scatter | solution.py:221
  8.5 24.6 %copy-start.10 = (s32[1,1,4]{2,1,0:T(1,128)S(1)}, s32[1,1,4]{2,1,0:T(1,128)}, u32[]{:S(2)}) copy-start(s32[1,1,4]{2,1,0:T(1,128)} %param.36) | copy-start | bytes 52
  8.5 24.7 %copy-start.8 = (f32[256,256]{1,0:T(8,128)S(1)}, f32[256,256]{1,0:T(8,128)}, u32[]{:S(2)}) copy-start(f32[256,256]{1,0:T(8,128)} %param.34) | copy-start | bytes 786436
  10.9 14.9 %collective-permute-start.2 = (bf16[2,128,1024]{2,1,0:T(8,128)(2,1)}, bf16[2,128,1024]{2,1,0:T(8,128)(2,1)S(1)}, u32[]{:S(2)}, u32[]{:S(2)}) collective-permute-start(bf16[2,128,1024]{2,1,0:T(8,128)(2,1)} %get-tuple-element.1697), channel_id=1, source_target_pairs={{0,8},{1,9},{2,10},{3,11},{4,12},{5,13},{6,14},{7,15},{16,24},{17,... | collective-permute-start | bytes 1572872 | tf_op jit(solution)/shard_map/ppermute | solution.py:18
  12.2 14.6 %collective-permute-start.3 = (bf16[2,128,1024]{2,1,0:T(8,128)(2,1)}, bf16[2,128,1024]{2,1,0:T(8,128)(2,1)S(1)}, u32[]{:S(2)}, u32[]{:S(2)}) collective-permute-start(bf16[2,128,1024]{2,1,0:T(8,128)(2,1)} %get-tuple-element.1698), channel_id=1, source_target_pairs={{8,0},{9,1},{10,2},{11,3},{12,4},{13,5},{14,6},{15,7},{24,16},{25,... | collective-permute-start | bytes 1572872 | tf_op jit(solution)/shard_map/ppermute | solution.py:19
  26.8 6.3 %copy-start.7 = (bf16[2,128,1024]{2,1,0:T(8,128)(2,1)}, bf16[2,128,1024]{2,1,0:T(8,128)(2,1)S(1)}, u32[]{:S(2)}) copy-start(bf16[2,128,1024]{2,1,0:T(8,128)(2,1)S(1)} %collective-permute-done.3) | copy-start | bytes 1572868
  26.9 11.6 %collective-permute-start.4 = (bf16[2,768,128]{2,1,0:T(8,128)(2,1)S(1)}, bf16[2,768,128]{2,1,0:T(8,128)(2,1)S(1)}, u32[]{:S(2)}, u32[]{:S(2)}) collective-permute-start(bf16[2,768,128]{2,1,0:T(8,128)(2,1)S(1)} %get-tuple-element.1695), channel_id=1, source_target_pairs={{0,1},{1,2},{2,3},{3,4},{4,5},{5,6},{6,7},{8,9},{9,10},{10,11},{11... | collective-permute-start | bytes 1179656 | tf_op jit(solution)/shard_map/ppermute | solution.py:18
  30.1 19.1 %collective-permute-start.5 = (bf16[2,768,128]{2,1,0:T(8,128)(2,1)S(1)}, bf16[2,768,128]{2,1,0:T(8,128)(2,1)S(1)}, u32[]{:S(2)}, u32[]{:S(2)}) collective-permute-start(bf16[2,768,128]{2,1,0:T(8,128)(2,1)S(1)} %get-tuple-element.1696), channel_id=1, source_target_pairs={{1,0},{2,1},{3,2},{4,3},{5,4},{6,5},{7,6},{9,8},{10,9},{11,10},{12... | collective-permute-start | bytes 1179656 | tf_op jit(solution)/shard_map/ppermute | solution.py:19
  119.1 15.3 %collective-permute-start = (bf16[2,2,256,256]{3,2,1,0:T(8,128)(2,1)}, bf16[2,2,256,256]{3,2,1,0:T(8,128)(2,1)S(1)}, u32[]{:S(2)}, u32[]{:S(2)}) collective-permute-start(bf16[2,2,256,256]{3,2,1,0:T(8,128)(2,1)} %get-tuple-element.1923), channel_id=1, source_target_pairs={{0,16},{1,17},{2,18},{3,19},{4,20},{5,21},{6,22},{7,23},{8,24},{9,... | collective-permute-start | bytes 1572872 | tf_op jit(solution)/shard_map/while/body/eval_jaxpr/ppermute | solution.py:31
  154.4 4.1 collective-permute-start
  178.5 4.0 collective-permute-start
  202.6 4.0 collective-permute-start
  226.7 4.1 collective-permute-start
  255.9 30.3 %collective-permute-start.1 = (bf16[2,2,256,256]{3,2,1,0:T(8,128)(2,1)}, bf16[2,2,256,256]{3,2,1,0:T(8,128)(2,1)S(1)}, u32[]{:S(2)}, u32[]{:S(2)}) collective-permute-start(bf16[2,2,256,256]{3,2,1,0:T(8,128)(2,1)} %get-tuple-element.1942), channel_id=1, source_target_pairs={{16,0},{17,1},{18,2},{19,3},{20,4},{21,5},{22,6},{23,7},{24,8},{25... | collective-permute-start | bytes 1572872 | tf_op jit(solution)/shard_map/while/body/eval_jaxpr/ppermute | solution.py:31
  307.0 31.6 %collective-permute-start.1 = (bf16[2,2,256,256]{3,2,1,0:T(8,128)(2,1)}, bf16[2,2,256,256]{3,2,1,0:T(8,128)(2,1)S(1)}, u32[]{:S(2)}, u32[]{:S(2)}) collective-permute-start(bf16[2,2,256,256]{3,2,1,0:T(8,128)(2,1)} %get-tuple-element.1942), channel_id=1, source_target_pairs={{16,0},{17,1},{18,2},{19,3},{20,4},{21,5},{22,6},{23,7},{24,8},{25... | collective-permute-start | bytes 1572872 | tf_op jit(solution)/shard_map/while/body/eval_jaxpr/ppermute | solution.py:31
  359.4 30.7 %collective-permute-start.1 = (bf16[2,2,256,256]{3,2,1,0:T(8,128)(2,1)}, bf16[2,2,256,256]{3,2,1,0:T(8,128)(2,1)S(1)}, u32[]{:S(2)}, u32[]{:S(2)}) collective-permute-start(bf16[2,2,256,256]{3,2,1,0:T(8,128)(2,1)} %get-tuple-element.1942), channel_id=1, source_target_pairs={{16,0},{17,1},{18,2},{19,3},{20,4},{21,5},{22,6},{23,7},{24,8},{25... | collective-permute-start | bytes 1572872 | tf_op jit(solution)/shard_map/while/body/eval_jaxpr/ppermute | solution.py:31
  410.8 31.5 %collective-permute-start.1 = (bf16[2,2,256,256]{3,2,1,0:T(8,128)(2,1)}, bf16[2,2,256,256]{3,2,1,0:T(8,128)(2,1)S(1)}, u32[]{:S(2)}, u32[]{:S(2)}) collective-permute-start(bf16[2,2,256,256]{3,2,1,0:T(8,128)(2,1)} %get-tuple-element.1942), channel_id=1, source_target_pairs={{16,0},{17,1},{18,2},{19,3},{20,4},{21,5},{22,6},{23,7},{24,8},{25... | collective-permute-start | bytes 1572872 | tf_op jit(solution)/shard_map/while/body/eval_jaxpr/ppermute | solution.py:31
  447.9 31.5 %collective-permute-start.1 = (bf16[2,2,256,256]{3,2,1,0:T(8,128)(2,1)}, bf16[2,2,256,256]{3,2,1,0:T(8,128)(2,1)S(1)}, u32[]{:S(2)}, u32[]{:S(2)}) collective-permute-start(bf16[2,2,256,256]{3,2,1,0:T(8,128)(2,1)} %get-tuple-element.1942), channel_id=1, source_target_pairs={{16,0},{17,1},{18,2},{19,3},{20,4},{21,5},{22,6},{23,7},{24,8},{25... | collective-permute-start | bytes 1572872 | tf_op jit(solution)/shard_map/while/body/eval_jaxpr/ppermute | solution.py:31
  480.4 11.9 %copy-start.5 = (f32[2,256,256]{1,2,0:T(8,128)S(1)}, f32[2,256,256]{1,2,0:T(8,128)}, u32[]{:S(2)}) copy-start(f32[2,256,256]{1,2,0:T(8,128)} %get-tuple-element.1092) | copy-start | bytes 1572868
  487.0 73.4 %collective-permute-start.6 = (bf16[2,128,1280]{2,1,0:T(8,128)(2,1)}, bf16[2,128,1280]{2,1,0:T(8,128)(2,1)S(1)}, u32[]{:S(2)}, u32[]{:S(2)}) collective-permute-start(bf16[2,128,1280]{2,1,0:T(8,128)(2,1)} %get-tuple-element.1693), channel_id=1, source_target_pairs={{0,8},{1,9},{2,10},{3,11},{4,12},{5,13},{6,14},{7,15},{16,24},{17,... | collective-permute-start | bytes 1966088 | tf_op jit(solution)/shard_map/ppermute | solution.py:18
  488.2 72.2 %collective-permute-start.7 = (bf16[2,128,1280]{2,1,0:T(8,128)(2,1)S(1)}, bf16[2,128,1280]{2,1,0:T(8,128)(2,1)S(1)}, u32[]{:S(2)}, u32[]{:S(2)}) collective-permute-start(bf16[2,128,1280]{2,1,0:T(8,128)(2,1)S(1)} %get-tuple-element.1694), channel_id=1, source_target_pairs={{8,0},{9,1},{10,2},{11,3},{12,4},{13,5},{14,6},{15,7},{24,16},{25,... | collective-permute-start | bytes 1966088 | tf_op jit(solution)/shard_map/ppermute | solution.py:19
  561.7 10.9 %collective-permute-start.8 = (bf16[2,1024,128]{2,1,0:T(8,128)(2,1)S(1)}, bf16[2,1024,128]{2,1,0:T(8,128)(2,1)S(1)}, u32[]{:S(2)}, u32[]{:S(2)}) collective-permute-start(bf16[2,1024,128]{2,1,0:T(8,128)(2,1)S(1)} %get-tuple-element.1691), channel_id=1, source_target_pairs={{0,1},{1,2},{2,3},{3,4},{4,5},{5,6},{6,7},{8,9},{9,10},{10,11},{11... | collective-permute-start | bytes 1572872 | tf_op jit(solution)/shard_map/ppermute | solution.py:18
  563.6 14.5 %collective-permute-start.9 = (bf16[2,1024,128]{2,1,0:T(8,128)(2,1)S(1)}, bf16[2,1024,128]{2,1,0:T(8,128)(2,1)S(1)}, u32[]{:S(2)}, u32[]{:S(2)}) collective-permute-start(bf16[2,1024,128]{2,1,0:T(8,128)(2,1)S(1)} %get-tuple-element.1692), channel_id=1, source_target_pairs={{1,0},{2,1},{3,2},{4,3},{5,4},{6,5},{7,6},{9,8},{10,9},{11,10},{12... | collective-permute-start | bytes 1572872 | tf_op jit(solution)/shard_map/ppermute | solution.py:19
  (17 other events, 16.8 us)
Sparse Core Ops, SparseCore 0:
  560.5 7.8 reduce-scatter.1
where the time goes:
time: 606 us; the launch traced here: 597 us
  local copies, waits for them, and re-layouts  195 us (32%)
  other arithmetic  107 us (18%)
  matrix products  76.9 us (13%)
  blocking collectives  67.8 us (11%)
  loops' own time  55.4 us (9%)
  waiting for transfers between devices  45.1 us (7%)
  starting transfers between devices  36 us (6%)
  between operations  14.6 us (2%)
    psum x1, blocking collectives, shards(): tiles_summed = lax.psum(probe_sum, ('row', 'col'))  67.8 us
    dynamic_update_slice x10, local copies, waits for them, and re-layouts, deposit(): return lax.dynamic_update_slice(buffer, current + addition, anchor)  67.1 us
    dot_general x64, matrix products, product(): return jnp.einsum('bjk,kl->bjl', data, matrix, precision=precise)  43.7 us
    another operation x5, loops' own time, backward_step(): gradient = lax.fori_loop(0, per_group, deposit, gradient)  39 us
    dot_general x64, matrix products, product(): return jnp.einsum('jk,bkl->bjl', matrix, data, precision=precise)  33.2 us
    gather x24, local copies, waits for them, and re-layouts  30.5 us
    ppermute x4, waiting for transfers between devices, padded_2(): after = lax.ppermute(first, axis, down)  17.2 us
    mul x14, other arithmetic, tables(): return (jnp.cos(angles) * scaling, jnp.sin(angles) * scaling)  17 us
  transfers between devices with their start and end apart: 19, of which 8 were waited for; matrix products, arithmetic and copies ran while one was open for 21% of the time, Pallas kernels for 0%

commit v1 on v0

v1 whole, which is shorter than its diff:
```python
import functools

import jax
import jax.numpy as jnp
import numpy as np
from jax import lax
from jax.experimental import pallas as pl
from jax.experimental.pallas import tpu as pltpu
from jax.sharding import PartitionSpec as P

f32 = jnp.float32
bf16 = jnp.bfloat16
ROWS = 16
LANES = 128
HBM = pl.BlockSpec(memory_space=pl.ANY)
SMEM = pl.BlockSpec(memory_space=pltpu.SMEM)
LIMIT = 56 * 1024 * 1024


def dft_tables(size):
    half = size // 2
    rows = np.arange(half)[:, None]
    cols = np.arange(half)[None, :]

    def packed(turns):
        angle = -2.0 * np.pi * (turns % size) / size
        re, im = np.cos(angle) / np.sqrt(size), np.sin(angle) / np.sqrt(size)
        return np.block([[re, im], [-im, re]])

    even, odd = packed(rows * 2 * cols), packed(rows * (2 * cols + 1))
    full = np.stack([even, odd, even.T, odd.T]).astype(np.float32)
    high = full.astype(jnp.bfloat16)
    low = (full - high.astype(np.float32)).astype(jnp.bfloat16)
    return np.stack([high, low], axis=1)


def sorting_table(size):
    order = np.concatenate([np.arange(0, size, 2), np.arange(1, size, 2)])
    table = np.zeros((size, size), np.float32)
    table[order, np.arange(size)] = 1.0
    return table.astype(jnp.bfloat16)


def split(x):
    high = x.astype(bf16)
    return high, (x - high.astype(f32)).astype(bf16)


def dot3(left, right):
    lhs = jnp.concatenate([left[0], left[0], left[1]], axis=1)
    rhs = jnp.concatenate([right[0], right[1], right[0]], axis=0)
    return jnp.dot(lhs, rhs, preferred_element_type=f32)


def rows_of(*parts):
    return jnp.concatenate(parts, axis=0)


def cols_of(*parts):
    return jnp.concatenate(parts, axis=1)


def prep_kernel(places, order_t, probe, *refs):
    step = pl.program_id(0)
    size = probe.shape[-1]
    half = size // 2
    blocks = size // LANES
    phases, frames = refs[:blocks], refs[blocks : 2 * blocks]
    kern, sorted_frames, waves = refs[2 * blocks :]

    def halved(parts, at):
        ids = [(at, pl.ds(start, half, stride=2), slice(None)) for start in range(2)]
        return rows_of(*(cols_of(*(part[i] for part in parts)) for i in ids))

    def in_order(rows):
        first, rest = split(rows)
        second, third = split(rows - first.astype(f32))
        table = order_t[...]
        return jnp.dot(
            cols_of(first, second, third), rows_of(table, table, table), preferred_element_type=f32
        )

    @pl.when(step == 0)
    def _():
        angles = in_order(halved(phases, 0))
        kern[0] = jnp.cos(angles)
        kern[1] = jnp.sin(angles)

    sorted_frames[0] = in_order(halved(frames, 0))
    down = places[2 * step] % ROWS
    across = places[2 * step + 1] % LANES
    for plane in range(2):
        moved = pltpu.roll(probe[plane], across, axis=1)
        waves[0, plane] = pltpu.roll(moved, down, axis=0)


def prepare(places, probe, phases, frames):
    count, size = frames.shape[0], phases.shape[-1]
    blocks = size // LANES
    full = lambda *shape: pl.BlockSpec(shape, lambda i: (0,) * len(shape))
    return pl.pallas_call(
        prep_kernel,
        grid=(count,),
        in_specs=[
            SMEM,
            full(size, size),
            full(2, size, size),
            *(pl.BlockSpec((1, size, LANES), lambda i, b=b: (0, 0, b)) for b in range(blocks)),
            *(pl.BlockSpec((1, size, LANES), lambda i, b=b: (i, 0, b)) for b in range(blocks)),
        ],
        out_specs=[
            full(2, size, size),
            pl.BlockSpec((1, size, size), lambda i: (i, 0, 0)),
            pl.BlockSpec((1, 2, size, size), lambda i: (i, 0, 0, 0)),
        ],
        out_shape=[
            jax.ShapeDtypeStruct((2, size, size), f32),
            jax.ShapeDtypeStruct((count, size, size), f32),
            jax.ShapeDtypeStruct((count, 2, size, size), f32),
        ],
        compiler_params=pltpu.CompilerParams(vmem_limit_bytes=LIMIT),
        cost_estimate=pl.CostEstimate(
            flops=2 * (count + 1) * 3 * size**3,
            bytes_accessed=4 * size * size * (4 * count + 6),
            transcendentals=2 * size * size,
        ),
        name="prepare",
    )(
        places,
        jnp.asarray(sorting_table(size)),
        probe,
        *[phases[None]] * blocks,
        *[frames] * blocks,
    )


def spot(places, at, size):
    row, col = places[2 * at], places[2 * at + 1]
    down, across = row % ROWS, col % LANES
    top = pl.multiple_of(row - down, ROWS)
    left = pl.multiple_of(col - across, LANES)
    return down, across, pl.ds(top, size + ROWS), pl.ds(left, size + LANES)


def gather_kernel(
    spots, edges, half, places, offsets, tile_re, tile_im, *rest
):
    strips, (mine, other, padded, sems) = rest[:-4], rest[-4:]
    tile_rows, tile_cols = tile_re.shape[1:]
    size = mine.shape[-1]
    body = (pl.ds(half, tile_rows), pl.ds(half, tile_cols))
    copies = []

    def bring(source, target):
        copies.append(pltpu.make_async_copy(source, target, sems.at[len(copies)]))
        copies[-1].start()

    bring(tile_re.at[0], padded.at[(0,) + body])
    bring(tile_im.at[0], padded.at[(1,) + body])
    columns = {-1: pl.ds(0, half), 0: body[1], 1: pl.ds(half + tile_cols, half)}
    for (side, across), strip in zip(edges, strips):
        if side is None:
            down = body[0]
        else:
            down = pl.ds(pl.multiple_of(offsets[side], half), half)
        bring(strip, padded.at[:, down, columns[across]])
    for copy in copies:
        copy.wait()

    sections = 2
    lane = lax.broadcasted_iota(jnp.int32, (size + ROWS, LANES), 1)
    row = lax.broadcasted_iota(jnp.int32, (ROWS, size), 0)
    here = offsets[len(offsets_names(edges))]

    def cut(at, target, place):
        down, across, tall, wide = spot(places, at, size)
        for plane in range(2):
            block = padded[plane, tall, wide].astype(f32)
            first = jnp.where(lane < across, block[:, size:], block[:, :LANES])
            block = cols_of(first, block[:, LANES:size])
            first = jnp.where(row < down, block[size:], block[:ROWS])
            target[place, plane] = rows_of(first, block[ROWS:size]).astype(bf16)

    def one(place, carry):
        cut(sections * place + here, mine, place)
        cut(sections * place + 1 - here, other, place)
        return carry

    lax.fori_loop(0, spots // sections, one, 0)


def offsets_names(edges):
    return sorted({side for side, _ in edges if side is not None})


def gather(places, offsets, tile_re, tile_im, edges, strips, size):
    half = size // 2
    spots = places.shape[0] // 2
    tile_rows, tile_cols = tile_re.shape[1:]
    shape = jax.ShapeDtypeStruct((spots // 2, 2, size, size), bf16)
    vmem = pl.BlockSpec(memory_space=pltpu.VMEM)
    return pl.pallas_call(
        functools.partial(gather_kernel, spots, edges, half),
        in_specs=[SMEM, SMEM] + [HBM] * (2 + len(strips)),
        out_specs=[vmem, vmem],
        out_shape=[shape, shape],
        scratch_shapes=[
            pltpu.VMEM((2, tile_rows + 2 * half, tile_cols + 2 * half), bf16),
            pltpu.SemaphoreType.DMA((2 + len(strips),)),
        ],
        compiler_params=pltpu.CompilerParams(vmem_limit_bytes=LIMIT),
        name="gather",
    )(places, offsets, tile_re, tile_im, *strips)


def chain_kernel(
    group, places, live, here, tables, kern, mine, theirs, frames, waves,
    keep, send, pulled, windows, middle, terms, sems,
):
    step = pl.program_id(0)
    steps = pl.num_programs(0)
    size = kern.shape[-1]
    half = size // 2
    me = here[0]

    def fetch(at, which):
        source, slot = ((mine, me), (theirs, 1 - me))[which]
        rows = pl.ds(at * group, group)
        return pltpu.make_async_copy(
            source.at[rows], windows.at[at, slot], sems.at[2 * at + which]
        )

    @pl.when(step == 0)
    def _():
        for at in range(windows.shape[0]):
            fetch(at, 0).start()
            fetch(at, 1).start()
        pulled[...] = jnp.zeros_like(pulled)

    fetch(step, 0).wait()
    fetch(step, 1).wait()

    def table(which):
        return tables[which, 0], tables[which, 1]

    def forward(re, im):
        halves = []
        for sign, which in ((1, 2), (-1, 3)):
            if sign > 0:
                part = rows_of(re[:half] + re[half:], im[:half] + im[half:])
            else:
                part = rows_of(re[:half] - re[half:], im[:half] - im[half:])
            halves.append(dot3(table(which), split(part)))
        outs = []
        for sign, which in ((1, 0), (-1, 1)):
            parts = []
            for out in halves:
                re, im = out[:half], out[half:]
                if sign > 0:
                    parts.append(cols_of(re[:, :half] + re[:, half:], im[:, :half] + im[:, half:]))
                else:
                    parts.append(cols_of(re[:, :half] - re[:, half:], im[:, :half] - im[:, half:]))
            outs.append(dot3(split(rows_of(*parts)), table(which)))
        return outs

    def inverse(even, odd):
        first = dot3(split(even), table(2))
        second = dot3(split(odd), table(3))
        plus, minus = first + second, first - second
        re = cols_of(plus[:, :half], minus[:, :half])
        im = cols_of(plus[:, half:], minus[:, half:])
        first = dot3(table(0), split(rows_of(re[:half], im[:half])))
        second = dot3(table(1), split(rows_of(re[half:], im[half:])))
        plus, minus = first + second, first - second
        return rows_of(plus[:half], minus[:half]), rows_of(plus[half:], minus[half:])

    def propagate(re, im, sign):
        outs = []
        for at, part in enumerate(forward(re, im)):
            cols = slice(at * half, (at + 1) * half)
            kre, kim = kern[0, :, cols], kern[1, :, cols] * sign
            re, im = part[:, :half], part[:, half:]
            outs.append(cols_of(re * kre - im * kim, re * kim + im * kre))
        return inverse(*outs)

    def rounded(x):
        return x.astype(bf16).astype(f32)

    def window(slot, at):
        return windows[step, slot, at, 0].astype(f32), windows[step, slot, at, 1].astype(f32)

    for at in range(group):
        wre, wim = window(0, at)
        pre, pim = waves[at, 0], waves[at, 1]
        re, im = propagate(pre * wre - pim * wim, pre * wim + pim * wre, 1.0)
        middle[at, 0] = re.astype(bf16)
        middle[at, 1] = im.astype(bf16)

    for at in range(group):
        wre, wim = window(1, at)
        pre, pim = middle[at, 0].astype(f32), middle[at, 1].astype(f32)
        back = []
        for k, part in enumerate(forward(pre * wre - pim * wim, pre * wim + pim * wre)):
            re, im = part[:, :half], part[:, half:]
            misfit = re * re + im * im - frames[at, :, k * half : (k + 1) * half]
            back.append(cols_of(re * misfit, im * misfit))
        cre, cim = inverse(*back)
        pre, pim = middle[at, 0].astype(f32), middle[at, 1].astype(f32)
        terms[1, at, 0] = pre * cre + pim * cim
        terms[1, at, 1] = pre * cim - pim * cre
        wre, wim = window(1, at)
        re, im = propagate(wre * cre + wim * cim, wre * cim - wim * cre, -1.0)
        cre, cim = rounded(re), rounded(im)
        pre, pim = waves[at, 0], waves[at, 1]
        terms[0, at, 0] = pre * cre + pim * cim
        terms[0, at, 1] = pre * cim - pim * cre
        wre, wim = window(0, at)
        spot_at = step * group + at
        up = (size - places[2 * spot_at] % ROWS) % size
        back_by = (size - places[2 * spot_at + 1] % LANES) % size
        weight = live[spot_at].astype(f32)
        for plane, value in enumerate((wre * cre + wim * cim, wre * cim - wim * cre)):
            value = pltpu.roll(pltpu.roll(value * weight, back_by, axis=1), up, axis=0)
            pulled[plane] += value

    keep[...] = terms[me]
    send[...] = terms[1 - me].astype(bf16)


def chain(places, live, here, kern, mine, theirs, frames, waves, group):
    count, size = frames.shape[0], frames.shape[-1]
    full = lambda *shape: pl.BlockSpec(shape, lambda i: (0,) * len(shape))
    block = pl.BlockSpec((group, 2, size, size), lambda i: (i, 0, 0, 0))
    return pl.pallas_call(
        functools.partial(chain_kernel, group),
        grid=(count // group,),
        in_specs=[
            SMEM,
            SMEM,
            SMEM,
            full(4, 2, size, size),
            full(2, size, size),
            HBM,
            HBM,
            pl.BlockSpec((group, size, size), lambda i: (i, 0, 0)),
            block,
        ],
        out_specs=[block, block, full(2, size, size)],
        out_shape=[
            jax.ShapeDtypeStruct((count, 2, size, size), f32),
            jax.ShapeDtypeStruct((count, 2, size, size), bf16),
            jax.ShapeDtypeStruct((2, size, size), f32),
        ],
        scratch_shapes=[
            pltpu.VMEM((count // group, 2, group, 2, size, size), bf16),
            pltpu.VMEM((group, 2, size, size), bf16),
            pltpu.VMEM((2, group, 2, size, size), f32),
            pltpu.SemaphoreType.DMA((2 * (count // group),)),
        ],
        compiler_params=pltpu.CompilerParams(vmem_limit_bytes=LIMIT),
        name="chain",
    )(places, live, here, jnp.asarray(dft_tables(size)), kern, mine, theirs, frames, waves)


def scatter_kernel(
    spots, edges, half, places, live, offsets, kept, arrived, tile, *rest
):
    strips, (total, sems) = rest[:-2], rest[-2:]
    size = kept.shape[-1]
    tile_rows, tile_cols = tile.shape[1:]
    sections = 2
    here = offsets[len(offsets_names(edges))]
    total[...] = jnp.zeros_like(total)
    lane = lax.broadcasted_iota(jnp.int32, (size, LANES), 1)
    row = lax.broadcasted_iota(jnp.int32, (ROWS, size + LANES), 0)

    def add(at, source, place):
        down, across, tall, wide = spot(places, at, size)

        @pl.when(live[at] > 0)
        def _():
            for plane in range(2):
                value = source[place, plane].astype(f32)
                first = value[:, :LANES]
                inside = lane >= across
                value = cols_of(
                    jnp.where(inside, first, 0.0), value[:, LANES:], jnp.where(inside, 0.0, first)
                )
                first = value[:ROWS]
                inside = row >= down
                value = rows_of(
                    jnp.where(inside, first, 0.0), value[ROWS:], jnp.where(inside, 0.0, first)
                )
                total[plane, tall, wide] += value

    def one(place, carry):
        add(sections * place + here, kept, place)
        add(sections * place + 1 - here, arrived, place)
        return carry

    lax.fori_loop(0, spots // sections, one, 0)
    body = (pl.ds(half, tile_rows), pl.ds(half, tile_cols))
    copy = pltpu.make_async_copy(total.at[(slice(None),) + body], tile, sems.at[0])
    copy.start()
    columns = {-1: pl.ds(0, half), 0: body[1], 1: pl.ds(half + tile_cols, half)}
    for (side, across), strip in zip(edges, strips):
        if side is None:
            rows = body[0]
        else:
            rows = pl.ds(pl.multiple_of(offsets[side], half), half)
        for plane in range(2):
            strip[plane] = total[plane, rows, columns[across]].astype(bf16)
    copy.wait()


def scatter(places, live, offsets, kept, arrived, edges, tile_rows, tile_cols):
    size = kept.shape[-1]
    half = size // 2
    spots = places.shape[0] // 2
    vmem = pl.BlockSpec(memory_space=pltpu.VMEM)
    shapes = [
        jax.ShapeDtypeStruct(
            (2, tile_rows if side is None else half, half if across else tile_cols), bf16
        )
        for side, across in edges
    ]
    return pl.pallas_call(
        functools.partial(scatter_kernel, spots, edges, half),
        in_specs=[SMEM, SMEM, SMEM, vmem, vmem],
        out_specs=[HBM] + [vmem] * len(edges),
        out_shape=[jax.ShapeDtypeStruct((2, tile_rows, tile_cols), f32)] + shapes,
        scratch_shapes=[
            pltpu.VMEM((2, tile_rows + 2 * half, tile_cols + 2 * half), f32),
            pltpu.SemaphoreType.DMA((1,)),
        ],
        compiler_params=pltpu.CompilerParams(vmem_limit_bytes=LIMIT),
        name="scatter",
    )(places, live, offsets, kept, arrived)


def border_kernel(edges, half, sides, offsets, tile_in, *rest):
    strips, (tile, total, in_sem, out_sem) = rest[:-4], rest[-4:]
    tile_rows, tile_cols = tile.shape[1:]
    copy = pltpu.make_async_copy(tile_in, total, in_sem)
    copy.start()
    copy.wait()
    columns = {
        -1: pl.ds(0, half),
        0: pl.ds(0, tile_cols),
        1: pl.ds(tile_cols - half, half),
    }
    for (side, across), strip in zip(edges, strips):
        if side is None:
            rows = pl.ds(0, tile_rows)
        else:
            rows = pl.ds(pl.multiple_of(offsets[side], half), half)
        for plane in range(2):
            total[plane, rows, columns[across]] += strip[plane].astype(f32)
    copy = pltpu.make_async_copy(total, tile, out_sem)
    copy.start()
    copy.wait()


def add_borders(offsets, tile, edges, strips, half):
    vmem = pl.BlockSpec(memory_space=pltpu.VMEM)
    return pl.pallas_call(
        functools.partial(border_kernel, edges, half, None),
        in_specs=[SMEM, HBM] + [vmem] * len(strips),
        out_specs=HBM,
        out_shape=jax.ShapeDtypeStruct(tile.shape, f32),
        scratch_shapes=[
            pltpu.VMEM(tile.shape, f32),
            pltpu.SemaphoreType.DMA,
            pltpu.SemaphoreType.DMA,
        ],
        compiler_params=pltpu.CompilerParams(vmem_limit_bytes=LIMIT),
        name="borders",
    )(offsets, tile, *strips)


def routes(edges, sides, rows, cols):
    result = []
    for side, across in edges:
        pairs = []
        for r in range(rows):
            if side is None:
                to_row = r
            elif rows == 2:
                to_row = 1 - r
            else:
                to_row = r + sides[side]
            for c in range(cols):
                to_col = c + across
                if 0 <= to_row < rows and 0 <= to_col < cols:
                    pairs.append((r * cols + c, to_row * cols + to_col))
        result.append(pairs)
    return result


def summed(block, axis):
    size = lax.axis_size(axis)
    if size & (size - 1):
        return lax.psum(block, axis)
    step = 1
    while step < size:
        block = block + lax.ppermute(block, axis, [(i, i ^ step) for i in range(size)])
        step *= 2
    return block


def shards(probe, object_re, object_im, phases, centres, occupied, measured):
    size = probe.shape[1]
    half = size // 2
    rows, cols = lax.axis_size("row"), lax.axis_size("col")
    sections = lax.axis_size("depth")
    assert sections == 2 and object_re.shape[0] == 1
    here = lax.axis_index("depth").astype(jnp.int32)
    row_at = lax.axis_index("row").astype(jnp.int32)
    tile_rows, tile_cols = object_re.shape[1:]
    batches, slots = centres.shape[2:4]
    spots = batches * slots
    count = spots // sections

    places = centres.reshape(2 * spots)
    slot_ids = jnp.arange(slots, dtype=jnp.int32)
    live = (slot_ids[None, :] < occupied[0, 0][:, None]).astype(jnp.int32)
    my_places = lax.dynamic_index_in_dim(
        centres.reshape(count, sections, 2), here, 1, False
    ).reshape(2 * count)
    my_live = lax.dynamic_index_in_dim(live.reshape(count, sections), here, 1, False)
    live = live.reshape(spots)
    frames = lax.dynamic_index_in_dim(
        measured.reshape(count, sections, size, size), here, 1, False
    )

    if rows == 1:
        sides, from_rows, pad_rows, fold_rows = [], [], [], []
    elif rows == 2:
        sides = [0]
        from_rows = [jnp.where(row_at == 0, tile_rows - half, 0)]
        pad_rows = [jnp.where(row_at == 0, tile_rows + half, 0)]
        fold_rows = from_rows
    else:
        sides = [1, -1]
        from_rows = [jnp.int32(tile_rows - half), jnp.int32(0)]
        pad_rows = [jnp.int32(0), jnp.int32(tile_rows + half)]
        fold_rows = [jnp.int32(0), jnp.int32(tile_rows - half)]
    edges = [(side, 0) for side in range(len(sides))]
    edges += [(None, 1), (None, -1)]
    edges += [(side, across) for side in range(len(sides)) for across in (1, -1)]
    paths = routes(edges, sides, rows, cols)
    both = ("row", "col")

    planes = jnp.stack([object_re[0], object_im[0]])
    strips = []
    for (side, across), path in zip(edges, paths):
        wide = tile_cols if across == 0 else half
        left = tile_cols - half if across == 1 else 0
        tall = tile_rows if side is None else half
        top = 0 if side is None else from_rows[side]
        strip = lax.dynamic_slice(planes, (0, top, left), (2, tall, wide))
        strips.append(lax.ppermute(strip, both, path))
    landed = [(side, -across) for side, across in edges]
    pads = jnp.stack(pad_rows + [here]).astype(jnp.int32)
    kern, sorted_frames, waves = prepare(my_places, probe, phases, frames)
    mine, other = gather(places, pads, object_re, object_im, landed, strips, size)
    across_depth = [(i, 1 - i) for i in range(sections)]
    theirs = lax.ppermute(other, "depth", across_depth)
    keep, send, pulled = chain(
        my_places, my_live, here.reshape(1), kern, mine, theirs, sorted_frames, waves, 2
    )
    arrived = lax.ppermute(send, "depth", across_depth)

    share = size // sections
    kept_rows = lax.dynamic_slice_in_dim(pulled, here * share, share, 1)
    sent_rows = lax.dynamic_slice_in_dim(pulled, (1 - here) * share, share, 1)
    probe_part = kept_rows + lax.ppermute(
        sent_rows.astype(bf16), "depth", across_depth
    ).astype(f32)

    if rows == 2:
        out_rows = pad_rows
    else:
        out_rows = pad_rows[::-1]
    outs = jnp.stack(out_rows + [here]).astype(jnp.int32)
    tile, *own = scatter(places, live, outs, keep, arrived, edges, tile_rows, tile_cols)
    added = [lax.ppermute(strip, both, path) for strip, path in zip(own, paths)]
    folds = jnp.stack(fold_rows + [here]).astype(jnp.int32)
    gradient = add_borders(folds, tile, landed, added, half)
    probe_share = summed(summed(probe_part, "row"), "col")
    return (gradient[:, None], probe_share)


def solution(mesh):
    in_specs = (
        P(),
        P("depth", "row", "col"),
        P("depth", "row", "col"),
        P(),
        P("row", "col", None, None, None),
        P("row", "col", None),
        P("row", "col", None, None, None, None),
    )
    out_specs = (P(None, "depth", "row", "col"), P(None, "depth", None))
    return jax.shard_map(shards, mesh=mesh, in_specs=in_specs, out_specs=out_specs, check_vma=False)
```

time: 606 us -> 126 us (0.21)
  the two profiles are of different devices: /device:TPU:27 before, /device:TPU:0 now
where the time goes in v1:
time: 126 us
  Pallas kernels  43.3 us (34%)
  starting transfers between devices  36.7 us (29%)
  waiting for transfers between devices  24.4 us (19%)
  local copies, waits for them, and re-layouts  16.4 us (13%)
  other arithmetic  3.97 us (3%)
    pallas_call x1, Pallas kernels, chain(): pl.pallas_call(functools.partial(chain_kernel, group), grid=(count // gro...  21.5 us
    ppermute x5, starting transfers between devices, shards(): strips.append(lax.ppermute(strip, both, path))  16.3 us
    ppermute x4, waiting for transfers between devices, summed(): lax.ppermute(block, axis, [(i, i ^ step) for i in range(size)])  16.2 us
    ppermute x5, starting transfers between devices, shards(): added = [lax.ppermute(strip, both, path) for strip, path in zip(own, paths)]  11 us
    ppermute x4, starting transfers between devices, summed(): lax.ppermute(block, axis, [(i, i ^ step) for i in range(size)])  8.79 us
    unnamed x32, local copies, waits for them, and re-layouts  6.3 us
    pallas_call x1, Pallas kernels, prepare(): pl.pallas_call(prep_kernel, grid=(count,), in_specs=[SMEM, full(size, siz...  5.88 us
    pallas_call x1, Pallas kernels, add_borders(): pl.pallas_call(functools.partial(border_kernel, edges, half, None), in_sp...  5.87 us
  transfers between devices with their start and end apart: 17, of which 7 were waited for; matrix products, arithmetic and copies ran while one was open for 10% of the time, Pallas kernels for 9%

profile of v1, /device:TPU:0, one launch (start us, length us, event | category | flops | bytes accessed | tf_op | source)
XLA Modules:
  0.0 125.8 jit_solution(13960504002129567381)
XLA Ops:
  0.7 2.4 %constant_dynamic-update-slice_fusion.1 = bf16[2,512,1024]{2,1,0:T(8,128)(2,1)} fusion(bf16[1,512,1024]{2,1,0:T(8,128)(2,1)} %tile_re.1), kind=kLoop, calls=%fused_computation.4 | loop fusion | bytes 2097152
  5.2 3.0 %collective-permute-start = (bf16[2,128,1024]{2,1,0:T(8,128)(2,1)S(1)}, bf16[2,128,1024]{2,1,0:T(8,128)(2,1)S(1)}, u32[]{:S(2)}, u32[]{:S(2)}) collective-permute-start(bf16[2,128,1024]{2,1,0:T(8,128)(2,1)S(1)} %constant_dynamic-slice_fusion.2), channel_id=1, source_target_pairs={{0,8},{1,9},{2,10},{3,11},{4,12},{5,13},{6,14},{7,15},{8,0},{9,1},... | collective-permute-start | bytes 1572872 | tf_op jit(solution)/shard_map/ppermute | solution.py:562
  8.2 1.8 %fusion.1 = (bf16[2,512,128]{2,1,0:T(8,128)(2,1)}, bf16[2,512,128]{2,1,0:T(8,128)(2,1)}) fusion(bf16[2,512,1024]{2,1,0:T(8,128)(2,1)} %constant_dynamic-update-slice_fusion), kind=kLoop, calls=%fused_computation.14 | loop fusion | bytes 1048576 | tf_op jit(solution)/shard_map/dynamic_slice | solution.py:561
  11.3 5.3 %collective-permute-start.1 = (bf16[2,512,128]{2,1,0:T(8,128)(2,1)}, bf16[2,512,128]{2,1,0:T(8,128)(2,1)}, u32[]{:S(2)}, u32[]{:S(2)}) collective-permute-start(bf16[2,512,128]{2,1,0:T(8,128)(2,1)} %get-tuple-element.37), channel_id=1, source_target_pairs={{0,1},{1,2},{2,3},{3,4},{4,5},{5,6},{6,7},{8,9},{9,10},{10,11},{11... | collective-permute-start | bytes 786440 | tf_op jit(solution)/shard_map/ppermute | solution.py:562
  16.6 1.5 %constant_dynamic-slice_fusion = (bf16[2,128,128]{2,1,0:T(8,128)(2,1)}, bf16[2,128,128]{2,1,0:T(8,128)(2,1)}) fusion(bf16[2,512,1024]{2,1,0:T(8,128)(2,1)} %constant_dynamic-update-slice_fusion, s32[]{:T(128)} %select_n.24), kind=kLoop, calls=%fused_computation.5 | loop fusion | bytes 262148 | tf_op jit(solution)/shard_map/dynamic_slice | solution.py:561
  19.4 5.4 %collective-permute-start.3 = (bf16[2,128,128]{2,1,0:T(8,128)(2,1)}, bf16[2,128,128]{2,1,0:T(8,128)(2,1)S(1)}, u32[]{:S(2)}, u32[]{:S(2)}) collective-permute-start(bf16[2,128,128]{2,1,0:T(8,128)(2,1)} %get-tuple-element.35), channel_id=1, source_target_pairs={{0,9},{1,10},{2,11},{3,12},{4,13},{5,14},{6,15},{8,1},{9,2},{10,3}... | collective-permute-start | bytes 196616 | tf_op jit(solution)/shard_map/ppermute | solution.py:562
  27.1 1.3 %collective-permute-done.1.rest_1_ = bf16[2,512,128]{2,1,0:T(8,128)(2,1)} collective-permute-done((bf16[2,512,128]{2,1,0:T(8,128)(2,1)}, bf16[2,512,128]{2,1,0:T(8,128)(2,1)}, u32[]{:S(2)}, u32[]{:S(2)}) %collective-permute-start.1) | collective-permute-done | bytes 262176 | tf_op jit(solution)/shard_map/ppermute | solution.py:562
  29.2 4.3 %gather.1 = (bf16[4,2,256,256]{3,2,1,0:T(8,128)(2,1)}, bf16[4,2,256,256]{3,2,1,0:T(8,128)(2,1)}) custom-call(s32[16]{0:T(128)} %reshape.25.places, s32[2]{0:T(128)} %pad_add_fusion.1.offsets, bf16[1,512,1024]{2,1,0:T(8,128)(2,1)} %tile_re.1, bf16[1,512,1024]{2,1,0:T(8,128)(2,1)} %tile_im.1, bf16[2,128,1024]{2,1,0:T(8,128)(2,1)} %copy-done.5, ...), custom_call_target="tpu_custom_call" | custom-call | tf_op jit(solution)/shard_map/gather/pallas_call | solution.py:202
  35.3 5.9 %prepare.1 = (f32[2,256,256]{2,1,0:T(8,128)}, f32[4,256,256]{2,1,0:T(8,128)}, f32[4,2,256,256]{3,2,1,0:T(8,128)}) custom-call(s32[8]{0:T(128)} %reshape.26.places, bf16[256,256]{1,0:T(8,128)(2,1)} %constant.45.clone.order_t, f32[2,256,256]{2,1,0:T(8,128)} %probe.1, f32[1,256,256]{2,1,0:T(8,128)} %bitcast.15, f32[1,256,256]{2,1,0:T(8,128)} %bitcast.16, ...), custom_call_target="tpu_custom_call" | custom-call | flops 503316480 | bytes 5767168 | tf_op jit(solution)/shard_map/prepare/pallas_call | solution.py:101
  42.8 21.5 %chain.1 = (f32[4,2,256,256]{3,2,1,0:T(8,128)}, bf16[4,2,256,256]{3,2,1,0:T(8,128)(2,1)}, f32[2,256,256]{2,1,0:T(8,128)}) custom-call(s32[8]{0:T(128)} %reshape.26.places, s32[4]{0:T(128)} %fusion.live, s32[1]{0:T(128)} %bitcast.1.here, bf16[4,2,256,256]{3,2,1,0:T(8,128)(2,1)} %constant.46.clone.tables, f32[2,256,256]{2,1,0:T(8,128)} %get-tuple-element.16.kern, ...), custom_call_target="tpu_custom_call" | custom-call | tf_op jit(solution)/shard_map/chain/pallas_call | solution.py:334
  66.0 1.4 %collective-permute-done.12 = bf16[2,128,256]{2,1,0:T(8,128)(2,1)S(1)} collective-permute-done((bf16[2,128,256]{2,1,0:T(8,128)(2,1)S(1)}, bf16[2,128,256]{2,1,0:T(8,128)(2,1)S(1)}, u32[]{:S(2)}, u32[]{:S(2)}) %collective-permute-start.12) | collective-permute-done | bytes 131104 | tf_op jit(solution)/shard_map/ppermute | solution.py:577
  69.0 8.0 %collective-permute-done.13 = f32[2,128,256]{2,1,0:T(8,128)S(1)} collective-permute-done((f32[2,128,256]{2,1,0:T(8,128)S(1)}, f32[2,128,256]{2,1,0:T(8,128)S(1)}, u32[]{:S(2)}, u32[]{:S(2)}) %collective-permute-start.13) | collective-permute-done | bytes 262176 | tf_op jit(solution)/shard_map/ppermute | solution.py:506
  77.1 2.5 %collective-permute-start.14 = (f32[2,128,256]{2,1,0:T(8,128)S(1)}, f32[2,128,256]{2,1,0:T(8,128)S(1)}, u32[]{:S(2)}, u32[]{:S(2)}) collective-permute-start(f32[2,128,256]{2,1,0:T(8,128)S(1)} %add.36), channel_id=1, source_target_pairs={{0,1},{1,0},{2,3},{3,2},{4,5},{5,4},{6,7},{7,6},{8,9},{9,8},{10,11... | collective-permute-start | bytes 786440 | tf_op jit(solution)/shard_map/ppermute | solution.py:506
  79.6 6.0 %collective-permute-done.14 = f32[2,128,256]{2,1,0:T(8,128)S(1)} collective-permute-done((f32[2,128,256]{2,1,0:T(8,128)S(1)}, f32[2,128,256]{2,1,0:T(8,128)S(1)}, u32[]{:S(2)}, u32[]{:S(2)}) %collective-permute-start.14) | collective-permute-done | bytes 262176 | tf_op jit(solution)/shard_map/ppermute | solution.py:506
  85.7 3.0 %collective-permute-start.15 = (f32[2,128,256]{2,1,0:T(8,128)S(1)}, f32[2,128,256]{2,1,0:T(8,128)}, u32[]{:S(2)}, u32[]{:S(2)}) collective-permute-start(f32[2,128,256]{2,1,0:T(8,128)S(1)} %add.37), channel_id=1, source_target_pairs={{0,2},{1,3},{2,0},{3,1},{4,6},{5,7},{6,4},{7,5},{8,10},{9,11},{10,... | collective-permute-start | bytes 786440 | tf_op jit(solution)/shard_map/ppermute | solution.py:506
  90.4 5.8 %scatter.1 = (f32[2,512,1024]{2,1,0:T(8,128)}, bf16[2,128,1024]{2,1,0:T(8,128)(2,1)}, bf16[2,512,128]{2,1,0:T(8,128)(2,1)}, bf16[2,512,128]{2,1,0:T(8,128)(2,1)}...) custom-call(s32[16]{0:T(128)} %reshape.25.places, s32[8]{0:T(128)} %reshape.27.live, ...), custom_call_target="tpu_custom_call" | custom-call | tf_op jit(solution)/shard_map/scatter/pallas_call | solution.py:427
  96.2 1.7 %collective-permute-start.7 = (bf16[2,128,1024]{2,1,0:T(8,128)(2,1)}, bf16[2,128,1024]{2,1,0:T(8,128)(2,1)S(1)}, u32[]{:S(2)}, u32[]{:S(2)}) collective-permute-start(bf16[2,128,1024]{2,1,0:T(8,128)(2,1)} %get-tuple-element.24), channel_id=1, source_target_pairs={{0,8},{1,9},{2,10},{3,11},{4,12},{5,13},{6,14},{7,15},{8,0},{9,1},... | collective-permute-start | bytes 1572872 | tf_op jit(solution)/shard_map/ppermute | solution.py:587
  98.8 2.6 %collective-permute-start.16 = (f32[2,128,256]{2,1,0:T(8,128)S(1)}, f32[2,128,256]{2,1,0:T(8,128)S(1)}, u32[]{:S(2)}, u32[]{:S(2)}) collective-permute-start(f32[2,128,256]{2,1,0:T(8,128)S(1)} %add.38), channel_id=1, source_target_pairs={{0,4},{1,5},{2,6},{3,7},{4,0},{5,1},{6,2},{7,3},{8,12},{9,13},{10,... | collective-permute-start | bytes 786440 | tf_op jit(solution)/shard_map/ppermute | solution.py:506
  101.4 1.9 %collective-permute-start.8 = (bf16[2,512,128]{2,1,0:T(8,128)(2,1)}, bf16[2,512,128]{2,1,0:T(8,128)(2,1)S(1)}, u32[]{:S(2)}, u32[]{:S(2)}) collective-permute-start(bf16[2,512,128]{2,1,0:T(8,128)(2,1)} %get-tuple-element.25), channel_id=1, source_target_pairs={{0,1},{1,2},{2,3},{3,4},{4,5},{5,6},{6,7},{8,9},{9,10},{10,11},{11... | collective-permute-start | bytes 786440 | tf_op jit(solution)/shard_map/ppermute | solution.py:587
  103.3 1.3 %collective-permute-start.9 = (bf16[2,512,128]{2,1,0:T(8,128)(2,1)}, bf16[2,512,128]{2,1,0:T(8,128)(2,1)S(1)}, u32[]{:S(2)}, u32[]{:S(2)}) collective-permute-start(bf16[2,512,128]{2,1,0:T(8,128)(2,1)} %get-tuple-element.26), channel_id=1, source_target_pairs={{1,0},{2,1},{3,2},{4,3},{5,4},{6,5},{7,6},{9,8},{10,9},{11,10},{12... | collective-permute-start | bytes 786440 | tf_op jit(solution)/shard_map/ppermute | solution.py:587
  104.6 4.8 %collective-permute-start.10 = (bf16[2,128,128]{2,1,0:T(8,128)(2,1)}, bf16[2,128,128]{2,1,0:T(8,128)(2,1)S(1)}, u32[]{:S(2)}, u32[]{:S(2)}) collective-permute-start(bf16[2,128,128]{2,1,0:T(8,128)(2,1)} %get-tuple-element.27), channel_id=1, source_target_pairs={{0,9},{1,10},{2,11},{3,12},{4,13},{5,14},{6,15},{8,1},{9,2},{10,3}... | collective-permute-start | bytes 196616 | tf_op jit(solution)/shard_map/ppermute | solution.py:587
  109.4 2.1 %collective-permute-done.16 = f32[2,128,256]{2,1,0:T(8,128)S(1)} collective-permute-done((f32[2,128,256]{2,1,0:T(8,128)S(1)}, f32[2,128,256]{2,1,0:T(8,128)S(1)}, u32[]{:S(2)}, u32[]{:S(2)}) %collective-permute-start.16) | collective-permute-done | bytes 262176 | tf_op jit(solution)/shard_map/ppermute | solution.py:506
  114.2 4.6 %collective-permute-done.11.rest_4_ = bf16[2,128,128]{2,1,0:T(8,128)(2,1)S(1)} collective-permute-done((bf16[2,128,128]{2,1,0:T(8,128)(2,1)}, bf16[2,128,128]{2,1,0:T(8,128)(2,1)S(1)}, u32[]{:S(2)}, u32[]{:S(2)}) %collective-permute-start.11) | collective-permute-done | bytes 65568 | tf_op jit(solution)/shard_map/ppermute | solution.py:587
  119.9 5.9 %borders.1 = f32[2,512,1024]{2,1,0:T(8,128)} custom-call(s32[2]{0:T(128)} %pad_add_fusion.offsets, f32[2,512,1024]{2,1,0:T(8,128)} %get-tuple-element.23.tile_in, bf16[2,128,1024]{2,1,0:T(8,128)(2,1)} %copy-done.4, bf16[2,512,128]{2,1,0:T(8,128)(2,1)} %copy-done.7, bf16[2,512,128]{2,1,0:T(8,128)(2,1)} %copy-done.8, bf16[2,128,128]{2,1,0:T(8,128)(2,1)} %copy-done.9, ...), custom_call_target="tpu_custom_call" | custom-call | tf_op jit(solution)/shard_map/borders/pallas_call | solution.py:466
  (68 shorter events, 20.7 us)
Async XLA Ops:
  0.6 33.6 %copy-start = (f32[1,1,4,2,256,256]{5,4,3,2,1,0:T(8,128)S(1)}, f32[1,1,4,2,256,256]{5,4,3,2,1,0:T(8,128)}, u32[]{:S(2)}) copy-start(f32[1,1,4,2,256,256]{5,4,3,2,1,0:T(8,128)} %param.15) | copy-start | bytes 6291460
  0.6 2.4 %copy-start.1 = (bf16[1,512,1024]{2,1,0:T(8,128)(2,1)S(1)}, bf16[1,512,1024]{2,1,0:T(8,128)(2,1)}, u32[]{:S(2)}) copy-start(bf16[1,512,1024]{2,1,0:T(8,128)(2,1)} %tile_im.1) | copy-start | bytes 3145732
  3.1 21.8 %copy-start.13 = (s32[1,1,4,2,2]{2,4,3,1,0:T(2,128)S(1)}, s32[1,1,4,2,2]{2,4,3,1,0:T(2,128)}, u32[]{:S(2)}) copy-start(s32[1,1,4,2,2]{2,4,3,1,0:T(2,128)} %param.13) | copy-start | bytes 196
  5.2 23.2 %collective-permute-start = (bf16[2,128,1024]{2,1,0:T(8,128)(2,1)S(1)}, bf16[2,128,1024]{2,1,0:T(8,128)(2,1)S(1)}, u32[]{:S(2)}, u32[]{:S(2)}) collective-permute-start(bf16[2,128,1024]{2,1,0:T(8,128)(2,1)S(1)} %constant_dynamic-slice_fusion.2), channel_id=1, source_target_pairs={{0,8},{1,9},{2,10},{3,11},{4,12},{5,13},{6,14},{7,15},{8,0},{9,1},... | collective-permute-start | bytes 1572872 | tf_op jit(solution)/shard_map/ppermute | solution.py:562
  10.1 17.0 %collective-permute-start.2 = (bf16[2,512,128]{2,1,0:T(8,128)(2,1)}, bf16[2,512,128]{2,1,0:T(8,128)(2,1)S(1)}, u32[]{:S(2)}, u32[]{:S(2)}) collective-permute-start(bf16[2,512,128]{2,1,0:T(8,128)(2,1)} %get-tuple-element.36), channel_id=1, source_target_pairs={{1,0},{2,1},{3,2},{4,3},{5,4},{6,5},{7,6},{9,8},{10,9},{11,10},{12... | collective-permute-start | bytes 786440 | tf_op jit(solution)/shard_map/ppermute | solution.py:562
  11.3 17.0 %collective-permute-start.1 = (bf16[2,512,128]{2,1,0:T(8,128)(2,1)}, bf16[2,512,128]{2,1,0:T(8,128)(2,1)}, u32[]{:S(2)}, u32[]{:S(2)}) collective-permute-start(bf16[2,512,128]{2,1,0:T(8,128)(2,1)} %get-tuple-element.37), channel_id=1, source_target_pairs={{0,1},{1,2},{2,3},{3,4},{4,5},{5,6},{6,7},{8,9},{9,10},{10,11},{11... | collective-permute-start | bytes 786440 | tf_op jit(solution)/shard_map/ppermute | solution.py:562
  18.1 8.0 %collective-permute-start.4 = (bf16[2,128,128]{2,1,0:T(8,128)(2,1)}, bf16[2,128,128]{2,1,0:T(8,128)(2,1)S(1)}, u32[]{:S(2)}, u32[]{:S(2)}) collective-permute-start(bf16[2,128,128]{2,1,0:T(8,128)(2,1)} %get-tuple-element.34), channel_id=1, source_target_pairs={{1,8},{2,9},{3,10},{4,11},{5,12},{6,13},{7,14},{9,0},{10,1},{11,2}... | collective-permute-start | bytes 196616 | tf_op jit(solution)/shard_map/ppermute | solution.py:562
  19.4 7.7 %collective-permute-start.3 = (bf16[2,128,128]{2,1,0:T(8,128)(2,1)}, bf16[2,128,128]{2,1,0:T(8,128)(2,1)S(1)}, u32[]{:S(2)}, u32[]{:S(2)}) collective-permute-start(bf16[2,128,128]{2,1,0:T(8,128)(2,1)} %get-tuple-element.35), channel_id=1, source_target_pairs={{0,9},{1,10},{2,11},{3,12},{4,13},{5,14},{6,15},{8,1},{9,2},{10,3}... | collective-permute-start | bytes 196616 | tf_op jit(solution)/shard_map/ppermute | solution.py:562
  26.2 2.2 %copy-start.11 = (bf16[2,128,128]{2,1,0:T(8,128)(2,1)}, bf16[2,128,128]{2,1,0:T(8,128)(2,1)S(1)}, u32[]{:S(2)}) copy-start(bf16[2,128,128]{2,1,0:T(8,128)(2,1)S(1)} %collective-permute-done.4.rest_4_) | copy-start | bytes 196612
  27.1 1.3 %copy-start.12 = (bf16[2,128,128]{2,1,0:T(8,128)(2,1)}, bf16[2,128,128]{2,1,0:T(8,128)(2,1)S(1)}, u32[]{:S(2)}) copy-start(bf16[2,128,128]{2,1,0:T(8,128)(2,1)S(1)} %collective-permute-done.3.rest_3_) | copy-start | bytes 196612
  33.5 8.4 %collective-permute-start.5 = (bf16[4,2,256,256]{3,2,1,0:T(8,128)(2,1)}, bf16[4,2,256,256]{3,2,1,0:T(8,128)(2,1)S(1)}, u32[]{:S(2)}, u32[]{:S(2)}) collective-permute-start(bf16[4,2,256,256]{3,2,1,0:T(8,128)(2,1)} %get-tuple-element.18), channel_id=1, source_target_pairs={{0,16},{16,0},{1,17},{17,1},{2,18},{18,2},{3,19},{19,3},{4,20},{20... | collective-permute-start | bytes 3145736 | tf_op jit(solution)/shard_map/ppermute | solution.py:568
  35.3 5.9 %copy-start.14 = (s32[1,1,4]{2,1,0:T(1,128)S(1)}, s32[1,1,4]{2,1,0:T(1,128)}, u32[]{:S(2)}) copy-start(s32[1,1,4]{2,1,0:T(1,128)} %param.14) | copy-start | bytes 52
  64.4 25.0 %collective-permute-start.6 = (bf16[4,2,256,256]{3,2,1,0:T(8,128)(2,1)}, bf16[4,2,256,256]{3,2,1,0:T(8,128)(2,1)S(1)}, u32[]{:S(2)}, u32[]{:S(2)}) collective-permute-start(bf16[4,2,256,256]{3,2,1,0:T(8,128)(2,1)} %get-tuple-element.22), channel_id=1, source_target_pairs={{0,16},{16,0},{1,17},{17,1},{2,18},{18,2},{3,19},{19,3},{4,20},{20... | collective-permute-start | bytes 3145736 | tf_op jit(solution)/shard_map/ppermute | solution.py:572
  65.9 1.5 %collective-permute-start.12 = (bf16[2,128,256]{2,1,0:T(8,128)(2,1)S(1)}, bf16[2,128,256]{2,1,0:T(8,128)(2,1)S(1)}, u32[]{:S(2)}, u32[]{:S(2)}) collective-permute-start(bf16[2,128,256]{2,1,0:T(8,128)(2,1)S(1)} %dynamic-slice_convert_fusion), channel_id=1, source_target_pairs={{0,16},{16,0},{1,17},{17,1},{2,18},{18,2},{3,19},{19,3},{4,20},{20... | collective-permute-start | bytes 393224 | tf_op jit(solution)/shard_map/ppermute | solution.py:577
  68.4 8.7 %collective-permute-start.13 = (f32[2,128,256]{2,1,0:T(8,128)S(1)}, f32[2,128,256]{2,1,0:T(8,128)S(1)}, u32[]{:S(2)}, u32[]{:S(2)}) collective-permute-start(f32[2,128,256]{2,1,0:T(8,128)S(1)} %convert_add_fusion), channel_id=1, source_target_pairs={{0,8},{8,0},{1,9},{9,1},{2,10},{10,2},{3,11},{11,3},{4,12},{12,4},... | collective-permute-start | bytes 786440 | tf_op jit(solution)/shard_map/ppermute | solution.py:506
  77.1 8.6 %collective-permute-start.14 = (f32[2,128,256]{2,1,0:T(8,128)S(1)}, f32[2,128,256]{2,1,0:T(8,128)S(1)}, u32[]{:S(2)}, u32[]{:S(2)}) collective-permute-start(f32[2,128,256]{2,1,0:T(8,128)S(1)} %add.36), channel_id=1, source_target_pairs={{0,1},{1,0},{2,3},{3,2},{4,5},{5,4},{6,7},{7,6},{8,9},{9,8},{10,11... | collective-permute-start | bytes 786440 | tf_op jit(solution)/shard_map/ppermute | solution.py:506
  85.7 12.2 %collective-permute-start.15 = (f32[2,128,256]{2,1,0:T(8,128)S(1)}, f32[2,128,256]{2,1,0:T(8,128)}, u32[]{:S(2)}, u32[]{:S(2)}) collective-permute-start(f32[2,128,256]{2,1,0:T(8,128)S(1)} %add.37), channel_id=1, source_target_pairs={{0,2},{1,3},{2,0},{3,1},{4,6},{5,7},{6,4},{7,5},{8,10},{9,11},{10,... | collective-permute-start | bytes 786440 | tf_op jit(solution)/shard_map/ppermute | solution.py:506
  96.2 22.7 %collective-permute-start.7 = (bf16[2,128,1024]{2,1,0:T(8,128)(2,1)}, bf16[2,128,1024]{2,1,0:T(8,128)(2,1)S(1)}, u32[]{:S(2)}, u32[]{:S(2)}) collective-permute-start(bf16[2,128,1024]{2,1,0:T(8,128)(2,1)} %get-tuple-element.24), channel_id=1, source_target_pairs={{0,8},{1,9},{2,10},{3,11},{4,12},{5,13},{6,14},{7,15},{8,0},{9,1},... | collective-permute-start | bytes 1572872 | tf_op jit(solution)/shard_map/ppermute | solution.py:587
  98.8 12.7 %collective-permute-start.16 = (f32[2,128,256]{2,1,0:T(8,128)S(1)}, f32[2,128,256]{2,1,0:T(8,128)S(1)}, u32[]{:S(2)}, u32[]{:S(2)}) collective-permute-start(f32[2,128,256]{2,1,0:T(8,128)S(1)} %add.38), channel_id=1, source_target_pairs={{0,4},{1,5},{2,6},{3,7},{4,0},{5,1},{6,2},{7,3},{8,12},{9,13},{10,... | collective-permute-start | bytes 786440 | tf_op jit(solution)/shard_map/ppermute | solution.py:506
  101.4 17.4 %collective-permute-start.8 = (bf16[2,512,128]{2,1,0:T(8,128)(2,1)}, bf16[2,512,128]{2,1,0:T(8,128)(2,1)S(1)}, u32[]{:S(2)}, u32[]{:S(2)}) collective-permute-start(bf16[2,512,128]{2,1,0:T(8,128)(2,1)} %get-tuple-element.25), channel_id=1, source_target_pairs={{0,1},{1,2},{2,3},{3,4},{4,5},{5,6},{6,7},{8,9},{9,10},{10,11},{11... | collective-permute-start | bytes 786440 | tf_op jit(solution)/shard_map/ppermute | solution.py:587
  103.3 15.5 %collective-permute-start.9 = (bf16[2,512,128]{2,1,0:T(8,128)(2,1)}, bf16[2,512,128]{2,1,0:T(8,128)(2,1)S(1)}, u32[]{:S(2)}, u32[]{:S(2)}) collective-permute-start(bf16[2,512,128]{2,1,0:T(8,128)(2,1)} %get-tuple-element.26), channel_id=1, source_target_pairs={{1,0},{2,1},{3,2},{4,3},{5,4},{6,5},{7,6},{9,8},{10,9},{11,10},{12... | collective-permute-start | bytes 786440 | tf_op jit(solution)/shard_map/ppermute | solution.py:587
  104.6 9.6 %collective-permute-start.10 = (bf16[2,128,128]{2,1,0:T(8,128)(2,1)}, bf16[2,128,128]{2,1,0:T(8,128)(2,1)S(1)}, u32[]{:S(2)}, u32[]{:S(2)}) collective-permute-start(bf16[2,128,128]{2,1,0:T(8,128)(2,1)} %get-tuple-element.27), channel_id=1, source_target_pairs={{0,9},{1,10},{2,11},{3,12},{4,13},{5,14},{6,15},{8,1},{9,2},{10,3}... | collective-permute-start | bytes 196616 | tf_op jit(solution)/shard_map/ppermute | solution.py:587
  111.6 7.3 %collective-permute-start.11 = (bf16[2,128,128]{2,1,0:T(8,128)(2,1)}, bf16[2,128,128]{2,1,0:T(8,128)(2,1)S(1)}, u32[]{:S(2)}, u32[]{:S(2)}) collective-permute-start(bf16[2,128,128]{2,1,0:T(8,128)(2,1)} %get-tuple-element.28), channel_id=1, source_target_pairs={{1,8},{2,9},{3,10},{4,11},{5,12},{6,13},{7,14},{9,0},{10,1},{11,2}... | collective-permute-start | bytes 196616 | tf_op jit(solution)/shard_map/ppermute | solution.py:587
  114.2 4.7 %copy-start.9 = (bf16[2,128,128]{2,1,0:T(8,128)(2,1)}, bf16[2,128,128]{2,1,0:T(8,128)(2,1)S(1)}, u32[]{:S(2)}) copy-start(bf16[2,128,128]{2,1,0:T(8,128)(2,1)S(1)} %collective-permute-done.10.rest_3_) | copy-start | bytes 196612
  (8 other events, 7.2 us)

commit v2 on v1

--- a/solution.py
+++ b/solution.py
@@ -14,7 +14,7 @@
 LANES = 128
 HBM = pl.BlockSpec(memory_space=pl.ANY)
 SMEM = pl.BlockSpec(memory_space=pltpu.SMEM)
-LIMIT = 56 * 1024 * 1024
+MIB = 1024 * 1024
 
 
 def dft_tables(size):
@@ -118,7 +118,7 @@
             jax.ShapeDtypeStruct((count, size, size), f32),
             jax.ShapeDtypeStruct((count, 2, size, size), f32),
         ],
-        compiler_params=pltpu.CompilerParams(vmem_limit_bytes=LIMIT),
+        compiler_params=pltpu.CompilerParams(vmem_limit_bytes=16 * MIB),
         cost_estimate=pl.CostEstimate(
             flops=2 * (count + 1) * 3 * size**3,
             bytes_accessed=4 * size * size * (4 * count + 6),
@@ -134,17 +134,55 @@
     )
 
 
-def spot(places, at, size):
+def pack_kernel(edges, half, offsets, tile_re, tile_im, *rest):
+    strips, sems = rest[:-1], rest[-1]
+    tile_rows, tile_cols = tile_re.shape[1:]
+    columns = {-1: pl.ds(0, half), 0: pl.ds(0, tile_cols), 1: pl.ds(tile_cols - half, half)}
+    copies = []
+    for (side, across), strip in zip(edges, strips):
+        if side is None:
+            rows = pl.ds(0, tile_rows)
+        else:
+            rows = pl.ds(pl.multiple_of(offsets[side], half), half)
+        for plane, tile in enumerate((tile_re, tile_im)):
+            copies.append(
+                pltpu.make_async_copy(
+                    tile.at[0, rows, columns[across]], strip.at[plane], sems.at[len(copies)]
+                )
+            )
+            copies[-1].start()
+    for copy in copies:
+        copy.wait()
+
+
+def strip_shapes(edges, tile_rows, tile_cols, half):
+    return [
+        jax.ShapeDtypeStruct(
+            (2, tile_rows if side is None else half, half if across else tile_cols), bf16
+        )
+        for side, across in edges
+    ]
+
+
+def pack(offsets, tile_re, tile_im, edges, half):
+    return pl.pallas_call(
+        functools.partial(pack_kernel, edges, half),
+        in_specs=[SMEM, HBM, HBM],
+        out_specs=[HBM] * len(edges),
+        out_shape=strip_shapes(edges, *tile_re.shape[1:], half),
+        scratch_shapes=[pltpu.SemaphoreType.DMA((2 * len(edges),))],
+        compiler_params=pltpu.CompilerParams(vmem_limit_bytes=4 * MIB),
+        name="pack",
+    )(offsets, tile_re, tile_im)
+
+
+def spot(places, at):
     row, col = places[2 * at], places[2 * at + 1]
     down, across = row % ROWS, col % LANES
-    top = pl.multiple_of(row - down, ROWS)
-    left = pl.multiple_of(col - across, LANES)
-    return down, across, pl.ds(top, size + ROWS), pl.ds(left, size + LANES)
-
-
-def gather_kernel(
-    spots, edges, half, places, offsets, tile_re, tile_im, *rest
-):
+    return down, across, pl.multiple_of(row - down, ROWS), pl.multiple_of(col - across, LANES)
+
+
+def gather_kernel(spots, edges, half, places, offsets, tile_re, tile_im, after, *rest):
     strips, (mine, other, padded, sems) = rest[:-4], rest[-4:]
     tile_rows, tile_cols = tile_re.shape[1:]
     size = mine.shape[-1]
@@ -168,32 +206,43 @@
         copy.wait()
 
     sections = 2
-    lane = lax.broadcasted_iota(jnp.int32, (size + ROWS, LANES), 1)
-    row = lax.broadcasted_iota(jnp.int32, (ROWS, size), 0)
-    here = offsets[len(offsets_names(edges))]
+    lane = lax.broadcasted_iota(jnp.int32, (size, LANES), 1)
+    top_lane = lax.broadcasted_iota(jnp.int32, (ROWS, LANES), 1)
+    top_row = lax.broadcasted_iota(jnp.int32, (ROWS, size), 0)
+    here = offsets[offsets.shape[0] - 1]
 
     def cut(at, target, place):
-        down, across, tall, wide = spot(places, at, size)
+        down, across, top, left = spot(places, at)
+        inner = size - LANES
+        rest = pl.ds(pl.multiple_of(top + ROWS, ROWS), size - ROWS)
+
+        def cols(start, width):
+            return pl.ds(pl.multiple_of(left + start, LANES), width)
+
         for plane in range(2):
-            block = padded[plane, tall, wide].astype(f32)
-            first = jnp.where(lane < across, block[:, size:], block[:, :LANES])
-            block = cols_of(first, block[:, LANES:size])
-            first = jnp.where(row < down, block[size:], block[:ROWS])
-            target[place, plane] = rows_of(first, block[ROWS:size]).astype(bf16)
-
-    def one(place, carry):
+            target[place, plane, ROWS:, LANES:] = padded[plane, rest, cols(LANES, inner)]
+            near = padded[plane, rest, cols(0, LANES)].astype(f32)
+            far = padded[plane, rest, cols(size, LANES)].astype(f32)
+            target[place, plane, ROWS:, :LANES] = jnp.where(
+                lane[ROWS:] < across, far, near
+            ).astype(bf16)
+            rows = []
+            for start in (0, size):
+                block = padded[
+                    plane, pl.ds(pl.multiple_of(top + start, ROWS), ROWS), cols(0, size + LANES)
+                ].astype(f32)
+                first = jnp.where(top_lane < across, block[:, size:], block[:, :LANES])
+                rows.append(cols_of(first, block[:, LANES:size]))
+            target[place, plane, :ROWS, :] = jnp.where(top_row < down, rows[1], rows[0]).astype(
+                bf16
+            )
+
+    for place in range(spots // sections):
+        cut(sections * place + 1 - here, other, place)
         cut(sections * place + here, mine, place)
-        cut(sections * place + 1 - here, other, place)
-        return carry
-
-    lax.fori_loop(0, spots // sections, one, 0)
-
-
-def offsets_names(edges):
-    return sorted({side for side, _ in edges if side is not None})
-
-
-def gather(places, offsets, tile_re, tile_im, edges, strips, size):
+
+
+def gather(places, offsets, tile_re, tile_im, after, edges, strips, size):
     half = size // 2
     spots = places.shape[0] // 2
     tile_rows, tile_cols = tile_re.shape[1:]
@@ -201,21 +250,21 @@
     vmem = pl.BlockSpec(memory_space=pltpu.VMEM)
     return pl.pallas_call(
         functools.partial(gather_kernel, spots, edges, half),
-        in_specs=[SMEM, SMEM] + [HBM] * (2 + len(strips)),
+        in_specs=[SMEM, SMEM] + [HBM] * (3 + len(strips)),
         out_specs=[vmem, vmem],
         out_shape=[shape, shape],
         scratch_shapes=[
             pltpu.VMEM((2, tile_rows + 2 * half, tile_cols + 2 * half), bf16),
             pltpu.SemaphoreType.DMA((2 + len(strips),)),
         ],
-        compiler_params=pltpu.CompilerParams(vmem_limit_bytes=LIMIT),
+        compiler_params=pltpu.CompilerParams(vmem_limit_bytes=16 * MIB),
         name="gather",
-    )(places, offsets, tile_re, tile_im, *strips)
+    )(places, offsets, tile_re, tile_im, after, *strips)
 
 
 def chain_kernel(
     group, places, live, here, tables, kern, mine, theirs, frames, waves,
-    keep, send, pulled, windows, middle, terms, sems,
+    keep, send, pulled_keep, pulled_send, windows, middle, terms, pulled, sems,
 ):
     step = pl.program_id(0)
     steps = pl.num_programs(0)
@@ -326,6 +375,15 @@
     keep[...] = terms[me]
     send[...] = terms[1 - me].astype(bf16)
 
+    @pl.when(step == steps - 1)
+    def _():
+        share = pulled_keep.shape[1]
+        for plane in range(2):
+            pulled_keep[plane] = pulled[plane, pl.ds(pl.multiple_of(me * share, share), share), :]
+            pulled_send[plane] = pulled[
+                plane, pl.ds(pl.multiple_of((1 - me) * share, share), share), :
+            ]
+
 
 def chain(places, live, here, kern, mine, theirs, frames, waves, group):
     count, size = frames.shape[0], frames.shape[-1]
@@ -345,37 +403,48 @@
             pl.BlockSpec((group, size, size), lambda i: (i, 0, 0)),
             block,
         ],
-        out_specs=[block, block, full(2, size, size)],
+        out_specs=[block, block, full(2, size // 2, size), full(2, size // 2, size)],
         out_shape=[
             jax.ShapeDtypeStruct((count, 2, size, size), f32),
             jax.ShapeDtypeStruct((count, 2, size, size), bf16),
-            jax.ShapeDtypeStruct((2, size, size), f32),
+            jax.ShapeDtypeStruct((2, size // 2, size), f32),
+            jax.ShapeDtypeStruct((2, size // 2, size), f32),
         ],
         scratch_shapes=[
             pltpu.VMEM((count // group, 2, group, 2, size, size), bf16),
             pltpu.VMEM((group, 2, size, size), bf16),
             pltpu.VMEM((2, group, 2, size, size), f32),
+            pltpu.VMEM((2, size, size), f32),
             pltpu.SemaphoreType.DMA((2 * (count // group),)),
         ],
-        compiler_params=pltpu.CompilerParams(vmem_limit_bytes=LIMIT),
+        compiler_params=pltpu.CompilerParams(vmem_limit_bytes=40 * MIB),
         name="chain",
     )(places, live, here, jnp.asarray(dft_tables(size)), kern, mine, theirs, frames, waves)
 
 
-def scatter_kernel(
-    spots, edges, half, places, live, offsets, kept, arrived, tile, *rest
-):
-    strips, (total, sems) = rest[:-2], rest[-2:]
-    size = kept.shape[-1]
+def scatter_kernel(edges, half, places, live, offsets, kept, arrived, tile, *rest):
+    strips, (total, near, far, sems) = rest[:-4], rest[-4:]
+    count, size = kept.shape[0], kept.shape[-1]
     tile_rows, tile_cols = tile.shape[1:]
     sections = 2
-    here = offsets[len(offsets_names(edges))]
+    here = offsets[offsets.shape[0] - 1]
+
+    def fetch(place, which):
+        source, target = ((kept, near), (arrived, far))[which]
+        return pltpu.make_async_copy(
+            source.at[place], target.at[place], sems.at[1 + 2 * place + which]
+        )
+
+    for which in range(2):
+        for place in range(count):
+            fetch(place, which).start()
     total[...] = jnp.zeros_like(total)
     lane = lax.broadcasted_iota(jnp.int32, (size, LANES), 1)
     row = lax.broadcasted_iota(jnp.int32, (ROWS, size + LANES), 0)
 
     def add(at, source, place):
-        down, across, tall, wide = spot(places, at, size)
+        down, across, top, left = spot(places, at)
+        wide = pl.ds(left, size + LANES)
 
         @pl.when(live[at] > 0)
         def _():
@@ -391,14 +460,12 @@
                 value = rows_of(
                     jnp.where(inside, first, 0.0), value[ROWS:], jnp.where(inside, 0.0, first)
                 )
-                total[plane, tall, wide] += value
-
-    def one(place, carry):
-        add(sections * place + here, kept, place)
-        add(sections * place + 1 - here, arrived, place)
-        return carry
-
-    lax.fori_loop(0, spots // sections, one, 0)
+                total[plane, pl.ds(top, size + ROWS), wide] += value
+
+    for which, (source, owner) in enumerate(((near, here), (far, 1 - here))):
+        for place in range(count):
+            fetch(place, which).wait()
+            add(sections * place + owner, source, place)
     body = (pl.ds(half, tile_rows), pl.ds(half, tile_cols))
     copy = pltpu.make_async_copy(total.at[(slice(None),) + body], tile, sems.at[0])
     copy.start()
@@ -414,66 +481,86 @@
 
 
 def scatter(places, live, offsets, kept, arrived, edges, tile_rows, tile_cols):
-    size = kept.shape[-1]
+    count, _, size, _ = kept.shape
     half = size // 2
-    spots = places.shape[0] // 2
     vmem = pl.BlockSpec(memory_space=pltpu.VMEM)
-    shapes = [
-        jax.ShapeDtypeStruct(
-            (2, tile_rows if side is None else half, half if across else tile_cols), bf16
-        )
-        for side, across in edges
-    ]
     return pl.pallas_call(
-        functools.partial(scatter_kernel, spots, edges, half),
-        in_specs=[SMEM, SMEM, SMEM, vmem, vmem],
+        functools.partial(scatter_kernel, edges, half),
+        in_specs=[SMEM, SMEM, SMEM, HBM, HBM],
         out_specs=[HBM] + [vmem] * len(edges),
-        out_shape=[jax.ShapeDtypeStruct((2, tile_rows, tile_cols), f32)] + shapes,
+        out_shape=[jax.ShapeDtypeStruct((2, tile_rows, tile_cols), f32)]
+        + strip_shapes(edges, tile_rows, tile_cols, half),
         scratch_shapes=[
             pltpu.VMEM((2, tile_rows + 2 * half, tile_cols + 2 * half), f32),
-            pltpu.SemaphoreType.DMA((1,)),
-        ],
-        compiler_params=pltpu.CompilerParams(vmem_limit_bytes=LIMIT),
+            pltpu.VMEM(kept.shape, f32),
+            pltpu.VMEM(arrived.shape, bf16),
+            pltpu.SemaphoreType.DMA((1 + 2 * count,)),
+        ],
+        compiler_params=pltpu.CompilerParams(vmem_limit_bytes=20 * MIB),
         name="scatter",
     )(places, live, offsets, kept, arrived)
 
 
-def border_kernel(edges, half, sides, offsets, tile_in, *rest):
-    strips, (tile, total, in_sem, out_sem) = rest[:-4], rest[-4:]
+def border_kernel(edges, half, offsets, tile_in, *rest):
+    sides = offsets.shape[0] - 1
+    strips, (tile, bands, left, right, in_sems, out_sems) = rest[: len(edges)], rest[len(edges) :]
     tile_rows, tile_cols = tile.shape[1:]
-    copy = pltpu.make_async_copy(tile_in, total, in_sem)
-    copy.start()
-    copy.wait()
-    columns = {
-        -1: pl.ds(0, half),
-        0: pl.ds(0, tile_cols),
-        1: pl.ds(tile_cols - half, half),
-    }
-    for (side, across), strip in zip(edges, strips):
-        if side is None:
-            rows = pl.ds(0, tile_rows)
-        else:
-            rows = pl.ds(pl.multiple_of(offsets[side], half), half)
+    strips = dict(zip(edges, strips))
+    tall = left.shape[1]
+    rows = pl.ds(pl.multiple_of(offsets[sides], half), tall)
+    regions = []
+    for side in range(sides):
+        band = pl.ds(pl.multiple_of(offsets[side], half), half)
+        regions.append((bands.at[side], band, pl.ds(0, tile_cols)))
+    regions.append((left, rows, pl.ds(0, half)))
+    regions.append((right, rows, pl.ds(tile_cols - half, half)))
+
+    def copy(k, out):
+        block, down, wide = regions[k]
+        if out:
+            return pltpu.make_async_copy(block, tile.at[:, down, wide], out_sems.at[k])
+        return pltpu.make_async_copy(tile_in.at[:, down, wide], block, in_sems.at[k])
+
+    order = [sides, sides + 1, *range(sides)]
+    for k in order:
+        copy(k, False).start()
+    for k in order:
+        copy(k, False).wait()
+        block, down, wide = regions[k]
         for plane in range(2):
-            total[plane, rows, columns[across]] += strip[plane].astype(f32)
-    copy = pltpu.make_async_copy(total, tile, out_sem)
-    copy.start()
-    copy.wait()
+            if k < sides:
+                block[plane] += strips[(k, 0)][plane].astype(f32)
+                for across, cols in ((-1, slice(0, half)), (1, slice(tile_cols - half, tile_cols))):
+                    block[plane, :, cols] += strips[(k, across)][plane].astype(f32) + strips[
+                        (None, across)
+                    ][plane, down, :].astype(f32)
+            else:
+                across = -1 if k == sides else 1
+                block[plane] += strips[(None, across)][plane, down, :].astype(f32)
+        copy(k, True).start()
+    for k in order:
+        copy(k, True).wait()
 
 
 def add_borders(offsets, tile, edges, strips, half):
     vmem = pl.BlockSpec(memory_space=pltpu.VMEM)
+    sides = offsets.shape[0] - 1
+    tile_rows, tile_cols = tile.shape[1:]
+    column = (2, tile_rows - sides * half, half)
     return pl.pallas_call(
-        functools.partial(border_kernel, edges, half, None),
+        functools.partial(border_kernel, edges, half),
         in_specs=[SMEM, HBM] + [vmem] * len(strips),
         out_specs=HBM,
         out_shape=jax.ShapeDtypeStruct(tile.shape, f32),
         scratch_shapes=[
-            pltpu.VMEM(tile.shape, f32),
-            pltpu.SemaphoreType.DMA,
-            pltpu.SemaphoreType.DMA,
-        ],
-        compiler_params=pltpu.CompilerParams(vmem_limit_bytes=LIMIT),
+            pltpu.VMEM((max(sides, 1), 2, half, tile_cols), f32),
+            pltpu.VMEM(column, f32),
+            pltpu.VMEM(column, f32),
+            pltpu.SemaphoreType.DMA((sides + 2,)),
+            pltpu.SemaphoreType.DMA((sides + 2,)),
+        ],
+        input_output_aliases={1: 0},
+        compiler_params=pltpu.CompilerParams(vmem_limit_bytes=12 * MIB),
         name="borders",
     )(offsets, tile, *strips)
 
@@ -497,14 +584,16 @@
     return result
 
 
-def summed(block, axis):
-    size = lax.axis_size(axis)
-    if size & (size - 1):
-        return lax.psum(block, axis)
-    step = 1
-    while step < size:
-        block = block + lax.ppermute(block, axis, [(i, i ^ step) for i in range(size)])
-        step *= 2
+def summed(block, axes):
+    for axis in axes:
+        size = lax.axis_size(axis)
+        if size & (size - 1):
+            block = lax.psum(block, axis)
+            continue
+        for step in reversed([1 << k for k in range(size.bit_length() - 1)]):
+            own = block.astype(bf16)
+            other = lax.ppermute(own, axis, [(i, i ^ step) for i in range(size)])
+            block = own.astype(f32) + other.astype(f32)
     return block
 
 
@@ -545,49 +634,39 @@
         from_rows = [jnp.int32(tile_rows - half), jnp.int32(0)]
         pad_rows = [jnp.int32(0), jnp.int32(tile_rows + half)]
         fold_rows = [jnp.int32(0), jnp.int32(tile_rows - half)]
-    edges = [(side, 0) for side in range(len(sides))]
+    edges = [(side, across) for side in range(len(sides)) for across in (1, -1)]
     edges += [(None, 1), (None, -1)]
-    edges += [(side, across) for side in range(len(sides)) for across in (1, -1)]
+    edges += [(side, 0) for side in range(len(sides))]
     paths = routes(edges, sides, rows, cols)
     both = ("row", "col")
-
-    planes = jnp.stack([object_re[0], object_im[0]])
-    strips = []
-    for (side, across), path in zip(edges, paths):
-        wide = tile_cols if across == 0 else half
-        left = tile_cols - half if across == 1 else 0
-        tall = tile_rows if side is None else half
-        top = 0 if side is None else from_rows[side]
-        strip = lax.dynamic_slice(planes, (0, top, left), (2, tall, wide))
-        strips.append(lax.ppermute(strip, both, path))
     landed = [(side, -across) for side, across in edges]
-    pads = jnp.stack(pad_rows + [here]).astype(jnp.int32)
+
+    def numbers(*values):
+        return jnp.stack(values).astype(jnp.int32)
+
+    own = pack(numbers(*from_rows, here), object_re, object_im, edges, half)
+    strips = [lax.ppermute(strip, both, path) for strip, path in zip(own, paths)]
     kern, sorted_frames, waves = prepare(my_places, probe, phases, frames)
-    mine, other = gather(places, pads, object_re, object_im, landed, strips, size)
+    mine, other = gather(
+        places, numbers(*pad_rows, here), object_re, object_im, waves, landed, strips, size
+    )
     across_depth = [(i, 1 - i) for i in range(sections)]
     theirs = lax.ppermute(other, "depth", across_depth)
-    keep, send, pulled = chain(
+    keep, send, pulled_keep, pulled_send = chain(
         my_places, my_live, here.reshape(1), kern, mine, theirs, sorted_frames, waves, 2
     )
     arrived = lax.ppermute(send, "depth", across_depth)
-
-    share = size // sections
-    kept_rows = lax.dynamic_slice_in_dim(pulled, here * share, share, 1)
-    sent_rows = lax.dynamic_slice_in_dim(pulled, (1 - here) * share, share, 1)
-    probe_part = kept_rows + lax.ppermute(
-        sent_rows.astype(bf16), "depth", across_depth
-    ).astype(f32)
-
-    if rows == 2:
-        out_rows = pad_rows
-    else:
-        out_rows = pad_rows[::-1]
-    outs = jnp.stack(out_rows + [here]).astype(jnp.int32)
-    tile, *own = scatter(places, live, outs, keep, arrived, edges, tile_rows, tile_cols)
+    pulled = pulled_keep + lax.ppermute(pulled_send, "depth", across_depth)
+
+    out_rows = pad_rows if rows == 2 else pad_rows[::-1]
+    tile, *own = scatter(
+        places, live, numbers(*out_rows, here), keep, arrived, edges, tile_rows, tile_cols
+    )
+    *own, pulled = lax.optimization_barrier((*own, pulled))
     added = [lax.ppermute(strip, both, path) for strip, path in zip(own, paths)]
-    folds = jnp.stack(fold_rows + [here]).astype(jnp.int32)
-    gradient = add_borders(folds, tile, landed, added, half)
-    probe_share = summed(summed(probe_part, "row"), "col")
+    first_row = jnp.where(row_at == 0, 0, half) if rows == 2 else jnp.int32(half * (rows > 1))
+    gradient = add_borders(numbers(*fold_rows, first_row), tile, landed, added, half)
+    probe_share = summed(pulled, ("col", "row"))
     return (gradient[:, None], probe_share)
 
 

time: 126 us -> 109 us (0.87)
  Pallas kernels: 43.3 us -> 34.1 us
  local copies, waits for them, and re-layouts: 16.4 us -> 8.47 us
  starting transfers between devices: 36.7 us -> 33 us
  waiting for transfers between devices: 24.4 us -> 28 us
    dynamic_slice x3 -> x0, local copies, waits for them, and re-layouts: 4.45 us -> none  [shards(): strip = lax.dynamic_slice(planes, (0, top, left), (2, tall, wide))]
    ppermute x5, starting transfers between devices: 11 us -> 7.8 us  [shards(): added = [lax.ppermute(strip, both, path) for strip, path in zip(own, paths)]]
    ppermute x5, waiting for transfers between devices: 4.63 us -> 7.75 us  [shards(): added = [lax.ppermute(strip, both, path) for strip, path in zip(own, paths)]]
    pallas_call x1, Pallas kernels: 21.5 us -> 18.9 us  [chain(): pl.pallas_call(functools.partial(chain_kernel, group), grid=(count // gro...]
    ppermute x1, waiting for transfers between devices: 0.01 us -> 2.61 us  [shards(): theirs = lax.ppermute(other, 'depth', across_depth)]
    pallas_call x1, Pallas kernels: 5.88 us -> 3.28 us  [prepare(): pl.pallas_call(prep_kernel, grid=(count,), in_specs=[SMEM, full(size, siz...]
    pallas_call x2 -> x3, Pallas kernels: 11.6 us -> 9.37 us  [the longest x1 4.53 us: scatter(): pl.pallas_call(functools.partial(scatter_kernel, edges, half), in_specs=[...]
    ppermute x10, waiting for transfers between devices: 19.8 us -> 17.6 us  [the longest x4 10.5 us: summed(): other = lax.ppermute(own, axis, [(i, i ^ step) for i in range(size)])]
  transfers between devices with their start and end apart: 17 -> 17, of which waited for: 7 -> 7; matrix products, arithmetic and copies ran while one was open for 10% -> 3% of each run, Pallas kernels for 9% -> 6%
where the time goes in v2:
time: 109 us; the launch traced here: 108 us
  Pallas kernels  34.1 us (31%)
  starting transfers between devices  33 us (30%)
  waiting for transfers between devices  28 us (26%)
  local copies, waits for them, and re-layouts  8.47 us (8%)
  other arithmetic  3.67 us (3%)
    pallas_call x1, Pallas kernels, chain(): pl.pallas_call(functools.partial(chain_kernel, group), grid=(count // gro...  18.9 us
    ppermute x5, starting transfers between devices, shards(): lax.ppermute(strip, both, path)  15.8 us
    ppermute x4, waiting for transfers between devices, summed(): other = lax.ppermute(own, axis, [(i, i ^ step) for i in range(size)])  10.5 us
    ppermute x4, starting transfers between devices, summed(): other = lax.ppermute(own, axis, [(i, i ^ step) for i in range(size)])  8.85 us
    ppermute x5, starting transfers between devices, shards(): added = [lax.ppermute(strip, both, path) for strip, path in zip(own, paths)]  7.8 us
    ppermute x5, waiting for transfers between devices, shards(): added = [lax.ppermute(strip, both, path) for strip, path in zip(own, paths)]  7.75 us
    unnamed x27, local copies, waits for them, and re-layouts  6.8 us
    pallas_call x1, Pallas kernels, scatter(): pl.pallas_call(functools.partial(scatter_kernel, edges, half), in_specs=[...  4.53 us
  transfers between devices with their start and end apart: 17, of which 7 were waited for; matrix products, arithmetic and copies ran while one was open for 3% of the time, Pallas kernels for 6%

profile of v2, /device:TPU:0, one launch (start us, length us, event | category | flops | bytes accessed | tf_op | source)
XLA Modules:
  0.0 108.2 jit_solution(1744760807119087457)
XLA Ops:
  0.7 1.4 %copy-done.1 = bf16[1,512,1024]{2,1,0:T(8,128)(2,1)S(1)} copy-done((bf16[1,512,1024]{2,1,0:T(8,128)(2,1)S(1)}, bf16[1,512,1024]{2,1,0:T(8,128)(2,1)}, u32[]{:S(2)}) %copy-start.1) | copy-done | bytes 1048600
  3.3 1.6 %pack.1 = (bf16[2,128,128]{2,1,0:T(8,128)(2,1)}, bf16[2,128,128]{2,1,0:T(8,128)(2,1)}, bf16[2,512,128]{2,1,0:T(8,128)(2,1)}, bf16[2,512,128]{2,1,0:T(8,128)(2,1)}, bf16[2,128,1024]{2,1,0:T(8,128)(2,1)}) custom-call(s32[2]{0:T(128)S(1)} %pad_add_fusion.2.offsets, bf16[1,512,1024]{2,1,0:T(8,128)(2,1)S(1)} %copy-done.1, bf16[1,512,1024]{2,1,0:T(8,128)(2,1)S(1)} %copy-done.3), custom_call_target="tpu_custom_call" | custom-call | tf_op jit(solution)/shard_map/pack/pallas_call | solution.py:168
  5.0 3.0 %collective-permute-start.4 = (bf16[2,128,1024]{2,1,0:T(8,128)(2,1)}, bf16[2,128,1024]{2,1,0:T(8,128)(2,1)}, u32[]{:S(2)}, u32[]{:S(2)}) collective-permute-start(bf16[2,128,1024]{2,1,0:T(8,128)(2,1)} %get-tuple-element.34), channel_id=1, source_target_pairs={{0,8},{1,9},{2,10},{3,11},{4,12},{5,13},{6,14},{7,15},{8,0},{9,1},... | collective-permute-start | bytes 1572872 | tf_op jit(solution)/shard_map/ppermute | solution.py:648
  8.0 4.0 %collective-permute-start = (bf16[2,128,128]{2,1,0:T(8,128)(2,1)}, bf16[2,128,128]{2,1,0:T(8,128)(2,1)}, u32[]{:S(2)}, u32[]{:S(2)}) collective-permute-start(bf16[2,128,128]{2,1,0:T(8,128)(2,1)} %get-tuple-element.30), channel_id=1, source_target_pairs={{0,9},{1,10},{2,11},{3,12},{4,13},{5,14},{6,15},{8,1},{9,2},{10,3}... | collective-permute-start | bytes 196616 | tf_op jit(solution)/shard_map/ppermute | solution.py:648
  13.3 6.2 %collective-permute-start.2 = (bf16[2,512,128]{2,1,0:T(8,128)(2,1)}, bf16[2,512,128]{2,1,0:T(8,128)(2,1)}, u32[]{:S(2)}, u32[]{:S(2)}) collective-permute-start(bf16[2,512,128]{2,1,0:T(8,128)(2,1)} %get-tuple-element.32), channel_id=1, source_target_pairs={{0,1},{1,2},{2,3},{3,4},{4,5},{5,6},{6,7},{8,9},{9,10},{10,11},{11... | collective-permute-start | bytes 786440 | tf_op jit(solution)/shard_map/ppermute | solution.py:648
  23.7 3.3 %prepare.1 = (f32[2,256,256]{2,1,0:T(8,128)S(1)}, f32[4,256,256]{2,1,0:T(8,128)S(1)}, f32[4,2,256,256]{3,2,1,0:T(8,128)S(1)}) custom-call(s32[8]{0:T(128)S(1)} %reshape.26.places, bf16[256,256]{1,0:T(8,128)(2,1)S(1)} %copy-done.10, f32[2,256,256]{2,1,0:T(8,128)S(1)} %copy-done.9, f32[1,256,256]{2,1,0:T(8,128)S(1)} %bitcast.15, f32[1,256,256]{2,1,0:T(8,128)S(1)} %bitcast.16, ...), custom_call_target="tpu_custom_call" | custom-call | flops 503316480 | bytes 5767168 | tf_op jit(solution)/shard_map/prepare/pallas_call | solution.py:101
  27.0 4.5 %collective-permute-done.2.rest_2_ = bf16[2,512,128]{2,1,0:T(8,128)(2,1)} collective-permute-done((bf16[2,512,128]{2,1,0:T(8,128)(2,1)}, bf16[2,512,128]{2,1,0:T(8,128)(2,1)}, u32[]{:S(2)}, u32[]{:S(2)}) %collective-permute-start.2) | collective-permute-done | bytes 262176 | tf_op jit(solution)/shard_map/ppermute | solution.py:648
  31.5 2.6 %gather.1 = (bf16[4,2,256,256]{3,2,1,0:T(8,128)(2,1)S(1)}, bf16[4,2,256,256]{3,2,1,0:T(8,128)(2,1)S(1)}) custom-call(s32[16]{0:T(128)S(1)} %reshape.25.places, s32[2]{0:T(128)S(1)} %pad_add_fusion.1.offsets, bf16[1,512,1024]{2,1,0:T(8,128)(2,1)S(1)} %copy-done.2, bf16[1,512,1024]{2,1,0:T(8,128)(2,1)S(1)} %copy-done.4, ...), custom_call_target="tpu_custom_call" | custom-call | tf_op jit(solution)/shard_map/gather/pallas_call | solution.py:251
  34.2 2.6 %collective-permute-done.5.theirs = bf16[4,2,256,256]{3,2,1,0:T(8,128)(2,1)S(1)} collective-permute-done((bf16[4,2,256,256]{3,2,1,0:T(8,128)(2,1)S(1)}, bf16[4,2,256,256]{3,2,1,0:T(8,128)(2,1)S(1)}, u32[]{:S(2)}, u32[]{:S(2)}) %collective-permute-start.5) | collective-permute-done | bytes 1048608 | tf_op jit(solution)/shard_map/ppermute | solution.py:654
  36.8 18.9 %chain.1 = (f32[4,2,256,256]{3,2,1,0:T(8,128)S(1)}, bf16[4,2,256,256]{3,2,1,0:T(8,128)(2,1)}, f32[2,128,256]{2,1,0:T(8,128)S(1)}, f32[2,128,256]{2,1,0:T(8,128)}) custom-call(s32[8]{0:T(128)S(1)} %reshape.26.places, s32[4]{0:T(128)S(1)} %fusion.live, s32[1]{0:T(128)} %bitcast.4.here, bf16[4,2,256,256]{3,2,1,0:T(8,128)(2,1)S(1)} %copy-done.7, ...), custom_call_target="tpu_custom_call" | custom-call | tf_op jit(solution)/shard_map/chain/pallas_call | solution.py:392
  57.7 2.7 %collective-permute-done.7 = f32[2,128,256]{2,1,0:T(8,128)} collective-permute-done((f32[2,128,256]{2,1,0:T(8,128)}, f32[2,128,256]{2,1,0:T(8,128)}, u32[]{:S(2)}, u32[]{:S(2)}) %collective-permute-start.7) | collective-permute-done | bytes 262176 | tf_op jit(solution)/shard_map/ppermute | solution.py:659
  61.4 1.6 %copy-done.6 = f32[4,2,256,256]{3,2,1,0:T(8,128)S(1)} copy-done((f32[4,2,256,256]{3,2,1,0:T(8,128)S(1)}, f32[4,2,256,256]{3,2,1,0:T(8,128)}, u32[]{:S(2)}) %copy-start.6) | copy-done | bytes 2097176
  63.0 4.5 %scatter.1 = (f32[2,512,1024]{2,1,0:T(8,128)}, bf16[2,128,128]{2,1,0:T(8,128)(2,1)}, bf16[2,128,128]{2,1,0:T(8,128)(2,1)S(1)}, bf16[2,512,128]{2,1,0:T(8,128)(2,...) custom-call(s32[16]{0:T(128)S(1)} %reshape.25.places, s32[8]{0:T(128)S(1)} %reshape.27.live, ...), custom_call_target="tpu_custom_call" | custom-call | tf_op jit(solution)/shard_map/scatter/pallas_call | solution.py:487
  67.5 4.3 %collective-permute-start.13 = (bf16[2,128,256]{2,1,0:T(8,128)(2,1)S(1)}, bf16[2,128,256]{2,1,0:T(8,128)(2,1)S(1)}, u32[]{:S(2)}, u32[]{:S(2)}) collective-permute-start(bf16[2,128,256]{2,1,0:T(8,128)(2,1)S(1)} %add.24), channel_id=1, source_target_pairs={{0,4},{1,5},{2,6},{3,7},{4,0},{5,1},{6,2},{7,3},{8,12},{9,13},{10,... | collective-permute-start | bytes 393224 | tf_op jit(solution)/shard_map/ppermute | solution.py:595
  71.8 6.6 %collective-permute-done.13 = bf16[2,128,256]{2,1,0:T(8,128)(2,1)S(1)} collective-permute-done((bf16[2,128,256]{2,1,0:T(8,128)(2,1)S(1)}, bf16[2,128,256]{2,1,0:T(8,128)(2,1)S(1)}, u32[]{:S(2)}, u32[]{:S(2)}) %collective-permute-start.13) | collective-permute-done | bytes 131104 | tf_op jit(solution)/shard_map/ppermute | solution.py:595
  79.7 3.9 %collective-permute-done.14 = bf16[2,128,256]{2,1,0:T(8,128)(2,1)S(1)} collective-permute-done((bf16[2,128,256]{2,1,0:T(8,128)(2,1)S(1)}, bf16[2,128,256]{2,1,0:T(8,128)(2,1)S(1)}, u32[]{:S(2)}, u32[]{:S(2)}) %collective-permute-start.14) | collective-permute-done | bytes 131104 | tf_op jit(solution)/shard_map/ppermute | solution.py:595
  83.6 1.5 %collective-permute-start.15 = (bf16[2,128,256]{2,1,0:T(8,128)(2,1)S(1)}, bf16[2,128,256]{2,1,0:T(8,128)(2,1)S(1)}, u32[]{:S(2)}, u32[]{:S(2)}) collective-permute-start(bf16[2,128,256]{2,1,0:T(8,128)(2,1)S(1)} %add_convert_fusion.1), channel_id=1, source_target_pairs={{0,1},{1,0},{2,3},{3,2},{4,5},{5,4},{6,7},{7,6},{8,9},{9,8},{10,11... | collective-permute-start | bytes 393224 | tf_op jit(solution)/shard_map/ppermute | solution.py:595
  85.1 2.3 %collective-permute-start.8 = (bf16[2,128,128]{2,1,0:T(8,128)(2,1)}, bf16[2,128,128]{2,1,0:T(8,128)(2,1)S(1)}, u32[]{:S(2)}, u32[]{:S(2)}) collective-permute-start(bf16[2,128,128]{2,1,0:T(8,128)(2,1)} %get-tuple-element.48), channel_id=1, source_target_pairs={{0,9},{1,10},{2,11},{3,12},{4,13},{5,14},{6,15},{8,1},{9,2},{10,3}... | collective-permute-start | bytes 196616 | tf_op jit(solution)/shard_map/ppermute | solution.py:666
  87.5 2.5 %collective-permute-start.10 = (bf16[2,512,128]{2,1,0:T(8,128)(2,1)}, bf16[2,512,128]{2,1,0:T(8,128)(2,1)S(1)}, u32[]{:S(2)}, u32[]{:S(2)}) collective-permute-start(bf16[2,512,128]{2,1,0:T(8,128)(2,1)} %get-tuple-element.50), channel_id=1, source_target_pairs={{0,1},{1,2},{2,3},{3,4},{4,5},{5,6},{6,7},{8,9},{9,10},{10,11},{11... | collective-permute-start | bytes 786440 | tf_op jit(solution)/shard_map/ppermute | solution.py:666
  91.9 2.2 %collective-permute-start.16 = (bf16[2,128,256]{2,1,0:T(8,128)(2,1)}, bf16[2,128,256]{2,1,0:T(8,128)(2,1)}, u32[]{:S(2)}, u32[]{:S(2)}) collective-permute-start(bf16[2,128,256]{2,1,0:T(8,128)(2,1)} %add_convert_fusion), channel_id=1, source_target_pairs={{0,8},{8,0},{1,9},{9,1},{2,10},{10,2},{3,11},{11,3},{4,12},{12,4},... | collective-permute-start | bytes 393224 | tf_op jit(solution)/shard_map/ppermute | solution.py:595
  95.5 5.7 %collective-permute-done.9.rest_1_ = bf16[2,128,128]{2,1,0:T(8,128)(2,1)S(1)} collective-permute-done((bf16[2,128,128]{2,1,0:T(8,128)(2,1)S(1)}, bf16[2,128,128]{2,1,0:T(8,128)(2,1)S(1)}, u32[]{:S(2)}, u32[]{:S(2)}) %collective-permute-start.9) | collective-permute-done | bytes 65568 | tf_op jit(solution)/shard_map/ppermute | solution.py:666
  101.2 2.1 %collective-permute-done.10.rest_2_ = bf16[2,512,128]{2,1,0:T(8,128)(2,1)S(1)} collective-permute-done((bf16[2,512,128]{2,1,0:T(8,128)(2,1)}, bf16[2,512,128]{2,1,0:T(8,128)(2,1)S(1)}, u32[]{:S(2)}, u32[]{:S(2)}) %collective-permute-start.10) | collective-permute-done | bytes 262176 | tf_op jit(solution)/shard_map/ppermute | solution.py:666
  103.3 3.2 %borders.1 = f32[2,512,1024]{2,1,0:T(8,128)} custom-call(s32[2]{0:T(128)S(1)} %pad_add_fusion.offsets, f32[2,512,1024]{2,1,0:T(8,128)} %get-tuple-element.40.tile_in, bf16[2,128,128]{2,1,0:T(8,128)(2,1)S(1)} %collective-permute-done.8.rest_0_, bf16[2,128,128]{2,1,0:T(8,128)(2,1)S(1)} %collective-permute-done.9.rest_1_, ...), custom_call_target="tpu_custom_call", output_to_operand_aliasing={{}: (1, {})} | custom-call | tf_op jit(solution)/shard_map/borders/pallas_call | solution.py:550
  106.5 1.7 %convert_add_fusion = f32[2,128,256]{2,1,0:T(8,128)} fusion(bf16[2,128,256]{2,1,0:T(8,128)(2,1)} %collective-permute-done.16, bf16[2,128,256]{2,1,0:T(8,128)(2,1)} %add_convert_fusion), kind=kLoop, calls=%fused_computation.1 | loop fusion | flops 196608 | bytes 524288 | tf_op jit(solution)/shard_map/add | solution.py:596
  (60 shorter events, 14.5 us)
Async XLA Ops:
  0.6 20.1 %copy-start = (f32[1,1,4,2,256,256]{5,4,3,2,1,0:T(8,128)S(1)}, f32[1,1,4,2,256,256]{5,4,3,2,1,0:T(8,128)}, u32[]{:S(2)}) copy-start(f32[1,1,4,2,256,256]{5,4,3,2,1,0:T(8,128)} %param.15) | copy-start | bytes 6291460
  3.3 17.5 %copy-start.11 = (s32[1,1,4,2,2]{2,4,3,1,0:T(2,128)S(1)}, s32[1,1,4,2,2]{2,4,3,1,0:T(2,128)}, u32[]{:S(2)}) copy-start(s32[1,1,4,2,2]{2,4,3,1,0:T(2,128)} %param.13) | copy-start | bytes 196
  3.3 19.1 %copy-start.8 = (f32[256,256]{1,0:T(8,128)S(1)}, f32[256,256]{1,0:T(8,128)}, u32[]{:S(2)}) copy-start(f32[256,256]{1,0:T(8,128)} %param.12) | copy-start | bytes 786436
  3.3 19.1 %copy-start.10 = (bf16[256,256]{1,0:T(8,128)(2,1)S(1)}, bf16[256,256]{1,0:T(8,128)(2,1)}, u32[]{:S(2)}) copy-start(bf16[256,256]{1,0:T(8,128)(2,1)} %constant.37.clone.order_t) | copy-start | bytes 393220
  5.0 26.5 %collective-permute-start.4 = (bf16[2,128,1024]{2,1,0:T(8,128)(2,1)}, bf16[2,128,1024]{2,1,0:T(8,128)(2,1)}, u32[]{:S(2)}, u32[]{:S(2)}) collective-permute-start(bf16[2,128,1024]{2,1,0:T(8,128)(2,1)} %get-tuple-element.34), channel_id=1, source_target_pairs={{0,8},{1,9},{2,10},{3,11},{4,12},{5,13},{6,14},{7,15},{8,0},{9,1},... | collective-permute-start | bytes 1572872 | tf_op jit(solution)/shard_map/ppermute | solution.py:648
  8.0 19.0 %collective-permute-start = (bf16[2,128,128]{2,1,0:T(8,128)(2,1)}, bf16[2,128,128]{2,1,0:T(8,128)(2,1)}, u32[]{:S(2)}, u32[]{:S(2)}) collective-permute-start(bf16[2,128,128]{2,1,0:T(8,128)(2,1)} %get-tuple-element.30), channel_id=1, source_target_pairs={{0,9},{1,10},{2,11},{3,12},{4,13},{5,14},{6,15},{8,1},{9,2},{10,3}... | collective-permute-start | bytes 196616 | tf_op jit(solution)/shard_map/ppermute | solution.py:648
  12.0 15.0 %collective-permute-start.1 = (bf16[2,128,128]{2,1,0:T(8,128)(2,1)}, bf16[2,128,128]{2,1,0:T(8,128)(2,1)}, u32[]{:S(2)}, u32[]{:S(2)}) collective-permute-start(bf16[2,128,128]{2,1,0:T(8,128)(2,1)} %get-tuple-element.31), channel_id=1, source_target_pairs={{1,8},{2,9},{3,10},{4,11},{5,12},{6,13},{7,14},{9,0},{10,1},{11,2}... | collective-permute-start | bytes 196616 | tf_op jit(solution)/shard_map/ppermute | solution.py:648
  13.3 18.1 %collective-permute-start.2 = (bf16[2,512,128]{2,1,0:T(8,128)(2,1)}, bf16[2,512,128]{2,1,0:T(8,128)(2,1)}, u32[]{:S(2)}, u32[]{:S(2)}) collective-permute-start(bf16[2,512,128]{2,1,0:T(8,128)(2,1)} %get-tuple-element.32), channel_id=1, source_target_pairs={{0,1},{1,2},{2,3},{3,4},{4,5},{5,6},{6,7},{8,9},{9,10},{10,11},{11... | collective-permute-start | bytes 786440 | tf_op jit(solution)/shard_map/ppermute | solution.py:648
  19.5 12.0 %collective-permute-start.3 = (bf16[2,512,128]{2,1,0:T(8,128)(2,1)}, bf16[2,512,128]{2,1,0:T(8,128)(2,1)}, u32[]{:S(2)}, u32[]{:S(2)}) collective-permute-start(bf16[2,512,128]{2,1,0:T(8,128)(2,1)} %get-tuple-element.33), channel_id=1, source_target_pairs={{1,0},{2,1},{3,2},{4,3},{5,4},{6,5},{7,6},{9,8},{10,9},{11,10},{12... | collective-permute-start | bytes 786440 | tf_op jit(solution)/shard_map/ppermute | solution.py:648
  22.4 9.0 %copy-start.2 = (bf16[1,512,1024]{2,1,0:T(8,128)(2,1)S(1)}, bf16[1,512,1024]{2,1,0:T(8,128)(2,1)}, u32[]{:S(2)}) copy-start(bf16[1,512,1024]{2,1,0:T(8,128)(2,1)} %tile_re.3) | copy-start | bytes 3145732
  22.4 9.0 %copy-start.4 = (bf16[1,512,1024]{2,1,0:T(8,128)(2,1)S(1)}, bf16[1,512,1024]{2,1,0:T(8,128)(2,1)}, u32[]{:S(2)}) copy-start(bf16[1,512,1024]{2,1,0:T(8,128)(2,1)} %tile_im.3) | copy-start | bytes 3145732
  31.4 5.4 %copy-start.7 = (bf16[4,2,256,256]{3,2,1,0:T(8,128)(2,1)S(1)}, bf16[4,2,256,256]{3,2,1,0:T(8,128)(2,1)}, u32[]{:S(2)}) copy-start(bf16[4,2,256,256]{3,2,1,0:T(8,128)(2,1)} %constant.38.clone.tables) | copy-start | bytes 3145732
  34.1 2.7 %collective-permute-start.5 = (bf16[4,2,256,256]{3,2,1,0:T(8,128)(2,1)S(1)}, bf16[4,2,256,256]{3,2,1,0:T(8,128)(2,1)S(1)}, u32[]{:S(2)}, u32[]{:S(2)}) collective-permute-start(bf16[4,2,256,256]{3,2,1,0:T(8,128)(2,1)S(1)} %get-tuple-element.36), channel_id=1, source_target_pairs={{0,16},{16,0},{1,17},{17,1},{2,18},{18,2},{3,19},{19,3},{4,20},{20... | collective-permute-start | bytes 3145736 | tf_op jit(solution)/shard_map/ppermute | solution.py:654
  57.0 4.4 %collective-permute-start.6 = (bf16[4,2,256,256]{3,2,1,0:T(8,128)(2,1)}, bf16[4,2,256,256]{3,2,1,0:T(8,128)(2,1)S(1)}, u32[]{:S(2)}, u32[]{:S(2)}) collective-permute-start(bf16[4,2,256,256]{3,2,1,0:T(8,128)(2,1)} %get-tuple-element.39), channel_id=1, source_target_pairs={{0,16},{16,0},{1,17},{17,1},{2,18},{18,2},{3,19},{19,3},{4,20},{20... | collective-permute-start | bytes 3145736 | tf_op jit(solution)/shard_map/ppermute | solution.py:658
  57.1 3.3 %collective-permute-start.7 = (f32[2,128,256]{2,1,0:T(8,128)}, f32[2,128,256]{2,1,0:T(8,128)}, u32[]{:S(2)}, u32[]{:S(2)}) collective-permute-start(f32[2,128,256]{2,1,0:T(8,128)} %get-tuple-element.47), channel_id=1, source_target_pairs={{0,16},{16,0},{1,17},{17,1},{2,18},{18,2},{3,19},{19,3},{4,20},{20... | collective-permute-start | bytes 786440 | tf_op jit(solution)/shard_map/ppermute | solution.py:659
  67.5 10.9 %collective-permute-start.13 = (bf16[2,128,256]{2,1,0:T(8,128)(2,1)S(1)}, bf16[2,128,256]{2,1,0:T(8,128)(2,1)S(1)}, u32[]{:S(2)}, u32[]{:S(2)}) collective-permute-start(bf16[2,128,256]{2,1,0:T(8,128)(2,1)S(1)} %add.24), channel_id=1, source_target_pairs={{0,4},{1,5},{2,6},{3,7},{4,0},{5,1},{6,2},{7,3},{8,12},{9,13},{10,... | collective-permute-start | bytes 393224 | tf_op jit(solution)/shard_map/ppermute | solution.py:595
  78.5 5.1 %collective-permute-start.14 = (bf16[2,128,256]{2,1,0:T(8,128)(2,1)S(1)}, bf16[2,128,256]{2,1,0:T(8,128)(2,1)S(1)}, u32[]{:S(2)}, u32[]{:S(2)}) collective-permute-start(bf16[2,128,256]{2,1,0:T(8,128)(2,1)S(1)} %add_convert_fusion.2), channel_id=1, source_target_pairs={{0,2},{1,3},{2,0},{3,1},{4,6},{5,7},{6,4},{7,5},{8,10},{9,11},{10,... | collective-permute-start | bytes 393224 | tf_op jit(solution)/shard_map/ppermute | solution.py:595
  79.3 24.0 %collective-permute-start.12 = (bf16[2,128,1024]{2,1,0:T(8,128)(2,1)}, bf16[2,128,1024]{2,1,0:T(8,128)(2,1)S(1)}, u32[]{:S(2)}, u32[]{:S(2)}) collective-permute-start(bf16[2,128,1024]{2,1,0:T(8,128)(2,1)} %get-tuple-element.52), channel_id=1, source_target_pairs={{0,8},{1,9},{2,10},{3,11},{4,12},{5,13},{6,14},{7,15},{8,0},{9,1},... | collective-permute-start | bytes 1572872 | tf_op jit(solution)/shard_map/ppermute | solution.py:666
  83.6 7.6 %collective-permute-start.15 = (bf16[2,128,256]{2,1,0:T(8,128)(2,1)S(1)}, bf16[2,128,256]{2,1,0:T(8,128)(2,1)S(1)}, u32[]{:S(2)}, u32[]{:S(2)}) collective-permute-start(bf16[2,128,256]{2,1,0:T(8,128)(2,1)S(1)} %add_convert_fusion.1), channel_id=1, source_target_pairs={{0,1},{1,0},{2,3},{3,2},{4,5},{5,4},{6,7},{7,6},{8,9},{9,8},{10,11... | collective-permute-start | bytes 393224 | tf_op jit(solution)/shard_map/ppermute | solution.py:595
  85.1 9.0 %collective-permute-start.8 = (bf16[2,128,128]{2,1,0:T(8,128)(2,1)}, bf16[2,128,128]{2,1,0:T(8,128)(2,1)S(1)}, u32[]{:S(2)}, u32[]{:S(2)}) collective-permute-start(bf16[2,128,128]{2,1,0:T(8,128)(2,1)} %get-tuple-element.48), channel_id=1, source_target_pairs={{0,9},{1,10},{2,11},{3,12},{4,13},{5,14},{6,15},{8,1},{9,2},{10,3}... | collective-permute-start | bytes 196616 | tf_op jit(solution)/shard_map/ppermute | solution.py:666
  87.5 15.8 %collective-permute-start.10 = (bf16[2,512,128]{2,1,0:T(8,128)(2,1)}, bf16[2,512,128]{2,1,0:T(8,128)(2,1)S(1)}, u32[]{:S(2)}, u32[]{:S(2)}) collective-permute-start(bf16[2,512,128]{2,1,0:T(8,128)(2,1)} %get-tuple-element.50), channel_id=1, source_target_pairs={{0,1},{1,2},{2,3},{3,4},{4,5},{5,6},{6,7},{8,9},{9,10},{10,11},{11... | collective-permute-start | bytes 786440 | tf_op jit(solution)/shard_map/ppermute | solution.py:666
  89.9 13.3 %collective-permute-start.11 = (bf16[2,512,128]{2,1,0:T(8,128)(2,1)S(1)}, bf16[2,512,128]{2,1,0:T(8,128)(2,1)S(1)}, u32[]{:S(2)}, u32[]{:S(2)}) collective-permute-start(bf16[2,512,128]{2,1,0:T(8,128)(2,1)S(1)} %get-tuple-element.51), channel_id=1, source_target_pairs={{1,0},{2,1},{3,2},{4,3},{5,4},{6,5},{7,6},{9,8},{10,9},{11,10},{12... | collective-permute-start | bytes 786440 | tf_op jit(solution)/shard_map/ppermute | solution.py:666
  91.9 14.6 %collective-permute-start.16 = (bf16[2,128,256]{2,1,0:T(8,128)(2,1)}, bf16[2,128,256]{2,1,0:T(8,128)(2,1)}, u32[]{:S(2)}, u32[]{:S(2)}) collective-permute-start(bf16[2,128,256]{2,1,0:T(8,128)(2,1)} %add_convert_fusion), channel_id=1, source_target_pairs={{0,8},{8,0},{1,9},{9,1},{2,10},{10,2},{3,11},{11,3},{4,12},{12,4},... | collective-permute-start | bytes 393224 | tf_op jit(solution)/shard_map/ppermute | solution.py:595
  94.2 7.0 %collective-permute-start.9 = (bf16[2,128,128]{2,1,0:T(8,128)(2,1)S(1)}, bf16[2,128,128]{2,1,0:T(8,128)(2,1)S(1)}, u32[]{:S(2)}, u32[]{:S(2)}) collective-permute-start(bf16[2,128,128]{2,1,0:T(8,128)(2,1)S(1)} %get-tuple-element.49), channel_id=1, source_target_pairs={{1,8},{2,9},{3,10},{4,11},{5,12},{6,13},{7,14},{9,0},{10,1},{11,2}... | collective-permute-start | bytes 196616 | tf_op jit(solution)/shard_map/ppermute | solution.py:666
  (6 other events, 9.4 us)

commit v3 on v2

--- a/solution.py
+++ b/solution.py
@@ -12,7 +12,8 @@
 bf16 = jnp.bfloat16
 ROWS = 16
 LANES = 128
-HBM = pl.BlockSpec(memory_space=pl.ANY)
+ANY = pl.BlockSpec(memory_space=pl.ANY)
+HBM = pl.BlockSpec(memory_space=pltpu.HBM)
 SMEM = pl.BlockSpec(memory_space=pltpu.SMEM)
 MIB = 1024 * 1024
 
@@ -134,20 +135,23 @@
     )
 
 
-def pack_kernel(edges, half, offsets, tile_re, tile_im, *rest):
+def span(key, offsets, names, half, whole):
+    if key is None:
+        return whole
+    return pl.ds(pl.multiple_of(offsets[names.index(key)], half), half)
+
+
+def pack_kernel(edges, names, half, offsets, tile_re, tile_im, *rest):
     strips, sems = rest[:-1], rest[-1]
     tile_rows, tile_cols = tile_re.shape[1:]
-    columns = {-1: pl.ds(0, half), 0: pl.ds(0, tile_cols), 1: pl.ds(tile_cols - half, half)}
     copies = []
-    for (side, across), strip in zip(edges, strips):
-        if side is None:
-            rows = pl.ds(0, tile_rows)
-        else:
-            rows = pl.ds(pl.multiple_of(offsets[side], half), half)
+    for (down, across), strip in zip(edges, strips):
+        rows = span(down, offsets, names, half, pl.ds(0, tile_rows))
+        cols = span(across, offsets, names, half, pl.ds(0, tile_cols))
         for plane, tile in enumerate((tile_re, tile_im)):
             copies.append(
                 pltpu.make_async_copy(
-                    tile.at[0, rows, columns[across]], strip.at[plane], sems.at[len(copies)]
+                    tile.at[0, rows, cols], strip.at[plane], sems.at[len(copies)]
                 )
             )
             copies[-1].start()
@@ -158,17 +162,17 @@
 def strip_shapes(edges, tile_rows, tile_cols, half):
     return [
         jax.ShapeDtypeStruct(
-            (2, tile_rows if side is None else half, half if across else tile_cols), bf16
+            (2, half if down else tile_rows, half if across else tile_cols), bf16
         )
-        for side, across in edges
+        for down, across in edges
     ]
 
 
-def pack(offsets, tile_re, tile_im, edges, half):
+def pack(offsets, tile_re, tile_im, edges, names, half):
     return pl.pallas_call(
-        functools.partial(pack_kernel, edges, half),
+        functools.partial(pack_kernel, edges, names, half),
         in_specs=[SMEM, HBM, HBM],
-        out_specs=[HBM] * len(edges),
+        out_specs=[ANY] * len(edges),
         out_shape=strip_shapes(edges, *tile_re.shape[1:], half),
         scratch_shapes=[pltpu.SemaphoreType.DMA((2 * len(edges),))],
         compiler_params=pltpu.CompilerParams(vmem_limit_bytes=4 * MIB),
@@ -182,7 +186,7 @@
     return down, across, pl.multiple_of(row - down, ROWS), pl.multiple_of(col - across, LANES)
 
 
-def gather_kernel(spots, edges, half, places, offsets, tile_re, tile_im, after, *rest):
+def gather_kernel(spots, edges, names, half, places, offsets, tile_re, tile_im, after, *rest):
     strips, (mine, other, padded, sems) = rest[:-4], rest[-4:]
     tile_rows, tile_cols = tile_re.shape[1:]
     size = mine.shape[-1]
@@ -195,13 +199,10 @@
 
     bring(tile_re.at[0], padded.at[(0,) + body])
     bring(tile_im.at[0], padded.at[(1,) + body])
-    columns = {-1: pl.ds(0, half), 0: body[1], 1: pl.ds(half + tile_cols, half)}
-    for (side, across), strip in zip(edges, strips):
-        if side is None:
-            down = body[0]
-        else:
-            down = pl.ds(pl.multiple_of(offsets[side], half), half)
-        bring(strip, padded.at[:, down, columns[across]])
+    for (down, across), strip in zip(edges, strips):
+        rows = span(down, offsets, names, half, body[0])
+        cols = span(across, offsets, names, half, body[1])
+        bring(strip, padded.at[:, rows, cols])
     for copy in copies:
         copy.wait()
 
@@ -242,15 +243,15 @@
         cut(sections * place + here, mine, place)
 
 
-def gather(places, offsets, tile_re, tile_im, after, edges, strips, size):
+def gather(places, offsets, tile_re, tile_im, after, edges, names, strips, size):
     half = size // 2
     spots = places.shape[0] // 2
     tile_rows, tile_cols = tile_re.shape[1:]
     shape = jax.ShapeDtypeStruct((spots // 2, 2, size, size), bf16)
     vmem = pl.BlockSpec(memory_space=pltpu.VMEM)
     return pl.pallas_call(
-        functools.partial(gather_kernel, spots, edges, half),
-        in_specs=[SMEM, SMEM] + [HBM] * (3 + len(strips)),
+        functools.partial(gather_kernel, spots, edges, names, half),
+        in_specs=[SMEM, SMEM, HBM, HBM] + [ANY] * (1 + len(strips)),
         out_specs=[vmem, vmem],
         out_shape=[shape, shape],
         scratch_shapes=[
@@ -264,7 +265,7 @@
 
 def chain_kernel(
     group, places, live, here, tables, kern, mine, theirs, frames, waves,
-    keep, send, pulled_keep, pulled_send, windows, middle, terms, pulled, sems,
+    keep, send, pulled_keep, pulled_send, windows, middle, terms, pulled, sems, keep_sems,
 ):
     step = pl.program_id(0)
     steps = pl.num_programs(0)
@@ -355,14 +356,14 @@
             back.append(cols_of(re * misfit, im * misfit))
         cre, cim = inverse(*back)
         pre, pim = middle[at, 0].astype(f32), middle[at, 1].astype(f32)
-        terms[1, at, 0] = pre * cre + pim * cim
-        terms[1, at, 1] = pre * cim - pim * cre
+        terms[step, 1, at, 0] = pre * cre + pim * cim
+        terms[step, 1, at, 1] = pre * cim - pim * cre
         wre, wim = window(1, at)
         re, im = propagate(wre * cre + wim * cim, wre * cim - wim * cre, -1.0)
         cre, cim = rounded(re), rounded(im)
         pre, pim = waves[at, 0], waves[at, 1]
-        terms[0, at, 0] = pre * cre + pim * cim
-        terms[0, at, 1] = pre * cim - pim * cre
+        terms[step, 0, at, 0] = pre * cre + pim * cim
+        terms[step, 0, at, 1] = pre * cim - pim * cre
         wre, wim = window(0, at)
         spot_at = step * group + at
         up = (size - places[2 * spot_at] % ROWS) % size
@@ -372,11 +373,18 @@
             value = pltpu.roll(pltpu.roll(value * weight, back_by, axis=1), up, axis=0)
             pulled[plane] += value
 
-    keep[...] = terms[me]
-    send[...] = terms[1 - me].astype(bf16)
+    send[...] = terms[step, 1 - me].astype(bf16)
+
+    def put(at):
+        rows = pl.ds(at * group, group)
+        return pltpu.make_async_copy(terms.at[at, me], keep.at[rows], keep_sems.at[at])
+
+    put(step).start()
 
     @pl.when(step == steps - 1)
     def _():
+        for at in range(terms.shape[0]):
+            put(at).wait()
         share = pulled_keep.shape[1]
         for plane in range(2):
             pulled_keep[plane] = pulled[plane, pl.ds(pl.multiple_of(me * share, share), share), :]
@@ -398,12 +406,12 @@
             SMEM,
             full(4, 2, size, size),
             full(2, size, size),
-            HBM,
-            HBM,
+            ANY,
+            ANY,
             pl.BlockSpec((group, size, size), lambda i: (i, 0, 0)),
             block,
         ],
-        out_specs=[block, block, full(2, size // 2, size), full(2, size // 2, size)],
+        out_specs=[HBM, block, full(2, size // 2, size), full(2, size // 2, size)],
         out_shape=[
             jax.ShapeDtypeStruct((count, 2, size, size), f32),
             jax.ShapeDtypeStruct((count, 2, size, size), bf16),
@@ -413,16 +421,17 @@
         scratch_shapes=[
             pltpu.VMEM((count // group, 2, group, 2, size, size), bf16),
             pltpu.VMEM((group, 2, size, size), bf16),
-            pltpu.VMEM((2, group, 2, size, size), f32),
+            pltpu.VMEM((count // group, 2, group, 2, size, size), f32),
             pltpu.VMEM((2, size, size), f32),
             pltpu.SemaphoreType.DMA((2 * (count // group),)),
+            pltpu.SemaphoreType.DMA((count // group,)),
         ],
         compiler_params=pltpu.CompilerParams(vmem_limit_bytes=40 * MIB),
         name="chain",
     )(places, live, here, jnp.asarray(dft_tables(size)), kern, mine, theirs, frames, waves)
 
 
-def scatter_kernel(edges, half, places, live, offsets, kept, arrived, tile, *rest):
+def scatter_kernel(edges, names, half, places, live, offsets, kept, arrived, tile, *rest):
     strips, (total, near, far, sems) = rest[:-4], rest[-4:]
     count, size = kept.shape[0], kept.shape[-1]
     tile_rows, tile_cols = tile.shape[1:]
@@ -469,24 +478,21 @@
     body = (pl.ds(half, tile_rows), pl.ds(half, tile_cols))
     copy = pltpu.make_async_copy(total.at[(slice(None),) + body], tile, sems.at[0])
     copy.start()
-    columns = {-1: pl.ds(0, half), 0: body[1], 1: pl.ds(half + tile_cols, half)}
-    for (side, across), strip in zip(edges, strips):
-        if side is None:
-            rows = body[0]
-        else:
-            rows = pl.ds(pl.multiple_of(offsets[side], half), half)
+    for (down, across), strip in zip(edges, strips):
+        rows = span(down, offsets, names, half, body[0])
+        cols = span(across, offsets, names, half, body[1])
         for plane in range(2):
-            strip[plane] = total[plane, rows, columns[across]].astype(bf16)
+            strip[plane] = total[plane, rows, cols].astype(bf16)
     copy.wait()
 
 
-def scatter(places, live, offsets, kept, arrived, edges, tile_rows, tile_cols):
+def scatter(places, live, offsets, kept, arrived, edges, names, tile_rows, tile_cols):
     count, _, size, _ = kept.shape
     half = size // 2
     vmem = pl.BlockSpec(memory_space=pltpu.VMEM)
     return pl.pallas_call(
-        functools.partial(scatter_kernel, edges, half),
-        in_specs=[SMEM, SMEM, SMEM, HBM, HBM],
+        functools.partial(scatter_kernel, edges, names, half),
+        in_specs=[SMEM, SMEM, SMEM, HBM, ANY],
         out_specs=[HBM] + [vmem] * len(edges),
         out_shape=[jax.ShapeDtypeStruct((2, tile_rows, tile_cols), f32)]
         + strip_shapes(edges, tile_rows, tile_cols, half),
@@ -501,98 +507,99 @@
     )(places, live, offsets, kept, arrived)
 
 
-def border_kernel(edges, half, offsets, tile_in, *rest):
-    sides = offsets.shape[0] - 1
-    strips, (tile, bands, left, right, in_sems, out_sems) = rest[: len(edges)], rest[len(edges) :]
+def border_kernel(edges, names, half, offsets, tile_in, *rest):
+    strips, (tile, bands, sides, in_sems, out_sems) = rest[: len(edges)], rest[len(edges) :]
     tile_rows, tile_cols = tile.shape[1:]
     strips = dict(zip(edges, strips))
-    tall = left.shape[1]
-    rows = pl.ds(pl.multiple_of(offsets[sides], half), tall)
+    downs = [key for key in names if key[0] == "row"]
+    acrosses = [key for key in names if key[0] == "col"]
+    tall = sides.shape[2]
+    rest_rows = pl.ds(pl.multiple_of(offsets[len(names)], half), tall)
+    spans = {key: span(key, offsets, names, half, None) for key in names}
     regions = []
-    for side in range(sides):
-        band = pl.ds(pl.multiple_of(offsets[side], half), half)
-        regions.append((bands.at[side], band, pl.ds(0, tile_cols)))
-    regions.append((left, rows, pl.ds(0, half)))
-    regions.append((right, rows, pl.ds(tile_cols - half, half)))
+    for k, key in enumerate(acrosses):
+        regions.append((key, sides.at[k], rest_rows, spans[key]))
+    for k, key in enumerate(downs):
+        regions.append((key, bands.at[k], spans[key], pl.ds(0, tile_cols)))
 
     def copy(k, out):
-        block, down, wide = regions[k]
+        _, block, rows, cols = regions[k]
         if out:
-            return pltpu.make_async_copy(block, tile.at[:, down, wide], out_sems.at[k])
-        return pltpu.make_async_copy(tile_in.at[:, down, wide], block, in_sems.at[k])
-
-    order = [sides, sides + 1, *range(sides)]
-    for k in order:
+            return pltpu.make_async_copy(block, tile.at[:, rows, cols], out_sems.at[k])
+        return pltpu.make_async_copy(tile_in.at[:, rows, cols], block, in_sems.at[k])
+
+    for k in range(len(regions)):
         copy(k, False).start()
-    for k in order:
+    for k, (key, block, rows, cols) in enumerate(regions):
         copy(k, False).wait()
-        block, down, wide = regions[k]
         for plane in range(2):
-            if k < sides:
-                block[plane] += strips[(k, 0)][plane].astype(f32)
-                for across, cols in ((-1, slice(0, half)), (1, slice(tile_cols - half, tile_cols))):
-                    block[plane, :, cols] += strips[(k, across)][plane].astype(f32) + strips[
-                        (None, across)
-                    ][plane, down, :].astype(f32)
+            if key in downs:
+                block[plane] += strips[(key, None)][plane].astype(f32)
+                for across in acrosses:
+                    block[plane, :, spans[across]] += strips[(key, across)][plane].astype(
+                        f32
+                    ) + strips[(None, across)][plane, rows, :].astype(f32)
             else:
-                across = -1 if k == sides else 1
-                block[plane] += strips[(None, across)][plane, down, :].astype(f32)
+                block[plane] += strips[(None, key)][plane, rows, :].astype(f32)
         copy(k, True).start()
-    for k in order:
+    for k in range(len(regions)):
         copy(k, True).wait()
 
 
-def add_borders(offsets, tile, edges, strips, half):
+def add_borders(offsets, tile, edges, names, strips, half):
     vmem = pl.BlockSpec(memory_space=pltpu.VMEM)
-    sides = offsets.shape[0] - 1
+    downs = sum(key[0] == "row" for key in names)
+    acrosses = len(names) - downs
     tile_rows, tile_cols = tile.shape[1:]
-    column = (2, tile_rows - sides * half, half)
     return pl.pallas_call(
-        functools.partial(border_kernel, edges, half),
+        functools.partial(border_kernel, edges, names, half),
         in_specs=[SMEM, HBM] + [vmem] * len(strips),
         out_specs=HBM,
         out_shape=jax.ShapeDtypeStruct(tile.shape, f32),
         scratch_shapes=[
-            pltpu.VMEM((max(sides, 1), 2, half, tile_cols), f32),
-            pltpu.VMEM(column, f32),
-            pltpu.VMEM(column, f32),
-            pltpu.SemaphoreType.DMA((sides + 2,)),
-            pltpu.SemaphoreType.DMA((sides + 2,)),
+            pltpu.VMEM((max(downs, 1), 2, half, tile_cols), f32),
+            pltpu.VMEM((max(acrosses, 1), 2, tile_rows - downs * half, half), f32),
+            pltpu.SemaphoreType.DMA((max(len(names), 1),)),
+            pltpu.SemaphoreType.DMA((max(len(names), 1),)),
         ],
         input_output_aliases={1: 0},
         compiler_params=pltpu.CompilerParams(vmem_limit_bytes=12 * MIB),
+        cost_estimate=pl.CostEstimate(
+            flops=2 * tile_rows * tile_cols,
+            bytes_accessed=16 * tile_rows * tile_cols,
+            transcendentals=0,
+        ),
         name="borders",
     )(offsets, tile, *strips)
 
 
-def routes(edges, sides, rows, cols):
-    result = []
-    for side, across in edges:
-        pairs = []
-        for r in range(rows):
-            if side is None:
-                to_row = r
-            elif rows == 2:
-                to_row = 1 - r
-            else:
-                to_row = r + sides[side]
-            for c in range(cols):
-                to_col = c + across
-                if 0 <= to_row < rows and 0 <= to_col < cols:
-                    pairs.append((r * cols + c, to_row * cols + to_col))
-        result.append(pairs)
-    return result
-
-
-def summed(block, axes):
+def partner(index, kind):
+    return index ^ 1 if kind == 0 else ((index + 1) ^ 1) - 1
+
+
+def route(edge, rows, cols):
+    down, across = edge
+    pairs = []
+    for r in range(rows):
+        to_row = partner(r, down[1]) if down else r
+        for c in range(cols):
+            to_col = partner(c, across[1]) if across else c
+            if 0 <= to_row < rows and 0 <= to_col < cols:
+                pairs.append((r * cols + c, to_row * cols + to_col))
+    return pairs
+
+
+def exchanged(block, axes, between=None):
     for axis in axes:
         size = lax.axis_size(axis)
         if size & (size - 1):
             block = lax.psum(block, axis)
             continue
-        for step in reversed([1 << k for k in range(size.bit_length() - 1)]):
+        for step in [1 << k for k in range(size.bit_length() - 1)]:
             own = block.astype(bf16)
             other = lax.ppermute(own, axis, [(i, i ^ step) for i in range(size)])
+            if between is not None:
+                other, between = between(other), None
             block = own.astype(f32) + other.astype(f32)
     return block
 
@@ -622,33 +629,32 @@
         measured.reshape(count, sections, size, size), here, 1, False
     )
 
-    if rows == 1:
-        sides, from_rows, pad_rows, fold_rows = [], [], [], []
-    elif rows == 2:
-        sides = [0]
-        from_rows = [jnp.where(row_at == 0, tile_rows - half, 0)]
-        pad_rows = [jnp.where(row_at == 0, tile_rows + half, 0)]
-        fold_rows = from_rows
-    else:
-        sides = [1, -1]
-        from_rows = [jnp.int32(tile_rows - half), jnp.int32(0)]
-        pad_rows = [jnp.int32(0), jnp.int32(tile_rows + half)]
-        fold_rows = [jnp.int32(0), jnp.int32(tile_rows - half)]
-    edges = [(side, across) for side in range(len(sides)) for across in (1, -1)]
-    edges += [(None, 1), (None, -1)]
-    edges += [(side, 0) for side in range(len(sides))]
-    paths = routes(edges, sides, rows, cols)
+    names, tile_at, padded_at = [], [], []
+    for axis, extent, own, length in (
+        ("row", rows, row_at, tile_rows),
+        ("col", cols, lax.axis_index("col").astype(jnp.int32), tile_cols),
+    ):
+        for kind in range(min(2, extent - 1)):
+            forward = own % 2 == kind
+            names.append((axis, kind))
+            tile_at.append(jnp.where(forward, length - half, 0))
+            padded_at.append(jnp.where(forward, length + half, 0))
+    downs = [key for key in names if key[0] == "row"]
+    acrosses = [key for key in names if key[0] == "col"]
+    edges = [(key, None) for key in downs] + [(None, key) for key in acrosses]
+    edges += [(down, across) for down in downs for across in acrosses]
+    paths = [route(edge, rows, cols) for edge in edges]
     both = ("row", "col")
-    landed = [(side, -across) for side, across in edges]
 
     def numbers(*values):
         return jnp.stack(values).astype(jnp.int32)
 
-    own = pack(numbers(*from_rows, here), object_re, object_im, edges, half)
+    padded_at = numbers(*padded_at, here)
+    own = pack(numbers(*tile_at, here), object_re, object_im, edges, names, half)
     strips = [lax.ppermute(strip, both, path) for strip, path in zip(own, paths)]
     kern, sorted_frames, waves = prepare(my_places, probe, phases, frames)
     mine, other = gather(
-        places, numbers(*pad_rows, here), object_re, object_im, waves, landed, strips, size
+        places, padded_at, object_re, object_im, waves, edges, names, strips, size
     )
     across_depth = [(i, 1 - i) for i in range(sections)]
     theirs = lax.ppermute(other, "depth", across_depth)
@@ -658,15 +664,20 @@
     arrived = lax.ppermute(send, "depth", across_depth)
     pulled = pulled_keep + lax.ppermute(pulled_send, "depth", across_depth)
 
-    out_rows = pad_rows if rows == 2 else pad_rows[::-1]
     tile, *own = scatter(
-        places, live, numbers(*out_rows, here), keep, arrived, edges, tile_rows, tile_cols
+        places, live, padded_at, keep, arrived, edges, names, tile_rows, tile_cols
     )
-    *own, pulled = lax.optimization_barrier((*own, pulled))
+
+    def after_scatter(other):
+        return lax.optimization_barrier((other, *own))[0]
+
+    probe_share = exchanged(pulled, ("row", "col"), after_scatter)
     added = [lax.ppermute(strip, both, path) for strip, path in zip(own, paths)]
-    first_row = jnp.where(row_at == 0, 0, half) if rows == 2 else jnp.int32(half * (rows > 1))
-    gradient = add_borders(numbers(*fold_rows, first_row), tile, landed, added, half)
-    probe_share = summed(pulled, ("col", "row"))
+    if rows == 2:
+        first_row = jnp.where(row_at == 0, 0, half)
+    else:
+        first_row = jnp.int32(half if downs else 0)
+    gradient = add_borders(numbers(*tile_at, first_row), tile, edges, names, added, half)
     return (gradient[:, None], probe_share)
 
 

time: 109 us -> 99.8 us (0.916)
  the two profiles are of different devices: /device:TPU:0 before, /device:TPU:12 now
where the time goes in v3:
time: 99.8 us; the launch traced here: 99.4 us
  Pallas kernels  33.9 us (34%)
  starting transfers between devices  26.9 us (27%)
  waiting for transfers between devices  25 us (25%)
  local copies, waits for them, and re-layouts  9.33 us (9%)
  other arithmetic  3.3 us (3%)
    pallas_call x1, Pallas kernels, chain(): pl.pallas_call(functools.partial(chain_kernel, group), grid=(count // gro...  19.4 us
    ppermute x5, starting transfers between devices, shards(): lax.ppermute(strip, both, path)  12.4 us
    ppermute x5, starting transfers between devices, shards(): added = [lax.ppermute(strip, both, path) for strip, path in zip(own, paths)]  11.7 us
    ppermute x4, waiting for transfers between devices, exchanged(): other = lax.ppermute(own, axis, [(i, i ^ step) for i in range(size)])  10.5 us
    unnamed x35, local copies, waits for them, and re-layouts  8.78 us
    ppermute x5, waiting for transfers between devices, shards(): lax.ppermute(strip, both, path)  5.2 us
    ppermute x5, waiting for transfers between devices, shards(): added = [lax.ppermute(strip, both, path) for strip, path in zip(own, paths)]  4.2 us
    pallas_call x1, Pallas kernels, scatter(): pl.pallas_call(functools.partial(scatter_kernel, edges, names, half), in_...  3.83 us
  transfers between devices with their start and end apart: 17, of which 8 were waited for; matrix products, arithmetic and copies ran while one was open for 2% of the time, Pallas kernels for 7%

profile of v3, /device:TPU:12, one launch (start us, length us, event | category | flops | bytes accessed | tf_op | source)
XLA Modules:
  0.0 99.4 jit_solution(10838482044767642225)
XLA Ops:
  1.3 1.2 %copy-done.1 = bf16[1,512,1024]{2,1,0:T(8,128)(2,1)S(1)} copy-done((bf16[1,512,1024]{2,1,0:T(8,128)(2,1)S(1)}, bf16[1,512,1024]{2,1,0:T(8,128)(2,1)}, u32[]{:S(2)}) %copy-start.1) | copy-done | bytes 1048600
  2.6 1.2 %copy-done.3 = bf16[1,512,1024]{2,1,0:T(8,128)(2,1)S(1)} copy-done((bf16[1,512,1024]{2,1,0:T(8,128)(2,1)S(1)}, bf16[1,512,1024]{2,1,0:T(8,128)(2,1)}, u32[]{:S(2)}) %copy-start.3) | copy-done | bytes 1048600
  3.8 1.6 %pack.1 = (bf16[2,128,1024]{2,1,0:T(8,128)(2,1)}, bf16[2,512,128]{2,1,0:T(8,128)(2,1)}, bf16[2,512,128]{2,1,0:T(8,128)(2,1)}, bf16[2,128,128]{2,1,0:T(8,128)(2,1)}, bf16[2,128,128]{2,1,0:T(8,128)(2,1)}) custom-call(s32[4]{0:T(128)S(1)} %get-tuple-element.48.offsets, bf16[1,512,1024]{2,1,0:T(8,128)(2,1)S(1)} %copy-done.1, bf16[1,512,1024]{2,1,0:T(8,128)(2,1)S(1)} %copy-done.3), custom_call_target="tpu_custom_call" | custom-call | tf_op jit(solution)/shard_map/pack/pallas_call | solution.py:172
  5.4 1.6 %collective-permute-start = (bf16[2,128,1024]{2,1,0:T(8,128)(2,1)}, bf16[2,128,1024]{2,1,0:T(8,128)(2,1)}, u32[]{:S(2)}, u32[]{:S(2)}) collective-permute-start(bf16[2,128,1024]{2,1,0:T(8,128)(2,1)} %get-tuple-element.25), channel_id=1, source_target_pairs={{0,8},{1,9},{2,10},{3,11},{4,12},{5,13},{6,14},{7,15},{8,0},{9,1},... | collective-permute-start | bytes 1572872 | tf_op jit(solution)/shard_map/ppermute | solution.py:654
  7.4 5.4 %collective-permute-start.4 = (bf16[2,128,128]{2,1,0:T(8,128)(2,1)}, bf16[2,128,128]{2,1,0:T(8,128)(2,1)}, u32[]{:S(2)}, u32[]{:S(2)}) collective-permute-start(bf16[2,128,128]{2,1,0:T(8,128)(2,1)} %get-tuple-element.29), channel_id=1, source_target_pairs={{1,10},{2,9},{3,12},{4,11},{5,14},{6,13},{9,2},{10,1},{11,4},{12,3... | collective-permute-start | bytes 196616 | tf_op jit(solution)/shard_map/ppermute | solution.py:654
  12.9 4.9 %collective-permute-start.2 = (bf16[2,512,128]{2,1,0:T(8,128)(2,1)}, bf16[2,512,128]{2,1,0:T(8,128)(2,1)}, u32[]{:S(2)}, u32[]{:S(2)}) collective-permute-start(bf16[2,512,128]{2,1,0:T(8,128)(2,1)} %get-tuple-element.27), channel_id=1, source_target_pairs={{1,2},{2,1},{3,4},{4,3},{5,6},{6,5},{9,10},{10,9},{11,12},{12,11},... | collective-permute-start | bytes 786440 | tf_op jit(solution)/shard_map/ppermute | solution.py:654
  18.5 1.2 %copy-done.9 = f32[2,256,256]{2,1,0:T(8,128)S(1)} copy-done((f32[2,256,256]{2,1,0:T(8,128)S(1)}, f32[2,256,256]{2,1,0:T(8,128)}, u32[]{:S(2)}) %copy-start.9) | copy-done | bytes 524312
  19.6 3.3 %prepare.1 = (f32[2,256,256]{2,1,0:T(8,128)S(1)}, f32[4,256,256]{2,1,0:T(8,128)S(1)}, f32[4,2,256,256]{3,2,1,0:T(8,128)S(1)}) custom-call(s32[8]{0:T(128)S(1)} %reshape.26.places, bf16[256,256]{1,0:T(8,128)(2,1)S(1)} %copy-done.10, f32[2,256,256]{2,1,0:T(8,128)S(1)} %copy-done.9, f32[1,256,256]{2,1,0:T(8,128)S(1)} %bitcast.19, f32[1,256,256]{2,1,0:T(8,128)S(1)} %bitcast.20, ...), custom_call_target="tpu_custom_call" | custom-call | flops 503316480 | bytes 5767168 | tf_op jit(solution)/shard_map/prepare/pallas_call | solution.py:102
  23.1 5.0 %collective-permute-done.1.rest_1_ = bf16[2,512,128]{2,1,0:T(8,128)(2,1)} collective-permute-done((bf16[2,512,128]{2,1,0:T(8,128)(2,1)}, bf16[2,512,128]{2,1,0:T(8,128)(2,1)}, u32[]{:S(2)}, u32[]{:S(2)}) %collective-permute-start.1) | collective-permute-done | bytes 262176 | tf_op jit(solution)/shard_map/ppermute | solution.py:654
  28.2 2.5 %gather.1 = (bf16[4,2,256,256]{3,2,1,0:T(8,128)(2,1)S(1)}, bf16[4,2,256,256]{3,2,1,0:T(8,128)(2,1)S(1)}) custom-call(s32[16]{0:T(128)S(1)} %reshape.25.places, s32[4]{0:T(128)S(1)} %add_add_fusion.offsets, bf16[1,512,1024]{2,1,0:T(8,128)(2,1)S(1)} %copy-done.2, bf16[1,512,1024]{2,1,0:T(8,128)(2,1)S(1)} %copy-done.4, ...), custom_call_target="tpu_custom_call" | custom-call | tf_op jit(solution)/shard_map/gather/pallas_call | solution.py:252
  30.8 2.6 %collective-permute-done.5.theirs = bf16[4,2,256,256]{3,2,1,0:T(8,128)(2,1)S(1)} collective-permute-done((bf16[4,2,256,256]{3,2,1,0:T(8,128)(2,1)S(1)}, bf16[4,2,256,256]{3,2,1,0:T(8,128)(2,1)S(1)}, u32[]{:S(2)}, u32[]{:S(2)}) %collective-permute-start.5) | collective-permute-done | bytes 1048608 | tf_op jit(solution)/shard_map/ppermute | solution.py:660
  33.4 19.4 %chain.1 = (f32[4,2,256,256]{3,2,1,0:T(8,128)S(1)}, bf16[4,2,256,256]{3,2,1,0:T(8,128)(2,1)}, f32[2,128,256]{2,1,0:T(8,128)S(1)}, f32[2,128,256]{2,1,0:T(8,128)S(1)}) custom-call(s32[8]{0:T(128)S(1)} %reshape.26.places, s32[4]{0:T(128)S(1)} %fusion.live, s32[1]{0:T(128)} %bitcast.8.here, bf16[4,2,256,256]{3,2,1,0:T(8,128)(2,1)S(1)} %copy-done.7, ...), custom_call_target="tpu_custom_call" | custom-call | tf_op jit(solution)/shard_map/chain/pallas_call | solution.py:400
  52.9 1.3 %copy-done.5 = f32[4,2,256,256]{3,2,1,0:T(8,128)} copy-done((f32[4,2,256,256]{3,2,1,0:T(8,128)}, f32[4,2,256,256]{3,2,1,0:T(8,128)S(1)}, u32[]{:S(2)}) %copy-start.5) | copy-done | bytes 2097176
  54.7 2.5 %collective-permute-done.12 = f32[2,128,256]{2,1,0:T(8,128)S(1)} collective-permute-done((f32[2,128,256]{2,1,0:T(8,128)S(1)}, f32[2,128,256]{2,1,0:T(8,128)S(1)}, u32[]{:S(2)}, u32[]{:S(2)}) %collective-permute-start.12) | collective-permute-done | bytes 262176 | tf_op jit(solution)/shard_map/ppermute | solution.py:665
  58.9 1.6 %copy-done.6 = f32[4,2,256,256]{3,2,1,0:T(8,128)S(1)} copy-done((f32[4,2,256,256]{3,2,1,0:T(8,128)S(1)}, f32[4,2,256,256]{3,2,1,0:T(8,128)}, u32[]{:S(2)}) %copy-start.6) | copy-done | bytes 2097176
  60.5 3.8 %scatter.1 = (f32[2,512,1024]{2,1,0:T(8,128)}, bf16[2,128,1024]{2,1,0:T(8,128)(2,1)S(1)}, bf16[2,512,128]{2,1,0:T(8,128)(2,1)S(1)}, bf16[2,512,128]{2,1,0:T(8,12...) custom-call(s32[16]{0:T(128)S(1)} %reshape.25.places, s32[8]{0:T(128)S(1)} %reshape.27.live, ...), custom_call_target="tpu_custom_call" | custom-call | tf_op jit(solution)/shard_map/scatter/pallas_call | solution.py:493
  68.3 4.6 %collective-permute-done.14 = bf16[2,128,256]{2,1,0:T(8,128)(2,1)S(1)} collective-permute-done((bf16[2,128,256]{2,1,0:T(8,128)(2,1)S(1)}, bf16[2,128,256]{2,1,0:T(8,128)(2,1)S(1)}, u32[]{:S(2)}, u32[]{:S(2)}) %collective-permute-start.14) | collective-permute-done | bytes 131104 | tf_op jit(solution)/shard_map/ppermute | solution.py:600
  73.7 4.4 %collective-permute-start.9 = (bf16[2,512,128]{2,1,0:T(8,128)(2,1)S(1)}, bf16[2,512,128]{2,1,0:T(8,128)(2,1)S(1)}, u32[]{:S(2)}, u32[]{:S(2)}) collective-permute-start(bf16[2,512,128]{2,1,0:T(8,128)(2,1)S(1)} %get-tuple-element.38), channel_id=1, source_target_pairs={{1,2},{2,1},{3,4},{4,3},{5,6},{6,5},{9,10},{10,9},{11,12},{12,11},... | collective-permute-start | bytes 786440 | tf_op jit(solution)/shard_map/ppermute | solution.py:675
  78.1 1.1 %collective-permute-start.7 = (bf16[2,128,1024]{2,1,0:T(8,128)(2,1)}, bf16[2,128,1024]{2,1,0:T(8,128)(2,1)S(1)}, u32[]{:S(2)}, u32[]{:S(2)}) collective-permute-start(bf16[2,128,1024]{2,1,0:T(8,128)(2,1)} %copy-done.11), channel_id=1, source_target_pairs={{0,8},{1,9},{2,10},{3,11},{4,12},{5,13},{6,14},{7,15},{8,0},{9,1},... | collective-permute-start | bytes 1572872 | tf_op jit(solution)/shard_map/ppermute | solution.py:675
  79.5 2.9 %collective-permute-start.10 = (bf16[2,128,128]{2,1,0:T(8,128)(2,1)}, bf16[2,128,128]{2,1,0:T(8,128)(2,1)S(1)}, u32[]{:S(2)}, u32[]{:S(2)}) collective-permute-start(bf16[2,128,128]{2,1,0:T(8,128)(2,1)} %copy-done.13), channel_id=1, source_target_pairs={{0,9},{1,8},{2,11},{3,10},{4,13},{5,12},{6,15},{7,14},{8,1},{9,0},... | collective-permute-start | bytes 196616 | tf_op jit(solution)/shard_map/ppermute | solution.py:675
  82.3 5.9 %collective-permute-done.16 = bf16[2,128,256]{2,1,0:T(8,128)(2,1)S(1)} collective-permute-done((bf16[2,128,256]{2,1,0:T(8,128)(2,1)S(1)}, bf16[2,128,256]{2,1,0:T(8,128)(2,1)S(1)}, u32[]{:S(2)}, u32[]{:S(2)}) %collective-permute-start.16) | collective-permute-done | bytes 131104 | tf_op jit(solution)/shard_map/ppermute | solution.py:600
  88.2 3.0 %collective-permute-start.11 = (bf16[2,128,128]{2,1,0:T(8,128)(2,1)S(1)}, bf16[2,128,128]{2,1,0:T(8,128)(2,1)S(1)}, u32[]{:S(2)}, u32[]{:S(2)}) collective-permute-start(bf16[2,128,128]{2,1,0:T(8,128)(2,1)S(1)} %get-tuple-element.40), channel_id=1, source_target_pairs={{1,10},{2,9},{3,12},{4,11},{5,14},{6,13},{9,2},{10,1},{11,4},{12,3... | collective-permute-start | bytes 196616 | tf_op jit(solution)/shard_map/ppermute | solution.py:675
  92.1 4.1 %collective-permute-done.11.rest_4_ = bf16[2,128,128]{2,1,0:T(8,128)(2,1)S(1)} collective-permute-done((bf16[2,128,128]{2,1,0:T(8,128)(2,1)S(1)}, bf16[2,128,128]{2,1,0:T(8,128)(2,1)S(1)}, u32[]{:S(2)}, u32[]{:S(2)}) %collective-permute-start.11) | collective-permute-done | bytes 65568 | tf_op jit(solution)/shard_map/ppermute | solution.py:675
  96.2 3.2 %borders.1 = f32[2,512,1024]{2,1,0:T(8,128)} custom-call(s32[4]{0:T(128)S(1)} %pad_add_fusion.offsets, f32[2,512,1024]{2,1,0:T(8,128)} %get-tuple-element.35.tile_in, bf16[2,128,1024]{2,1,0:T(8,128)(2,1)S(1)} %collective-permute-done.7.rest_0_, bf16[2,512,128]{2,1,0:T(8,128)(2,1)S(1)} %collective-permute-done.8.rest_1_, ...), custom_call_target="tpu_custom_call", output_to_operand_aliasing={{}: (1, {})} | custom-call | flops 1048576 | bytes 8388608 | tf_op jit(solution)/shard_map/borders/pallas_call | solution.py:554
  (68 shorter events, 10.1 us)
Async XLA Ops:
  0.6 17.2 %copy-start = (f32[1,1,4,2,256,256]{5,4,3,2,1,0:T(8,128)S(1)}, f32[1,1,4,2,256,256]{5,4,3,2,1,0:T(8,128)}, u32[]{:S(2)}) copy-start(f32[1,1,4,2,256,256]{5,4,3,2,1,0:T(8,128)} %param.15) | copy-start | bytes 6291460
  3.8 14.2 %copy-start.14 = (s32[1,1,4,2,2]{2,4,3,1,0:T(2,128)S(1)}, s32[1,1,4,2,2]{2,4,3,1,0:T(2,128)}, u32[]{:S(2)}) copy-start(s32[1,1,4,2,2]{2,4,3,1,0:T(2,128)} %param.13) | copy-start | bytes 196
  3.8 14.6 %copy-start.8 = (f32[256,256]{1,0:T(8,128)S(1)}, f32[256,256]{1,0:T(8,128)}, u32[]{:S(2)}) copy-start(f32[256,256]{1,0:T(8,128)} %param.12) | copy-start | bytes 786436
  3.8 14.7 %copy-start.10 = (bf16[256,256]{1,0:T(8,128)(2,1)S(1)}, bf16[256,256]{1,0:T(8,128)(2,1)}, u32[]{:S(2)}) copy-start(bf16[256,256]{1,0:T(8,128)(2,1)} %constant.62.clone.order_t) | copy-start | bytes 393220
  5.4 22.7 %collective-permute-start = (bf16[2,128,1024]{2,1,0:T(8,128)(2,1)}, bf16[2,128,1024]{2,1,0:T(8,128)(2,1)}, u32[]{:S(2)}, u32[]{:S(2)}) collective-permute-start(bf16[2,128,1024]{2,1,0:T(8,128)(2,1)} %get-tuple-element.25), channel_id=1, source_target_pairs={{0,8},{1,9},{2,10},{3,11},{4,12},{5,13},{6,14},{7,15},{8,0},{9,1},... | collective-permute-start | bytes 1572872 | tf_op jit(solution)/shard_map/ppermute | solution.py:654
  7.0 16.1 %collective-permute-start.3 = (bf16[2,128,128]{2,1,0:T(8,128)(2,1)}, bf16[2,128,128]{2,1,0:T(8,128)(2,1)}, u32[]{:S(2)}, u32[]{:S(2)}) collective-permute-start(bf16[2,128,128]{2,1,0:T(8,128)(2,1)} %get-tuple-element.28), channel_id=1, source_target_pairs={{0,9},{1,8},{2,11},{3,10},{4,13},{5,12},{6,15},{7,14},{8,1},{9,0},... | collective-permute-start | bytes 196616 | tf_op jit(solution)/shard_map/ppermute | solution.py:654
  7.4 15.7 %collective-permute-start.4 = (bf16[2,128,128]{2,1,0:T(8,128)(2,1)}, bf16[2,128,128]{2,1,0:T(8,128)(2,1)}, u32[]{:S(2)}, u32[]{:S(2)}) collective-permute-start(bf16[2,128,128]{2,1,0:T(8,128)(2,1)} %get-tuple-element.29), channel_id=1, source_target_pairs={{1,10},{2,9},{3,12},{4,11},{5,14},{6,13},{9,2},{10,1},{11,4},{12,3... | collective-permute-start | bytes 196616 | tf_op jit(solution)/shard_map/ppermute | solution.py:654
  12.8 15.3 %collective-permute-start.1 = (bf16[2,512,128]{2,1,0:T(8,128)(2,1)}, bf16[2,512,128]{2,1,0:T(8,128)(2,1)}, u32[]{:S(2)}, u32[]{:S(2)}) collective-permute-start(bf16[2,512,128]{2,1,0:T(8,128)(2,1)} %get-tuple-element.26), channel_id=1, source_target_pairs={{0,1},{1,0},{2,3},{3,2},{4,5},{5,4},{6,7},{7,6},{8,9},{9,8},{10,11... | collective-permute-start | bytes 786440 | tf_op jit(solution)/shard_map/ppermute | solution.py:654
  12.9 15.2 %collective-permute-start.2 = (bf16[2,512,128]{2,1,0:T(8,128)(2,1)}, bf16[2,512,128]{2,1,0:T(8,128)(2,1)}, u32[]{:S(2)}, u32[]{:S(2)}) collective-permute-start(bf16[2,512,128]{2,1,0:T(8,128)(2,1)} %get-tuple-element.27), channel_id=1, source_target_pairs={{1,2},{2,1},{3,4},{4,3},{5,6},{6,5},{9,10},{10,9},{11,12},{12,11},... | collective-permute-start | bytes 786440 | tf_op jit(solution)/shard_map/ppermute | solution.py:654
  18.4 9.7 %copy-start.2 = (bf16[1,512,1024]{2,1,0:T(8,128)(2,1)S(1)}, bf16[1,512,1024]{2,1,0:T(8,128)(2,1)}, u32[]{:S(2)}) copy-start(bf16[1,512,1024]{2,1,0:T(8,128)(2,1)} %tile_re.3) | copy-start | bytes 3145732
  18.4 9.7 %copy-start.4 = (bf16[1,512,1024]{2,1,0:T(8,128)(2,1)S(1)}, bf16[1,512,1024]{2,1,0:T(8,128)(2,1)}, u32[]{:S(2)}) copy-start(bf16[1,512,1024]{2,1,0:T(8,128)(2,1)} %tile_im.3) | copy-start | bytes 3145732
  30.7 2.7 %collective-permute-start.5 = (bf16[4,2,256,256]{3,2,1,0:T(8,128)(2,1)S(1)}, bf16[4,2,256,256]{3,2,1,0:T(8,128)(2,1)S(1)}, u32[]{:S(2)}, u32[]{:S(2)}) collective-permute-start(bf16[4,2,256,256]{3,2,1,0:T(8,128)(2,1)S(1)} %get-tuple-element.31), channel_id=1, source_target_pairs={{0,16},{16,0},{1,17},{17,1},{2,18},{18,2},{3,19},{19,3},{4,20},{20... | collective-permute-start | bytes 3145736 | tf_op jit(solution)/shard_map/ppermute | solution.py:660
  54.2 4.7 %collective-permute-start.6 = (bf16[4,2,256,256]{3,2,1,0:T(8,128)(2,1)}, bf16[4,2,256,256]{3,2,1,0:T(8,128)(2,1)S(1)}, u32[]{:S(2)}, u32[]{:S(2)}) collective-permute-start(bf16[4,2,256,256]{3,2,1,0:T(8,128)(2,1)} %get-tuple-element.34), channel_id=1, source_target_pairs={{0,16},{16,0},{1,17},{17,1},{2,18},{18,2},{3,19},{19,3},{4,20},{20... | collective-permute-start | bytes 3145736 | tf_op jit(solution)/shard_map/ppermute | solution.py:664
  54.4 2.9 %collective-permute-start.12 = (f32[2,128,256]{2,1,0:T(8,128)S(1)}, f32[2,128,256]{2,1,0:T(8,128)S(1)}, u32[]{:S(2)}, u32[]{:S(2)}) collective-permute-start(f32[2,128,256]{2,1,0:T(8,128)S(1)} %get-tuple-element.42), channel_id=1, source_target_pairs={{0,16},{16,0},{1,17},{17,1},{2,18},{18,2},{3,19},{19,3},{4,20},{20... | collective-permute-start | bytes 786440 | tf_op jit(solution)/shard_map/ppermute | solution.py:665
  57.9 8.6 %collective-permute-start.13 = (bf16[2,128,256]{2,1,0:T(8,128)(2,1)}, bf16[2,128,256]{2,1,0:T(8,128)(2,1)}, u32[]{:S(2)}, u32[]{:S(2)}) collective-permute-start(bf16[2,128,256]{2,1,0:T(8,128)(2,1)} %add_convert_fusion.3), channel_id=1, source_target_pairs={{0,8},{8,0},{1,9},{9,1},{2,10},{10,2},{3,11},{11,3},{4,12},{12,4},... | collective-permute-start | bytes 393224 | tf_op jit(solution)/shard_map/ppermute | solution.py:600
  60.5 18.8 %copy-start.15 = (s32[4]{0:T(128)S(1)}, s32[4]{0:T(128)}, u32[]{:S(2)}) copy-start(s32[4]{0:T(128)} %get-tuple-element.49) | copy-start | bytes 52
  67.5 5.3 %collective-permute-start.14 = (bf16[2,128,256]{2,1,0:T(8,128)(2,1)S(1)}, bf16[2,128,256]{2,1,0:T(8,128)(2,1)S(1)}, u32[]{:S(2)}, u32[]{:S(2)}) collective-permute-start(bf16[2,128,256]{2,1,0:T(8,128)(2,1)S(1)} %add_convert_fusion.2), channel_id=1, source_target_pairs={{0,1},{1,0},{2,3},{3,2},{4,5},{5,4},{6,7},{7,6},{8,9},{9,8},{10,11... | collective-permute-start | bytes 393224 | tf_op jit(solution)/shard_map/ppermute | solution.py:600
  72.9 6.4 %collective-permute-start.15 = (bf16[2,128,256]{2,1,0:T(8,128)(2,1)S(1)}, bf16[2,128,256]{2,1,0:T(8,128)(2,1)S(1)}, u32[]{:S(2)}, u32[]{:S(2)}) collective-permute-start(bf16[2,128,256]{2,1,0:T(8,128)(2,1)S(1)} %add_convert_fusion.1), channel_id=1, source_target_pairs={{0,2},{1,3},{2,0},{3,1},{4,6},{5,7},{6,4},{7,5},{8,10},{9,11},{10,... | collective-permute-start | bytes 393224 | tf_op jit(solution)/shard_map/ppermute | solution.py:600
  73.4 22.8 %collective-permute-start.8 = (bf16[2,512,128]{2,1,0:T(8,128)(2,1)}, bf16[2,512,128]{2,1,0:T(8,128)(2,1)S(1)}, u32[]{:S(2)}, u32[]{:S(2)}) collective-permute-start(bf16[2,512,128]{2,1,0:T(8,128)(2,1)} %copy-done.12), channel_id=1, source_target_pairs={{0,1},{1,0},{2,3},{3,2},{4,5},{5,4},{6,7},{7,6},{8,9},{9,8},{10,11... | collective-permute-start | bytes 786440 | tf_op jit(solution)/shard_map/ppermute | solution.py:675
  73.7 22.5 %collective-permute-start.9 = (bf16[2,512,128]{2,1,0:T(8,128)(2,1)S(1)}, bf16[2,512,128]{2,1,0:T(8,128)(2,1)S(1)}, u32[]{:S(2)}, u32[]{:S(2)}) collective-permute-start(bf16[2,512,128]{2,1,0:T(8,128)(2,1)S(1)} %get-tuple-element.38), channel_id=1, source_target_pairs={{1,2},{2,1},{3,4},{4,3},{5,6},{6,5},{9,10},{10,9},{11,12},{12,11},... | collective-permute-start | bytes 786440 | tf_op jit(solution)/shard_map/ppermute | solution.py:675
  78.1 18.1 %collective-permute-start.7 = (bf16[2,128,1024]{2,1,0:T(8,128)(2,1)}, bf16[2,128,1024]{2,1,0:T(8,128)(2,1)S(1)}, u32[]{:S(2)}, u32[]{:S(2)}) collective-permute-start(bf16[2,128,1024]{2,1,0:T(8,128)(2,1)} %copy-done.11), channel_id=1, source_target_pairs={{0,8},{1,9},{2,10},{3,11},{4,12},{5,13},{6,14},{7,15},{8,0},{9,1},... | collective-permute-start | bytes 1572872 | tf_op jit(solution)/shard_map/ppermute | solution.py:675
  79.3 8.9 %collective-permute-start.16 = (bf16[2,128,256]{2,1,0:T(8,128)(2,1)S(1)}, bf16[2,128,256]{2,1,0:T(8,128)(2,1)S(1)}, u32[]{:S(2)}, u32[]{:S(2)}) collective-permute-start(bf16[2,128,256]{2,1,0:T(8,128)(2,1)S(1)} %add_convert_fusion), channel_id=1, source_target_pairs={{0,4},{1,5},{2,6},{3,7},{4,0},{5,1},{6,2},{7,3},{8,12},{9,13},{10,... | collective-permute-start | bytes 393224 | tf_op jit(solution)/shard_map/ppermute | solution.py:600
  79.5 12.6 %collective-permute-start.10 = (bf16[2,128,128]{2,1,0:T(8,128)(2,1)}, bf16[2,128,128]{2,1,0:T(8,128)(2,1)S(1)}, u32[]{:S(2)}, u32[]{:S(2)}) collective-permute-start(bf16[2,128,128]{2,1,0:T(8,128)(2,1)} %copy-done.13), channel_id=1, source_target_pairs={{0,9},{1,8},{2,11},{3,10},{4,13},{5,12},{6,15},{7,14},{8,1},{9,0},... | collective-permute-start | bytes 196616 | tf_op jit(solution)/shard_map/ppermute | solution.py:675
  88.2 7.9 %collective-permute-start.11 = (bf16[2,128,128]{2,1,0:T(8,128)(2,1)S(1)}, bf16[2,128,128]{2,1,0:T(8,128)(2,1)S(1)}, u32[]{:S(2)}, u32[]{:S(2)}) collective-permute-start(bf16[2,128,128]{2,1,0:T(8,128)(2,1)S(1)} %get-tuple-element.40), channel_id=1, source_target_pairs={{1,10},{2,9},{3,12},{4,11},{5,14},{6,13},{9,2},{10,1},{11,4},{12,3... | collective-permute-start | bytes 196616 | tf_op jit(solution)/shard_map/ppermute | solution.py:675
  (10 other events, 16.6 us)

commit v4 on v3

--- a/solution.py
+++ b/solution.py
@@ -120,11 +120,7 @@
             jax.ShapeDtypeStruct((count, 2, size, size), f32),
         ],
         compiler_params=pltpu.CompilerParams(vmem_limit_bytes=16 * MIB),
-        cost_estimate=pl.CostEstimate(
-            flops=2 * (count + 1) * 3 * size**3,
-            bytes_accessed=4 * size * size * (4 * count + 6),
-            transcendentals=2 * size * size,
-        ),
+        cost_estimate=pl.CostEstimate(flops=0, bytes_accessed=0, transcendentals=0),
         name="prepare",
     )(
         places,
@@ -265,7 +261,7 @@
 
 def chain_kernel(
     group, places, live, here, tables, kern, mine, theirs, frames, waves,
-    keep, send, pulled_keep, pulled_send, windows, middle, terms, pulled, sems, keep_sems,
+    keep, send, pulled_keep, pulled_send, windows, middle, terms, pulled, sems,
 ):
     step = pl.program_id(0)
     steps = pl.num_programs(0)
@@ -293,45 +289,69 @@
     def table(which):
         return tables[which, 0], tables[which, 1]
 
-    def forward(re, im):
+    group_ids = range(group)
+
+    def forward(waves):
         halves = []
         for sign, which in ((1, 2), (-1, 3)):
-            if sign > 0:
-                part = rows_of(re[:half] + re[half:], im[:half] + im[half:])
-            else:
-                part = rows_of(re[:half] - re[half:], im[:half] - im[half:])
-            halves.append(dot3(table(which), split(part)))
+            parts = []
+            for pair in waves:
+                if sign > 0:
+                    parts.append(rows_of(*(x[:half] + x[half:] for x in pair)))
+                else:
+                    parts.append(rows_of(*(x[:half] - x[half:] for x in pair)))
+            halves.append(dot3(table(which), split(cols_of(*parts))))
         outs = []
         for sign, which in ((1, 0), (-1, 1)):
             parts = []
-            for out in halves:
-                re, im = out[:half], out[half:]
-                if sign > 0:
-                    parts.append(cols_of(re[:, :half] + re[:, half:], im[:, :half] + im[:, half:]))
-                else:
-                    parts.append(cols_of(re[:, :half] - re[:, half:], im[:, :half] - im[:, half:]))
+            for at in group_ids:
+                for out in halves:
+                    x = out[:, at * size : (at + 1) * size]
+                    if sign > 0:
+                        x = x[:, :half] + x[:, half:]
+                    else:
+                        x = x[:, :half] - x[:, half:]
+                    parts.append(cols_of(x[:half], x[half:]))
             outs.append(dot3(split(rows_of(*parts)), table(which)))
+        return [[out[at * size : (at + 1) * size] for out in outs] for at in group_ids]
+
+    def inverse(parts):
+        first = dot3(split(rows_of(*(part[0] for part in parts))), table(2))
+        second = dot3(split(rows_of(*(part[1] for part in parts))), table(3))
+        evens, odds = [], []
+        for at in group_ids:
+            rows = slice(at * size, (at + 1) * size)
+            plus, minus = first[rows] + second[rows], first[rows] - second[rows]
+            re = cols_of(plus[:, :half], minus[:, :half])
+            im = cols_of(plus[:, half:], minus[:, half:])
+            evens.append(rows_of(re[:half], im[:half]))
+            odds.append(rows_of(re[half:], im[half:]))
+        first = dot3(table(0), split(cols_of(*evens)))
+        second = dot3(table(1), split(cols_of(*odds)))
+        outs = []
+        for at in group_ids:
+            cols = slice(at * size, (at + 1) * size)
+            plus, minus = first[:, cols] + second[:, cols], first[:, cols] - second[:, cols]
+            outs.append((rows_of(plus[:half], minus[:half]), rows_of(plus[half:], minus[half:])))
         return outs
 
-    def inverse(even, odd):
-        first = dot3(split(even), table(2))
-        second = dot3(split(odd), table(3))
-        plus, minus = first + second, first - second
-        re = cols_of(plus[:, :half], minus[:, :half])
-        im = cols_of(plus[:, half:], minus[:, half:])
-        first = dot3(table(0), split(rows_of(re[:half], im[:half])))
-        second = dot3(table(1), split(rows_of(re[half:], im[half:])))
-        plus, minus = first + second, first - second
-        return rows_of(plus[:half], minus[:half]), rows_of(plus[half:], minus[half:])
-
-    def propagate(re, im, sign):
-        outs = []
-        for at, part in enumerate(forward(re, im)):
-            cols = slice(at * half, (at + 1) * half)
-            kre, kim = kern[0, :, cols], kern[1, :, cols] * sign
-            re, im = part[:, :half], part[:, half:]
-            outs.append(cols_of(re * kre - im * kim, re * kim + im * kre))
-        return inverse(*outs)
+    def propagate(waves, sign):
+        kept = []
+        for parts in forward(waves):
+            outs = []
+            for k, part in enumerate(parts):
+                cols = slice(k * half, (k + 1) * half)
+                kre, kim = kern[0, :, cols], kern[1, :, cols] * sign
+                re, im = part[:, :half], part[:, half:]
+                outs.append(cols_of(re * kre - im * kim, re * kim + im * kre))
+            kept.append(outs)
+        return inverse(kept)
+
+    def product(left, right):
+        return left[0] * right[0] - left[1] * right[1], left[0] * right[1] + left[1] * right[0]
+
+    def conj_product(left, right):
+        return left[0] * right[0] + left[1] * right[1], left[0] * right[1] - left[1] * right[0]
 
     def rounded(x):
         return x.astype(bf16).astype(f32)
@@ -339,52 +359,44 @@
     def window(slot, at):
         return windows[step, slot, at, 0].astype(f32), windows[step, slot, at, 1].astype(f32)
 
-    for at in range(group):
-        wre, wim = window(0, at)
-        pre, pim = waves[at, 0], waves[at, 1]
-        re, im = propagate(pre * wre - pim * wim, pre * wim + pim * wre, 1.0)
-        middle[at, 0] = re.astype(bf16)
-        middle[at, 1] = im.astype(bf16)
-
-    for at in range(group):
-        wre, wim = window(1, at)
-        pre, pim = middle[at, 0].astype(f32), middle[at, 1].astype(f32)
-        back = []
-        for k, part in enumerate(forward(pre * wre - pim * wim, pre * wim + pim * wre)):
+    def wave(at):
+        return waves[at, 0], waves[at, 1]
+
+    def passed(at):
+        return middle[at, 0].astype(f32), middle[at, 1].astype(f32)
+
+    outs = propagate([product(wave(at), window(0, at)) for at in group_ids], 1.0)
+    for at in group_ids:
+        middle[at, 0] = outs[at][0].astype(bf16)
+        middle[at, 1] = outs[at][1].astype(bf16)
+
+    far = forward([product(passed(at), window(1, at)) for at in group_ids])
+    for at in group_ids:
+        for k, part in enumerate(far[at]):
             re, im = part[:, :half], part[:, half:]
             misfit = re * re + im * im - frames[at, :, k * half : (k + 1) * half]
-            back.append(cols_of(re * misfit, im * misfit))
-        cre, cim = inverse(*back)
-        pre, pim = middle[at, 0].astype(f32), middle[at, 1].astype(f32)
-        terms[step, 1, at, 0] = pre * cre + pim * cim
-        terms[step, 1, at, 1] = pre * cim - pim * cre
-        wre, wim = window(1, at)
-        re, im = propagate(wre * cre + wim * cim, wre * cim - wim * cre, -1.0)
-        cre, cim = rounded(re), rounded(im)
-        pre, pim = waves[at, 0], waves[at, 1]
-        terms[step, 0, at, 0] = pre * cre + pim * cim
-        terms[step, 0, at, 1] = pre * cim - pim * cre
-        wre, wim = window(0, at)
+            far[at][k] = cols_of(re * misfit, im * misfit)
+    pulls = []
+    for at, chi in enumerate(inverse(far)):
+        terms[1, at, 0], terms[1, at, 1] = conj_product(passed(at), chi)
+        pulls.append(conj_product(window(1, at), chi))
+
+    for at, chi in enumerate(propagate(pulls, -1.0)):
+        chi = rounded(chi[0]), rounded(chi[1])
+        terms[0, at, 0], terms[0, at, 1] = conj_product(wave(at), chi)
         spot_at = step * group + at
         up = (size - places[2 * spot_at] % ROWS) % size
         back_by = (size - places[2 * spot_at + 1] % LANES) % size
         weight = live[spot_at].astype(f32)
-        for plane, value in enumerate((wre * cre + wim * cim, wre * cim - wim * cre)):
+        for plane, value in enumerate(conj_product(window(0, at), chi)):
             value = pltpu.roll(pltpu.roll(value * weight, back_by, axis=1), up, axis=0)
             pulled[plane] += value
 
-    send[...] = terms[step, 1 - me].astype(bf16)
-
-    def put(at):
-        rows = pl.ds(at * group, group)
-        return pltpu.make_async_copy(terms.at[at, me], keep.at[rows], keep_sems.at[at])
-
-    put(step).start()
+    keep[...] = terms[me]
+    send[...] = terms[1 - me].astype(bf16)
 
     @pl.when(step == steps - 1)
     def _():
-        for at in range(terms.shape[0]):
-            put(at).wait()
         share = pulled_keep.shape[1]
         for plane in range(2):
             pulled_keep[plane] = pulled[plane, pl.ds(pl.multiple_of(me * share, share), share), :]
@@ -411,7 +423,7 @@
             pl.BlockSpec((group, size, size), lambda i: (i, 0, 0)),
             block,
         ],
-        out_specs=[HBM, block, full(2, size // 2, size), full(2, size // 2, size)],
+        out_specs=[block, block, full(2, size // 2, size), full(2, size // 2, size)],
         out_shape=[
             jax.ShapeDtypeStruct((count, 2, size, size), f32),
             jax.ShapeDtypeStruct((count, 2, size, size), bf16),
@@ -421,10 +433,9 @@
         scratch_shapes=[
             pltpu.VMEM((count // group, 2, group, 2, size, size), bf16),
             pltpu.VMEM((group, 2, size, size), bf16),
-            pltpu.VMEM((count // group, 2, group, 2, size, size), f32),
+            pltpu.VMEM((2, group, 2, size, size), f32),
             pltpu.VMEM((2, size, size), f32),
             pltpu.SemaphoreType.DMA((2 * (count // group),)),
-            pltpu.SemaphoreType.DMA((count // group,)),
         ],
         compiler_params=pltpu.CompilerParams(vmem_limit_bytes=40 * MIB),
         name="chain",
@@ -432,21 +443,12 @@
 
 
 def scatter_kernel(edges, names, half, places, live, offsets, kept, arrived, tile, *rest):
-    strips, (total, near, far, sems) = rest[:-4], rest[-4:]
+    strips, (total, sems) = rest[:-2], rest[-2:]
     count, size = kept.shape[0], kept.shape[-1]
     tile_rows, tile_cols = tile.shape[1:]
     sections = 2
     here = offsets[offsets.shape[0] - 1]
 
-    def fetch(place, which):
-        source, target = ((kept, near), (arrived, far))[which]
-        return pltpu.make_async_copy(
-            source.at[place], target.at[place], sems.at[1 + 2 * place + which]
-        )
-
-    for which in range(2):
-        for place in range(count):
-            fetch(place, which).start()
     total[...] = jnp.zeros_like(total)
     lane = lax.broadcasted_iota(jnp.int32, (size, LANES), 1)
     row = lax.broadcasted_iota(jnp.int32, (ROWS, size + LANES), 0)
@@ -471,9 +473,8 @@
                 )
                 total[plane, pl.ds(top, size + ROWS), wide] += value
 
-    for which, (source, owner) in enumerate(((near, here), (far, 1 - here))):
+    for source, owner in ((kept, here), (arrived, 1 - here)):
         for place in range(count):
-            fetch(place, which).wait()
             add(sections * place + owner, source, place)
     body = (pl.ds(half, tile_rows), pl.ds(half, tile_cols))
     copy = pltpu.make_async_copy(total.at[(slice(None),) + body], tile, sems.at[0])
@@ -492,23 +493,25 @@
     vmem = pl.BlockSpec(memory_space=pltpu.VMEM)
     return pl.pallas_call(
         functools.partial(scatter_kernel, edges, names, half),
-        in_specs=[SMEM, SMEM, SMEM, HBM, ANY],
+        in_specs=[SMEM, SMEM, SMEM, vmem, vmem],
         out_specs=[HBM] + [vmem] * len(edges),
         out_shape=[jax.ShapeDtypeStruct((2, tile_rows, tile_cols), f32)]
         + strip_shapes(edges, tile_rows, tile_cols, half),
         scratch_shapes=[
             pltpu.VMEM((2, tile_rows + 2 * half, tile_cols + 2 * half), f32),
-            pltpu.VMEM(kept.shape, f32),
-            pltpu.VMEM(arrived.shape, bf16),
-            pltpu.SemaphoreType.DMA((1 + 2 * count,)),
+            pltpu.SemaphoreType.DMA((1,)),
         ],
         compiler_params=pltpu.CompilerParams(vmem_limit_bytes=20 * MIB),
+        cost_estimate=pl.CostEstimate(
+            flops=0, bytes_accessed=16 * tile_rows * tile_cols, transcendentals=0
+        ),
         name="scatter",
     )(places, live, offsets, kept, arrived)
 
 
-def border_kernel(edges, names, half, offsets, tile_in, *rest):
-    strips, (tile, bands, sides, in_sems, out_sems) = rest[: len(edges)], rest[len(edges) :]
+def border_kernel(edges, names, half, offsets, tile_in, part, other, *rest):
+    strips, rest = rest[: len(edges)], rest[len(edges) :]
+    tile, probe_share, bands, sides, in_sems, out_sems = rest
     tile_rows, tile_cols = tile.shape[1:]
     strips = dict(zip(edges, strips))
     downs = [key for key in names if key[0] == "row"]
@@ -530,6 +533,7 @@
 
     for k in range(len(regions)):
         copy(k, False).start()
+    probe_share[...] = part[...].astype(f32) + other[...].astype(f32)
     for k, (key, block, rows, cols) in enumerate(regions):
         copy(k, False).wait()
         for plane in range(2):
@@ -546,16 +550,19 @@
         copy(k, True).wait()
 
 
-def add_borders(offsets, tile, edges, names, strips, half):
+def add_borders(offsets, tile, probe_parts, edges, names, strips, half):
     vmem = pl.BlockSpec(memory_space=pltpu.VMEM)
     downs = sum(key[0] == "row" for key in names)
     acrosses = len(names) - downs
     tile_rows, tile_cols = tile.shape[1:]
     return pl.pallas_call(
         functools.partial(border_kernel, edges, names, half),
-        in_specs=[SMEM, HBM] + [vmem] * len(strips),
-        out_specs=HBM,
-        out_shape=jax.ShapeDtypeStruct(tile.shape, f32),
+        in_specs=[SMEM, HBM] + [vmem] * (2 + len(strips)),
+        out_specs=[HBM, vmem],
+        out_shape=[
+            jax.ShapeDtypeStruct(tile.shape, f32),
+            jax.ShapeDtypeStruct(probe_parts[0].shape, f32),
+        ],
         scratch_shapes=[
             pltpu.VMEM((max(downs, 1), 2, half, tile_cols), f32),
             pltpu.VMEM((max(acrosses, 1), 2, tile_rows - downs * half, half), f32),
@@ -570,7 +577,7 @@
             transcendentals=0,
         ),
         name="borders",
-    )(offsets, tile, *strips)
+    )(offsets, tile, *probe_parts, *strips)
 
 
 def partner(index, kind):
@@ -589,19 +596,10 @@
     return pairs
 
 
-def exchanged(block, axes, between=None):
-    for axis in axes:
-        size = lax.axis_size(axis)
-        if size & (size - 1):
-            block = lax.psum(block, axis)
-            continue
-        for step in [1 << k for k in range(size.bit_length() - 1)]:
-            own = block.astype(bf16)
-            other = lax.ppermute(own, axis, [(i, i ^ step) for i in range(size)])
-            if between is not None:
-                other, between = between(other), None
-            block = own.astype(f32) + other.astype(f32)
-    return block
+def doublings(axis):
+    size = lax.axis_size(axis)
+    assert size & (size - 1) == 0
+    return size.bit_length() - 1
 
 
 def shards(probe, object_re, object_im, phases, centres, occupied, measured):
@@ -650,7 +648,9 @@
         return jnp.stack(values).astype(jnp.int32)
 
     padded_at = numbers(*padded_at, here)
-    own = pack(numbers(*tile_at, here), object_re, object_im, edges, names, half)
+    tile_at = numbers(*tile_at, here)
+    bulk = len(names)
+    own = pack(tile_at, object_re, object_im, edges, names, half)
     strips = [lax.ppermute(strip, both, path) for strip, path in zip(own, paths)]
     kern, sorted_frames, waves = prepare(my_places, probe, phases, frames)
     mine, other = gather(
@@ -668,16 +668,22 @@
         places, live, padded_at, keep, arrived, edges, names, tile_rows, tile_cols
     )
 
-    def after_scatter(other):
-        return lax.optimization_barrier((other, *own))[0]
-
-    probe_share = exchanged(pulled, ("row", "col"), after_scatter)
-    added = [lax.ppermute(strip, both, path) for strip, path in zip(own, paths)]
+    steps = [(axis, 1 << k) for axis in ("row", "col") for k in range(doublings(axis))]
+    if len(steps) < 3:
+        added = [lax.ppermute(strip, both, path) for strip, path in zip(own, paths)]
+    for at, (axis, step) in enumerate(steps):
+        mine = pulled.astype(bf16)
+        theirs = lax.ppermute(mine, axis, [(i, i ^ step) for i in range(lax.axis_size(axis))])
+        if at == len(steps) - 3:
+            theirs, *own = lax.optimization_barrier((theirs, *own))
+            added = [lax.ppermute(strip, both, path) for strip, path in zip(own, paths)]
+        if at < len(steps) - 1:
+            pulled = mine.astype(f32) + theirs.astype(f32)
     if rows == 2:
         first_row = jnp.where(row_at == 0, 0, half)
     else:
         first_row = jnp.int32(half if downs else 0)
-    gradient = add_borders(numbers(*tile_at, first_row), tile, edges, names, added, half)
+    gradient, probe_share = add_borders(lax.dynamic_update_index_in_dim(tile_at, first_row.astype(jnp.int32), bulk, 0), tile, (mine, theirs), edges, names, added, half)
     return (gradient[:, None], probe_share)
 
 

time: 99.8 us -> 95.7 us (0.959)
  the two profiles are of different devices: /device:TPU:12 before, /device:TPU:8 now
where the time goes in v4:
time: 95.7 us; the launch traced here: 95.4 us
  Pallas kernels  32.9 us (34%)
  waiting for transfers between devices  28.8 us (30%)
  starting transfers between devices  26.2 us (27%)
  local copies, waits for them, and re-layouts  6.18 us (6%)
  between operations  0.96 us (1%)
    pallas_call x1, Pallas kernels, chain(): pl.pallas_call(functools.partial(chain_kernel, group), grid=(count // gro...  17.2 us
    ppermute x5, starting transfers between devices, shards(): lax.ppermute(strip, both, path)  10.9 us
    ppermute x5, waiting for transfers between devices, shards(): added = [lax.ppermute(strip, both, path) for strip, path in zip(own, paths)]  10.5 us
    ppermute x5, starting transfers between devices, shards(): added = [lax.ppermute(strip, both, path) for strip, path in zip(own, paths)]  10.4 us
    ppermute x5, waiting for transfers between devices, shards(): lax.ppermute(strip, both, path)  8.25 us
    unnamed x27, local copies, waits for them, and re-layouts  5.63 us
    ppermute x4, waiting for transfers between devices, shards(): lax.ppermute(mine, axis, [(i, i ^ step) for i in range(lax.axis_size(axis...  4.88 us
    pallas_call x1, Pallas kernels, scatter(): pl.pallas_call(functools.partial(scatter_kernel, edges, names, half), in_...  4.5 us
  transfers between devices with their start and end apart: 17, of which 7 were waited for; matrix products, arithmetic and copies ran while one was open for 1% of the time, Pallas kernels for 8%

profile of v4, /device:TPU:8, one launch (start us, length us, event | category | flops | bytes accessed | tf_op | source)
XLA Modules:
  0.0 95.4 jit_solution(11385574418107773948)
XLA Ops:
  0.8 1.3 %copy-done.1 = bf16[1,512,1024]{2,1,0:T(8,128)(2,1)S(1)} copy-done((bf16[1,512,1024]{2,1,0:T(8,128)(2,1)S(1)}, bf16[1,512,1024]{2,1,0:T(8,128)(2,1)}, u32[]{:S(2)}) %copy-start.1) | copy-done | bytes 1048600
  3.4 1.6 %pack.1 = (bf16[2,128,1024]{2,1,0:T(8,128)(2,1)}, bf16[2,512,128]{2,1,0:T(8,128)(2,1)}, bf16[2,512,128]{2,1,0:T(8,128)(2,1)}, bf16[2,128,128]{2,1,0:T(8,128)(2,1)}, bf16[2,128,128]{2,1,0:T(8,128)(2,1)}) custom-call(s32[4]{0:T(128)S(1)} %add_add_fusion.offsets, bf16[1,512,1024]{2,1,0:T(8,128)(2,1)S(1)} %copy-done.1, bf16[1,512,1024]{2,1,0:T(8,128)(2,1)S(1)} %copy-done.3), custom_call_target="tpu_custom_call" | custom-call | tf_op jit(solution)/shard_map/pack/pallas_call | solution.py:168
  5.0 1.6 %collective-permute-start = (bf16[2,128,1024]{2,1,0:T(8,128)(2,1)}, bf16[2,128,1024]{2,1,0:T(8,128)(2,1)S(1)}, u32[]{:S(2)}, u32[]{:S(2)}) collective-permute-start(bf16[2,128,1024]{2,1,0:T(8,128)(2,1)} %get-tuple-element.32), channel_id=1, source_target_pairs={{0,8},{1,9},{2,10},{3,11},{4,12},{5,13},{6,14},{7,15},{8,0},{9,1},... | collective-permute-start | bytes 1572872 | tf_op jit(solution)/shard_map/ppermute | solution.py:654
  6.5 1.5 %collective-permute-start.3 = (bf16[2,128,128]{2,1,0:T(8,128)(2,1)}, bf16[2,128,128]{2,1,0:T(8,128)(2,1)}, u32[]{:S(2)}, u32[]{:S(2)}) collective-permute-start(bf16[2,128,128]{2,1,0:T(8,128)(2,1)} %get-tuple-element.35), channel_id=1, source_target_pairs={{0,9},{1,8},{2,11},{3,10},{4,13},{5,12},{6,15},{7,14},{8,1},{9,0},... | collective-permute-start | bytes 196616 | tf_op jit(solution)/shard_map/ppermute | solution.py:654
  8.0 3.2 %collective-permute-start.4 = (bf16[2,128,128]{2,1,0:T(8,128)(2,1)}, bf16[2,128,128]{2,1,0:T(8,128)(2,1)}, u32[]{:S(2)}, u32[]{:S(2)}) collective-permute-start(bf16[2,128,128]{2,1,0:T(8,128)(2,1)} %get-tuple-element.36), channel_id=1, source_target_pairs={{1,10},{2,9},{3,12},{4,11},{5,14},{6,13},{9,2},{10,1},{11,4},{12,3... | collective-permute-start | bytes 196616 | tf_op jit(solution)/shard_map/ppermute | solution.py:654
  11.2 2.7 %collective-permute-start.1 = (bf16[2,512,128]{2,1,0:T(8,128)(2,1)}, bf16[2,512,128]{2,1,0:T(8,128)(2,1)}, u32[]{:S(2)}, u32[]{:S(2)}) collective-permute-start(bf16[2,512,128]{2,1,0:T(8,128)(2,1)} %get-tuple-element.33), channel_id=1, source_target_pairs={{0,1},{1,0},{2,3},{3,2},{4,5},{5,4},{6,7},{7,6},{8,9},{9,8},{10,11... | collective-permute-start | bytes 786440 | tf_op jit(solution)/shard_map/ppermute | solution.py:654
  14.0 1.9 %collective-permute-start.2 = (bf16[2,512,128]{2,1,0:T(8,128)(2,1)}, bf16[2,512,128]{2,1,0:T(8,128)(2,1)}, u32[]{:S(2)}, u32[]{:S(2)}) collective-permute-start(bf16[2,512,128]{2,1,0:T(8,128)(2,1)} %get-tuple-element.34), channel_id=1, source_target_pairs={{1,2},{2,1},{3,4},{4,3},{5,6},{6,5},{9,10},{10,9},{11,12},{12,11},... | collective-permute-start | bytes 786440 | tf_op jit(solution)/shard_map/ppermute | solution.py:654
  16.4 3.3 %prepare.1 = (f32[2,256,256]{2,1,0:T(8,128)S(1)}, f32[4,256,256]{2,1,0:T(8,128)S(1)}, f32[4,2,256,256]{3,2,1,0:T(8,128)S(1)}) custom-call(s32[8]{0:T(128)S(1)} %reshape.26.places, bf16[256,256]{1,0:T(8,128)(2,1)S(1)} %copy-done.10, f32[2,256,256]{2,1,0:T(8,128)S(1)} %copy-done.9, f32[1,256,256]{2,1,0:T(8,128)S(1)} %bitcast.19, f32[1,256,256]{2,1,0:T(8,128)S(1)} %bitcast.20, ...), custom_call_target="tpu_custom_call" | custom-call | tf_op jit(solution)/shard_map/prepare/pallas_call | solution.py:102
  19.8 3.9 %collective-permute-done.3.rest_3_ = bf16[2,128,128]{2,1,0:T(8,128)(2,1)} collective-permute-done((bf16[2,128,128]{2,1,0:T(8,128)(2,1)}, bf16[2,128,128]{2,1,0:T(8,128)(2,1)}, u32[]{:S(2)}, u32[]{:S(2)}) %collective-permute-start.3) | collective-permute-done | bytes 65568 | tf_op jit(solution)/shard_map/ppermute | solution.py:654
  23.7 4.3 %collective-permute-done.1.rest_1_ = bf16[2,512,128]{2,1,0:T(8,128)(2,1)} collective-permute-done((bf16[2,512,128]{2,1,0:T(8,128)(2,1)}, bf16[2,512,128]{2,1,0:T(8,128)(2,1)}, u32[]{:S(2)}, u32[]{:S(2)}) %collective-permute-start.1) | collective-permute-done | bytes 262176 | tf_op jit(solution)/shard_map/ppermute | solution.py:654
  28.1 2.4 %gather.1 = (bf16[4,2,256,256]{3,2,1,0:T(8,128)(2,1)S(1)}, bf16[4,2,256,256]{3,2,1,0:T(8,128)(2,1)S(1)}) custom-call(s32[16]{0:T(128)S(1)} %reshape.25.places, s32[4]{0:T(128)S(1)} %add_add_fusion.1.offsets, bf16[1,512,1024]{2,1,0:T(8,128)(2,1)S(1)} %copy-done.2, bf16[1,512,1024]{2,1,0:T(8,128)(2,1)S(1)} %copy-done.4, ...), custom_call_target="tpu_custom_call" | custom-call | tf_op jit(solution)/shard_map/gather/pallas_call | solution.py:248
  30.6 2.6 %collective-permute-done.5.theirs = bf16[4,2,256,256]{3,2,1,0:T(8,128)(2,1)S(1)} collective-permute-done((bf16[4,2,256,256]{3,2,1,0:T(8,128)(2,1)S(1)}, bf16[4,2,256,256]{3,2,1,0:T(8,128)(2,1)S(1)}, u32[]{:S(2)}, u32[]{:S(2)}) %collective-permute-start.5) | collective-permute-done | bytes 1048608 | tf_op jit(solution)/shard_map/ppermute | solution.py:660
  33.2 17.2 %chain.1 = (f32[4,2,256,256]{3,2,1,0:T(8,128)S(1)}, bf16[4,2,256,256]{3,2,1,0:T(8,128)(2,1)}, f32[2,128,256]{2,1,0:T(8,128)S(1)}, f32[2,128,256]{2,1,0:T(8,128)S(1)}) custom-call(s32[8]{0:T(128)S(1)} %reshape.26.places, s32[4]{0:T(128)S(1)} %fusion.live, s32[1]{0:T(128)} %bitcast.3.here, bf16[4,2,256,256]{3,2,1,0:T(8,128)(2,1)S(1)} %copy-done.7, ...), custom_call_target="tpu_custom_call" | custom-call | tf_op jit(solution)/shard_map/chain/pallas_call | solution.py:412
  50.4 1.3 %copy-done.5 = f32[4,2,256,256]{3,2,1,0:T(8,128)} copy-done((f32[4,2,256,256]{3,2,1,0:T(8,128)}, f32[4,2,256,256]{3,2,1,0:T(8,128)S(1)}, u32[]{:S(2)}) %copy-start.5) | copy-done | bytes 2097176
  52.2 2.5 %collective-permute-done.7 = f32[2,128,256]{2,1,0:T(8,128)S(1)} collective-permute-done((f32[2,128,256]{2,1,0:T(8,128)S(1)}, f32[2,128,256]{2,1,0:T(8,128)S(1)}, u32[]{:S(2)}, u32[]{:S(2)}) %collective-permute-start.7) | collective-permute-done | bytes 262176 | tf_op jit(solution)/shard_map/ppermute | solution.py:665
  55.5 4.9 %collective-permute-done.8 = bf16[2,128,256]{2,1,0:T(8,128)(2,1)S(1)} collective-permute-done((bf16[2,128,256]{2,1,0:T(8,128)(2,1)S(1)}, bf16[2,128,256]{2,1,0:T(8,128)(2,1)S(1)}, u32[]{:S(2)}, u32[]{:S(2)}) %collective-permute-start.8) | collective-permute-done | bytes 131104 | tf_op jit(solution)/shard_map/ppermute | solution.py:676
  61.9 1.6 %copy-done.6 = f32[4,2,256,256]{3,2,1,0:T(8,128)S(1)} copy-done((f32[4,2,256,256]{3,2,1,0:T(8,128)S(1)}, f32[4,2,256,256]{3,2,1,0:T(8,128)}, u32[]{:S(2)}) %copy-start.6) | copy-done | bytes 2097176
  63.5 4.5 %scatter.1 = (f32[2,512,1024]{2,1,0:T(8,128)}, bf16[2,128,1024]{2,1,0:T(8,128)(2,1)}, bf16[2,512,128]{2,1,0:T(8,128)(2,1)}, bf16[2,512,128]{2,1,0:T(8,128)(2,1)}...) custom-call(s32[16]{0:T(128)S(1)} %reshape.25.places, s32[8]{0:T(128)S(1)} %reshape.27.live, ...), custom_call_target="tpu_custom_call" | custom-call | bytes 8388608 | tf_op jit(solution)/shard_map/scatter/pallas_call | solution.py:494
  71.8 4.1 %collective-permute-start.14 = (bf16[2,512,128]{2,1,0:T(8,128)(2,1)}, bf16[2,512,128]{2,1,0:T(8,128)(2,1)S(1)}, u32[]{:S(2)}, u32[]{:S(2)}) collective-permute-start(bf16[2,512,128]{2,1,0:T(8,128)(2,1)} %get-tuple-element.53), channel_id=1, source_target_pairs={{1,2},{2,1},{3,4},{4,3},{5,6},{6,5},{9,10},{10,9},{11,12},{12,11},... | collective-permute-start | bytes 786440 | tf_op jit(solution)/shard_map/ppermute | solution.py:679
  76.0 1.7 %collective-permute-start.11 = (bf16[2,128,256]{2,1,0:T(8,128)(2,1)S(1)}, bf16[2,128,256]{2,1,0:T(8,128)(2,1)S(1)}, u32[]{:S(2)}, u32[]{:S(2)}) collective-permute-start(bf16[2,128,256]{2,1,0:T(8,128)(2,1)S(1)} %add_convert_fusion.part), channel_id=1, source_target_pairs={{0,4},{1,5},{2,6},{3,7},{4,0},{5,1},{6,2},{7,3},{8,12},{9,13},{10,... | collective-permute-start | bytes 393224 | tf_op jit(solution)/shard_map/ppermute | solution.py:676
  77.7 5.6 %collective-permute-done.15.rest_3_ = bf16[2,128,128]{2,1,0:T(8,128)(2,1)S(1)} collective-permute-done((bf16[2,128,128]{2,1,0:T(8,128)(2,1)S(1)}, bf16[2,128,128]{2,1,0:T(8,128)(2,1)S(1)}, u32[]{:S(2)}, u32[]{:S(2)}) %collective-permute-start.15) | collective-permute-done | bytes 65568 | tf_op jit(solution)/shard_map/ppermute | solution.py:679
  83.3 3.2 %collective-permute-start.16 = (bf16[2,128,128]{2,1,0:T(8,128)(2,1)}, bf16[2,128,128]{2,1,0:T(8,128)(2,1)S(1)}, u32[]{:S(2)}, u32[]{:S(2)}) collective-permute-start(bf16[2,128,128]{2,1,0:T(8,128)(2,1)} %get-tuple-element.55), channel_id=1, source_target_pairs={{1,10},{2,9},{3,12},{4,11},{5,14},{6,13},{9,2},{10,1},{11,4},{12,3... | collective-permute-start | bytes 196616 | tf_op jit(solution)/shard_map/ppermute | solution.py:679
  86.5 5.0 %collective-permute-done.16.rest_4_ = bf16[2,128,128]{2,1,0:T(8,128)(2,1)S(1)} collective-permute-done((bf16[2,128,128]{2,1,0:T(8,128)(2,1)}, bf16[2,128,128]{2,1,0:T(8,128)(2,1)S(1)}, u32[]{:S(2)}, u32[]{:S(2)}) %collective-permute-start.16) | collective-permute-done | bytes 65568 | tf_op jit(solution)/shard_map/ppermute | solution.py:679
  91.5 3.9 %borders.1 = (f32[2,512,1024]{2,1,0:T(8,128)}, f32[2,128,256]{2,1,0:T(8,128)}) custom-call(s32[4]{0:T(128)S(1)} %constant_dynamic-update-slice_fusion.offsets, f32[2,512,1024]{2,1,0:T(8,128)} %get-tuple-element.42.tile_in, bf16[2,128,256]{2,1,0:T(8,128)(2,1)S(1)} %add_convert_fusion.part, ...), custom_call_target="tpu_custom_call", output_to_operand_aliasing={{0}: (1, {})} | custom-call | flops 1048576 | bytes 8388608 | tf_op jit(solution)/shard_map/borders/pallas_call | solution.py:558
  (59 shorter events, 8.6 us)
Async XLA Ops:
  0.6 15.7 %copy-start = (f32[1,1,4,2,256,256]{5,4,3,2,1,0:T(8,128)S(1)}, f32[1,1,4,2,256,256]{5,4,3,2,1,0:T(8,128)}, u32[]{:S(2)}) copy-start(f32[1,1,4,2,256,256]{5,4,3,2,1,0:T(8,128)} %param.15) | copy-start | bytes 6291460
  0.6 15.2 %copy-start.11 = (s32[1,1,4,2,2]{2,4,3,1,0:T(2,128)S(1)}, s32[1,1,4,2,2]{2,4,3,1,0:T(2,128)}, u32[]{:S(2)}) copy-start(s32[1,1,4,2,2]{2,4,3,1,0:T(2,128)} %param.13) | copy-start | bytes 196
  3.3 13.0 %copy-start.8 = (f32[256,256]{1,0:T(8,128)S(1)}, f32[256,256]{1,0:T(8,128)}, u32[]{:S(2)}) copy-start(f32[256,256]{1,0:T(8,128)} %param.12) | copy-start | bytes 786436
  3.3 13.1 %copy-start.9 = (f32[2,256,256]{2,1,0:T(8,128)S(1)}, f32[2,256,256]{2,1,0:T(8,128)}, u32[]{:S(2)}) copy-start(f32[2,256,256]{2,1,0:T(8,128)} %probe.1) | copy-start | bytes 1572868
  3.3 13.1 %copy-start.10 = (bf16[256,256]{1,0:T(8,128)(2,1)S(1)}, bf16[256,256]{1,0:T(8,128)(2,1)}, u32[]{:S(2)}) copy-start(bf16[256,256]{1,0:T(8,128)(2,1)} %constant.69.clone.order_t) | copy-start | bytes 393220
  5.0 23.1 %collective-permute-start = (bf16[2,128,1024]{2,1,0:T(8,128)(2,1)}, bf16[2,128,1024]{2,1,0:T(8,128)(2,1)S(1)}, u32[]{:S(2)}, u32[]{:S(2)}) collective-permute-start(bf16[2,128,1024]{2,1,0:T(8,128)(2,1)} %get-tuple-element.32), channel_id=1, source_target_pairs={{0,8},{1,9},{2,10},{3,11},{4,12},{5,13},{6,14},{7,15},{8,0},{9,1},... | collective-permute-start | bytes 1572872 | tf_op jit(solution)/shard_map/ppermute | solution.py:654
  6.5 17.2 %collective-permute-start.3 = (bf16[2,128,128]{2,1,0:T(8,128)(2,1)}, bf16[2,128,128]{2,1,0:T(8,128)(2,1)}, u32[]{:S(2)}, u32[]{:S(2)}) collective-permute-start(bf16[2,128,128]{2,1,0:T(8,128)(2,1)} %get-tuple-element.35), channel_id=1, source_target_pairs={{0,9},{1,8},{2,11},{3,10},{4,13},{5,12},{6,15},{7,14},{8,1},{9,0},... | collective-permute-start | bytes 196616 | tf_op jit(solution)/shard_map/ppermute | solution.py:654
  8.0 15.7 %collective-permute-start.4 = (bf16[2,128,128]{2,1,0:T(8,128)(2,1)}, bf16[2,128,128]{2,1,0:T(8,128)(2,1)}, u32[]{:S(2)}, u32[]{:S(2)}) collective-permute-start(bf16[2,128,128]{2,1,0:T(8,128)(2,1)} %get-tuple-element.36), channel_id=1, source_target_pairs={{1,10},{2,9},{3,12},{4,11},{5,14},{6,13},{9,2},{10,1},{11,4},{12,3... | collective-permute-start | bytes 196616 | tf_op jit(solution)/shard_map/ppermute | solution.py:654
  11.2 16.8 %collective-permute-start.1 = (bf16[2,512,128]{2,1,0:T(8,128)(2,1)}, bf16[2,512,128]{2,1,0:T(8,128)(2,1)}, u32[]{:S(2)}, u32[]{:S(2)}) collective-permute-start(bf16[2,512,128]{2,1,0:T(8,128)(2,1)} %get-tuple-element.33), channel_id=1, source_target_pairs={{0,1},{1,0},{2,3},{3,2},{4,5},{5,4},{6,7},{7,6},{8,9},{9,8},{10,11... | collective-permute-start | bytes 786440 | tf_op jit(solution)/shard_map/ppermute | solution.py:654
  14.0 14.1 %collective-permute-start.2 = (bf16[2,512,128]{2,1,0:T(8,128)(2,1)}, bf16[2,512,128]{2,1,0:T(8,128)(2,1)}, u32[]{:S(2)}, u32[]{:S(2)}) collective-permute-start(bf16[2,512,128]{2,1,0:T(8,128)(2,1)} %get-tuple-element.34), channel_id=1, source_target_pairs={{1,2},{2,1},{3,4},{4,3},{5,6},{6,5},{9,10},{10,9},{11,12},{12,11},... | collective-permute-start | bytes 786440 | tf_op jit(solution)/shard_map/ppermute | solution.py:654
  16.4 11.7 %copy-start.2 = (bf16[1,512,1024]{2,1,0:T(8,128)(2,1)S(1)}, bf16[1,512,1024]{2,1,0:T(8,128)(2,1)}, u32[]{:S(2)}) copy-start(bf16[1,512,1024]{2,1,0:T(8,128)(2,1)} %tile_re.3) | copy-start | bytes 3145732
  16.4 11.7 %copy-start.4 = (bf16[1,512,1024]{2,1,0:T(8,128)(2,1)S(1)}, bf16[1,512,1024]{2,1,0:T(8,128)(2,1)}, u32[]{:S(2)}) copy-start(bf16[1,512,1024]{2,1,0:T(8,128)(2,1)} %tile_im.3) | copy-start | bytes 3145732
  30.5 2.7 %collective-permute-start.5 = (bf16[4,2,256,256]{3,2,1,0:T(8,128)(2,1)S(1)}, bf16[4,2,256,256]{3,2,1,0:T(8,128)(2,1)S(1)}, u32[]{:S(2)}, u32[]{:S(2)}) collective-permute-start(bf16[4,2,256,256]{3,2,1,0:T(8,128)(2,1)S(1)} %get-tuple-element.38), channel_id=1, source_target_pairs={{0,16},{16,0},{1,17},{17,1},{2,18},{18,2},{3,19},{19,3},{4,20},{20... | collective-permute-start | bytes 3145736 | tf_op jit(solution)/shard_map/ppermute | solution.py:660
  51.7 10.1 %collective-permute-start.6 = (bf16[4,2,256,256]{3,2,1,0:T(8,128)(2,1)}, bf16[4,2,256,256]{3,2,1,0:T(8,128)(2,1)S(1)}, u32[]{:S(2)}, u32[]{:S(2)}) collective-permute-start(bf16[4,2,256,256]{3,2,1,0:T(8,128)(2,1)} %get-tuple-element.41), channel_id=1, source_target_pairs={{0,16},{16,0},{1,17},{17,1},{2,18},{18,2},{3,19},{19,3},{4,20},{20... | collective-permute-start | bytes 3145736 | tf_op jit(solution)/shard_map/ppermute | solution.py:664
  51.9 2.9 %collective-permute-start.7 = (f32[2,128,256]{2,1,0:T(8,128)S(1)}, f32[2,128,256]{2,1,0:T(8,128)S(1)}, u32[]{:S(2)}, u32[]{:S(2)}) collective-permute-start(f32[2,128,256]{2,1,0:T(8,128)S(1)} %get-tuple-element.44), channel_id=1, source_target_pairs={{0,16},{16,0},{1,17},{17,1},{2,18},{18,2},{3,19},{19,3},{4,20},{20... | collective-permute-start | bytes 786440 | tf_op jit(solution)/shard_map/ppermute | solution.py:665
  54.8 5.6 %collective-permute-start.8 = (bf16[2,128,256]{2,1,0:T(8,128)(2,1)S(1)}, bf16[2,128,256]{2,1,0:T(8,128)(2,1)S(1)}, u32[]{:S(2)}, u32[]{:S(2)}) collective-permute-start(bf16[2,128,256]{2,1,0:T(8,128)(2,1)S(1)} %add_convert_fusion.3), channel_id=1, source_target_pairs={{0,8},{8,0},{1,9},{9,1},{2,10},{10,2},{3,11},{11,3},{4,12},{12,4},... | collective-permute-start | bytes 393224 | tf_op jit(solution)/shard_map/ppermute | solution.py:676
  60.4 7.5 %collective-permute-start.9 = (bf16[2,128,256]{2,1,0:T(8,128)(2,1)S(1)}, bf16[2,128,256]{2,1,0:T(8,128)(2,1)S(1)}, u32[]{:S(2)}, u32[]{:S(2)}) collective-permute-start(bf16[2,128,256]{2,1,0:T(8,128)(2,1)S(1)} %add_convert_fusion.2), channel_id=1, source_target_pairs={{0,1},{1,0},{2,3},{3,2},{4,5},{5,4},{6,7},{7,6},{8,9},{9,8},{10,11... | collective-permute-start | bytes 393224 | tf_op jit(solution)/shard_map/ppermute | solution.py:676
  68.0 23.5 %collective-permute-start.12 = (bf16[2,128,1024]{2,1,0:T(8,128)(2,1)}, bf16[2,128,1024]{2,1,0:T(8,128)(2,1)S(1)}, u32[]{:S(2)}, u32[]{:S(2)}) collective-permute-start(bf16[2,128,1024]{2,1,0:T(8,128)(2,1)} %get-tuple-element.51), channel_id=1, source_target_pairs={{0,8},{1,9},{2,10},{3,11},{4,12},{5,13},{6,14},{7,15},{8,0},{9,1},... | collective-permute-start | bytes 1572872 | tf_op jit(solution)/shard_map/ppermute | solution.py:679
  68.6 7.3 %collective-permute-start.10 = (bf16[2,128,256]{2,1,0:T(8,128)(2,1)S(1)}, bf16[2,128,256]{2,1,0:T(8,128)(2,1)S(1)}, u32[]{:S(2)}, u32[]{:S(2)}) collective-permute-start(bf16[2,128,256]{2,1,0:T(8,128)(2,1)S(1)} %add_convert_fusion.1), channel_id=1, source_target_pairs={{0,2},{1,3},{2,0},{3,1},{4,6},{5,7},{6,4},{7,5},{8,10},{9,11},{10,... | collective-permute-start | bytes 393224 | tf_op jit(solution)/shard_map/ppermute | solution.py:676
  69.3 13.9 %collective-permute-start.15 = (bf16[2,128,128]{2,1,0:T(8,128)(2,1)S(1)}, bf16[2,128,128]{2,1,0:T(8,128)(2,1)S(1)}, u32[]{:S(2)}, u32[]{:S(2)}) collective-permute-start(bf16[2,128,128]{2,1,0:T(8,128)(2,1)S(1)} %get-tuple-element.54), channel_id=1, source_target_pairs={{0,9},{1,8},{2,11},{3,10},{4,13},{5,12},{6,15},{7,14},{8,1},{9,0},... | collective-permute-start | bytes 196616 | tf_op jit(solution)/shard_map/ppermute | solution.py:679
  70.6 20.8 %collective-permute-start.13 = (bf16[2,512,128]{2,1,0:T(8,128)(2,1)}, bf16[2,512,128]{2,1,0:T(8,128)(2,1)S(1)}, u32[]{:S(2)}, u32[]{:S(2)}) collective-permute-start(bf16[2,512,128]{2,1,0:T(8,128)(2,1)} %get-tuple-element.52), channel_id=1, source_target_pairs={{0,1},{1,0},{2,3},{3,2},{4,5},{5,4},{6,7},{7,6},{8,9},{9,8},{10,11... | collective-permute-start | bytes 786440 | tf_op jit(solution)/shard_map/ppermute | solution.py:679
  71.8 19.6 %collective-permute-start.14 = (bf16[2,512,128]{2,1,0:T(8,128)(2,1)}, bf16[2,512,128]{2,1,0:T(8,128)(2,1)S(1)}, u32[]{:S(2)}, u32[]{:S(2)}) collective-permute-start(bf16[2,512,128]{2,1,0:T(8,128)(2,1)} %get-tuple-element.53), channel_id=1, source_target_pairs={{1,2},{2,1},{3,4},{4,3},{5,6},{6,5},{9,10},{10,9},{11,12},{12,11},... | collective-permute-start | bytes 786440 | tf_op jit(solution)/shard_map/ppermute | solution.py:679
  76.0 15.5 %collective-permute-start.11 = (bf16[2,128,256]{2,1,0:T(8,128)(2,1)S(1)}, bf16[2,128,256]{2,1,0:T(8,128)(2,1)S(1)}, u32[]{:S(2)}, u32[]{:S(2)}) collective-permute-start(bf16[2,128,256]{2,1,0:T(8,128)(2,1)S(1)} %add_convert_fusion.part), channel_id=1, source_target_pairs={{0,4},{1,5},{2,6},{3,7},{4,0},{5,1},{6,2},{7,3},{8,12},{9,13},{10,... | collective-permute-start | bytes 393224 | tf_op jit(solution)/shard_map/ppermute | solution.py:676
  83.3 8.2 %collective-permute-start.16 = (bf16[2,128,128]{2,1,0:T(8,128)(2,1)}, bf16[2,128,128]{2,1,0:T(8,128)(2,1)S(1)}, u32[]{:S(2)}, u32[]{:S(2)}) collective-permute-start(bf16[2,128,128]{2,1,0:T(8,128)(2,1)} %get-tuple-element.55), channel_id=1, source_target_pairs={{1,10},{2,9},{3,12},{4,11},{5,14},{6,13},{9,2},{10,1},{11,4},{12,3... | collective-permute-start | bytes 196616 | tf_op jit(solution)/shard_map/ppermute | solution.py:679
  (6 other events, 13.2 us)

commit v5 on v4

--- a/solution.py
+++ b/solution.py
@@ -61,7 +61,7 @@
     return jnp.concatenate(parts, axis=1)
 
 
-def prep_kernel(places, order_t, probe, *refs):
+def prep_kernel(places, order_t, after, probe, *refs):
     step = pl.program_id(0)
     size = probe.shape[-1]
     half = size // 2
@@ -95,7 +95,7 @@
         waves[0, plane] = pltpu.roll(moved, down, axis=0)
 
 
-def prepare(places, probe, phases, frames):
+def prepare(places, after, probe, phases, frames):
     count, size = frames.shape[0], phases.shape[-1]
     blocks = size // LANES
     full = lambda *shape: pl.BlockSpec(shape, lambda i: (0,) * len(shape))
@@ -105,6 +105,7 @@
         in_specs=[
             SMEM,
             full(size, size),
+            ANY,
             full(2, size, size),
             *(pl.BlockSpec((1, size, LANES), lambda i, b=b: (0, 0, b)) for b in range(blocks)),
             *(pl.BlockSpec((1, size, LANES), lambda i, b=b: (i, 0, b)) for b in range(blocks)),
@@ -125,6 +126,7 @@
     )(
         places,
         jnp.asarray(sorting_table(size)),
+        after,
         probe,
         *[phases[None]] * blocks,
         *[frames] * blocks,
@@ -165,13 +167,14 @@
 
 
 def pack(offsets, tile_re, tile_im, edges, names, half):
+    vmem = pl.BlockSpec(memory_space=pltpu.VMEM)
     return pl.pallas_call(
         functools.partial(pack_kernel, edges, names, half),
         in_specs=[SMEM, HBM, HBM],
-        out_specs=[ANY] * len(edges),
+        out_specs=[vmem] * len(edges),
         out_shape=strip_shapes(edges, *tile_re.shape[1:], half),
         scratch_shapes=[pltpu.SemaphoreType.DMA((2 * len(edges),))],
-        compiler_params=pltpu.CompilerParams(vmem_limit_bytes=4 * MIB),
+        compiler_params=pltpu.CompilerParams(vmem_limit_bytes=56 * MIB),
         name="pack",
     )(offsets, tile_re, tile_im)
 
@@ -182,7 +185,7 @@
     return down, across, pl.multiple_of(row - down, ROWS), pl.multiple_of(col - across, LANES)
 
 
-def gather_kernel(spots, edges, names, half, places, offsets, tile_re, tile_im, after, *rest):
+def gather_kernel(spots, edges, names, half, places, offsets, tile_re, tile_im, *rest):
     strips, (mine, other, padded, sems) = rest[:-4], rest[-4:]
     tile_rows, tile_cols = tile_re.shape[1:]
     size = mine.shape[-1]
@@ -239,7 +242,7 @@
         cut(sections * place + here, mine, place)
 
 
-def gather(places, offsets, tile_re, tile_im, after, edges, names, strips, size):
+def gather(places, offsets, tile_re, tile_im, edges, names, strips, size):
     half = size // 2
     spots = places.shape[0] // 2
     tile_rows, tile_cols = tile_re.shape[1:]
@@ -247,7 +250,7 @@
     vmem = pl.BlockSpec(memory_space=pltpu.VMEM)
     return pl.pallas_call(
         functools.partial(gather_kernel, spots, edges, names, half),
-        in_specs=[SMEM, SMEM, HBM, HBM] + [ANY] * (1 + len(strips)),
+        in_specs=[SMEM, SMEM, HBM, HBM] + [ANY] * len(strips),
         out_specs=[vmem, vmem],
         out_shape=[shape, shape],
         scratch_shapes=[
@@ -256,7 +259,7 @@
         ],
         compiler_params=pltpu.CompilerParams(vmem_limit_bytes=16 * MIB),
         name="gather",
-    )(places, offsets, tile_re, tile_im, after, *strips)
+    )(places, offsets, tile_re, tile_im, *strips)
 
 
 def chain_kernel(
@@ -392,7 +395,7 @@
             value = pltpu.roll(pltpu.roll(value * weight, back_by, axis=1), up, axis=0)
             pulled[plane] += value
 
-    keep[...] = terms[me]
+    keep[...] = terms[me].astype(bf16)
     send[...] = terms[1 - me].astype(bf16)
 
     @pl.when(step == steps - 1)
@@ -425,7 +428,7 @@
         ],
         out_specs=[block, block, full(2, size // 2, size), full(2, size // 2, size)],
         out_shape=[
-            jax.ShapeDtypeStruct((count, 2, size, size), f32),
+            jax.ShapeDtypeStruct((count, 2, size, size), bf16),
             jax.ShapeDtypeStruct((count, 2, size, size), bf16),
             jax.ShapeDtypeStruct((2, size // 2, size), f32),
             jax.ShapeDtypeStruct((2, size // 2, size), f32),
@@ -484,19 +487,32 @@
         cols = span(across, offsets, names, half, body[1])
         for plane in range(2):
             strip[plane] = total[plane, rows, cols].astype(bf16)
+    for (down, acrosses), strip in zip(corner_keys(names), strips[len(edges) :]):
+        rows = span(down, offsets, names, half, None)
+        for k, across in enumerate(acrosses):
+            cols = span(across, offsets, names, half, None)
+            for plane in range(2):
+                strip[plane, k] = total[plane, rows, cols].astype(bf16)
     copy.wait()
+
+
+def corner_keys(names):
+    acrosses = [key for key in names if key[0] == "col"]
+    return [(key, acrosses) for key in names if key[0] == "row" and acrosses]
 
 
 def scatter(places, live, offsets, kept, arrived, edges, names, tile_rows, tile_cols):
     count, _, size, _ = kept.shape
     half = size // 2
+    corners = corner_keys(names)
     vmem = pl.BlockSpec(memory_space=pltpu.VMEM)
     return pl.pallas_call(
         functools.partial(scatter_kernel, edges, names, half),
         in_specs=[SMEM, SMEM, SMEM, vmem, vmem],
-        out_specs=[HBM] + [vmem] * len(edges),
+        out_specs=[HBM] + [vmem] * (len(edges) + len(corners)),
         out_shape=[jax.ShapeDtypeStruct((2, tile_rows, tile_cols), f32)]
-        + strip_shapes(edges, tile_rows, tile_cols, half),
+        + strip_shapes(edges, tile_rows, tile_cols, half)
+        + [jax.ShapeDtypeStruct((2, len(keys), half, half), bf16) for _, keys in corners],
         scratch_shapes=[
             pltpu.VMEM((2, tile_rows + 2 * half, tile_cols + 2 * half), f32),
             pltpu.SemaphoreType.DMA((1,)),
@@ -507,6 +523,32 @@
         ),
         name="scatter",
     )(places, live, offsets, kept, arrived)
+
+
+def corner_kernel(names, half, offsets, *refs):
+    corners = corner_keys(names)
+    arrived, refs = refs[: len(corners)], refs[len(corners) :]
+    ins, outs = refs[: len(refs) // 2], refs[len(refs) // 2 :]
+    for k, (before, strip) in enumerate(zip(ins, outs)):
+        strip[...] = before[...]
+        for (down, _), block in zip(corners, arrived):
+            rows = span(down, offsets, names, half, None)
+            for plane in range(2):
+                strip[plane, rows, :] = (
+                    strip[plane, rows, :].astype(f32) + block[plane, k].astype(f32)
+                ).astype(bf16)
+
+
+def add_corners(offsets, strips, arrived, names, half):
+    vmem = pl.BlockSpec(memory_space=pltpu.VMEM)
+    return pl.pallas_call(
+        functools.partial(corner_kernel, names, half),
+        in_specs=[SMEM] + [vmem] * (len(arrived) + len(strips)),
+        out_specs=[vmem] * len(strips),
+        out_shape=[jax.ShapeDtypeStruct(strip.shape, bf16) for strip in strips],
+        compiler_params=pltpu.CompilerParams(vmem_limit_bytes=8 * MIB),
+        name="corners",
+    )(offsets, *arrived, *strips)
 
 
 def border_kernel(edges, names, half, offsets, tile_in, part, other, *rest):
@@ -540,9 +582,9 @@
             if key in downs:
                 block[plane] += strips[(key, None)][plane].astype(f32)
                 for across in acrosses:
-                    block[plane, :, spans[across]] += strips[(key, across)][plane].astype(
-                        f32
-                    ) + strips[(None, across)][plane, rows, :].astype(f32)
+                    block[plane, :, spans[across]] += strips[(None, across)][
+                        plane, rows, :
+                    ].astype(f32)
             else:
                 block[plane] += strips[(None, key)][plane, rows, :].astype(f32)
         copy(k, True).start()
@@ -594,12 +636,6 @@
             if 0 <= to_row < rows and 0 <= to_col < cols:
                 pairs.append((r * cols + c, to_row * cols + to_col))
     return pairs
-
-
-def doublings(axis):
-    size = lax.axis_size(axis)
-    assert size & (size - 1) == 0
-    return size.bit_length() - 1
 
 
 def shards(probe, object_re, object_im, phases, centres, occupied, measured):
@@ -640,8 +676,9 @@
     downs = [key for key in names if key[0] == "row"]
     acrosses = [key for key in names if key[0] == "col"]
     edges = [(key, None) for key in downs] + [(None, key) for key in acrosses]
-    edges += [(down, across) for down in downs for across in acrosses]
-    paths = [route(edge, rows, cols) for edge in edges]
+    outer, paths = edges, [route(edge, rows, cols) for edge in edges]
+    edges = edges + [(down, across) for down in downs for across in acrosses]
+    paths += [route(edge, rows, cols) for edge in edges[len(outer) :]]
     both = ("row", "col")
 
     def numbers(*values):
@@ -652,38 +689,57 @@
     bulk = len(names)
     own = pack(tile_at, object_re, object_im, edges, names, half)
     strips = [lax.ppermute(strip, both, path) for strip, path in zip(own, paths)]
-    kern, sorted_frames, waves = prepare(my_places, probe, phases, frames)
-    mine, other = gather(
-        places, padded_at, object_re, object_im, waves, edges, names, strips, size
-    )
+    mine, other = gather(places, padded_at, object_re, object_im, edges, names, strips, size)
     across_depth = [(i, 1 - i) for i in range(sections)]
     theirs = lax.ppermute(other, "depth", across_depth)
+    kern, sorted_frames, waves = prepare(my_places, mine, probe, phases, frames)
     keep, send, pulled_keep, pulled_send = chain(
-        my_places, my_live, here.reshape(1), kern, mine, theirs, sorted_frames, waves, 2
+        my_places, my_live, here.reshape(1), kern, mine, theirs, sorted_frames, waves, count
     )
     arrived = lax.ppermute(send, "depth", across_depth)
     pulled = pulled_keep + lax.ppermute(pulled_send, "depth", across_depth)
 
     tile, *own = scatter(
-        places, live, padded_at, keep, arrived, edges, names, tile_rows, tile_cols
+        places, live, padded_at, keep, arrived, outer, names, tile_rows, tile_cols
     )
 
-    steps = [(axis, 1 << k) for axis in ("row", "col") for k in range(doublings(axis))]
-    if len(steps) < 3:
-        added = [lax.ppermute(strip, both, path) for strip, path in zip(own, paths)]
-    for at, (axis, step) in enumerate(steps):
+    bits = rows.bit_length() + cols.bit_length() - 2
+    assert rows * cols == 1 << bits
+    flips = [cols << k for k in range(rows.bit_length() - 1)]
+    flips += [1 << k for k in range(cols.bit_length() - 1)]
+    early, late = flips[: max(bits - 2, 0)], flips[max(bits - 2, 0) :]
+    rounds = [early[k : k + 2] for k in range(0, len(early), 2)] + [[flip] for flip in late]
+
+    def fetch(block, flip):
+        return lax.ppermute(block, both, [(i, i ^ flip) for i in range(rows * cols)])
+
+    def sent(own):
+        own, corners = own[: len(outer)], own[len(outer) :]
+        if corners:
+            corners = [lax.ppermute(x, both, path) for x, path in zip(corners, paths)]
+            own[len(downs) :] = add_corners(tile_at, own[len(downs) :], corners, names, half)
+        return [lax.ppermute(strip, both, path) for strip, path in zip(own, paths)]
+
+    added = None
+    for at, flips in enumerate(rounds):
         mine = pulled.astype(bf16)
-        theirs = lax.ppermute(mine, axis, [(i, i ^ step) for i in range(lax.axis_size(axis))])
-        if at == len(steps) - 3:
-            theirs, *own = lax.optimization_barrier((theirs, *own))
-            added = [lax.ppermute(strip, both, path) for strip, path in zip(own, paths)]
-        if at < len(steps) - 1:
-            pulled = mine.astype(f32) + theirs.astype(f32)
+        theirs = [fetch(mine, flip) for flip in flips]
+        if len(flips) == 2:
+            theirs.append(fetch(mine, flips[0] ^ flips[1]))
+        if added is None and at >= len(rounds) - 3:
+            *theirs, own = lax.optimization_barrier((*theirs, own))
+            added = sent(own)
+        if at < len(rounds) - 1:
+            sums = [part.astype(f32) for part in (mine, *theirs)]
+            pulled = sums[0] + sums[1]
+            if len(flips) == 2:
+                pulled = pulled + (sums[2] + sums[3])
+    (theirs,) = theirs
     if rows == 2:
         first_row = jnp.where(row_at == 0, 0, half)
     else:
         first_row = jnp.int32(half if downs else 0)
-    gradient, probe_share = add_borders(lax.dynamic_update_index_in_dim(tile_at, first_row.astype(jnp.int32), bulk, 0), tile, (mine, theirs), edges, names, added, half)
+    gradient, probe_share = add_borders(lax.dynamic_update_index_in_dim(tile_at, first_row.astype(jnp.int32), bulk, 0), tile, (mine, theirs), outer, names, added, half)
     return (gradient[:, None], probe_share)
 
 

time: 95.7 us -> 100 us (1.045)
  the two profiles are of different devices: /device:TPU:8 before, /device:TPU:0 now
where the time goes in v5:
time: 100 us; the launch traced here: 99.4 us
  Pallas kernels  37.4 us (37%)
  starting transfers between devices  26.1 us (26%)
  waiting for transfers between devices  21.1 us (21%)
  local copies, waits for them, and re-layouts  11.1 us (11%)
  other arithmetic  2.56 us (3%)
  between operations  1.09 us (1%)
    pallas_call x1, Pallas kernels, chain(): pl.pallas_call(functools.partial(chain_kernel, group), grid=(count // gro...  18 us
    ppermute x5, starting transfers between devices, fetch(): lax.ppermute(block, both, [(i, i ^ flip) for i in range(rows * cols)])  11.4 us
    ppermute x5, waiting for transfers between devices, fetch(): lax.ppermute(block, both, [(i, i ^ flip) for i in range(rows * cols)])  10.4 us
    ppermute x5, starting transfers between devices, shards(): lax.ppermute(strip, both, path)  10.2 us
    unnamed x39, local copies, waits for them, and re-layouts  9.34 us
    ppermute x5, waiting for transfers between devices, shards(): lax.ppermute(strip, both, path)  7.33 us
    pallas_call x1, Pallas kernels, scatter(): pl.pallas_call(functools.partial(scatter_kernel, edges, names, half), in_...  4.34 us
    pallas_call x1, Pallas kernels, add_borders(): pl.pallas_call(functools.partial(border_kernel, edges, names, half), in_s...  3.92 us
  transfers between devices with their start and end apart: 17, of which 6 were waited for; matrix products, arithmetic and copies ran while one was open for 4% of the time, Pallas kernels for 9%

profile of v5, /device:TPU:0, one launch (start us, length us, event | category | flops | bytes accessed | tf_op | source)
XLA Modules:
  0.0 99.4 jit_solution(15843082773363742677)
XLA Ops:
  1.3 3.2 %pack.1 = (bf16[2,128,1024]{2,1,0:T(8,128)(2,1)}, bf16[2,512,128]{2,1,0:T(8,128)(2,1)}, bf16[2,512,128]{2,1,0:T(8,128)(2,1)}, bf16[2,128,128]{2,1,0:T(8,128)(2,1)}, bf16[2,128,128]{2,1,0:T(8,128)(2,1)}) custom-call(s32[4]{0:T(128)} %add_add_fusion.offsets, bf16[1,512,1024]{2,1,0:T(8,128)(2,1)} %tile_re.3, bf16[1,512,1024]{2,1,0:T(8,128)(2,1)} %tile_im.3), custom_call_target="tpu_custom_call" | custom-call | tf_op jit(solution)/shard_map/pack/pallas_call | solution.py:171
  4.5 3.3 %collective-permute-start = (bf16[2,128,1024]{2,1,0:T(8,128)(2,1)}, bf16[2,128,1024]{2,1,0:T(8,128)(2,1)}, u32[]{:S(2)}, u32[]{:S(2)}) collective-permute-start(bf16[2,128,1024]{2,1,0:T(8,128)(2,1)} %get-tuple-element.32), channel_id=1, source_target_pairs={{0,8},{1,9},{2,10},{3,11},{4,12},{5,13},{6,14},{7,15},{8,0},{9,1},... | collective-permute-start | bytes 1572872 | tf_op jit(solution)/shard_map/ppermute | solution.py:691
  7.8 1.5 %collective-permute-start.1 = (bf16[2,512,128]{2,1,0:T(8,128)(2,1)}, bf16[2,512,128]{2,1,0:T(8,128)(2,1)S(1)}, u32[]{:S(2)}, u32[]{:S(2)}) collective-permute-start(bf16[2,512,128]{2,1,0:T(8,128)(2,1)} %get-tuple-element.33), channel_id=1, source_target_pairs={{0,1},{1,0},{2,3},{3,2},{4,5},{5,4},{6,7},{7,6},{8,9},{9,8},{10,11... | collective-permute-start | bytes 786440 | tf_op jit(solution)/shard_map/ppermute | solution.py:691
  9.3 1.4 %collective-permute-start.2 = (bf16[2,512,128]{2,1,0:T(8,128)(2,1)}, bf16[2,512,128]{2,1,0:T(8,128)(2,1)}, u32[]{:S(2)}, u32[]{:S(2)}) collective-permute-start(bf16[2,512,128]{2,1,0:T(8,128)(2,1)} %get-tuple-element.34), channel_id=1, source_target_pairs={{1,2},{2,1},{3,4},{4,3},{5,6},{6,5},{9,10},{10,9},{11,12},{12,11},... | collective-permute-start | bytes 786440 | tf_op jit(solution)/shard_map/ppermute | solution.py:691
  10.6 3.3 %collective-permute-start.3 = (bf16[2,128,128]{2,1,0:T(8,128)(2,1)}, bf16[2,128,128]{2,1,0:T(8,128)(2,1)S(1)}, u32[]{:S(2)}, u32[]{:S(2)}) collective-permute-start(bf16[2,128,128]{2,1,0:T(8,128)(2,1)} %get-tuple-element.35), channel_id=1, source_target_pairs={{0,9},{1,8},{2,11},{3,10},{4,13},{5,12},{6,15},{7,14},{8,1},{9,0},... | collective-permute-start | bytes 196616 | tf_op jit(solution)/shard_map/ppermute | solution.py:691
  14.9 7.3 %collective-permute-done.3.rest_3_ = bf16[2,128,128]{2,1,0:T(8,128)(2,1)S(1)} collective-permute-done((bf16[2,128,128]{2,1,0:T(8,128)(2,1)}, bf16[2,128,128]{2,1,0:T(8,128)(2,1)S(1)}, u32[]{:S(2)}, u32[]{:S(2)}) %collective-permute-start.3) | collective-permute-done | bytes 65568 | tf_op jit(solution)/shard_map/ppermute | solution.py:691
  24.2 1.2 %copy-done.2 = bf16[1,512,1024]{2,1,0:T(8,128)(2,1)S(1)} copy-done((bf16[1,512,1024]{2,1,0:T(8,128)(2,1)S(1)}, bf16[1,512,1024]{2,1,0:T(8,128)(2,1)}, u32[]{:S(2)}) %copy-start.2) | copy-done | bytes 1048600
  28.1 3.4 %gather.1 = (bf16[4,2,256,256]{3,2,1,0:T(8,128)(2,1)S(1)}, bf16[4,2,256,256]{3,2,1,0:T(8,128)(2,1)}) custom-call(s32[16]{0:T(128)S(1)} %reshape.25.places, s32[4]{0:T(128)S(1)} %add_add_fusion.1.offsets, bf16[1,512,1024]{2,1,0:T(8,128)(2,1)S(1)} %copy-done.1, bf16[1,512,1024]{2,1,0:T(8,128)(2,1)S(1)} %copy-done.2, ...), custom_call_target="tpu_custom_call" | custom-call | tf_op jit(solution)/shard_map/gather/pallas_call | solution.py:251
  31.5 1.0 copy-done.3
  34.9 3.3 %prepare.1 = (f32[2,256,256]{2,1,0:T(8,128)S(1)}, f32[4,256,256]{2,1,0:T(8,128)S(1)}, f32[4,2,256,256]{3,2,1,0:T(8,128)S(1)}) custom-call(s32[8]{0:T(128)S(1)} %reshape.26.places, bf16[256,256]{1,0:T(8,128)(2,1)S(1)} %copy-done.12, bf16[4,2,256,256]{3,2,1,0:T(8,128)(2,1)S(1)} %copy-done.4, f32[2,256,256]{2,1,0:T(8,128)S(1)} %copy-done.9, ...), custom_call_target="tpu_custom_call" | custom-call | tf_op jit(solution)/shard_map/prepare/pallas_call | solution.py:102
  38.2 18.0 %chain.1 = (bf16[4,2,256,256]{3,2,1,0:T(8,128)(2,1)S(1)}, bf16[4,2,256,256]{3,2,1,0:T(8,128)(2,1)}, f32[2,128,256]{2,1,0:T(8,128)S(1)}, f32[2,128,256]{2,1,0:T(8,128)S(1)}) custom-call(s32[8]{0:T(128)S(1)} %reshape.26.places, s32[4]{0:T(128)S(1)} %fusion.live, s32[1]{0:T(128)} %bitcast.3.here, bf16[4,2,256,256]{3,2,1,0:T(8,128)(2,1)S(1)} %copy-done.8, ...), custom_call_target="tpu_custom_call" | custom-call | tf_op jit(solution)/shard_map/chain/pallas_call | solution.py:415
  56.2 1.0 copy-done.6
  57.7 2.5 %collective-permute-done.7 = f32[2,128,256]{2,1,0:T(8,128)S(1)} collective-permute-done((f32[2,128,256]{2,1,0:T(8,128)S(1)}, f32[2,128,256]{2,1,0:T(8,128)S(1)}, u32[]{:S(2)}, u32[]{:S(2)}) %collective-permute-start.7) | collective-permute-done | bytes 262176 | tf_op jit(solution)/shard_map/ppermute | solution.py:700
  60.3 3.3 %collective-permute-start.10 = (bf16[2,128,256]{2,1,0:T(8,128)(2,1)S(1)}, bf16[2,128,256]{2,1,0:T(8,128)(2,1)}, u32[]{:S(2)}, u32[]{:S(2)}) collective-permute-start(bf16[2,128,256]{2,1,0:T(8,128)(2,1)S(1)} %add_convert_fusion.2), channel_id=1, source_target_pairs={{0,9},{1,8},{2,11},{3,10},{4,13},{5,12},{6,15},{7,14},{8,1},{9,0},... | collective-permute-start | bytes 393224 | tf_op jit(solution)/shard_map/ppermute | solution.py:714
  64.4 1.2 %copy-done.7 = bf16[4,2,256,256]{3,2,1,0:T(8,128)(2,1)S(1)} copy-done((bf16[4,2,256,256]{3,2,1,0:T(8,128)(2,1)S(1)}, bf16[4,2,256,256]{3,2,1,0:T(8,128)(2,1)}, u32[]{:S(2)}) %copy-start.7) | copy-done | bytes 1048600
  65.6 4.3 %scatter.1 = (f32[2,512,1024]{2,1,0:T(8,128)}, bf16[2,128,1024]{2,1,0:T(8,128)(2,1)}, bf16[2,512,128]{2,1,0:T(8,128)(2,1)S(1)}, bf16[2,512,128]{2,1,0:T(8,128)(2,1)S(1)}, bf16[2,2,128,128]{3,2,1,0:T(8,128)(2,1)S(1)}) custom-call(s32[16]{0:T(128)S(1)} %reshape.25.places, s32[8]{0:T(128)S(1)} %reshape.27.live, s32[4]{0:T(128)S(1)} %add_add_fusion.1.offsets, ...), custom_call_target="tpu_custom_call" | custom-call | bytes 8388608 | tf_op jit(solution)/shard_map/scatter/pallas_call | solution.py:509
  70.5 1.6 %collective-permute-start.14 = (bf16[2,2,128,128]{3,2,1,0:T(8,128)(2,1)S(1)}, bf16[2,2,128,128]{3,2,1,0:T(8,128)(2,1)S(1)}, u32[]{:S(2)}, u32[]{:S(2)}) collective-permute-start(bf16[2,2,128,128]{3,2,1,0:T(8,128)(2,1)S(1)} %get-tuple-element.55), channel_id=1, source_target_pairs={{0,8},{1,9},{2,10},{3,11},{4,12},{5,13},{6,14},{7,15},{8,0},{9,1},... | collective-permute-start | bytes 393224 | tf_op jit(solution)/shard_map/ppermute | solution.py:719
  72.5 1.1 %add_convert_fusion.1 = bf16[2,128,256]{2,1,0:T(8,128)(2,1)S(1)} fusion(bf16[2,128,256]{2,1,0:T(8,128)(2,1)} %collective-permute-done.10, bf16[2,128,256]{2,1,0:T(8,128)(2,1)} %collective-permute-done.9, bf16[2,128,256]{2,1,0:T(8,128)(2,1)} %collective-permute-done.8, bf16[2,128,256]{2,1,0:T(8,128)(2,1)S(1)} %add_convert_fusion.2), kind=kLoop, calls=%fused_computation.2 | loop fusion | flops 524288 | bytes 655360 | tf_op jit(solution)/shard_map/convert_element_type | solution.py:725
  73.6 2.4 %collective-permute-start.11 = (bf16[2,128,256]{2,1,0:T(8,128)(2,1)S(1)}, bf16[2,128,256]{2,1,0:T(8,128)(2,1)S(1)}, u32[]{:S(2)}, u32[]{:S(2)}) collective-permute-start(bf16[2,128,256]{2,1,0:T(8,128)(2,1)S(1)} %add_convert_fusion.1), channel_id=1, source_target_pairs={{0,2},{1,3},{2,0},{3,1},{4,6},{5,7},{6,4},{7,5},{8,10},{9,11},{10,... | collective-permute-start | bytes 393224 | tf_op jit(solution)/shard_map/ppermute | solution.py:714
  76.9 1.4 %corners.1 = (bf16[2,512,128]{2,1,0:T(8,128)(2,1)}, bf16[2,512,128]{2,1,0:T(8,128)(2,1)}) custom-call(s32[4]{0:T(128)S(1)} %copy-done.17, bf16[2,2,128,128]{3,2,1,0:T(8,128)(2,1)S(1)} %collective-permute-done.14.refs_0_, bf16[2,512,128]{2,1,0:T(8,128)(2,1)S(1)} %get-tuple-element.56.refs_1_, bf16[2,512,128]{2,1,0:T(8,128)(2,1)S(1)} %get-tuple-element.57.refs_2_), custom_call_target="tpu_custom_call" | custom-call | tf_op jit(solution)/shard_map/corners/pallas_call | solution.py:544
  78.2 1.4 %collective-permute-start.15 = (bf16[2,512,128]{2,1,0:T(8,128)(2,1)}, bf16[2,512,128]{2,1,0:T(8,128)(2,1)S(1)}, u32[]{:S(2)}, u32[]{:S(2)}) collective-permute-start(bf16[2,512,128]{2,1,0:T(8,128)(2,1)} %get-tuple-element.58), channel_id=1, source_target_pairs={{0,1},{1,0},{2,3},{3,2},{4,5},{5,4},{6,7},{7,6},{8,9},{9,8},{10,11... | collective-permute-start | bytes 786440 | tf_op jit(solution)/shard_map/ppermute | solution.py:721
  80.4 5.1 %collective-permute-start.12 = (bf16[2,128,256]{2,1,0:T(8,128)(2,1)S(1)}, bf16[2,128,256]{2,1,0:T(8,128)(2,1)S(1)}, u32[]{:S(2)}, u32[]{:S(2)}) collective-permute-start(bf16[2,128,256]{2,1,0:T(8,128)(2,1)S(1)} %add_convert_fusion.part), channel_id=1, source_target_pairs={{0,4},{1,5},{2,6},{3,7},{4,0},{5,1},{6,2},{7,3},{8,12},{9,13},{10,... | collective-permute-start | bytes 393224 | tf_op jit(solution)/shard_map/ppermute | solution.py:714
  85.5 9.9 %collective-permute-done.12.other = bf16[2,128,256]{2,1,0:T(8,128)(2,1)S(1)} collective-permute-done((bf16[2,128,256]{2,1,0:T(8,128)(2,1)S(1)}, bf16[2,128,256]{2,1,0:T(8,128)(2,1)S(1)}, u32[]{:S(2)}, u32[]{:S(2)}) %collective-permute-start.12) | collective-permute-done | bytes 131104 | tf_op jit(solution)/shard_map/ppermute | solution.py:714
  95.3 3.9 %borders.1 = (f32[2,512,1024]{2,1,0:T(8,128)}, f32[2,128,256]{2,1,0:T(8,128)}) custom-call(s32[4]{0:T(128)S(1)} %constant_dynamic-update-slice_fusion.offsets, f32[2,512,1024]{2,1,0:T(8,128)} %get-tuple-element.44.tile_in, bf16[2,128,256]{2,1,0:T(8,128)(2,1)S(1)} %add_convert_fusion.part, ...), custom_call_target="tpu_custom_call", output_to_operand_aliasing={{0}: (1, {})} | custom-call | flops 1048576 | bytes 8388608 | tf_op jit(solution)/shard_map/borders/pallas_call | solution.py:600
  (71 shorter events, 12.5 us)
Async XLA Ops:
  0.6 34.0 %copy-start = (f32[1,1,4,2,256,256]{5,4,3,2,1,0:T(8,128)S(1)}, f32[1,1,4,2,256,256]{5,4,3,2,1,0:T(8,128)}, u32[]{:S(2)}) copy-start(f32[1,1,4,2,256,256]{5,4,3,2,1,0:T(8,128)} %param.15) | copy-start | bytes 6291460
  0.6 23.6 %copy-start.1 = (bf16[1,512,1024]{2,1,0:T(8,128)(2,1)S(1)}, bf16[1,512,1024]{2,1,0:T(8,128)(2,1)}, u32[]{:S(2)}) copy-start(bf16[1,512,1024]{2,1,0:T(8,128)(2,1)} %tile_re.3) | copy-start | bytes 3145732
  0.7 14.0 %copy-start.18 = (s32[1,1,4,2,2]{2,4,3,1,0:T(2,128)S(1)}, s32[1,1,4,2,2]{2,4,3,1,0:T(2,128)}, u32[]{:S(2)}) copy-start(s32[1,1,4,2,2]{2,4,3,1,0:T(2,128)} %param.13) | copy-start | bytes 196
  4.5 19.7 %collective-permute-start = (bf16[2,128,1024]{2,1,0:T(8,128)(2,1)}, bf16[2,128,1024]{2,1,0:T(8,128)(2,1)}, u32[]{:S(2)}, u32[]{:S(2)}) collective-permute-start(bf16[2,128,1024]{2,1,0:T(8,128)(2,1)} %get-tuple-element.32), channel_id=1, source_target_pairs={{0,8},{1,9},{2,10},{3,11},{4,12},{5,13},{6,14},{7,15},{8,0},{9,1},... | collective-permute-start | bytes 1572872 | tf_op jit(solution)/shard_map/ppermute | solution.py:691
  7.8 15.8 %collective-permute-start.1 = (bf16[2,512,128]{2,1,0:T(8,128)(2,1)}, bf16[2,512,128]{2,1,0:T(8,128)(2,1)S(1)}, u32[]{:S(2)}, u32[]{:S(2)}) collective-permute-start(bf16[2,512,128]{2,1,0:T(8,128)(2,1)} %get-tuple-element.33), channel_id=1, source_target_pairs={{0,1},{1,0},{2,3},{3,2},{4,5},{5,4},{6,7},{7,6},{8,9},{9,8},{10,11... | collective-permute-start | bytes 786440 | tf_op jit(solution)/shard_map/ppermute | solution.py:691
  9.3 14.9 %collective-permute-start.2 = (bf16[2,512,128]{2,1,0:T(8,128)(2,1)}, bf16[2,512,128]{2,1,0:T(8,128)(2,1)}, u32[]{:S(2)}, u32[]{:S(2)}) collective-permute-start(bf16[2,512,128]{2,1,0:T(8,128)(2,1)} %get-tuple-element.34), channel_id=1, source_target_pairs={{1,2},{2,1},{3,4},{4,3},{5,6},{6,5},{9,10},{10,9},{11,12},{12,11},... | collective-permute-start | bytes 786440 | tf_op jit(solution)/shard_map/ppermute | solution.py:691
  10.6 11.6 %collective-permute-start.3 = (bf16[2,128,128]{2,1,0:T(8,128)(2,1)}, bf16[2,128,128]{2,1,0:T(8,128)(2,1)S(1)}, u32[]{:S(2)}, u32[]{:S(2)}) collective-permute-start(bf16[2,128,128]{2,1,0:T(8,128)(2,1)} %get-tuple-element.35), channel_id=1, source_target_pairs={{0,9},{1,8},{2,11},{3,10},{4,13},{5,12},{6,15},{7,14},{8,1},{9,0},... | collective-permute-start | bytes 196616 | tf_op jit(solution)/shard_map/ppermute | solution.py:691
  14.0 8.9 %collective-permute-start.4 = (bf16[2,128,128]{2,1,0:T(8,128)(2,1)}, bf16[2,128,128]{2,1,0:T(8,128)(2,1)S(1)}, u32[]{:S(2)}, u32[]{:S(2)}) collective-permute-start(bf16[2,128,128]{2,1,0:T(8,128)(2,1)} %get-tuple-element.36), channel_id=1, source_target_pairs={{1,10},{2,9},{3,12},{4,11},{5,14},{6,13},{9,2},{10,1},{11,4},{12,3... | collective-permute-start | bytes 196616 | tf_op jit(solution)/shard_map/ppermute | solution.py:691
  28.1 6.6 %copy-start.5 = (f32[256,256]{1,0:T(8,128)S(1)}, f32[256,256]{1,0:T(8,128)}, u32[]{:S(2)}) copy-start(f32[256,256]{1,0:T(8,128)} %param.12) | copy-start | bytes 786436
  28.1 6.6 %copy-start.12 = (bf16[256,256]{1,0:T(8,128)(2,1)S(1)}, bf16[256,256]{1,0:T(8,128)(2,1)}, u32[]{:S(2)}) copy-start(bf16[256,256]{1,0:T(8,128)(2,1)} %constant.69.clone.order_t) | copy-start | bytes 393220
  32.4 5.8 %collective-permute-start.5 = (bf16[4,2,256,256]{3,2,1,0:T(8,128)(2,1)}, bf16[4,2,256,256]{3,2,1,0:T(8,128)(2,1)}, u32[]{:S(2)}, u32[]{:S(2)}) collective-permute-start(bf16[4,2,256,256]{3,2,1,0:T(8,128)(2,1)} %get-tuple-element.39), channel_id=1, source_target_pairs={{0,16},{16,0},{1,17},{17,1},{2,18},{18,2},{3,19},{19,3},{4,20},{20... | collective-permute-start | bytes 3145736 | tf_op jit(solution)/shard_map/ppermute | solution.py:694
  34.9 3.3 %copy-start.8 = (bf16[4,2,256,256]{3,2,1,0:T(8,128)(2,1)S(1)}, bf16[4,2,256,256]{3,2,1,0:T(8,128)(2,1)}, u32[]{:S(2)}) copy-start(bf16[4,2,256,256]{3,2,1,0:T(8,128)(2,1)} %constant.70.clone.tables) | copy-start | bytes 3145732
  57.2 19.6 %copy-start.17 = (s32[4]{0:T(128)S(1)}, s32[4]{0:T(128)}, u32[]{:S(2)}) copy-start(s32[4]{0:T(128)} %add_add_fusion.offsets) | copy-start | bytes 52
  57.2 7.2 %collective-permute-start.6 = (bf16[4,2,256,256]{3,2,1,0:T(8,128)(2,1)}, bf16[4,2,256,256]{3,2,1,0:T(8,128)(2,1)S(1)}, u32[]{:S(2)}, u32[]{:S(2)}) collective-permute-start(bf16[4,2,256,256]{3,2,1,0:T(8,128)(2,1)} %get-tuple-element.43), channel_id=1, source_target_pairs={{0,16},{16,0},{1,17},{17,1},{2,18},{18,2},{3,19},{19,3},{4,20},{20... | collective-permute-start | bytes 3145736 | tf_op jit(solution)/shard_map/ppermute | solution.py:699
  57.7 2.5 %collective-permute-start.7 = (f32[2,128,256]{2,1,0:T(8,128)S(1)}, f32[2,128,256]{2,1,0:T(8,128)S(1)}, u32[]{:S(2)}, u32[]{:S(2)}) collective-permute-start(f32[2,128,256]{2,1,0:T(8,128)S(1)} %get-tuple-element.46), channel_id=1, source_target_pairs={{0,16},{16,0},{1,17},{17,1},{2,18},{18,2},{3,19},{19,3},{4,20},{20... | collective-permute-start | bytes 786440 | tf_op jit(solution)/shard_map/ppermute | solution.py:700
  60.3 9.7 %collective-permute-start.10 = (bf16[2,128,256]{2,1,0:T(8,128)(2,1)S(1)}, bf16[2,128,256]{2,1,0:T(8,128)(2,1)}, u32[]{:S(2)}, u32[]{:S(2)}) collective-permute-start(bf16[2,128,256]{2,1,0:T(8,128)(2,1)S(1)} %add_convert_fusion.2), channel_id=1, source_target_pairs={{0,9},{1,8},{2,11},{3,10},{4,13},{5,12},{6,15},{7,14},{8,1},{9,0},... | collective-permute-start | bytes 393224 | tf_op jit(solution)/shard_map/ppermute | solution.py:714
  63.6 6.7 %collective-permute-start.9 = (bf16[2,128,256]{2,1,0:T(8,128)(2,1)S(1)}, bf16[2,128,256]{2,1,0:T(8,128)(2,1)}, u32[]{:S(2)}, u32[]{:S(2)}) collective-permute-start(bf16[2,128,256]{2,1,0:T(8,128)(2,1)S(1)} %add_convert_fusion.2), channel_id=1, source_target_pairs={{0,1},{1,0},{2,3},{3,2},{4,5},{5,4},{6,7},{7,6},{8,9},{9,8},{10,11... | collective-permute-start | bytes 393224 | tf_op jit(solution)/shard_map/ppermute | solution.py:714
  63.6 6.9 %collective-permute-start.8 = (bf16[2,128,256]{2,1,0:T(8,128)(2,1)S(1)}, bf16[2,128,256]{2,1,0:T(8,128)(2,1)}, u32[]{:S(2)}, u32[]{:S(2)}) collective-permute-start(bf16[2,128,256]{2,1,0:T(8,128)(2,1)S(1)} %add_convert_fusion.2), channel_id=1, source_target_pairs={{0,8},{1,9},{2,10},{3,11},{4,12},{5,13},{6,14},{7,15},{8,0},{9,1},... | collective-permute-start | bytes 393224 | tf_op jit(solution)/shard_map/ppermute | solution.py:714
  70.5 6.4 %collective-permute-start.14 = (bf16[2,2,128,128]{3,2,1,0:T(8,128)(2,1)S(1)}, bf16[2,2,128,128]{3,2,1,0:T(8,128)(2,1)S(1)}, u32[]{:S(2)}, u32[]{:S(2)}) collective-permute-start(bf16[2,2,128,128]{3,2,1,0:T(8,128)(2,1)S(1)} %get-tuple-element.55), channel_id=1, source_target_pairs={{0,8},{1,9},{2,10},{3,11},{4,12},{5,13},{6,14},{7,15},{8,0},{9,1},... | collective-permute-start | bytes 393224 | tf_op jit(solution)/shard_map/ppermute | solution.py:719
  72.1 23.3 %collective-permute-start.13 = (bf16[2,128,1024]{2,1,0:T(8,128)(2,1)}, bf16[2,128,1024]{2,1,0:T(8,128)(2,1)S(1)}, u32[]{:S(2)}, u32[]{:S(2)}) collective-permute-start(bf16[2,128,1024]{2,1,0:T(8,128)(2,1)} %get-tuple-element.54), channel_id=1, source_target_pairs={{0,8},{1,9},{2,10},{3,11},{4,12},{5,13},{6,14},{7,15},{8,0},{9,1},... | collective-permute-start | bytes 1572872 | tf_op jit(solution)/shard_map/ppermute | solution.py:721
  73.6 6.7 %collective-permute-start.11 = (bf16[2,128,256]{2,1,0:T(8,128)(2,1)S(1)}, bf16[2,128,256]{2,1,0:T(8,128)(2,1)S(1)}, u32[]{:S(2)}, u32[]{:S(2)}) collective-permute-start(bf16[2,128,256]{2,1,0:T(8,128)(2,1)S(1)} %add_convert_fusion.1), channel_id=1, source_target_pairs={{0,2},{1,3},{2,0},{3,1},{4,6},{5,7},{6,4},{7,5},{8,10},{9,11},{10,... | collective-permute-start | bytes 393224 | tf_op jit(solution)/shard_map/ppermute | solution.py:714
  78.2 17.1 %collective-permute-start.15 = (bf16[2,512,128]{2,1,0:T(8,128)(2,1)}, bf16[2,512,128]{2,1,0:T(8,128)(2,1)S(1)}, u32[]{:S(2)}, u32[]{:S(2)}) collective-permute-start(bf16[2,512,128]{2,1,0:T(8,128)(2,1)} %get-tuple-element.58), channel_id=1, source_target_pairs={{0,1},{1,0},{2,3},{3,2},{4,5},{5,4},{6,7},{7,6},{8,9},{9,8},{10,11... | collective-permute-start | bytes 786440 | tf_op jit(solution)/shard_map/ppermute | solution.py:721
  79.6 15.7 %collective-permute-start.16 = (bf16[2,512,128]{2,1,0:T(8,128)(2,1)}, bf16[2,512,128]{2,1,0:T(8,128)(2,1)S(1)}, u32[]{:S(2)}, u32[]{:S(2)}) collective-permute-start(bf16[2,512,128]{2,1,0:T(8,128)(2,1)} %get-tuple-element.59), channel_id=1, source_target_pairs={{1,2},{2,1},{3,4},{4,3},{5,6},{6,5},{9,10},{10,9},{11,12},{12,11},... | collective-permute-start | bytes 786440 | tf_op jit(solution)/shard_map/ppermute | solution.py:721
  80.4 15.0 %collective-permute-start.12 = (bf16[2,128,256]{2,1,0:T(8,128)(2,1)S(1)}, bf16[2,128,256]{2,1,0:T(8,128)(2,1)S(1)}, u32[]{:S(2)}, u32[]{:S(2)}) collective-permute-start(bf16[2,128,256]{2,1,0:T(8,128)(2,1)S(1)} %add_convert_fusion.part), channel_id=1, source_target_pairs={{0,4},{1,5},{2,6},{3,7},{4,0},{5,1},{6,2},{7,3},{8,12},{9,13},{10,... | collective-permute-start | bytes 393224 | tf_op jit(solution)/shard_map/ppermute | solution.py:714
  (12 other events, 12.3 us)

commit v6 on v5

--- a/solution.py
+++ b/solution.py
@@ -61,7 +61,7 @@
     return jnp.concatenate(parts, axis=1)
 
 
-def prep_kernel(places, order_t, after, probe, *refs):
+def prep_kernel(places, offsets, order_t, after, probe, *refs):
     step = pl.program_id(0)
     size = probe.shape[-1]
     half = size // 2
@@ -70,7 +70,7 @@
     kern, sorted_frames, waves = refs[2 * blocks :]
 
     def halved(parts, at):
-        ids = [(at, pl.ds(start, half, stride=2), slice(None)) for start in range(2)]
+        ids = [at + (pl.ds(start, half, stride=2), slice(None)) for start in range(2)]
         return rows_of(*(cols_of(*(part[i] for part in parts)) for i in ids))
 
     def in_order(rows):
@@ -83,38 +83,48 @@
 
     @pl.when(step == 0)
     def _():
-        angles = in_order(halved(phases, 0))
+        angles = in_order(halved(phases, ()))
         kern[0] = jnp.cos(angles)
         kern[1] = jnp.sin(angles)
 
-    sorted_frames[0] = in_order(halved(frames, 0))
-    down = places[2 * step] % ROWS
-    across = places[2 * step + 1] % LANES
+    sorted_frames[0] = in_order(halved(frames, (0, 0)))
+    at = 2 * step + offsets[offsets.shape[0] - 1]
+    down = places[2 * at] % ROWS
+    across = places[2 * at + 1] % LANES
     for plane in range(2):
         moved = pltpu.roll(probe[plane], across, axis=1)
         waves[0, plane] = pltpu.roll(moved, down, axis=0)
 
 
-def prepare(places, after, probe, phases, frames):
-    count, size = frames.shape[0], phases.shape[-1]
+def prepare(places, offsets, after, probe, phases, frames):
+    count, sections, size = frames.shape[:3]
     blocks = size // LANES
-    full = lambda *shape: pl.BlockSpec(shape, lambda i: (0,) * len(shape))
+    last = offsets.shape[0] - 1
+    full = lambda *shape: pl.BlockSpec(shape, lambda i, p, o: (0,) * len(shape))
     return pl.pallas_call(
         prep_kernel,
-        grid=(count,),
-        in_specs=[
-            SMEM,
-            full(size, size),
-            ANY,
-            full(2, size, size),
-            *(pl.BlockSpec((1, size, LANES), lambda i, b=b: (0, 0, b)) for b in range(blocks)),
-            *(pl.BlockSpec((1, size, LANES), lambda i, b=b: (i, 0, b)) for b in range(blocks)),
-        ],
-        out_specs=[
-            full(2, size, size),
-            pl.BlockSpec((1, size, size), lambda i: (i, 0, 0)),
-            pl.BlockSpec((1, 2, size, size), lambda i: (i, 0, 0, 0)),
-        ],
+        grid_spec=pltpu.PrefetchScalarGridSpec(
+            num_scalar_prefetch=2,
+            grid=(count,),
+            in_specs=[
+                full(size, size),
+                ANY,
+                full(2, size, size),
+                *(
+                    pl.BlockSpec((size, LANES), lambda i, p, o, b=b: (0, b))
+                    for b in range(blocks)
+                ),
+                *(
+                    pl.BlockSpec((1, 1, size, LANES), lambda i, p, o, b=b: (i, o[last], 0, b))
+                    for b in range(blocks)
+                ),
+            ],
+            out_specs=[
+                full(2, size, size),
+                pl.BlockSpec((1, size, size), lambda i, p, o: (i, 0, 0)),
+                pl.BlockSpec((1, 2, size, size), lambda i, p, o: (i, 0, 0, 0)),
+            ],
+        ),
         out_shape=[
             jax.ShapeDtypeStruct((2, size, size), f32),
             jax.ShapeDtypeStruct((count, size, size), f32),
@@ -125,10 +135,11 @@
         name="prepare",
     )(
         places,
+        offsets,
         jnp.asarray(sorting_table(size)),
         after,
         probe,
-        *[phases[None]] * blocks,
+        *[phases] * blocks,
         *[frames] * blocks,
     )
 
@@ -167,14 +178,13 @@
 
 
 def pack(offsets, tile_re, tile_im, edges, names, half):
-    vmem = pl.BlockSpec(memory_space=pltpu.VMEM)
     return pl.pallas_call(
         functools.partial(pack_kernel, edges, names, half),
         in_specs=[SMEM, HBM, HBM],
-        out_specs=[vmem] * len(edges),
+        out_specs=[ANY] * len(edges),
         out_shape=strip_shapes(edges, *tile_re.shape[1:], half),
         scratch_shapes=[pltpu.SemaphoreType.DMA((2 * len(edges),))],
-        compiler_params=pltpu.CompilerParams(vmem_limit_bytes=56 * MIB),
+        compiler_params=pltpu.CompilerParams(vmem_limit_bytes=4 * MIB),
         name="pack",
     )(offsets, tile_re, tile_im)
 
@@ -183,6 +193,11 @@
     row, col = places[2 * at], places[2 * at + 1]
     down, across = row % ROWS, col % LANES
     return down, across, pl.multiple_of(row - down, ROWS), pl.multiple_of(col - across, LANES)
+
+
+def is_live(occupied, places, at):
+    slots = places.shape[0] // 2 // occupied.shape[0]
+    return at % slots < occupied[at // slots]
 
 
 def gather_kernel(spots, edges, names, half, places, offsets, tile_re, tile_im, *rest):
@@ -263,14 +278,14 @@
 
 
 def chain_kernel(
-    group, places, live, here, tables, kern, mine, theirs, frames, waves,
+    group, places, occupied, offsets, tables, kern, mine, theirs, frames, waves,
     keep, send, pulled_keep, pulled_send, windows, middle, terms, pulled, sems,
 ):
     step = pl.program_id(0)
     steps = pl.num_programs(0)
     size = kern.shape[-1]
     half = size // 2
-    me = here[0]
+    me = offsets[offsets.shape[0] - 1]
 
     def fetch(at, which):
         source, slot = ((mine, me), (theirs, 1 - me))[which]
@@ -387,10 +402,10 @@
     for at, chi in enumerate(propagate(pulls, -1.0)):
         chi = rounded(chi[0]), rounded(chi[1])
         terms[0, at, 0], terms[0, at, 1] = conj_product(wave(at), chi)
-        spot_at = step * group + at
+        spot_at = 2 * (step * group + at) + me
         up = (size - places[2 * spot_at] % ROWS) % size
         back_by = (size - places[2 * spot_at + 1] % LANES) % size
-        weight = live[spot_at].astype(f32)
+        weight = is_live(occupied, places, spot_at).astype(f32)
         for plane, value in enumerate(conj_product(window(0, at), chi)):
             value = pltpu.roll(pltpu.roll(value * weight, back_by, axis=1), up, axis=0)
             pulled[plane] += value
@@ -408,8 +423,8 @@
             ]
 
 
-def chain(places, live, here, kern, mine, theirs, frames, waves, group):
-    count, size = frames.shape[0], frames.shape[-1]
+def chain(places, occupied, offsets, kern, mine, theirs, frames, waves, group):
+    count, size = waves.shape[0], waves.shape[-1]
     full = lambda *shape: pl.BlockSpec(shape, lambda i: (0,) * len(shape))
     block = pl.BlockSpec((group, 2, size, size), lambda i: (i, 0, 0, 0))
     return pl.pallas_call(
@@ -442,10 +457,10 @@
         ],
         compiler_params=pltpu.CompilerParams(vmem_limit_bytes=40 * MIB),
         name="chain",
-    )(places, live, here, jnp.asarray(dft_tables(size)), kern, mine, theirs, frames, waves)
-
-
-def scatter_kernel(edges, names, half, places, live, offsets, kept, arrived, tile, *rest):
+    )(places, occupied, offsets, jnp.asarray(dft_tables(size)), kern, mine, theirs, frames, waves)
+
+
+def scatter_kernel(edges, names, half, places, occupied, offsets, kept, arrived, tile, *rest):
     strips, (total, sems) = rest[:-2], rest[-2:]
     count, size = kept.shape[0], kept.shape[-1]
     tile_rows, tile_cols = tile.shape[1:]
@@ -460,7 +475,7 @@
         down, across, top, left = spot(places, at)
         wide = pl.ds(left, size + LANES)
 
-        @pl.when(live[at] > 0)
+        @pl.when(is_live(occupied, places, at))
         def _():
             for plane in range(2):
                 value = source[place, plane].astype(f32)
@@ -501,7 +516,7 @@
     return [(key, acrosses) for key in names if key[0] == "row" and acrosses]
 
 
-def scatter(places, live, offsets, kept, arrived, edges, names, tile_rows, tile_cols):
+def scatter(places, occupied, offsets, kept, arrived, edges, names, tile_rows, tile_cols):
     count, _, size, _ = kept.shape
     half = size // 2
     corners = corner_keys(names)
@@ -522,7 +537,7 @@
             flops=0, bytes_accessed=16 * tile_rows * tile_cols, transcendentals=0
         ),
         name="scatter",
-    )(places, live, offsets, kept, arrived)
+    )(places, occupied, offsets, kept, arrived)
 
 
 def corner_kernel(names, half, offsets, *refs):
@@ -652,16 +667,8 @@
     count = spots // sections
 
     places = centres.reshape(2 * spots)
-    slot_ids = jnp.arange(slots, dtype=jnp.int32)
-    live = (slot_ids[None, :] < occupied[0, 0][:, None]).astype(jnp.int32)
-    my_places = lax.dynamic_index_in_dim(
-        centres.reshape(count, sections, 2), here, 1, False
-    ).reshape(2 * count)
-    my_live = lax.dynamic_index_in_dim(live.reshape(count, sections), here, 1, False)
-    live = live.reshape(spots)
-    frames = lax.dynamic_index_in_dim(
-        measured.reshape(count, sections, size, size), here, 1, False
-    )
+    live_counts = occupied.reshape(batches)
+    frames = measured.reshape(count, sections, size, size)
 
     names, tile_at, padded_at = [], [], []
     for axis, extent, own, length in (
@@ -692,16 +699,17 @@
     mine, other = gather(places, padded_at, object_re, object_im, edges, names, strips, size)
     across_depth = [(i, 1 - i) for i in range(sections)]
     theirs = lax.ppermute(other, "depth", across_depth)
-    kern, sorted_frames, waves = prepare(my_places, mine, probe, phases, frames)
+    kern, sorted_frames, waves = prepare(places, padded_at, mine, probe, phases, frames)
     keep, send, pulled_keep, pulled_send = chain(
-        my_places, my_live, here.reshape(1), kern, mine, theirs, sorted_frames, waves, count
+        places, live_counts, padded_at, kern, mine, theirs, sorted_frames, waves, count
     )
     arrived = lax.ppermute(send, "depth", across_depth)
     pulled = pulled_keep + lax.ppermute(pulled_send, "depth", across_depth)
 
     tile, *own = scatter(
-        places, live, padded_at, keep, arrived, outer, names, tile_rows, tile_cols
+        places, live_counts, padded_at, keep, arrived, outer, names, tile_rows, tile_cols
     )
+    own, corners = own[: len(outer)], own[len(outer) :]
 
     bits = rows.bit_length() + cols.bit_length() - 2
     assert rows * cols == 1 << bits
@@ -713,22 +721,22 @@
     def fetch(block, flip):
         return lax.ppermute(block, both, [(i, i ^ flip) for i in range(rows * cols)])
 
-    def sent(own):
-        own, corners = own[: len(outer)], own[len(outer) :]
-        if corners:
-            corners = [lax.ppermute(x, both, path) for x, path in zip(corners, paths)]
-            own[len(downs) :] = add_corners(tile_at, own[len(downs) :], corners, names, half)
-        return [lax.ppermute(strip, both, path) for strip, path in zip(own, paths)]
-
+    *own, pulled = lax.optimization_barrier((*own, pulled))
+    if corners:
+        corners = [lax.ppermute(x, both, path) for x, path in zip(corners, paths)]
     added = None
     for at, flips in enumerate(rounds):
         mine = pulled.astype(bf16)
         theirs = [fetch(mine, flip) for flip in flips]
         if len(flips) == 2:
             theirs.append(fetch(mine, flips[0] ^ flips[1]))
+        if at == 0 and corners:
+            theirs, corners = lax.optimization_barrier((theirs, corners))
+            own[len(downs) :] = add_corners(tile_at, own[len(downs) :], corners, names, half)
         if added is None and at >= len(rounds) - 3:
-            *theirs, own = lax.optimization_barrier((*theirs, own))
-            added = sent(own)
+            if at:
+                theirs, own = lax.optimization_barrier((theirs, own))
+            added = [lax.ppermute(strip, both, path) for strip, path in zip(own, paths)]
         if at < len(rounds) - 1:
             sums = [part.astype(f32) for part in (mine, *theirs)]
             pulled = sums[0] + sums[1]
@@ -739,7 +747,10 @@
         first_row = jnp.where(row_at == 0, 0, half)
     else:
         first_row = jnp.int32(half if downs else 0)
-    gradient, probe_share = add_borders(lax.dynamic_update_index_in_dim(tile_at, first_row.astype(jnp.int32), bulk, 0), tile, (mine, theirs), outer, names, added, half)
+    fold_at = numbers(*(tile_at[k] for k in range(bulk)), first_row)
+    gradient, probe_share = add_borders(
+        fold_at, tile, (mine, theirs), outer, names, added, half
+    )
     return (gradient[:, None], probe_share)
 
 

time: 100 us -> 93.9 us (0.939)
  waiting for transfers between devices: 21.1 us -> 29.5 us
  Pallas kernels: 37.4 us -> 30.6 us
  starting transfers between devices: 26.1 us -> 23.1 us
  local copies, waits for them, and re-layouts: 11.1 us -> 8.79 us
  other arithmetic: 2.56 us -> 0.37 us
    ppermute x4, waiting for transfers between devices: 0.91 us -> 7.84 us  [the longest x3 5.39 us: shards(): added = [lax.ppermute(strip, both, path) for strip, path in zip(own, paths)]]
    ppermute x5, starting transfers between devices: 11.4 us -> 8.98 us  [fetch(): lax.ppermute(block, both, [(i, i ^ flip) for i in range(rows * cols)])]
    pallas_call x1, Pallas kernels: 18 us -> 15.9 us  [chain(): pl.pallas_call(functools.partial(chain_kernel, group), grid=(count // gro...]
    pallas_call x1, Pallas kernels: 3.36 us -> 1.51 us  [gather(): pl.pallas_call(functools.partial(gather_kernel, spots, edges, names, half...]
    pallas_call x1, Pallas kernels: 3.18 us -> 1.52 us  [pack(): pl.pallas_call(functools.partial(pack_kernel, edges, names, half), in_spe...]
    dynamic_slice x2 -> x0, local copies, waits for them, and re-layouts: 1.33 us -> none  [shards(): lax.dynamic_index_in_dim(centres.reshape(count, sections, 2), here, 1, Fa...]
    ppermute x5, waiting for transfers between devices: 10.4 us -> 11.7 us  [fetch(): lax.ppermute(block, both, [(i, i ^ flip) for i in range(rows * cols)])]
    convert_element_type x3 -> x2, other arithmetic: 1.17 us -> 0.1 us  [shards(): mine = pulled.astype(bf16)]
  transfers between devices with their start and end apart: 17 -> 17, of which waited for: 6 -> 10; matrix products, arithmetic and copies ran while one was open for 4% -> 1% of each run, Pallas kernels for 9% -> 4%
where the time goes in v6:
time: 93.9 us; the launch traced here: 93.4 us
  Pallas kernels  30.6 us (33%)
  waiting for transfers between devices  29.5 us (31%)
  starting transfers between devices  23.1 us (25%)
  local copies, waits for them, and re-layouts  8.79 us (9%)
  between operations  1.03 us (1%)
    pallas_call x1, Pallas kernels, chain(): pl.pallas_call(functools.partial(chain_kernel, group), grid=(count // gro...  15.9 us
    ppermute x5, waiting for transfers between devices, fetch(): lax.ppermute(block, both, [(i, i ^ flip) for i in range(rows * cols)])  11.7 us
    ppermute x5, starting transfers between devices, shards(): lax.ppermute(strip, both, path)  10.1 us
    ppermute x5, starting transfers between devices, fetch(): lax.ppermute(block, both, [(i, i ^ flip) for i in range(rows * cols)])  8.98 us
    unnamed x21, local copies, waits for them, and re-layouts  8.7 us
    ppermute x5, waiting for transfers between devices, shards(): lax.ppermute(strip, both, path)  7.43 us
    ppermute x3, waiting for transfers between devices, shards(): added = [lax.ppermute(strip, both, path) for strip, path in zip(own, paths)]  5.39 us
    pallas_call x1, Pallas kernels, add_borders(): pl.pallas_call(functools.partial(border_kernel, edges, names, half), in_s...  3.91 us
  transfers between devices with their start and end apart: 17, of which 10 were waited for; matrix products, arithmetic and copies ran while one was open for 1% of the time, Pallas kernels for 4%

profile of v6, /device:TPU:0, one launch (start us, length us, event | category | flops | bytes accessed | tf_op | source)
XLA Modules:
  0.0 93.4 jit_solution(17984515931837399353)
XLA Ops:
  0.8 1.4 %copy-done.1 = bf16[1,512,1024]{2,1,0:T(8,128)(2,1)S(1)} copy-done((bf16[1,512,1024]{2,1,0:T(8,128)(2,1)S(1)}, bf16[1,512,1024]{2,1,0:T(8,128)(2,1)}, u32[]{:S(2)}) %copy-start.1) | copy-done | bytes 1048600
  3.3 1.5 %pack.1 = (bf16[2,128,1024]{2,1,0:T(8,128)(2,1)}, bf16[2,512,128]{2,1,0:T(8,128)(2,1)}, bf16[2,512,128]{2,1,0:T(8,128)(2,1)S(1)}, bf16[2,128,128]{2,1,0:T(8,128)(2,1)}, bf16[2,128,128]{2,1,0:T(8,128)(2,1)}) custom-call(s32[4]{0:T(128)S(1)} %get-tuple-element.68.offsets, bf16[1,512,1024]{2,1,0:T(8,128)(2,1)S(1)} %copy-done.1, bf16[1,512,1024]{2,1,0:T(8,128)(2,1)S(1)} %copy-done.3), custom_call_target="tpu_custom_call" | custom-call | tf_op jit(solution)/shard_map/pack/pallas_call | solution.py:181
  4.9 3.0 %collective-permute-start = (bf16[2,128,1024]{2,1,0:T(8,128)(2,1)}, bf16[2,128,1024]{2,1,0:T(8,128)(2,1)S(1)}, u32[]{:S(2)}, u32[]{:S(2)}) collective-permute-start(bf16[2,128,1024]{2,1,0:T(8,128)(2,1)} %get-tuple-element.33), channel_id=1, source_target_pairs={{0,8},{1,9},{2,10},{3,11},{4,12},{5,13},{6,14},{7,15},{8,0},{9,1},... | collective-permute-start | bytes 1572872 | tf_op jit(solution)/shard_map/ppermute | solution.py:698
  7.9 1.5 %collective-permute-start.1 = (bf16[2,512,128]{2,1,0:T(8,128)(2,1)}, bf16[2,512,128]{2,1,0:T(8,128)(2,1)S(1)}, u32[]{:S(2)}, u32[]{:S(2)}) collective-permute-start(bf16[2,512,128]{2,1,0:T(8,128)(2,1)} %get-tuple-element.34), channel_id=1, source_target_pairs={{0,1},{1,0},{2,3},{3,2},{4,5},{5,4},{6,7},{7,6},{8,9},{9,8},{10,11... | collective-permute-start | bytes 786440 | tf_op jit(solution)/shard_map/ppermute | solution.py:698
  10.1 4.3 %collective-permute-start.3 = (bf16[2,128,128]{2,1,0:T(8,128)(2,1)}, bf16[2,128,128]{2,1,0:T(8,128)(2,1)S(1)}, u32[]{:S(2)}, u32[]{:S(2)}) collective-permute-start(bf16[2,128,128]{2,1,0:T(8,128)(2,1)} %get-tuple-element.36), channel_id=1, source_target_pairs={{0,9},{1,8},{2,11},{3,10},{4,13},{5,12},{6,15},{7,14},{8,1},{9,0},... | collective-permute-start | bytes 196616 | tf_op jit(solution)/shard_map/ppermute | solution.py:698
  16.0 6.6 %collective-permute-done.3.rest_3_ = bf16[2,128,128]{2,1,0:T(8,128)(2,1)S(1)} collective-permute-done((bf16[2,128,128]{2,1,0:T(8,128)(2,1)}, bf16[2,128,128]{2,1,0:T(8,128)(2,1)S(1)}, u32[]{:S(2)}, u32[]{:S(2)}) %collective-permute-start.3) | collective-permute-done | bytes 65568 | tf_op jit(solution)/shard_map/ppermute | solution.py:698
  23.4 1.2 %copy-done.2 = bf16[1,512,1024]{2,1,0:T(8,128)(2,1)S(1)} copy-done((bf16[1,512,1024]{2,1,0:T(8,128)(2,1)S(1)}, bf16[1,512,1024]{2,1,0:T(8,128)(2,1)}, u32[]{:S(2)}) %copy-start.2) | copy-done | bytes 1048600
  24.6 1.2 %copy-done.4 = bf16[1,512,1024]{2,1,0:T(8,128)(2,1)S(1)} copy-done((bf16[1,512,1024]{2,1,0:T(8,128)(2,1)S(1)}, bf16[1,512,1024]{2,1,0:T(8,128)(2,1)}, u32[]{:S(2)}) %copy-start.4) | copy-done | bytes 1048600
  25.9 1.5 %gather.1 = (bf16[4,2,256,256]{3,2,1,0:T(8,128)(2,1)S(1)}, bf16[4,2,256,256]{3,2,1,0:T(8,128)(2,1)S(1)}) custom-call(s32[16]{0:T(128)S(1)} %reshape.13.places, s32[4]{0:T(128)S(1)} %add_add_fusion.offsets, bf16[1,512,1024]{2,1,0:T(8,128)(2,1)S(1)} %copy-done.2, bf16[1,512,1024]{2,1,0:T(8,128)(2,1)S(1)} %copy-done.4, ...), custom_call_target="tpu_custom_call" | custom-call | tf_op jit(solution)/shard_map/gather/pallas_call | solution.py:266
  30.4 3.4 %prepare.1 = (f32[2,256,256]{2,1,0:T(8,128)S(1)}, f32[4,256,256]{2,1,0:T(8,128)S(1)}, f32[4,2,256,256]{3,2,1,0:T(8,128)S(1)}) custom-call(s32[16]{0:T(128)S(1)} %reshape.13.places, s32[4]{0:T(128)S(1)} %add_add_fusion.offsets, bf16[256,256]{1,0:T(8,128)(2,1)S(1)} %copy-done.8, bf16[4,2,256,256]{3,2,1,0:T(8,128)(2,1)S(1)} %get-tuple-element.38.after.mine, ...), custom_call_target="tpu_custom_call" | custom-call | tf_op jit(solution)/shard_map/prepare/pallas_call | solution.py:104
  33.8 15.9 %chain.1 = (bf16[4,2,256,256]{3,2,1,0:T(8,128)(2,1)S(1)}, bf16[4,2,256,256]{3,2,1,0:T(8,128)(2,1)S(1)}, f32[2,128,256]{2,1,0:T(8,128)S(1)}, f32[2,128,256]{2,1,0:T(8,128)S(1)}) custom-call(s32[16]{0:T(128)S(1)} %reshape.13.places, s32[4]{0:T(128)S(1)} %bitcast.15, s32[4]{0:T(128)S(1)} %add_add_fusion.offsets, bf16[4,2,256,256]{3,2,1,0:T(8,128)(2,1)S(1)} %copy-done.5, ...), custom_call_target="tpu_custom_call" | custom-call | tf_op jit(solution)/shard_map/chain/pallas_call | solution.py:430
  50.4 2.6 %collective-permute-done.7 = f32[2,128,256]{2,1,0:T(8,128)S(1)} collective-permute-done((f32[2,128,256]{2,1,0:T(8,128)S(1)}, f32[2,128,256]{2,1,0:T(8,128)S(1)}, u32[]{:S(2)}, u32[]{:S(2)}) %collective-permute-start.7) | collective-permute-done | bytes 262176 | tf_op jit(solution)/shard_map/ppermute | solution.py:707
  53.0 3.7 %scatter.1 = (f32[2,512,1024]{2,1,0:T(8,128)}, bf16[2,128,1024]{2,1,0:T(8,128)(2,1)S(1)}, bf16[2,512,128]{2,1,0:T(8,128)(2,1)S(1)}, bf16[2,512,128]{2,1,0:T(8,128)(2,1)S(1)}, bf16[2,2,128,128]{3,2,1,0:T(8,128)(2,1)S(1)}) custom-call(s32[16]{0:T(128)S(1)} %reshape.13.places, s32[4]{0:T(128)S(1)} %bitcast.16, s32[4]{0:T(128)S(1)} %add_add_fusion.offsets, ...), custom_call_target="tpu_custom_call" | custom-call | bytes 8388608 | tf_op jit(solution)/shard_map/scatter/pallas_call | solution.py:524
  56.7 2.3 %collective-permute-start.9 = (bf16[2,128,256]{2,1,0:T(8,128)(2,1)S(1)}, bf16[2,128,256]{2,1,0:T(8,128)(2,1)S(1)}, u32[]{:S(2)}, u32[]{:S(2)}) collective-permute-start(bf16[2,128,256]{2,1,0:T(8,128)(2,1)S(1)} %add.25), channel_id=1, source_target_pairs={{0,1},{1,0},{2,3},{3,2},{4,5},{5,4},{6,7},{7,6},{8,9},{9,8},{10,11... | collective-permute-start | bytes 393224 | tf_op jit(solution)/shard_map/ppermute | solution.py:722
  61.1 1.9 %collective-permute-done.9 = bf16[2,128,256]{2,1,0:T(8,128)(2,1)S(1)} collective-permute-done((bf16[2,128,256]{2,1,0:T(8,128)(2,1)S(1)}, bf16[2,128,256]{2,1,0:T(8,128)(2,1)S(1)}, u32[]{:S(2)}, u32[]{:S(2)}) %collective-permute-start.9) | collective-permute-done | bytes 131104 | tf_op jit(solution)/shard_map/ppermute | solution.py:722
  63.0 2.3 %collective-permute-done.8 = bf16[2,128,256]{2,1,0:T(8,128)(2,1)S(1)} collective-permute-done((bf16[2,128,256]{2,1,0:T(8,128)(2,1)S(1)}, bf16[2,128,256]{2,1,0:T(8,128)(2,1)S(1)}, u32[]{:S(2)}, u32[]{:S(2)}) %collective-permute-start.8) | collective-permute-done | bytes 131104 | tf_op jit(solution)/shard_map/ppermute | solution.py:722
  65.4 2.3 %collective-permute-done.10 = bf16[2,128,256]{2,1,0:T(8,128)(2,1)S(1)} collective-permute-done((bf16[2,128,256]{2,1,0:T(8,128)(2,1)S(1)}, bf16[2,128,256]{2,1,0:T(8,128)(2,1)S(1)}, u32[]{:S(2)}, u32[]{:S(2)}) %collective-permute-start.10) | collective-permute-done | bytes 131104 | tf_op jit(solution)/shard_map/ppermute | solution.py:722
  67.7 2.5 %collective-permute-done.11.refs_0_ = bf16[2,2,128,128]{3,2,1,0:T(8,128)(2,1)S(1)} collective-permute-done((bf16[2,2,128,128]{3,2,1,0:T(8,128)(2,1)S(1)}, bf16[2,2,128,128]{3,2,1,0:T(8,128)(2,1)S(1)}, u32[]{:S(2)}, u32[]{:S(2)}) %collective-permute-start.11) | collective-permute-done | bytes 131104 | tf_op jit(solution)/shard_map/ppermute | solution.py:726
  70.2 1.5 %collective-permute-start.12 = (bf16[2,128,256]{2,1,0:T(8,128)(2,1)S(1)}, bf16[2,128,256]{2,1,0:T(8,128)(2,1)S(1)}, u32[]{:S(2)}, u32[]{:S(2)}) collective-permute-start(bf16[2,128,256]{2,1,0:T(8,128)(2,1)S(1)} %add_convert_fusion.1), channel_id=1, source_target_pairs={{0,2},{1,3},{2,0},{3,1},{4,6},{5,7},{6,4},{7,5},{8,10},{9,11},{10,... | collective-permute-start | bytes 393224 | tf_op jit(solution)/shard_map/ppermute | solution.py:722
  73.1 1.3 %collective-permute-start.15 = (bf16[2,512,128]{2,1,0:T(8,128)(2,1)S(1)}, bf16[2,512,128]{2,1,0:T(8,128)(2,1)S(1)}, u32[]{:S(2)}, u32[]{:S(2)}) collective-permute-start(bf16[2,512,128]{2,1,0:T(8,128)(2,1)S(1)} %get-tuple-element.60), channel_id=1, source_target_pairs={{0,1},{1,0},{2,3},{3,2},{4,5},{5,4},{6,7},{7,6},{8,9},{9,8},{10,11... | collective-permute-start | bytes 786440 | tf_op jit(solution)/shard_map/ppermute | solution.py:739
  75.2 3.7 %collective-permute-start.13 = (bf16[2,128,256]{2,1,0:T(8,128)(2,1)S(1)}, bf16[2,128,256]{2,1,0:T(8,128)(2,1)S(1)}, u32[]{:S(2)}, u32[]{:S(2)}) collective-permute-start(bf16[2,128,256]{2,1,0:T(8,128)(2,1)S(1)} %add_convert_fusion.part), channel_id=1, source_target_pairs={{0,4},{1,5},{2,6},{3,7},{4,0},{5,1},{6,2},{7,3},{8,12},{9,13},{10,... | collective-permute-start | bytes 393224 | tf_op jit(solution)/shard_map/ppermute | solution.py:722
  79.0 5.4 %collective-permute-done.15.rest_1_ = bf16[2,512,128]{2,1,0:T(8,128)(2,1)S(1)} collective-permute-done((bf16[2,512,128]{2,1,0:T(8,128)(2,1)S(1)}, bf16[2,512,128]{2,1,0:T(8,128)(2,1)S(1)}, u32[]{:S(2)}, u32[]{:S(2)}) %collective-permute-start.15) | collective-permute-done | bytes 262176 | tf_op jit(solution)/shard_map/ppermute | solution.py:739
  84.4 4.9 %collective-permute-done.13.other = bf16[2,128,256]{2,1,0:T(8,128)(2,1)S(1)} collective-permute-done((bf16[2,128,256]{2,1,0:T(8,128)(2,1)S(1)}, bf16[2,128,256]{2,1,0:T(8,128)(2,1)S(1)}, u32[]{:S(2)}, u32[]{:S(2)}) %collective-permute-start.13) | collective-permute-done | bytes 131104 | tf_op jit(solution)/shard_map/ppermute | solution.py:722
  89.3 3.9 %borders.1 = (f32[2,512,1024]{2,1,0:T(8,128)}, f32[2,128,256]{2,1,0:T(8,128)}) custom-call(s32[4]{0:T(128)S(1)} %pad_add_fusion.offsets, f32[2,512,1024]{2,1,0:T(8,128)} %get-tuple-element.45.tile_in, bf16[2,128,256]{2,1,0:T(8,128)(2,1)S(1)} %add_convert_fusion.part, ...), custom_call_target="tpu_custom_call", output_to_operand_aliasing={{0}: (1, {})} | custom-call | flops 1048576 | bytes 8388608 | tf_op jit(solution)/shard_map/borders/pallas_call | solution.py:615
  (45 shorter events, 12.5 us)
Async XLA Ops:
  0.6 26.8 %copy-start = (f32[1,1,4,2,256,256]{5,4,3,2,1,0:T(8,128)S(1)}, f32[1,1,4,2,256,256]{5,4,3,2,1,0:T(8,128)}, u32[]{:S(2)}) copy-start(f32[1,1,4,2,256,256]{5,4,3,2,1,0:T(8,128)} %param.15) | copy-start | bytes 6291460
  0.8 1.4 %copy-start.1 = (bf16[1,512,1024]{2,1,0:T(8,128)(2,1)S(1)}, bf16[1,512,1024]{2,1,0:T(8,128)(2,1)}, u32[]{:S(2)}) copy-start(bf16[1,512,1024]{2,1,0:T(8,128)(2,1)} %tile_re.3) | copy-start | bytes 3145732
  2.1 1.2 %copy-start.3 = (bf16[1,512,1024]{2,1,0:T(8,128)(2,1)S(1)}, bf16[1,512,1024]{2,1,0:T(8,128)(2,1)}, u32[]{:S(2)}) copy-start(bf16[1,512,1024]{2,1,0:T(8,128)(2,1)} %tile_im.3) | copy-start | bytes 3145732
  4.9 18.6 %collective-permute-start = (bf16[2,128,1024]{2,1,0:T(8,128)(2,1)}, bf16[2,128,1024]{2,1,0:T(8,128)(2,1)S(1)}, u32[]{:S(2)}, u32[]{:S(2)}) collective-permute-start(bf16[2,128,1024]{2,1,0:T(8,128)(2,1)} %get-tuple-element.33), channel_id=1, source_target_pairs={{0,8},{1,9},{2,10},{3,11},{4,12},{5,13},{6,14},{7,15},{8,0},{9,1},... | collective-permute-start | bytes 1572872 | tf_op jit(solution)/shard_map/ppermute | solution.py:698
  7.9 15.5 %collective-permute-start.1 = (bf16[2,512,128]{2,1,0:T(8,128)(2,1)}, bf16[2,512,128]{2,1,0:T(8,128)(2,1)S(1)}, u32[]{:S(2)}, u32[]{:S(2)}) collective-permute-start(bf16[2,512,128]{2,1,0:T(8,128)(2,1)} %get-tuple-element.34), channel_id=1, source_target_pairs={{0,1},{1,0},{2,3},{3,2},{4,5},{5,4},{6,7},{7,6},{8,9},{9,8},{10,11... | collective-permute-start | bytes 786440 | tf_op jit(solution)/shard_map/ppermute | solution.py:698
  9.4 14.0 %collective-permute-start.2 = (bf16[2,512,128]{2,1,0:T(8,128)(2,1)S(1)}, bf16[2,512,128]{2,1,0:T(8,128)(2,1)S(1)}, u32[]{:S(2)}, u32[]{:S(2)}) collective-permute-start(bf16[2,512,128]{2,1,0:T(8,128)(2,1)S(1)} %get-tuple-element.35), channel_id=1, source_target_pairs={{1,2},{2,1},{3,4},{4,3},{5,6},{6,5},{9,10},{10,9},{11,12},{12,11},... | collective-permute-start | bytes 786440 | tf_op jit(solution)/shard_map/ppermute | solution.py:698
  10.1 12.5 %collective-permute-start.3 = (bf16[2,128,128]{2,1,0:T(8,128)(2,1)}, bf16[2,128,128]{2,1,0:T(8,128)(2,1)S(1)}, u32[]{:S(2)}, u32[]{:S(2)}) collective-permute-start(bf16[2,128,128]{2,1,0:T(8,128)(2,1)} %get-tuple-element.36), channel_id=1, source_target_pairs={{0,9},{1,8},{2,11},{3,10},{4,13},{5,12},{6,15},{7,14},{8,1},{9,0},... | collective-permute-start | bytes 196616 | tf_op jit(solution)/shard_map/ppermute | solution.py:698
  14.4 8.2 %collective-permute-start.4 = (bf16[2,128,128]{2,1,0:T(8,128)(2,1)}, bf16[2,128,128]{2,1,0:T(8,128)(2,1)S(1)}, u32[]{:S(2)}, u32[]{:S(2)}) collective-permute-start(bf16[2,128,128]{2,1,0:T(8,128)(2,1)} %get-tuple-element.37), channel_id=1, source_target_pairs={{1,10},{2,9},{3,12},{4,11},{5,14},{6,13},{9,2},{10,1},{11,4},{12,3... | collective-permute-start | bytes 196616 | tf_op jit(solution)/shard_map/ppermute | solution.py:698
  15.9 17.9 %copy-start.9 = (s32[1,1,4]{2,1,0:T(1,128)S(1)}, s32[1,1,4]{2,1,0:T(1,128)}, u32[]{:S(2)}) copy-start(s32[1,1,4]{2,1,0:T(1,128)} %param.14) | copy-start | bytes 52
  23.4 1.2 %copy-start.2 = (bf16[1,512,1024]{2,1,0:T(8,128)(2,1)S(1)}, bf16[1,512,1024]{2,1,0:T(8,128)(2,1)}, u32[]{:S(2)}) copy-start(bf16[1,512,1024]{2,1,0:T(8,128)(2,1)} %tile_re.3) | copy-start | bytes 3145732
  24.6 1.2 %copy-start.4 = (bf16[1,512,1024]{2,1,0:T(8,128)(2,1)S(1)}, bf16[1,512,1024]{2,1,0:T(8,128)(2,1)}, u32[]{:S(2)}) copy-start(bf16[1,512,1024]{2,1,0:T(8,128)(2,1)} %tile_im.3) | copy-start | bytes 3145732
  25.9 7.9 %copy-start.5 = (bf16[4,2,256,256]{3,2,1,0:T(8,128)(2,1)S(1)}, bf16[4,2,256,256]{3,2,1,0:T(8,128)(2,1)}, u32[]{:S(2)}) copy-start(bf16[4,2,256,256]{3,2,1,0:T(8,128)(2,1)} %constant.49.clone.tables) | copy-start | bytes 3145732
  27.4 6.4 %collective-permute-start.5 = (bf16[4,2,256,256]{3,2,1,0:T(8,128)(2,1)S(1)}, bf16[4,2,256,256]{3,2,1,0:T(8,128)(2,1)S(1)}, u32[]{:S(2)}, u32[]{:S(2)}) collective-permute-start(bf16[4,2,256,256]{3,2,1,0:T(8,128)(2,1)S(1)} %get-tuple-element.40), channel_id=1, source_target_pairs={{0,16},{16,0},{1,17},{17,1},{2,18},{18,2},{3,19},{19,3},{4,20},{20... | collective-permute-start | bytes 3145736 | tf_op jit(solution)/shard_map/ppermute | solution.py:701
  49.8 3.3 %collective-permute-start.6 = (bf16[4,2,256,256]{3,2,1,0:T(8,128)(2,1)S(1)}, bf16[4,2,256,256]{3,2,1,0:T(8,128)(2,1)S(1)}, u32[]{:S(2)}, u32[]{:S(2)}) collective-permute-start(bf16[4,2,256,256]{3,2,1,0:T(8,128)(2,1)S(1)} %get-tuple-element.44), channel_id=1, source_target_pairs={{0,16},{16,0},{1,17},{17,1},{2,18},{18,2},{3,19},{19,3},{4,20},{20... | collective-permute-start | bytes 3145736 | tf_op jit(solution)/shard_map/ppermute | solution.py:706
  50.3 2.7 %collective-permute-start.7 = (f32[2,128,256]{2,1,0:T(8,128)S(1)}, f32[2,128,256]{2,1,0:T(8,128)S(1)}, u32[]{:S(2)}, u32[]{:S(2)}) collective-permute-start(f32[2,128,256]{2,1,0:T(8,128)S(1)} %get-tuple-element.50), channel_id=1, source_target_pairs={{0,16},{16,0},{1,17},{17,1},{2,18},{18,2},{3,19},{19,3},{4,20},{20... | collective-permute-start | bytes 786440 | tf_op jit(solution)/shard_map/ppermute | solution.py:707
  56.7 6.3 %collective-permute-start.9 = (bf16[2,128,256]{2,1,0:T(8,128)(2,1)S(1)}, bf16[2,128,256]{2,1,0:T(8,128)(2,1)S(1)}, u32[]{:S(2)}, u32[]{:S(2)}) collective-permute-start(bf16[2,128,256]{2,1,0:T(8,128)(2,1)S(1)} %add.25), channel_id=1, source_target_pairs={{0,1},{1,0},{2,3},{3,2},{4,5},{5,4},{6,7},{7,6},{8,9},{9,8},{10,11... | collective-permute-start | bytes 393224 | tf_op jit(solution)/shard_map/ppermute | solution.py:722
  59.0 6.4 %collective-permute-start.8 = (bf16[2,128,256]{2,1,0:T(8,128)(2,1)S(1)}, bf16[2,128,256]{2,1,0:T(8,128)(2,1)S(1)}, u32[]{:S(2)}, u32[]{:S(2)}) collective-permute-start(bf16[2,128,256]{2,1,0:T(8,128)(2,1)S(1)} %add.25), channel_id=1, source_target_pairs={{0,8},{1,9},{2,10},{3,11},{4,12},{5,13},{6,14},{7,15},{8,0},{9,1},... | collective-permute-start | bytes 393224 | tf_op jit(solution)/shard_map/ppermute | solution.py:722
  59.5 8.1 %collective-permute-start.10 = (bf16[2,128,256]{2,1,0:T(8,128)(2,1)S(1)}, bf16[2,128,256]{2,1,0:T(8,128)(2,1)S(1)}, u32[]{:S(2)}, u32[]{:S(2)}) collective-permute-start(bf16[2,128,256]{2,1,0:T(8,128)(2,1)S(1)} %add.25), channel_id=1, source_target_pairs={{0,9},{1,8},{2,11},{3,10},{4,13},{5,12},{6,15},{7,14},{8,1},{9,0},... | collective-permute-start | bytes 393224 | tf_op jit(solution)/shard_map/ppermute | solution.py:722
  60.6 9.6 %collective-permute-start.11 = (bf16[2,2,128,128]{3,2,1,0:T(8,128)(2,1)S(1)}, bf16[2,2,128,128]{3,2,1,0:T(8,128)(2,1)S(1)}, u32[]{:S(2)}, u32[]{:S(2)}) collective-permute-start(bf16[2,2,128,128]{3,2,1,0:T(8,128)(2,1)S(1)} %get-tuple-element.52), channel_id=1, source_target_pairs={{0,8},{1,9},{2,10},{3,11},{4,12},{5,13},{6,14},{7,15},{8,0},{9,1},... | collective-permute-start | bytes 393224 | tf_op jit(solution)/shard_map/ppermute | solution.py:726
  70.2 5.0 %collective-permute-start.12 = (bf16[2,128,256]{2,1,0:T(8,128)(2,1)S(1)}, bf16[2,128,256]{2,1,0:T(8,128)(2,1)S(1)}, u32[]{:S(2)}, u32[]{:S(2)}) collective-permute-start(bf16[2,128,256]{2,1,0:T(8,128)(2,1)S(1)} %add_convert_fusion.1), channel_id=1, source_target_pairs={{0,2},{1,3},{2,0},{3,1},{4,6},{5,7},{6,4},{7,5},{8,10},{9,11},{10,... | collective-permute-start | bytes 393224 | tf_op jit(solution)/shard_map/ppermute | solution.py:722
  71.7 17.7 %collective-permute-start.14 = (bf16[2,128,1024]{2,1,0:T(8,128)(2,1)S(1)}, bf16[2,128,1024]{2,1,0:T(8,128)(2,1)S(1)}, u32[]{:S(2)}, u32[]{:S(2)}) collective-permute-start(bf16[2,128,1024]{2,1,0:T(8,128)(2,1)S(1)} %get-tuple-element.56), channel_id=1, source_target_pairs={{0,8},{1,9},{2,10},{3,11},{4,12},{5,13},{6,14},{7,15},{8,0},{9,1},... | collective-permute-start | bytes 1572872 | tf_op jit(solution)/shard_map/ppermute | solution.py:739
  73.1 11.3 %collective-permute-start.15 = (bf16[2,512,128]{2,1,0:T(8,128)(2,1)S(1)}, bf16[2,512,128]{2,1,0:T(8,128)(2,1)S(1)}, u32[]{:S(2)}, u32[]{:S(2)}) collective-permute-start(bf16[2,512,128]{2,1,0:T(8,128)(2,1)S(1)} %get-tuple-element.60), channel_id=1, source_target_pairs={{0,1},{1,0},{2,3},{3,2},{4,5},{5,4},{6,7},{7,6},{8,9},{9,8},{10,11... | collective-permute-start | bytes 786440 | tf_op jit(solution)/shard_map/ppermute | solution.py:739
  74.4 10.0 %collective-permute-start.16 = (bf16[2,512,128]{2,1,0:T(8,128)(2,1)S(1)}, bf16[2,512,128]{2,1,0:T(8,128)(2,1)S(1)}, u32[]{:S(2)}, u32[]{:S(2)}) collective-permute-start(bf16[2,512,128]{2,1,0:T(8,128)(2,1)S(1)} %get-tuple-element.61), channel_id=1, source_target_pairs={{1,2},{2,1},{3,4},{4,3},{5,6},{6,5},{9,10},{10,9},{11,12},{12,11},... | collective-permute-start | bytes 786440 | tf_op jit(solution)/shard_map/ppermute | solution.py:739
  75.2 14.1 %collective-permute-start.13 = (bf16[2,128,256]{2,1,0:T(8,128)(2,1)S(1)}, bf16[2,128,256]{2,1,0:T(8,128)(2,1)S(1)}, u32[]{:S(2)}, u32[]{:S(2)}) collective-permute-start(bf16[2,128,256]{2,1,0:T(8,128)(2,1)S(1)} %add_convert_fusion.part), channel_id=1, source_target_pairs={{0,4},{1,5},{2,6},{3,7},{4,0},{5,1},{6,2},{7,3},{8,12},{9,13},{10,... | collective-permute-start | bytes 393224 | tf_op jit(solution)/shard_map/ppermute | solution.py:722
  (3 other events, 2.9 us)

commit v7 on v6

--- a/solution.py
+++ b/solution.py
@@ -51,6 +51,14 @@
     lhs = jnp.concatenate([left[0], left[0], left[1]], axis=1)
     rhs = jnp.concatenate([right[0], right[1], right[0]], axis=0)
     return jnp.dot(lhs, rhs, preferred_element_type=f32)
+
+
+def dot(left, right):
+    if len(left) == 2 and len(right) == 2:
+        return dot3(left, right)
+    lhs = left if len(left) == 2 else left * 2
+    rhs = right if len(right) == 2 else right * 2
+    return jnp.dot(cols_of(*lhs), rows_of(*rhs), preferred_element_type=f32)
 
 
 def rows_of(*parts):
@@ -200,7 +208,7 @@
     return at % slots < occupied[at // slots]
 
 
-def gather_kernel(spots, edges, names, half, places, offsets, tile_re, tile_im, *rest):
+def gather_kernel(spots, edges, names, half, places, offsets, tile_re, tile_im, after, *rest):
     strips, (mine, other, padded, sems) = rest[:-4], rest[-4:]
     tile_rows, tile_cols = tile_re.shape[1:]
     size = mine.shape[-1]
@@ -257,7 +265,7 @@
         cut(sections * place + here, mine, place)
 
 
-def gather(places, offsets, tile_re, tile_im, edges, names, strips, size):
+def gather(places, offsets, tile_re, tile_im, after, edges, names, strips, size):
     half = size // 2
     spots = places.shape[0] // 2
     tile_rows, tile_cols = tile_re.shape[1:]
@@ -265,7 +273,7 @@
     vmem = pl.BlockSpec(memory_space=pltpu.VMEM)
     return pl.pallas_call(
         functools.partial(gather_kernel, spots, edges, names, half),
-        in_specs=[SMEM, SMEM, HBM, HBM] + [ANY] * len(strips),
+        in_specs=[SMEM, SMEM, HBM, HBM] + [ANY] * (1 + len(strips)),
         out_specs=[vmem, vmem],
         out_shape=[shape, shape],
         scratch_shapes=[
@@ -274,7 +282,7 @@
         ],
         compiler_params=pltpu.CompilerParams(vmem_limit_bytes=16 * MIB),
         name="gather",
-    )(places, offsets, tile_re, tile_im, *strips)
+    )(places, offsets, tile_re, tile_im, after, *strips)
 
 
 def chain_kernel(
@@ -309,7 +317,7 @@
 
     group_ids = range(group)
 
-    def forward(waves):
+    def forward(waves, cut):
         halves = []
         for sign, which in ((1, 2), (-1, 3)):
             parts = []
@@ -318,7 +326,7 @@
                     parts.append(rows_of(*(x[:half] + x[half:] for x in pair)))
                 else:
                     parts.append(rows_of(*(x[:half] - x[half:] for x in pair)))
-            halves.append(dot3(table(which), split(cols_of(*parts))))
+            halves.append(dot(table(which), cut(cols_of(*parts))))
         outs = []
         for sign, which in ((1, 0), (-1, 1)):
             parts = []
@@ -330,12 +338,12 @@
                     else:
                         x = x[:, :half] - x[:, half:]
                     parts.append(cols_of(x[:half], x[half:]))
-            outs.append(dot3(split(rows_of(*parts)), table(which)))
+            outs.append(dot(cut(rows_of(*parts)), table(which)))
         return [[out[at * size : (at + 1) * size] for out in outs] for at in group_ids]
 
-    def inverse(parts):
-        first = dot3(split(rows_of(*(part[0] for part in parts))), table(2))
-        second = dot3(split(rows_of(*(part[1] for part in parts))), table(3))
+    def inverse(parts, cut):
+        first = dot(cut(rows_of(*(part[0] for part in parts))), table(2))
+        second = dot(cut(rows_of(*(part[1] for part in parts))), table(3))
         evens, odds = [], []
         for at in group_ids:
             rows = slice(at * size, (at + 1) * size)
@@ -344,8 +352,8 @@
             im = cols_of(plus[:, half:], minus[:, half:])
             evens.append(rows_of(re[:half], im[:half]))
             odds.append(rows_of(re[half:], im[half:]))
-        first = dot3(table(0), split(cols_of(*evens)))
-        second = dot3(table(1), split(cols_of(*odds)))
+        first = dot(table(0), cut(cols_of(*evens)))
+        second = dot(table(1), cut(cols_of(*odds)))
         outs = []
         for at in group_ids:
             cols = slice(at * size, (at + 1) * size)
@@ -353,9 +361,9 @@
             outs.append((rows_of(plus[:half], minus[:half]), rows_of(plus[half:], minus[half:])))
         return outs
 
-    def propagate(waves, sign):
+    def propagate(waves, sign, cut):
         kept = []
-        for parts in forward(waves):
+        for parts in forward(waves, cut):
             outs = []
             for k, part in enumerate(parts):
                 cols = slice(k * half, (k + 1) * half)
@@ -363,7 +371,7 @@
                 re, im = part[:, :half], part[:, half:]
                 outs.append(cols_of(re * kre - im * kim, re * kim + im * kre))
             kept.append(outs)
-        return inverse(kept)
+        return inverse(kept, cut)
 
     def product(left, right):
         return left[0] * right[0] - left[1] * right[1], left[0] * right[1] + left[1] * right[0]
@@ -383,23 +391,23 @@
     def passed(at):
         return middle[at, 0].astype(f32), middle[at, 1].astype(f32)
 
-    outs = propagate([product(wave(at), window(0, at)) for at in group_ids], 1.0)
+    outs = propagate([product(wave(at), window(0, at)) for at in group_ids], 1.0, split)
     for at in group_ids:
         middle[at, 0] = outs[at][0].astype(bf16)
         middle[at, 1] = outs[at][1].astype(bf16)
 
-    far = forward([product(passed(at), window(1, at)) for at in group_ids])
+    far = forward([product(passed(at), window(1, at)) for at in group_ids], split)
     for at in group_ids:
         for k, part in enumerate(far[at]):
             re, im = part[:, :half], part[:, half:]
             misfit = re * re + im * im - frames[at, :, k * half : (k + 1) * half]
             far[at][k] = cols_of(re * misfit, im * misfit)
     pulls = []
-    for at, chi in enumerate(inverse(far)):
+    for at, chi in enumerate(inverse(far, split)):
         terms[1, at, 0], terms[1, at, 1] = conj_product(passed(at), chi)
         pulls.append(conj_product(window(1, at), chi))
 
-    for at, chi in enumerate(propagate(pulls, -1.0)):
+    for at, chi in enumerate(propagate(pulls, -1.0, lambda x: (x.astype(bf16),))):
         chi = rounded(chi[0]), rounded(chi[1])
         terms[0, at, 0], terms[0, at, 1] = conj_product(wave(at), chi)
         spot_at = 2 * (step * group + at) + me
@@ -460,7 +468,7 @@
     )(places, occupied, offsets, jnp.asarray(dft_tables(size)), kern, mine, theirs, frames, waves)
 
 
-def scatter_kernel(edges, names, half, places, occupied, offsets, kept, arrived, tile, *rest):
+def scatter_kernel(edges, names, half, places, occupied, offsets, folds, kept, arrived, tile, *rest):
     strips, (total, sems) = rest[:-2], rest[-2:]
     count, size = kept.shape[0], kept.shape[-1]
     tile_rows, tile_cols = tile.shape[1:]
@@ -497,11 +505,16 @@
     body = (pl.ds(half, tile_rows), pl.ds(half, tile_cols))
     copy = pltpu.make_async_copy(total.at[(slice(None),) + body], tile, sems.at[0])
     copy.start()
+    bands, strips = strips[: len(names)], strips[len(names) :]
     for (down, across), strip in zip(edges, strips):
         rows = span(down, offsets, names, half, body[0])
         cols = span(across, offsets, names, half, body[1])
         for plane in range(2):
             strip[plane] = total[plane, rows, cols].astype(bf16)
+    for (rows, cols), band in zip(band_places(names, folds, half, bands, tile_cols), bands):
+        rows = pl.ds(pl.multiple_of(rows.start + half, half), rows.size)
+        cols = pl.ds(pl.multiple_of(cols.start + half, half), cols.size)
+        band[...] = total[:, rows, cols]
     for (down, acrosses), strip in zip(corner_keys(names), strips[len(edges) :]):
         rows = span(down, offsets, names, half, None)
         for k, across in enumerate(acrosses):
@@ -511,21 +524,39 @@
     copy.wait()
 
 
+def band_shapes(names, tile_rows, tile_cols, half):
+    tall = tile_rows - half * sum(key[0] == "row" for key in names)
+    return [(2, half, tile_cols) if key[0] == "row" else (2, tall, half) for key in names]
+
+
+def band_places(names, folds, half, bands, tile_cols):
+    result = []
+    for k, (key, band) in enumerate(zip(names, bands)):
+        own = pl.ds(pl.multiple_of(folds[k], half), half)
+        if key[0] == "row":
+            result.append((own, pl.ds(0, tile_cols)))
+        else:
+            first = pl.multiple_of(folds[len(names)], half)
+            result.append((pl.ds(first, band.shape[1]), own))
+    return result
+
+
 def corner_keys(names):
     acrosses = [key for key in names if key[0] == "col"]
     return [(key, acrosses) for key in names if key[0] == "row" and acrosses]
 
 
-def scatter(places, occupied, offsets, kept, arrived, edges, names, tile_rows, tile_cols):
+def scatter(places, occupied, offsets, folds, kept, arrived, edges, names, tile_rows, tile_cols):
     count, _, size, _ = kept.shape
     half = size // 2
     corners = corner_keys(names)
     vmem = pl.BlockSpec(memory_space=pltpu.VMEM)
     return pl.pallas_call(
         functools.partial(scatter_kernel, edges, names, half),
-        in_specs=[SMEM, SMEM, SMEM, vmem, vmem],
-        out_specs=[HBM] + [vmem] * (len(edges) + len(corners)),
+        in_specs=[SMEM, SMEM, SMEM, SMEM, vmem, vmem],
+        out_specs=[HBM] + [vmem] * (len(names) + len(edges) + len(corners)),
         out_shape=[jax.ShapeDtypeStruct((2, tile_rows, tile_cols), f32)]
+        + [jax.ShapeDtypeStruct(x, f32) for x in band_shapes(names, tile_rows, tile_cols, half)]
         + strip_shapes(edges, tile_rows, tile_cols, half)
         + [jax.ShapeDtypeStruct((2, len(keys), half, half), bf16) for _, keys in corners],
         scratch_shapes=[
@@ -537,7 +568,7 @@
             flops=0, bytes_accessed=16 * tile_rows * tile_cols, transcendentals=0
         ),
         name="scatter",
-    )(places, occupied, offsets, kept, arrived)
+    )(places, occupied, offsets, folds, kept, arrived)
 
 
 def corner_kernel(names, half, offsets, *refs):
@@ -566,75 +597,55 @@
     )(offsets, *arrived, *strips)
 
 
-def border_kernel(edges, names, half, offsets, tile_in, part, other, *rest):
+def border_kernel(edges, names, half, folds, tile_in, part, other, *rest):
+    bands, rest = rest[: len(names)], rest[len(names) :]
     strips, rest = rest[: len(edges)], rest[len(edges) :]
-    tile, probe_share, bands, sides, in_sems, out_sems = rest
-    tile_rows, tile_cols = tile.shape[1:]
+    tile, probe_share, sems = rest[0], rest[1], rest[-1]
+    sums = rest[2:-1]
     strips = dict(zip(edges, strips))
-    downs = [key for key in names if key[0] == "row"]
-    acrosses = [key for key in names if key[0] == "col"]
-    tall = sides.shape[2]
-    rest_rows = pl.ds(pl.multiple_of(offsets[len(names)], half), tall)
-    spans = {key: span(key, offsets, names, half, None) for key in names}
-    regions = []
-    for k, key in enumerate(acrosses):
-        regions.append((key, sides.at[k], rest_rows, spans[key]))
-    for k, key in enumerate(downs):
-        regions.append((key, bands.at[k], spans[key], pl.ds(0, tile_cols)))
-
-    def copy(k, out):
-        _, block, rows, cols = regions[k]
-        if out:
-            return pltpu.make_async_copy(block, tile.at[:, rows, cols], out_sems.at[k])
-        return pltpu.make_async_copy(tile_in.at[:, rows, cols], block, in_sems.at[k])
-
-    for k in range(len(regions)):
-        copy(k, False).start()
+    tile_cols = tile.shape[2]
+    regions = band_places(names, folds, half, bands, tile_cols)
+    copies = []
+    for k, (key, (rows, cols)) in enumerate(zip(names, regions)):
+        for plane in range(2):
+            block = sums[k]
+            if key[0] == "row":
+                block[plane] = bands[k][plane] + strips[(key, None)][plane].astype(f32)
+                for j, across in enumerate(names):
+                    if across[0] == "col":
+                        wide = pl.ds(pl.multiple_of(folds[j], half), half)
+                        block[plane, :, wide] += strips[(None, across)][plane, rows, :].astype(f32)
+            else:
+                block[plane] = bands[k][plane] + strips[(None, key)][plane, rows, :].astype(f32)
+            copies.append(
+                pltpu.make_async_copy(
+                    block.at[plane], tile.at[plane, rows, cols], sems.at[len(copies)]
+                )
+            )
+            copies[-1].start()
     probe_share[...] = part[...].astype(f32) + other[...].astype(f32)
-    for k, (key, block, rows, cols) in enumerate(regions):
-        copy(k, False).wait()
-        for plane in range(2):
-            if key in downs:
-                block[plane] += strips[(key, None)][plane].astype(f32)
-                for across in acrosses:
-                    block[plane, :, spans[across]] += strips[(None, across)][
-                        plane, rows, :
-                    ].astype(f32)
-            else:
-                block[plane] += strips[(None, key)][plane, rows, :].astype(f32)
-        copy(k, True).start()
-    for k in range(len(regions)):
-        copy(k, True).wait()
-
-
-def add_borders(offsets, tile, probe_parts, edges, names, strips, half):
+    for copy in copies:
+        copy.wait()
+
+
+def add_borders(folds, tile, bands, probe_parts, edges, names, strips, half):
     vmem = pl.BlockSpec(memory_space=pltpu.VMEM)
-    downs = sum(key[0] == "row" for key in names)
-    acrosses = len(names) - downs
-    tile_rows, tile_cols = tile.shape[1:]
     return pl.pallas_call(
         functools.partial(border_kernel, edges, names, half),
-        in_specs=[SMEM, HBM] + [vmem] * (2 + len(strips)),
+        in_specs=[SMEM, HBM] + [vmem] * (2 + len(bands) + len(strips)),
         out_specs=[HBM, vmem],
         out_shape=[
             jax.ShapeDtypeStruct(tile.shape, f32),
             jax.ShapeDtypeStruct(probe_parts[0].shape, f32),
         ],
         scratch_shapes=[
-            pltpu.VMEM((max(downs, 1), 2, half, tile_cols), f32),
-            pltpu.VMEM((max(acrosses, 1), 2, tile_rows - downs * half, half), f32),
-            pltpu.SemaphoreType.DMA((max(len(names), 1),)),
-            pltpu.SemaphoreType.DMA((max(len(names), 1),)),
+            *(pltpu.VMEM(band.shape, f32) for band in bands),
+            pltpu.SemaphoreType.DMA((max(2 * len(bands), 1),)),
         ],
         input_output_aliases={1: 0},
         compiler_params=pltpu.CompilerParams(vmem_limit_bytes=12 * MIB),
-        cost_estimate=pl.CostEstimate(
-            flops=2 * tile_rows * tile_cols,
-            bytes_accessed=16 * tile_rows * tile_cols,
-            transcendentals=0,
-        ),
         name="borders",
-    )(offsets, tile, *probe_parts, *strips)
+    )(folds, tile, *probe_parts, *bands, *strips)
 
 
 def partner(index, kind):
@@ -693,64 +704,59 @@
 
     padded_at = numbers(*padded_at, here)
     tile_at = numbers(*tile_at, here)
-    bulk = len(names)
+    if rows == 2:
+        first_row = jnp.where(row_at == 0, 0, half)
+    else:
+        first_row = jnp.int32(half if downs else 0)
+    fold_at = numbers(*(tile_at[k] for k in range(len(names))), first_row)
     own = pack(tile_at, object_re, object_im, edges, names, half)
     strips = [lax.ppermute(strip, both, path) for strip, path in zip(own, paths)]
-    mine, other = gather(places, padded_at, object_re, object_im, edges, names, strips, size)
+    kern, sorted_frames, waves = prepare(places, padded_at, own[0], probe, phases, frames)
+    mine, other = gather(
+        places, padded_at, object_re, object_im, waves, edges, names, strips, size
+    )
     across_depth = [(i, 1 - i) for i in range(sections)]
     theirs = lax.ppermute(other, "depth", across_depth)
-    kern, sorted_frames, waves = prepare(places, padded_at, mine, probe, phases, frames)
     keep, send, pulled_keep, pulled_send = chain(
         places, live_counts, padded_at, kern, mine, theirs, sorted_frames, waves, count
     )
     arrived = lax.ppermute(send, "depth", across_depth)
     pulled = pulled_keep + lax.ppermute(pulled_send, "depth", across_depth)
 
+    assert rows & (rows - 1) == 0 and cols & (cols - 1) == 0
+    flips = [cols << k for k in range(rows.bit_length() - 1)]
+    across = [1 << k for k in range(cols.bit_length() - 1)]
+    flips += across[-1:] + across[:-1]
+    corner_at = max(len(flips) - 3, 0)
+
+    def exchange(block, flip):
+        own = block.astype(bf16)
+        return own, lax.ppermute(own, both, [(i, i ^ flip) for i in range(rows * cols)])
+
+    def summed(pair):
+        return pair[0].astype(f32) + pair[1].astype(f32)
+
+    pair = pulled, jnp.zeros_like(pulled)
+    for at in range(corner_at):
+        pair = exchange(summed(pair), flips[at])
+
     tile, *own = scatter(
-        places, live_counts, padded_at, keep, arrived, outer, names, tile_rows, tile_cols
+        places, live_counts, padded_at, fold_at, keep, arrived, outer, names, tile_rows, tile_cols
     )
+    bands, own = own[: len(names)], own[len(names) :]
     own, corners = own[: len(outer)], own[len(outer) :]
-
-    bits = rows.bit_length() + cols.bit_length() - 2
-    assert rows * cols == 1 << bits
-    flips = [cols << k for k in range(rows.bit_length() - 1)]
-    flips += [1 << k for k in range(cols.bit_length() - 1)]
-    early, late = flips[: max(bits - 2, 0)], flips[max(bits - 2, 0) :]
-    rounds = [early[k : k + 2] for k in range(0, len(early), 2)] + [[flip] for flip in late]
-
-    def fetch(block, flip):
-        return lax.ppermute(block, both, [(i, i ^ flip) for i in range(rows * cols)])
-
-    *own, pulled = lax.optimization_barrier((*own, pulled))
+    pair, own, corners = lax.optimization_barrier((pair, own, corners))
     if corners:
         corners = [lax.ppermute(x, both, path) for x, path in zip(corners, paths)]
-    added = None
-    for at, flips in enumerate(rounds):
-        mine = pulled.astype(bf16)
-        theirs = [fetch(mine, flip) for flip in flips]
-        if len(flips) == 2:
-            theirs.append(fetch(mine, flips[0] ^ flips[1]))
-        if at == 0 and corners:
-            theirs, corners = lax.optimization_barrier((theirs, corners))
-            own[len(downs) :] = add_corners(tile_at, own[len(downs) :], corners, names, half)
-        if added is None and at >= len(rounds) - 3:
-            if at:
-                theirs, own = lax.optimization_barrier((theirs, own))
-            added = [lax.ppermute(strip, both, path) for strip, path in zip(own, paths)]
-        if at < len(rounds) - 1:
-            sums = [part.astype(f32) for part in (mine, *theirs)]
-            pulled = sums[0] + sums[1]
-            if len(flips) == 2:
-                pulled = pulled + (sums[2] + sums[3])
-    (theirs,) = theirs
-    if rows == 2:
-        first_row = jnp.where(row_at == 0, 0, half)
-    else:
-        first_row = jnp.int32(half if downs else 0)
-    fold_at = numbers(*(tile_at[k] for k in range(bulk)), first_row)
-    gradient, probe_share = add_borders(
-        fold_at, tile, (mine, theirs), outer, names, added, half
-    )
+    if corner_at < len(flips):
+        pair = exchange(summed(pair), flips[corner_at])
+    if corners:
+        pair, corners = lax.optimization_barrier((pair, corners))
+        own[len(downs) :] = add_corners(tile_at, own[len(downs) :], corners, names, half)
+    added = [lax.ppermute(strip, both, path) for strip, path in zip(own, paths)]
+    for flip in flips[corner_at + 1 :]:
+        pair = exchange(summed(pair), flip)
+    gradient, probe_share = add_borders(fold_at, tile, bands, pair, outer, names, added, half)
     return (gradient[:, None], probe_share)
 
 

time: 93.9 us -> 84.5 us (0.90)
  waiting for transfers between devices: 29.5 us -> 20.1 us
  Pallas kernels: 30.6 us -> 28.7 us
  starting transfers between devices: 23.1 us -> 24.6 us
  other arithmetic: 0.37 us -> 1.84 us
  local copies, waits for them, and re-layouts: 8.79 us -> 7.82 us
    ppermute x5, waiting for transfers between devices: 7.43 us -> 0.01 us  [shards(): lax.ppermute(strip, both, path)]
    ppermute x5 -> x4, waiting for transfers between devices: 11.7 us -> 7.12 us  [exchange(): lax.ppermute(own, both, [(i, i ^ flip) for i in range(rows * cols)])]
    ppermute x1, waiting for transfers between devices: 0.01 us -> 2.65 us  [shards(): theirs = lax.ppermute(other, 'depth', across_depth)]
    ppermute x5 -> x4, starting transfers between devices: 8.98 us -> 11 us  [exchange(): lax.ppermute(own, both, [(i, i ^ flip) for i in range(rows * cols)])]
    ppermute x1, waiting for transfers between devices: 2.46 us -> 0.51 us  [shards(): corners = [lax.ppermute(x, both, path) for x, path in zip(corners, paths)]]
    ppermute x3, waiting for transfers between devices: 5.39 us -> 6.92 us  [shards(): added = [lax.ppermute(strip, both, path) for strip, path in zip(own, paths)]]
    pallas_call x1, Pallas kernels: 15.9 us -> 14.5 us  [chain(): pl.pallas_call(functools.partial(chain_kernel, group), grid=(count // gro...]
    pallas_call x1, Pallas kernels: 3.91 us -> 2.6 us  [add_borders(): pl.pallas_call(functools.partial(border_kernel, edges, names, half), in_s...]
  transfers between devices with their start and end apart: 17 -> 16, of which waited for: 10 -> 8; matrix products, arithmetic and copies ran while one was open for 1% -> 2% of each run, Pallas kernels for 4% -> 9%
where the time goes in v7:
time: 84.5 us; the launch traced here: 84 us
  Pallas kernels  28.7 us (34%)
  starting transfers between devices  24.6 us (29%)
  waiting for transfers between devices  20.1 us (24%)
  local copies, waits for them, and re-layouts  7.82 us (9%)
  other arithmetic  1.84 us (2%)
  between operations  1.03 us (1%)
    pallas_call x1, Pallas kernels, chain(): pl.pallas_call(functools.partial(chain_kernel, group), grid=(count // gro...  14.5 us
    ppermute x4, starting transfers between devices, exchange(): lax.ppermute(own, both, [(i, i ^ flip) for i in range(rows * cols)])  11 us
    ppermute x5, starting transfers between devices, shards(): lax.ppermute(strip, both, path)  10.2 us
    unnamed x23, local copies, waits for them, and re-layouts  7.73 us
    ppermute x4, waiting for transfers between devices, exchange(): lax.ppermute(own, both, [(i, i ^ flip) for i in range(rows * cols)])  7.12 us
    ppermute x3, waiting for transfers between devices, shards(): added = [lax.ppermute(strip, both, path) for strip, path in zip(own, paths)]  6.92 us
    pallas_call x1, Pallas kernels, scatter(): pl.pallas_call(functools.partial(scatter_kernel, edges, names, half), in_...  3.79 us
    pallas_call x1, Pallas kernels, prepare(): pl.pallas_call(prep_kernel, grid_spec=pltpu.PrefetchScalarGridSpec(num_sc...  3.35 us
  transfers between devices with their start and end apart: 16, of which 8 were waited for; matrix products, arithmetic and copies ran while one was open for 2% of the time, Pallas kernels for 9%

profile of v7, /device:TPU:0, one launch (start us, length us, event | category | flops | bytes accessed | tf_op | source)
XLA Modules:
  0.0 84.0 jit_solution(1685023250192779282)
XLA Ops:
  1.3 1.2 %copy-done.1 = bf16[1,512,1024]{2,1,0:T(8,128)(2,1)S(1)} copy-done((bf16[1,512,1024]{2,1,0:T(8,128)(2,1)S(1)}, bf16[1,512,1024]{2,1,0:T(8,128)(2,1)}, u32[]{:S(2)}) %copy-start.1) | copy-done | bytes 1048600
  2.5 1.2 %copy-done.3 = bf16[1,512,1024]{2,1,0:T(8,128)(2,1)S(1)} copy-done((bf16[1,512,1024]{2,1,0:T(8,128)(2,1)S(1)}, bf16[1,512,1024]{2,1,0:T(8,128)(2,1)}, u32[]{:S(2)}) %copy-start.3) | copy-done | bytes 1048600
  3.7 1.5 %pack.1 = (bf16[2,128,1024]{2,1,0:T(8,128)(2,1)S(1)}, bf16[2,512,128]{2,1,0:T(8,128)(2,1)}, bf16[2,512,128]{2,1,0:T(8,128)(2,1)}, bf16[2,128,128]{2,1,0:T(8,128)(2,1)}, bf16[2,128,128]{2,1,0:T(8,128)(2,1)}) custom-call(s32[4]{0:T(128)S(1)} %get-tuple-element.76.offsets, bf16[1,512,1024]{2,1,0:T(8,128)(2,1)S(1)} %copy-done.1, bf16[1,512,1024]{2,1,0:T(8,128)(2,1)S(1)} %copy-done.3), custom_call_target="tpu_custom_call" | custom-call | tf_op jit(solution)/shard_map/pack/pallas_call | solution.py:189
  5.2 3.0 %collective-permute-start = (bf16[2,128,1024]{2,1,0:T(8,128)(2,1)S(1)}, bf16[2,128,1024]{2,1,0:T(8,128)(2,1)S(1)}, u32[]{:S(2)}, u32[]{:S(2)}) collective-permute-start(bf16[2,128,1024]{2,1,0:T(8,128)(2,1)S(1)} %get-tuple-element.37.after), channel_id=1, source_target_pairs={{0,8},{1,9},{2,10},{3,11},{4,12},{5,13},{6,14},{7,15},{8,0},{9,1},... | collective-permute-start | bytes 1572872 | tf_op jit(solution)/shard_map/ppermute | solution.py:713
  8.2 1.5 %collective-permute-start.1 = (bf16[2,512,128]{2,1,0:T(8,128)(2,1)}, bf16[2,512,128]{2,1,0:T(8,128)(2,1)S(1)}, u32[]{:S(2)}, u32[]{:S(2)}) collective-permute-start(bf16[2,512,128]{2,1,0:T(8,128)(2,1)} %get-tuple-element.40), channel_id=1, source_target_pairs={{0,1},{1,0},{2,3},{3,2},{4,5},{5,4},{6,7},{7,6},{8,9},{9,8},{10,11... | collective-permute-start | bytes 786440 | tf_op jit(solution)/shard_map/ppermute | solution.py:713
  9.8 1.4 %collective-permute-start.2 = (bf16[2,512,128]{2,1,0:T(8,128)(2,1)}, bf16[2,512,128]{2,1,0:T(8,128)(2,1)}, u32[]{:S(2)}, u32[]{:S(2)}) collective-permute-start(bf16[2,512,128]{2,1,0:T(8,128)(2,1)} %get-tuple-element.41), channel_id=1, source_target_pairs={{1,2},{2,1},{3,4},{4,3},{5,6},{6,5},{9,10},{10,9},{11,12},{12,11},... | collective-permute-start | bytes 786440 | tf_op jit(solution)/shard_map/ppermute | solution.py:713
  11.1 3.6 %collective-permute-start.3 = (bf16[2,128,128]{2,1,0:T(8,128)(2,1)}, bf16[2,128,128]{2,1,0:T(8,128)(2,1)S(1)}, u32[]{:S(2)}, u32[]{:S(2)}) collective-permute-start(bf16[2,128,128]{2,1,0:T(8,128)(2,1)} %get-tuple-element.42), channel_id=1, source_target_pairs={{0,9},{1,8},{2,11},{3,10},{4,13},{5,12},{6,15},{7,14},{8,1},{9,0},... | collective-permute-start | bytes 196616 | tf_op jit(solution)/shard_map/ppermute | solution.py:713
  16.4 1.6 %copy-done = f32[1,1,4,2,256,256]{5,4,3,2,1,0:T(8,128)S(1)} copy-done((f32[1,1,4,2,256,256]{5,4,3,2,1,0:T(8,128)S(1)}, f32[1,1,4,2,256,256]{5,4,3,2,1,0:T(8,128)}, u32[]{:S(2)}) %copy-start) | copy-done | bytes 2097176
  18.9 1.0 %copy-done.7 = f32[2,256,256]{2,1,0:T(8,128)S(1)} copy-done((f32[2,256,256]{2,1,0:T(8,128)S(1)}, f32[2,256,256]{2,1,0:T(8,128)}, u32[]{:S(2)}) %copy-start.7) | copy-done | bytes 524312
  20.9 3.3 %prepare.1 = (f32[2,256,256]{2,1,0:T(8,128)S(1)}, f32[4,256,256]{2,1,0:T(8,128)S(1)}, f32[4,2,256,256]{3,2,1,0:T(8,128)S(1)}) custom-call(s32[16]{0:T(128)S(1)} %reshape.13.places, s32[4]{0:T(128)S(1)} %add_add_fusion.offsets, bf16[256,256]{1,0:T(8,128)(2,1)S(1)} %copy-done.8, bf16[2,128,1024]{2,1,0:T(8,128)(2,1)S(1)} %get-tuple-element.37.after, ...), custom_call_target="tpu_custom_call" | custom-call | tf_op jit(solution)/shard_map/prepare/pallas_call | solution.py:112
  24.3 2.4 %gather.1 = (bf16[4,2,256,256]{3,2,1,0:T(8,128)(2,1)S(1)}, bf16[4,2,256,256]{3,2,1,0:T(8,128)(2,1)S(1)}) custom-call(s32[16]{0:T(128)S(1)} %reshape.13.places, s32[4]{0:T(128)S(1)} %add_add_fusion.offsets, bf16[1,512,1024]{2,1,0:T(8,128)(2,1)S(1)} %copy-done.2, bf16[1,512,1024]{2,1,0:T(8,128)(2,1)S(1)} %copy-done.4, ...), custom_call_target="tpu_custom_call" | custom-call | tf_op jit(solution)/shard_map/gather/pallas_call | solution.py:274
  26.8 2.6 %collective-permute-done.5.theirs = bf16[4,2,256,256]{3,2,1,0:T(8,128)(2,1)S(1)} collective-permute-done((bf16[4,2,256,256]{3,2,1,0:T(8,128)(2,1)S(1)}, bf16[4,2,256,256]{3,2,1,0:T(8,128)(2,1)S(1)}, u32[]{:S(2)}, u32[]{:S(2)}) %collective-permute-start.5) | collective-permute-done | bytes 1048608 | tf_op jit(solution)/shard_map/ppermute | solution.py:719
  29.4 14.5 %chain.1 = (bf16[4,2,256,256]{3,2,1,0:T(8,128)(2,1)S(1)}, bf16[4,2,256,256]{3,2,1,0:T(8,128)(2,1)S(1)}, f32[2,128,256]{2,1,0:T(8,128)S(1)}, f32[2,128,256]{2,1,0:T(8,128)}) custom-call(s32[16]{0:T(128)S(1)} %reshape.13.places, s32[4]{0:T(128)S(1)} %bitcast.15, s32[4]{0:T(128)S(1)} %add_add_fusion.offsets, bf16[4,2,256,256]{3,2,1,0:T(8,128)(2,1)S(1)} %copy-done.6, ...), custom_call_target="tpu_custom_call" | custom-call | tf_op jit(solution)/shard_map/chain/pallas_call | solution.py:438
  44.5 2.9 %collective-permute-done.7 = f32[2,128,256]{2,1,0:T(8,128)} collective-permute-done((f32[2,128,256]{2,1,0:T(8,128)}, f32[2,128,256]{2,1,0:T(8,128)}, u32[]{:S(2)}, u32[]{:S(2)}) %collective-permute-start.7) | collective-permute-done | bytes 262176 | tf_op jit(solution)/shard_map/ppermute | solution.py:724
  48.3 1.6 %collective-permute-start.8 = (bf16[2,128,256]{2,1,0:T(8,128)(2,1)S(1)}, bf16[2,128,256]{2,1,0:T(8,128)(2,1)S(1)}, u32[]{:S(2)}, u32[]{:S(2)}) collective-permute-start(bf16[2,128,256]{2,1,0:T(8,128)(2,1)S(1)} %add_convert_fusion.3), channel_id=1, source_target_pairs={{0,8},{1,9},{2,10},{3,11},{4,12},{5,13},{6,14},{7,15},{8,0},{9,1},... | collective-permute-start | bytes 393224 | tf_op jit(solution)/shard_map/ppermute | solution.py:734
  50.0 3.8 %scatter.1 = (f32[2,512,1024]{2,1,0:T(8,128)}, f32[2,128,1024]{2,1,0:T(8,128)S(1)}, f32[2,384,128]{2,1,0:T(8,128)S(1)}, f32[2,384,128]{2,1,0:T(8,128)S(1)}, bf16...) custom-call(s32[16]{0:T(128)S(1)} %reshape.13.places, ...), custom_call_target="tpu_custom_call" | custom-call | bytes 8388608 | tf_op jit(solution)/shard_map/scatter/pallas_call | solution.py:554
  54.0 4.1 %collective-permute-start.9 = (bf16[2,128,256]{2,1,0:T(8,128)(2,1)S(1)}, bf16[2,128,256]{2,1,0:T(8,128)(2,1)S(1)}, u32[]{:S(2)}, u32[]{:S(2)}) collective-permute-start(bf16[2,128,256]{2,1,0:T(8,128)(2,1)S(1)} %add_convert_fusion.2), channel_id=1, source_target_pairs={{0,4},{1,5},{2,6},{3,7},{4,0},{5,1},{6,2},{7,3},{8,12},{9,13},{10,... | collective-permute-start | bytes 393224 | tf_op jit(solution)/shard_map/ppermute | solution.py:734
  58.1 1.3 %collective-permute-start.10 = (bf16[2,2,128,128]{3,2,1,0:T(8,128)(2,1)S(1)}, bf16[2,2,128,128]{3,2,1,0:T(8,128)(2,1)S(1)}, u32[]{:S(2)}, u32[]{:S(2)}) collective-permute-start(bf16[2,2,128,128]{3,2,1,0:T(8,128)(2,1)S(1)} %get-tuple-element.58), channel_id=1, source_target_pairs={{0,8},{1,9},{2,10},{3,11},{4,12},{5,13},{6,14},{7,15},{8,0},{9,1},... | collective-permute-start | bytes 393224 | tf_op jit(solution)/shard_map/ppermute | solution.py:750
  60.1 3.9 %collective-permute-done.9 = bf16[2,128,256]{2,1,0:T(8,128)(2,1)S(1)} collective-permute-done((bf16[2,128,256]{2,1,0:T(8,128)(2,1)S(1)}, bf16[2,128,256]{2,1,0:T(8,128)(2,1)S(1)}, u32[]{:S(2)}, u32[]{:S(2)}) %collective-permute-start.9) | collective-permute-done | bytes 131104 | tf_op jit(solution)/shard_map/ppermute | solution.py:734
  64.6 3.2 %collective-permute-start.11 = (bf16[2,128,256]{2,1,0:T(8,128)(2,1)S(1)}, bf16[2,128,256]{2,1,0:T(8,128)(2,1)S(1)}, u32[]{:S(2)}, u32[]{:S(2)}) collective-permute-start(bf16[2,128,256]{2,1,0:T(8,128)(2,1)S(1)} %add_convert_fusion.1), channel_id=1, source_target_pairs={{0,1},{1,0},{2,3},{3,2},{4,5},{5,4},{6,7},{7,6},{8,9},{9,8},{10,11... | collective-permute-start | bytes 393224 | tf_op jit(solution)/shard_map/ppermute | solution.py:734
  69.2 2.7 %collective-permute-done.11 = bf16[2,128,256]{2,1,0:T(8,128)(2,1)S(1)} collective-permute-done((bf16[2,128,256]{2,1,0:T(8,128)(2,1)S(1)}, bf16[2,128,256]{2,1,0:T(8,128)(2,1)S(1)}, u32[]{:S(2)}, u32[]{:S(2)}) %collective-permute-start.11) | collective-permute-done | bytes 131104 | tf_op jit(solution)/shard_map/ppermute | solution.py:734
  71.9 2.1 %collective-permute-start.12 = (bf16[2,128,256]{2,1,0:T(8,128)(2,1)S(1)}, bf16[2,128,256]{2,1,0:T(8,128)(2,1)S(1)}, u32[]{:S(2)}, u32[]{:S(2)}) collective-permute-start(bf16[2,128,256]{2,1,0:T(8,128)(2,1)S(1)} %add_convert_fusion.part), channel_id=1, source_target_pairs={{0,2},{1,3},{2,0},{3,1},{4,6},{5,7},{6,4},{7,5},{8,10},{9,11},{10,... | collective-permute-start | bytes 393224 | tf_op jit(solution)/shard_map/ppermute | solution.py:734
  74.0 6.9 %collective-permute-done.14.rest_4_ = bf16[2,512,128]{2,1,0:T(8,128)(2,1)S(1)} collective-permute-done((bf16[2,512,128]{2,1,0:T(8,128)(2,1)S(1)}, bf16[2,512,128]{2,1,0:T(8,128)(2,1)S(1)}, u32[]{:S(2)}, u32[]{:S(2)}) %collective-permute-start.14) | collective-permute-done | bytes 262176 | tf_op jit(solution)/shard_map/ppermute | solution.py:756
  81.3 2.6 %borders.1 = (f32[2,512,1024]{2,1,0:T(8,128)}, f32[2,128,256]{2,1,0:T(8,128)}) custom-call(s32[4]{0:T(128)S(1)} %pad_add_fusion.folds, f32[2,512,1024]{2,1,0:T(8,128)} %get-tuple-element.49.tile_in, bf16[2,128,256]{2,1,0:T(8,128)(2,1)S(1)} %add_convert_fusion.part, ...), custom_call_target="tpu_custom_call", output_to_operand_aliasing={{0}: (1, {})} | custom-call | tf_op jit(solution)/shard_map/borders/pallas_call | solution.py:633
  (46 shorter events, 9.0 us)
Async XLA Ops:
  1.3 1.2 %copy-start.1 = (bf16[1,512,1024]{2,1,0:T(8,128)(2,1)S(1)}, bf16[1,512,1024]{2,1,0:T(8,128)(2,1)}, u32[]{:S(2)}) copy-start(bf16[1,512,1024]{2,1,0:T(8,128)(2,1)} %tile_re.3) | copy-start | bytes 3145732
  2.5 1.2 %copy-start.3 = (bf16[1,512,1024]{2,1,0:T(8,128)(2,1)S(1)}, bf16[1,512,1024]{2,1,0:T(8,128)(2,1)}, u32[]{:S(2)}) copy-start(bf16[1,512,1024]{2,1,0:T(8,128)(2,1)} %tile_im.3) | copy-start | bytes 3145732
  3.7 20.5 %copy-start.2 = (bf16[1,512,1024]{2,1,0:T(8,128)(2,1)S(1)}, bf16[1,512,1024]{2,1,0:T(8,128)(2,1)}, u32[]{:S(2)}) copy-start(bf16[1,512,1024]{2,1,0:T(8,128)(2,1)} %tile_re.3) | copy-start | bytes 3145732
  3.7 20.5 %copy-start.4 = (bf16[1,512,1024]{2,1,0:T(8,128)(2,1)S(1)}, bf16[1,512,1024]{2,1,0:T(8,128)(2,1)}, u32[]{:S(2)}) copy-start(bf16[1,512,1024]{2,1,0:T(8,128)(2,1)} %tile_im.3) | copy-start | bytes 3145732
  5.2 19.0 %collective-permute-start = (bf16[2,128,1024]{2,1,0:T(8,128)(2,1)S(1)}, bf16[2,128,1024]{2,1,0:T(8,128)(2,1)S(1)}, u32[]{:S(2)}, u32[]{:S(2)}) collective-permute-start(bf16[2,128,1024]{2,1,0:T(8,128)(2,1)S(1)} %get-tuple-element.37.after), channel_id=1, source_target_pairs={{0,8},{1,9},{2,10},{3,11},{4,12},{5,13},{6,14},{7,15},{8,0},{9,1},... | collective-permute-start | bytes 1572872 | tf_op jit(solution)/shard_map/ppermute | solution.py:713
  8.2 16.0 %collective-permute-start.1 = (bf16[2,512,128]{2,1,0:T(8,128)(2,1)}, bf16[2,512,128]{2,1,0:T(8,128)(2,1)S(1)}, u32[]{:S(2)}, u32[]{:S(2)}) collective-permute-start(bf16[2,512,128]{2,1,0:T(8,128)(2,1)} %get-tuple-element.40), channel_id=1, source_target_pairs={{0,1},{1,0},{2,3},{3,2},{4,5},{5,4},{6,7},{7,6},{8,9},{9,8},{10,11... | collective-permute-start | bytes 786440 | tf_op jit(solution)/shard_map/ppermute | solution.py:713
  9.8 14.5 %collective-permute-start.2 = (bf16[2,512,128]{2,1,0:T(8,128)(2,1)}, bf16[2,512,128]{2,1,0:T(8,128)(2,1)}, u32[]{:S(2)}, u32[]{:S(2)}) collective-permute-start(bf16[2,512,128]{2,1,0:T(8,128)(2,1)} %get-tuple-element.41), channel_id=1, source_target_pairs={{1,2},{2,1},{3,4},{4,3},{5,6},{6,5},{9,10},{10,9},{11,12},{12,11},... | collective-permute-start | bytes 786440 | tf_op jit(solution)/shard_map/ppermute | solution.py:713
  11.1 13.1 %collective-permute-start.3 = (bf16[2,128,128]{2,1,0:T(8,128)(2,1)}, bf16[2,128,128]{2,1,0:T(8,128)(2,1)S(1)}, u32[]{:S(2)}, u32[]{:S(2)}) collective-permute-start(bf16[2,128,128]{2,1,0:T(8,128)(2,1)} %get-tuple-element.42), channel_id=1, source_target_pairs={{0,9},{1,8},{2,11},{3,10},{4,13},{5,12},{6,15},{7,14},{8,1},{9,0},... | collective-permute-start | bytes 196616 | tf_op jit(solution)/shard_map/ppermute | solution.py:713
  14.7 9.5 %collective-permute-start.4 = (bf16[2,128,128]{2,1,0:T(8,128)(2,1)}, bf16[2,128,128]{2,1,0:T(8,128)(2,1)S(1)}, u32[]{:S(2)}, u32[]{:S(2)}) collective-permute-start(bf16[2,128,128]{2,1,0:T(8,128)(2,1)} %get-tuple-element.43), channel_id=1, source_target_pairs={{1,10},{2,9},{3,12},{4,11},{5,14},{6,13},{9,2},{10,1},{11,4},{12,3... | collective-permute-start | bytes 196616 | tf_op jit(solution)/shard_map/ppermute | solution.py:713
  16.4 1.6 %copy-start = (f32[1,1,4,2,256,256]{5,4,3,2,1,0:T(8,128)S(1)}, f32[1,1,4,2,256,256]{5,4,3,2,1,0:T(8,128)}, u32[]{:S(2)}) copy-start(f32[1,1,4,2,256,256]{5,4,3,2,1,0:T(8,128)} %param.15) | copy-start | bytes 6291460
  20.8 8.6 %copy-start.6 = (bf16[4,2,256,256]{3,2,1,0:T(8,128)(2,1)S(1)}, bf16[4,2,256,256]{3,2,1,0:T(8,128)(2,1)}, u32[]{:S(2)}) copy-start(bf16[4,2,256,256]{3,2,1,0:T(8,128)(2,1)} %constant.49.clone.tables) | copy-start | bytes 3145732
  20.9 8.6 %copy-start.9 = (s32[1,1,4]{2,1,0:T(1,128)S(1)}, s32[1,1,4]{2,1,0:T(1,128)}, u32[]{:S(2)}) copy-start(s32[1,1,4]{2,1,0:T(1,128)} %param.14) | copy-start | bytes 52
  26.7 23.2 %copy-start.10 = (s32[4]{0:T(128)S(1)}, s32[4]{0:T(128)}, u32[]{:S(2)}) copy-start(s32[4]{0:T(128)} %get-tuple-element.77) | copy-start | bytes 52
  26.7 2.7 %collective-permute-start.5 = (bf16[4,2,256,256]{3,2,1,0:T(8,128)(2,1)S(1)}, bf16[4,2,256,256]{3,2,1,0:T(8,128)(2,1)S(1)}, u32[]{:S(2)}, u32[]{:S(2)}) collective-permute-start(bf16[4,2,256,256]{3,2,1,0:T(8,128)(2,1)S(1)} %get-tuple-element.45), channel_id=1, source_target_pairs={{0,16},{16,0},{1,17},{17,1},{2,18},{18,2},{3,19},{19,3},{4,20},{20... | collective-permute-start | bytes 3145736 | tf_op jit(solution)/shard_map/ppermute | solution.py:719
  43.9 6.1 %collective-permute-start.6 = (bf16[4,2,256,256]{3,2,1,0:T(8,128)(2,1)S(1)}, bf16[4,2,256,256]{3,2,1,0:T(8,128)(2,1)S(1)}, u32[]{:S(2)}, u32[]{:S(2)}) collective-permute-start(bf16[4,2,256,256]{3,2,1,0:T(8,128)(2,1)S(1)} %get-tuple-element.48), channel_id=1, source_target_pairs={{0,16},{16,0},{1,17},{17,1},{2,18},{18,2},{3,19},{19,3},{4,20},{20... | collective-permute-start | bytes 3145736 | tf_op jit(solution)/shard_map/ppermute | solution.py:723
  44.1 3.2 %collective-permute-start.7 = (f32[2,128,256]{2,1,0:T(8,128)}, f32[2,128,256]{2,1,0:T(8,128)}, u32[]{:S(2)}, u32[]{:S(2)}) collective-permute-start(f32[2,128,256]{2,1,0:T(8,128)} %get-tuple-element.51), channel_id=1, source_target_pairs={{0,16},{16,0},{1,17},{17,1},{2,18},{18,2},{3,19},{19,3},{4,20},{20... | collective-permute-start | bytes 786440 | tf_op jit(solution)/shard_map/ppermute | solution.py:724
  48.3 5.6 %collective-permute-start.8 = (bf16[2,128,256]{2,1,0:T(8,128)(2,1)S(1)}, bf16[2,128,256]{2,1,0:T(8,128)(2,1)S(1)}, u32[]{:S(2)}, u32[]{:S(2)}) collective-permute-start(bf16[2,128,256]{2,1,0:T(8,128)(2,1)S(1)} %add_convert_fusion.3), channel_id=1, source_target_pairs={{0,8},{1,9},{2,10},{3,11},{4,12},{5,13},{6,14},{7,15},{8,0},{9,1},... | collective-permute-start | bytes 393224 | tf_op jit(solution)/shard_map/ppermute | solution.py:734
  54.0 10.0 %collective-permute-start.9 = (bf16[2,128,256]{2,1,0:T(8,128)(2,1)S(1)}, bf16[2,128,256]{2,1,0:T(8,128)(2,1)S(1)}, u32[]{:S(2)}, u32[]{:S(2)}) collective-permute-start(bf16[2,128,256]{2,1,0:T(8,128)(2,1)S(1)} %add_convert_fusion.2), channel_id=1, source_target_pairs={{0,4},{1,5},{2,6},{3,7},{4,0},{5,1},{6,2},{7,3},{8,12},{9,13},{10,... | collective-permute-start | bytes 393224 | tf_op jit(solution)/shard_map/ppermute | solution.py:734
  58.1 6.4 %collective-permute-start.10 = (bf16[2,2,128,128]{3,2,1,0:T(8,128)(2,1)S(1)}, bf16[2,2,128,128]{3,2,1,0:T(8,128)(2,1)S(1)}, u32[]{:S(2)}, u32[]{:S(2)}) collective-permute-start(bf16[2,2,128,128]{3,2,1,0:T(8,128)(2,1)S(1)} %get-tuple-element.58), channel_id=1, source_target_pairs={{0,8},{1,9},{2,10},{3,11},{4,12},{5,13},{6,14},{7,15},{8,0},{9,1},... | collective-permute-start | bytes 393224 | tf_op jit(solution)/shard_map/ppermute | solution.py:750
  59.4 21.9 %collective-permute-start.13 = (bf16[2,128,1024]{2,1,0:T(8,128)(2,1)S(1)}, bf16[2,128,1024]{2,1,0:T(8,128)(2,1)S(1)}, u32[]{:S(2)}, u32[]{:S(2)}) collective-permute-start(bf16[2,128,1024]{2,1,0:T(8,128)(2,1)S(1)} %get-tuple-element.64), channel_id=1, source_target_pairs={{0,8},{1,9},{2,10},{3,11},{4,12},{5,13},{6,14},{7,15},{8,0},{9,1},... | collective-permute-start | bytes 1572872 | tf_op jit(solution)/shard_map/ppermute | solution.py:756
  64.6 7.3 %collective-permute-start.11 = (bf16[2,128,256]{2,1,0:T(8,128)(2,1)S(1)}, bf16[2,128,256]{2,1,0:T(8,128)(2,1)S(1)}, u32[]{:S(2)}, u32[]{:S(2)}) collective-permute-start(bf16[2,128,256]{2,1,0:T(8,128)(2,1)S(1)} %add_convert_fusion.1), channel_id=1, source_target_pairs={{0,1},{1,0},{2,3},{3,2},{4,5},{5,4},{6,7},{7,6},{8,9},{9,8},{10,11... | collective-permute-start | bytes 393224 | tf_op jit(solution)/shard_map/ppermute | solution.py:734
  68.4 12.5 %collective-permute-start.14 = (bf16[2,512,128]{2,1,0:T(8,128)(2,1)S(1)}, bf16[2,512,128]{2,1,0:T(8,128)(2,1)S(1)}, u32[]{:S(2)}, u32[]{:S(2)}) collective-permute-start(bf16[2,512,128]{2,1,0:T(8,128)(2,1)S(1)} %get-tuple-element.68), channel_id=1, source_target_pairs={{0,1},{1,0},{2,3},{3,2},{4,5},{5,4},{6,7},{7,6},{8,9},{9,8},{10,11... | collective-permute-start | bytes 786440 | tf_op jit(solution)/shard_map/ppermute | solution.py:756
  68.5 12.4 %collective-permute-start.15 = (bf16[2,512,128]{2,1,0:T(8,128)(2,1)S(1)}, bf16[2,512,128]{2,1,0:T(8,128)(2,1)S(1)}, u32[]{:S(2)}, u32[]{:S(2)}) collective-permute-start(bf16[2,512,128]{2,1,0:T(8,128)(2,1)S(1)} %get-tuple-element.69), channel_id=1, source_target_pairs={{1,2},{2,1},{3,4},{4,3},{5,6},{6,5},{9,10},{10,9},{11,12},{12,11},... | collective-permute-start | bytes 786440 | tf_op jit(solution)/shard_map/ppermute | solution.py:756
  71.9 9.4 %collective-permute-start.12 = (bf16[2,128,256]{2,1,0:T(8,128)(2,1)S(1)}, bf16[2,128,256]{2,1,0:T(8,128)(2,1)S(1)}, u32[]{:S(2)}, u32[]{:S(2)}) collective-permute-start(bf16[2,128,256]{2,1,0:T(8,128)(2,1)S(1)} %add_convert_fusion.part), channel_id=1, source_target_pairs={{0,2},{1,3},{2,0},{3,1},{4,6},{5,7},{6,4},{7,5},{8,10},{9,11},{10,... | collective-permute-start | bytes 393224 | tf_op jit(solution)/shard_map/ppermute | solution.py:734
  (3 other events, 2.9 us)

commit v8 on v7

--- a/solution.py
+++ b/solution.py
@@ -35,13 +35,6 @@
     return np.stack([high, low], axis=1)
 
 
-def sorting_table(size):
-    order = np.concatenate([np.arange(0, size, 2), np.arange(1, size, 2)])
-    table = np.zeros((size, size), np.float32)
-    table[order, np.arange(size)] = 1.0
-    return table.astype(jnp.bfloat16)
-
-
 def split(x):
     high = x.astype(bf16)
     return high, (x - high.astype(f32)).astype(bf16)
@@ -69,13 +62,13 @@
     return jnp.concatenate(parts, axis=1)
 
 
-def prep_kernel(places, offsets, order_t, after, probe, *refs):
+def prep_kernel(places, offsets, after, probe, *refs):
     step = pl.program_id(0)
     size = probe.shape[-1]
     half = size // 2
     blocks = size // LANES
     phases, frames = refs[:blocks], refs[blocks : 2 * blocks]
-    kern, sorted_frames, waves = refs[2 * blocks :]
+    kern, sorted_frames, waves, order = refs[2 * blocks :]
 
     def halved(parts, at):
         ids = [at + (pl.ds(start, half, stride=2), slice(None)) for start in range(2)]
@@ -84,13 +77,17 @@
     def in_order(rows):
         first, rest = split(rows)
         second, third = split(rows - first.astype(f32))
-        table = order_t[...]
+        table = order[...]
         return jnp.dot(
             cols_of(first, second, third), rows_of(table, table, table), preferred_element_type=f32
         )
 
     @pl.when(step == 0)
     def _():
+        source = lax.broadcasted_iota(jnp.int32, (size, size), 0)
+        target = lax.broadcasted_iota(jnp.int32, (size, size), 1)
+        chosen = source == 2 * (target % half) + target // half
+        order[...] = jnp.where(chosen, 1.0, 0.0).astype(bf16)
         angles = in_order(halved(phases, ()))
         kern[0] = jnp.cos(angles)
         kern[1] = jnp.sin(angles)
@@ -115,7 +112,6 @@
             num_scalar_prefetch=2,
             grid=(count,),
             in_specs=[
-                full(size, size),
                 ANY,
                 full(2, size, size),
                 *(
@@ -132,6 +128,7 @@
                 pl.BlockSpec((1, size, size), lambda i, p, o: (i, 0, 0)),
                 pl.BlockSpec((1, 2, size, size), lambda i, p, o: (i, 0, 0, 0)),
             ],
+            scratch_shapes=[pltpu.VMEM((size, size), bf16)],
         ),
         out_shape=[
             jax.ShapeDtypeStruct((2, size, size), f32),
@@ -144,7 +141,6 @@
     )(
         places,
         offsets,
-        jnp.asarray(sorting_table(size)),
         after,
         probe,
         *[phases] * blocks,
@@ -424,11 +420,9 @@
     @pl.when(step == steps - 1)
     def _():
         share = pulled_keep.shape[1]
-        for plane in range(2):
-            pulled_keep[plane] = pulled[plane, pl.ds(pl.multiple_of(me * share, share), share), :]
-            pulled_send[plane] = pulled[
-                plane, pl.ds(pl.multiple_of((1 - me) * share, share), share), :
-            ]
+        for out, owner in ((pulled_keep, me), (pulled_send, 1 - me)):
+            rows = pl.ds(pl.multiple_of(owner * share, share), share)
+            out[...] = pulled[:, rows, :].astype(bf16)
 
 
 def chain(places, occupied, offsets, kern, mine, theirs, frames, waves, group):
@@ -453,8 +447,8 @@
         out_shape=[
             jax.ShapeDtypeStruct((count, 2, size, size), bf16),
             jax.ShapeDtypeStruct((count, 2, size, size), bf16),
-            jax.ShapeDtypeStruct((2, size // 2, size), f32),
-            jax.ShapeDtypeStruct((2, size // 2, size), f32),
+            jax.ShapeDtypeStruct((2, size // 2, size), bf16),
+            jax.ShapeDtypeStruct((2, size // 2, size), bf16),
         ],
         scratch_shapes=[
             pltpu.VMEM((count // group, 2, group, 2, size, size), bf16),
@@ -717,44 +711,49 @@
     )
     across_depth = [(i, 1 - i) for i in range(sections)]
     theirs = lax.ppermute(other, "depth", across_depth)
-    keep, send, pulled_keep, pulled_send = chain(
+    keep, send, own_rows, other_rows = chain(
         places, live_counts, padded_at, kern, mine, theirs, sorted_frames, waves, count
     )
     arrived = lax.ppermute(send, "depth", across_depth)
-    pulled = pulled_keep + lax.ppermute(pulled_send, "depth", across_depth)
 
     assert rows & (rows - 1) == 0 and cols & (cols - 1) == 0
-    flips = [cols << k for k in range(rows.bit_length() - 1)]
-    across = [1 << k for k in range(cols.bit_length() - 1)]
-    flips += across[-1:] + across[:-1]
-    corner_at = max(len(flips) - 3, 0)
+    tiles = rows * cols
+    flips = [1 << k for k in range(cols.bit_length() - 1)]
+    flips = flips[-1:] + flips[:-1] + [cols << k for k in range(rows.bit_length() - 1)]
+
+    def fetched(block, flip):
+        pairs = [(i, i ^ flip) for i in range(sections * tiles)]
+        return lax.ppermute(block, ("depth",) + both, pairs)
 
     def exchange(block, flip):
         own = block.astype(bf16)
-        return own, lax.ppermute(own, both, [(i, i ^ flip) for i in range(rows * cols)])
+        return own, fetched(own, flip)
 
     def summed(pair):
         return pair[0].astype(f32) + pair[1].astype(f32)
 
-    pair = pulled, jnp.zeros_like(pulled)
-    for at in range(corner_at):
-        pair = exchange(summed(pair), flips[at])
+    parts = [own_rows, fetched(other_rows, tiles)]
+    if flips:
+        parts += [fetched(own_rows, flips[0]), fetched(other_rows, tiles ^ flips[0])]
 
     tile, *own = scatter(
         places, live_counts, padded_at, fold_at, keep, arrived, outer, names, tile_rows, tile_cols
     )
     bands, own = own[: len(names)], own[len(names) :]
     own, corners = own[: len(outer)], own[len(outer) :]
-    pair, own, corners = lax.optimization_barrier((pair, own, corners))
+    parts, own, corners = lax.optimization_barrier((parts, own, corners))
+    pair = parts[0].astype(f32), parts[1].astype(f32)
+    if flips:
+        pair = summed(parts[::2]), summed(parts[1::2])
     if corners:
         corners = [lax.ppermute(x, both, path) for x, path in zip(corners, paths)]
-    if corner_at < len(flips):
-        pair = exchange(summed(pair), flips[corner_at])
+    if flips[1:]:
+        pair = exchange(summed(pair), flips[1])
     if corners:
         pair, corners = lax.optimization_barrier((pair, corners))
         own[len(downs) :] = add_corners(tile_at, own[len(downs) :], corners, names, half)
     added = [lax.ppermute(strip, both, path) for strip, path in zip(own, paths)]
-    for flip in flips[corner_at + 1 :]:
+    for flip in flips[2:]:
         pair = exchange(summed(pair), flip)
     gradient, probe_share = add_borders(fold_at, tile, bands, pair, outer, names, added, half)
     return (gradient[:, None], probe_share)

time: 84.5 us -> 85.6 us (1.013)
  waiting for transfers between devices: 20.1 us -> 26 us
  starting transfers between devices: 24.6 us -> 21.8 us
  other arithmetic: 1.84 us -> 0.9 us
  local copies, waits for them, and re-layouts: 7.82 us -> 6.92 us
    ppermute x5 -> x6, waiting for transfers between devices: 9.99 us -> 16.5 us  [fetched(): return lax.ppermute(block, ('depth',) + both, pairs)]
    ppermute x3, waiting for transfers between devices: 6.92 us -> 3.25 us  [shards(): added = [lax.ppermute(strip, both, path) for strip, path in zip(own, paths)]]
    ppermute x5 -> x6, starting transfers between devices: 11.3 us -> 8.6 us  [fetched(): return lax.ppermute(block, ('depth',) + both, pairs)]
    ppermute x1, waiting for transfers between devices: 0.51 us -> 3.13 us  [shards(): corners = [lax.ppermute(x, both, path) for x, path in zip(corners, paths)]]
    convert_element_type x4 -> x3, other arithmetic: 1.08 us -> 0.13 us  [exchange(): own = block.astype(bf16)]
    unnamed x23 -> x21, local copies, waits for them, and re-layouts: 7.73 us -> 6.83 us
  transfers between devices with their start and end apart: 16 -> 17, of which waited for: 8 -> 8; matrix products, arithmetic and copies ran while one was open for 2% -> 1% of each run, Pallas kernels for 9% -> 9%
where the time goes in v8:
time: 85.6 us; the launch traced here: 85.2 us
  Pallas kernels  28.6 us (33%)
  waiting for transfers between devices  26 us (30%)
  starting transfers between devices  21.8 us (25%)
  local copies, waits for them, and re-layouts  6.92 us (8%)
  between operations  1.01 us (1%)
  other arithmetic  0.9 us (1%)
    ppermute x6, waiting for transfers between devices, fetched(): return lax.ppermute(block, ('depth',) + both, pairs)  16.5 us
    pallas_call x1, Pallas kernels, chain(): pl.pallas_call(functools.partial(chain_kernel, group), grid=(count // gro...  14.4 us
    ppermute x5, starting transfers between devices, shards(): lax.ppermute(strip, both, path)  10.2 us
    ppermute x6, starting transfers between devices, fetched(): return lax.ppermute(block, ('depth',) + both, pairs)  8.6 us
    unnamed x21, local copies, waits for them, and re-layouts  6.83 us
    pallas_call x1, Pallas kernels, scatter(): pl.pallas_call(functools.partial(scatter_kernel, edges, names, half), in_...  3.72 us
    pallas_call x1, Pallas kernels, prepare(): pl.pallas_call(prep_kernel, grid_spec=pltpu.PrefetchScalarGridSpec(num_sc...  3.37 us
    ppermute x3, waiting for transfers between devices, shards(): added = [lax.ppermute(strip, both, path) for strip, path in zip(own, paths)]  3.25 us
  transfers between devices with their start and end apart: 17, of which 8 were waited for; matrix products, arithmetic and copies ran while one was open for 1% of the time, Pallas kernels for 9%

profile of v8, /device:TPU:0, one launch (start us, length us, event | category | flops | bytes accessed | tf_op | source)
XLA Modules:
  0.0 85.2 jit_solution(17635260324411889507)
XLA Ops:
  1.3 1.2 %copy-done.1 = bf16[1,512,1024]{2,1,0:T(8,128)(2,1)S(1)} copy-done((bf16[1,512,1024]{2,1,0:T(8,128)(2,1)S(1)}, bf16[1,512,1024]{2,1,0:T(8,128)(2,1)}, u32[]{:S(2)}) %copy-start.1) | copy-done | bytes 1048600
  2.5 1.2 %copy-done.3 = bf16[1,512,1024]{2,1,0:T(8,128)(2,1)S(1)} copy-done((bf16[1,512,1024]{2,1,0:T(8,128)(2,1)S(1)}, bf16[1,512,1024]{2,1,0:T(8,128)(2,1)}, u32[]{:S(2)}) %copy-start.3) | copy-done | bytes 1048600
  3.7 1.5 %pack.1 = (bf16[2,128,1024]{2,1,0:T(8,128)(2,1)S(1)}, bf16[2,512,128]{2,1,0:T(8,128)(2,1)}, bf16[2,512,128]{2,1,0:T(8,128)(2,1)}, bf16[2,128,128]{2,1,0:T(8,128)(2,1)}, bf16[2,128,128]{2,1,0:T(8,128)(2,1)}) custom-call(s32[4]{0:T(128)S(1)} %get-tuple-element.80.offsets, bf16[1,512,1024]{2,1,0:T(8,128)(2,1)S(1)} %copy-done.1, bf16[1,512,1024]{2,1,0:T(8,128)(2,1)S(1)} %copy-done.3), custom_call_target="tpu_custom_call" | custom-call | tf_op jit(solution)/shard_map/pack/pallas_call | solution.py:185
  5.2 3.0 %collective-permute-start = (bf16[2,128,1024]{2,1,0:T(8,128)(2,1)S(1)}, bf16[2,128,1024]{2,1,0:T(8,128)(2,1)S(1)}, u32[]{:S(2)}, u32[]{:S(2)}) collective-permute-start(bf16[2,128,1024]{2,1,0:T(8,128)(2,1)S(1)} %get-tuple-element.39.after), channel_id=1, source_target_pairs={{0,8},{1,9},{2,10},{3,11},{4,12},{5,13},{6,14},{7,15},{8,0},{9,1},... | collective-permute-start | bytes 1572872 | tf_op jit(solution)/shard_map/ppermute | solution.py:707
  8.2 1.5 %collective-permute-start.1 = (bf16[2,512,128]{2,1,0:T(8,128)(2,1)}, bf16[2,512,128]{2,1,0:T(8,128)(2,1)S(1)}, u32[]{:S(2)}, u32[]{:S(2)}) collective-permute-start(bf16[2,512,128]{2,1,0:T(8,128)(2,1)} %get-tuple-element.42), channel_id=1, source_target_pairs={{0,1},{1,0},{2,3},{3,2},{4,5},{5,4},{6,7},{7,6},{8,9},{9,8},{10,11... | collective-permute-start | bytes 786440 | tf_op jit(solution)/shard_map/ppermute | solution.py:707
  9.8 1.4 %collective-permute-start.2 = (bf16[2,512,128]{2,1,0:T(8,128)(2,1)}, bf16[2,512,128]{2,1,0:T(8,128)(2,1)}, u32[]{:S(2)}, u32[]{:S(2)}) collective-permute-start(bf16[2,512,128]{2,1,0:T(8,128)(2,1)} %get-tuple-element.43), channel_id=1, source_target_pairs={{1,2},{2,1},{3,4},{4,3},{5,6},{6,5},{9,10},{10,9},{11,12},{12,11},... | collective-permute-start | bytes 786440 | tf_op jit(solution)/shard_map/ppermute | solution.py:707
  11.1 3.6 %collective-permute-start.3 = (bf16[2,128,128]{2,1,0:T(8,128)(2,1)}, bf16[2,128,128]{2,1,0:T(8,128)(2,1)S(1)}, u32[]{:S(2)}, u32[]{:S(2)}) collective-permute-start(bf16[2,128,128]{2,1,0:T(8,128)(2,1)} %get-tuple-element.44), channel_id=1, source_target_pairs={{0,9},{1,8},{2,11},{3,10},{4,13},{5,12},{6,15},{7,14},{8,1},{9,0},... | collective-permute-start | bytes 196616 | tf_op jit(solution)/shard_map/ppermute | solution.py:707
  16.4 1.6 %copy-done = f32[1,1,4,2,256,256]{5,4,3,2,1,0:T(8,128)S(1)} copy-done((f32[1,1,4,2,256,256]{5,4,3,2,1,0:T(8,128)S(1)}, f32[1,1,4,2,256,256]{5,4,3,2,1,0:T(8,128)}, u32[]{:S(2)}) %copy-start) | copy-done | bytes 2097176
  18.9 1.0 %copy-done.7 = f32[2,256,256]{2,1,0:T(8,128)S(1)} copy-done((f32[2,256,256]{2,1,0:T(8,128)S(1)}, f32[2,256,256]{2,1,0:T(8,128)}, u32[]{:S(2)}) %copy-start.7) | copy-done | bytes 524312
  19.9 3.4 %prepare.1 = (f32[2,256,256]{2,1,0:T(8,128)S(1)}, f32[4,256,256]{2,1,0:T(8,128)S(1)}, f32[4,2,256,256]{3,2,1,0:T(8,128)S(1)}) custom-call(s32[16]{0:T(128)S(1)} %reshape.13.places, s32[4]{0:T(128)S(1)} %add_add_fusion.offsets, bf16[2,128,1024]{2,1,0:T(8,128)(2,1)S(1)} %get-tuple-element.39.after, f32[2,256,256]{2,1,0:T(8,128)S(1)} %copy-done.7, ...), custom_call_target="tpu_custom_call" | custom-call | tf_op jit(solution)/shard_map/prepare/pallas_call | solution.py:109
  23.8 2.4 %gather.1 = (bf16[4,2,256,256]{3,2,1,0:T(8,128)(2,1)S(1)}, bf16[4,2,256,256]{3,2,1,0:T(8,128)(2,1)S(1)}) custom-call(s32[16]{0:T(128)S(1)} %reshape.13.places, s32[4]{0:T(128)S(1)} %add_add_fusion.offsets, bf16[1,512,1024]{2,1,0:T(8,128)(2,1)S(1)} %copy-done.2, bf16[1,512,1024]{2,1,0:T(8,128)(2,1)S(1)} %copy-done.4, ...), custom_call_target="tpu_custom_call" | custom-call | tf_op jit(solution)/shard_map/gather/pallas_call | solution.py:270
  26.3 2.6 %collective-permute-done.5.theirs = bf16[4,2,256,256]{3,2,1,0:T(8,128)(2,1)S(1)} collective-permute-done((bf16[4,2,256,256]{3,2,1,0:T(8,128)(2,1)S(1)}, bf16[4,2,256,256]{3,2,1,0:T(8,128)(2,1)S(1)}, u32[]{:S(2)}, u32[]{:S(2)}) %collective-permute-start.5) | collective-permute-done | bytes 1048608 | tf_op jit(solution)/shard_map/ppermute | solution.py:713
  28.9 14.4 %chain.1 = (bf16[4,2,256,256]{3,2,1,0:T(8,128)(2,1)S(1)}, bf16[4,2,256,256]{3,2,1,0:T(8,128)(2,1)S(1)}, bf16[2,128,256]{2,1,0:T(8,128)(2,1)S(1)}, bf16[2,128,256]{2,1,0:T(8,128)(2,1)S(1)}) custom-call(s32[16]{0:T(128)S(1)} %reshape.13.places, s32[4]{0:T(128)S(1)} %bitcast.15, s32[4]{0:T(128)S(1)} %add_add_fusion.offsets, ...), custom_call_target="tpu_custom_call" | custom-call | tf_op jit(solution)/shard_map/chain/pallas_call | solution.py:432
  43.6 3.6 %collective-permute-start.9 = (bf16[2,128,256]{2,1,0:T(8,128)(2,1)S(1)}, bf16[2,128,256]{2,1,0:T(8,128)(2,1)S(1)}, u32[]{:S(2)}, u32[]{:S(2)}) collective-permute-start(bf16[2,128,256]{2,1,0:T(8,128)(2,1)S(1)} %get-tuple-element.53), channel_id=1, source_target_pairs={{0,20},{1,21},{2,22},{3,23},{4,16},{5,17},{6,18},{7,19},{8,28},{9,... | collective-permute-start | bytes 393224 | tf_op jit(solution)/shard_map/ppermute | solution.py:726
  47.6 3.7 %scatter.1 = (f32[2,512,1024]{2,1,0:T(8,128)}, f32[2,128,1024]{2,1,0:T(8,128)S(1)}, f32[2,384,128]{2,1,0:T(8,128)S(1)}, f32[2,384,128]{2,1,0:T(8,128)S(1)}, bf16...) custom-call(s32[16]{0:T(128)S(1)} %reshape.13.places, ...), custom_call_target="tpu_custom_call" | custom-call | bytes 8388608 | tf_op jit(solution)/shard_map/scatter/pallas_call | solution.py:548
  51.4 8.3 %collective-permute-done.8 = bf16[2,128,256]{2,1,0:T(8,128)(2,1)S(1)} collective-permute-done((bf16[2,128,256]{2,1,0:T(8,128)(2,1)S(1)}, bf16[2,128,256]{2,1,0:T(8,128)(2,1)S(1)}, u32[]{:S(2)}, u32[]{:S(2)}) %collective-permute-start.8) | collective-permute-done | bytes 131104 | tf_op jit(solution)/shard_map/ppermute | solution.py:726
  59.7 3.9 %collective-permute-start.10 = (bf16[2,128,256]{2,1,0:T(8,128)(2,1)S(1)}, bf16[2,128,256]{2,1,0:T(8,128)(2,1)S(1)}, u32[]{:S(2)}, u32[]{:S(2)}) collective-permute-start(bf16[2,128,256]{2,1,0:T(8,128)(2,1)S(1)} %add_convert_fusion.2), channel_id=1, source_target_pairs={{0,1},{1,0},{2,3},{3,2},{4,5},{5,4},{6,7},{7,6},{8,9},{9,8},{10,11... | collective-permute-start | bytes 393224 | tf_op jit(solution)/shard_map/ppermute | solution.py:726
  64.2 1.5 %collective-permute-start.14 = (bf16[2,128,1024]{2,1,0:T(8,128)(2,1)S(1)}, bf16[2,128,1024]{2,1,0:T(8,128)(2,1)S(1)}, u32[]{:S(2)}, u32[]{:S(2)}) collective-permute-start(bf16[2,128,1024]{2,1,0:T(8,128)(2,1)S(1)} %get-tuple-element.68), channel_id=1, source_target_pairs={{0,8},{1,9},{2,10},{3,11},{4,12},{5,13},{6,14},{7,15},{8,0},{9,1},... | collective-permute-start | bytes 1572872 | tf_op jit(solution)/shard_map/ppermute | solution.py:755
  65.7 1.3 %collective-permute-done.10 = bf16[2,128,256]{2,1,0:T(8,128)(2,1)S(1)} collective-permute-done((bf16[2,128,256]{2,1,0:T(8,128)(2,1)S(1)}, bf16[2,128,256]{2,1,0:T(8,128)(2,1)S(1)}, u32[]{:S(2)}, u32[]{:S(2)}) %collective-permute-start.10) | collective-permute-done | bytes 131104 | tf_op jit(solution)/shard_map/ppermute | solution.py:726
  67.0 3.1 %collective-permute-done.11.refs_0_ = bf16[2,2,128,128]{3,2,1,0:T(8,128)(2,1)S(1)} collective-permute-done((bf16[2,2,128,128]{3,2,1,0:T(8,128)(2,1)S(1)}, bf16[2,2,128,128]{3,2,1,0:T(8,128)(2,1)S(1)}, u32[]{:S(2)}, u32[]{:S(2)}) %collective-permute-start.11) | collective-permute-done | bytes 131104 | tf_op jit(solution)/shard_map/ppermute | solution.py:749
  71.6 5.0 %collective-permute-done.12 = bf16[2,128,256]{2,1,0:T(8,128)(2,1)S(1)} collective-permute-done((bf16[2,128,256]{2,1,0:T(8,128)(2,1)S(1)}, bf16[2,128,256]{2,1,0:T(8,128)(2,1)S(1)}, u32[]{:S(2)}, u32[]{:S(2)}) %collective-permute-start.12) | collective-permute-done | bytes 131104 | tf_op jit(solution)/shard_map/ppermute | solution.py:726
  77.2 3.2 %collective-permute-done.15.rest_4_ = bf16[2,512,128]{2,1,0:T(8,128)(2,1)S(1)} collective-permute-done((bf16[2,512,128]{2,1,0:T(8,128)(2,1)S(1)}, bf16[2,512,128]{2,1,0:T(8,128)(2,1)S(1)}, u32[]{:S(2)}, u32[]{:S(2)}) %collective-permute-start.15) | collective-permute-done | bytes 262176 | tf_op jit(solution)/shard_map/ppermute | solution.py:755
  80.4 2.0 %collective-permute-done.13.other = bf16[2,128,256]{2,1,0:T(8,128)(2,1)S(1)} collective-permute-done((bf16[2,128,256]{2,1,0:T(8,128)(2,1)S(1)}, bf16[2,128,256]{2,1,0:T(8,128)(2,1)S(1)}, u32[]{:S(2)}, u32[]{:S(2)}) %collective-permute-start.13) | collective-permute-done | bytes 131104 | tf_op jit(solution)/shard_map/ppermute | solution.py:726
  82.5 2.6 %borders.1 = (f32[2,512,1024]{2,1,0:T(8,128)}, f32[2,128,256]{2,1,0:T(8,128)}) custom-call(s32[4]{0:T(128)S(1)} %pad_add_fusion.folds, f32[2,512,1024]{2,1,0:T(8,128)} %get-tuple-element.51.tile_in, bf16[2,128,256]{2,1,0:T(8,128)(2,1)S(1)} %add_convert_fusion.part, ...), custom_call_target="tpu_custom_call", output_to_operand_aliasing={{0}: (1, {})} | custom-call | tf_op jit(solution)/shard_map/borders/pallas_call | solution.py:627
  (45 shorter events, 7.1 us)
Async XLA Ops:
  1.3 1.2 %copy-start.1 = (bf16[1,512,1024]{2,1,0:T(8,128)(2,1)S(1)}, bf16[1,512,1024]{2,1,0:T(8,128)(2,1)}, u32[]{:S(2)}) copy-start(bf16[1,512,1024]{2,1,0:T(8,128)(2,1)} %tile_re.3) | copy-start | bytes 3145732
  3.7 20.1 %copy-start.2 = (bf16[1,512,1024]{2,1,0:T(8,128)(2,1)S(1)}, bf16[1,512,1024]{2,1,0:T(8,128)(2,1)}, u32[]{:S(2)}) copy-start(bf16[1,512,1024]{2,1,0:T(8,128)(2,1)} %tile_re.3) | copy-start | bytes 3145732
  3.7 20.1 %copy-start.4 = (bf16[1,512,1024]{2,1,0:T(8,128)(2,1)S(1)}, bf16[1,512,1024]{2,1,0:T(8,128)(2,1)}, u32[]{:S(2)}) copy-start(bf16[1,512,1024]{2,1,0:T(8,128)(2,1)} %tile_im.3) | copy-start | bytes 3145732
  5.2 18.6 %collective-permute-start = (bf16[2,128,1024]{2,1,0:T(8,128)(2,1)S(1)}, bf16[2,128,1024]{2,1,0:T(8,128)(2,1)S(1)}, u32[]{:S(2)}, u32[]{:S(2)}) collective-permute-start(bf16[2,128,1024]{2,1,0:T(8,128)(2,1)S(1)} %get-tuple-element.39.after), channel_id=1, source_target_pairs={{0,8},{1,9},{2,10},{3,11},{4,12},{5,13},{6,14},{7,15},{8,0},{9,1},... | collective-permute-start | bytes 1572872 | tf_op jit(solution)/shard_map/ppermute | solution.py:707
  8.2 15.5 %collective-permute-start.1 = (bf16[2,512,128]{2,1,0:T(8,128)(2,1)}, bf16[2,512,128]{2,1,0:T(8,128)(2,1)S(1)}, u32[]{:S(2)}, u32[]{:S(2)}) collective-permute-start(bf16[2,512,128]{2,1,0:T(8,128)(2,1)} %get-tuple-element.42), channel_id=1, source_target_pairs={{0,1},{1,0},{2,3},{3,2},{4,5},{5,4},{6,7},{7,6},{8,9},{9,8},{10,11... | collective-permute-start | bytes 786440 | tf_op jit(solution)/shard_map/ppermute | solution.py:707
  9.8 14.0 %collective-permute-start.2 = (bf16[2,512,128]{2,1,0:T(8,128)(2,1)}, bf16[2,512,128]{2,1,0:T(8,128)(2,1)}, u32[]{:S(2)}, u32[]{:S(2)}) collective-permute-start(bf16[2,512,128]{2,1,0:T(8,128)(2,1)} %get-tuple-element.43), channel_id=1, source_target_pairs={{1,2},{2,1},{3,4},{4,3},{5,6},{6,5},{9,10},{10,9},{11,12},{12,11},... | collective-permute-start | bytes 786440 | tf_op jit(solution)/shard_map/ppermute | solution.py:707
  11.1 12.2 %collective-permute-start.3 = (bf16[2,128,128]{2,1,0:T(8,128)(2,1)}, bf16[2,128,128]{2,1,0:T(8,128)(2,1)S(1)}, u32[]{:S(2)}, u32[]{:S(2)}) collective-permute-start(bf16[2,128,128]{2,1,0:T(8,128)(2,1)} %get-tuple-element.44), channel_id=1, source_target_pairs={{0,9},{1,8},{2,11},{3,10},{4,13},{5,12},{6,15},{7,14},{8,1},{9,0},... | collective-permute-start | bytes 196616 | tf_op jit(solution)/shard_map/ppermute | solution.py:707
  14.7 8.6 %collective-permute-start.4 = (bf16[2,128,128]{2,1,0:T(8,128)(2,1)}, bf16[2,128,128]{2,1,0:T(8,128)(2,1)S(1)}, u32[]{:S(2)}, u32[]{:S(2)}) collective-permute-start(bf16[2,128,128]{2,1,0:T(8,128)(2,1)} %get-tuple-element.45), channel_id=1, source_target_pairs={{1,10},{2,9},{3,12},{4,11},{5,14},{6,13},{9,2},{10,1},{11,4},{12,3... | collective-permute-start | bytes 196616 | tf_op jit(solution)/shard_map/ppermute | solution.py:707
  16.4 1.6 %copy-start = (f32[1,1,4,2,256,256]{5,4,3,2,1,0:T(8,128)S(1)}, f32[1,1,4,2,256,256]{5,4,3,2,1,0:T(8,128)}, u32[]{:S(2)}) copy-start(f32[1,1,4,2,256,256]{5,4,3,2,1,0:T(8,128)} %param.14) | copy-start | bytes 6291460
  19.9 9.0 %copy-start.6 = (bf16[4,2,256,256]{3,2,1,0:T(8,128)(2,1)S(1)}, bf16[4,2,256,256]{3,2,1,0:T(8,128)(2,1)}, u32[]{:S(2)}) copy-start(bf16[4,2,256,256]{3,2,1,0:T(8,128)(2,1)} %constant.46.clone.tables) | copy-start | bytes 3145732
  19.9 9.0 %copy-start.8 = (s32[1,1,4]{2,1,0:T(1,128)S(1)}, s32[1,1,4]{2,1,0:T(1,128)}, u32[]{:S(2)}) copy-start(s32[1,1,4]{2,1,0:T(1,128)} %param.13) | copy-start | bytes 52
  26.2 21.4 %copy-start.9 = (s32[4]{0:T(128)S(1)}, s32[4]{0:T(128)}, u32[]{:S(2)}) copy-start(s32[4]{0:T(128)} %get-tuple-element.81) | copy-start | bytes 52
  26.2 2.7 %collective-permute-start.5 = (bf16[4,2,256,256]{3,2,1,0:T(8,128)(2,1)S(1)}, bf16[4,2,256,256]{3,2,1,0:T(8,128)(2,1)S(1)}, u32[]{:S(2)}, u32[]{:S(2)}) collective-permute-start(bf16[4,2,256,256]{3,2,1,0:T(8,128)(2,1)S(1)} %get-tuple-element.47), channel_id=1, source_target_pairs={{0,16},{16,0},{1,17},{17,1},{2,18},{18,2},{3,19},{19,3},{4,20},{20... | collective-permute-start | bytes 3145736 | tf_op jit(solution)/shard_map/ppermute | solution.py:713
  43.3 4.3 %collective-permute-start.6 = (bf16[4,2,256,256]{3,2,1,0:T(8,128)(2,1)S(1)}, bf16[4,2,256,256]{3,2,1,0:T(8,128)(2,1)S(1)}, u32[]{:S(2)}, u32[]{:S(2)}) collective-permute-start(bf16[4,2,256,256]{3,2,1,0:T(8,128)(2,1)S(1)} %get-tuple-element.50), channel_id=1, source_target_pairs={{0,16},{16,0},{1,17},{17,1},{2,18},{18,2},{3,19},{19,3},{4,20},{20... | collective-permute-start | bytes 3145736 | tf_op jit(solution)/shard_map/ppermute | solution.py:717
  43.6 16.1 %collective-permute-start.9 = (bf16[2,128,256]{2,1,0:T(8,128)(2,1)S(1)}, bf16[2,128,256]{2,1,0:T(8,128)(2,1)S(1)}, u32[]{:S(2)}, u32[]{:S(2)}) collective-permute-start(bf16[2,128,256]{2,1,0:T(8,128)(2,1)S(1)} %get-tuple-element.53), channel_id=1, source_target_pairs={{0,20},{1,21},{2,22},{3,23},{4,16},{5,17},{6,18},{7,19},{8,28},{9,... | collective-permute-start | bytes 393224 | tf_op jit(solution)/shard_map/ppermute | solution.py:726
  47.2 12.5 %collective-permute-start.7 = (bf16[2,128,256]{2,1,0:T(8,128)(2,1)S(1)}, bf16[2,128,256]{2,1,0:T(8,128)(2,1)S(1)}, u32[]{:S(2)}, u32[]{:S(2)}) collective-permute-start(bf16[2,128,256]{2,1,0:T(8,128)(2,1)S(1)} %get-tuple-element.53), channel_id=1, source_target_pairs={{0,16},{1,17},{2,18},{3,19},{4,20},{5,21},{6,22},{7,23},{8,24},{9,... | collective-permute-start | bytes 393224 | tf_op jit(solution)/shard_map/ppermute | solution.py:726
  47.3 12.3 %collective-permute-start.8 = (bf16[2,128,256]{2,1,0:T(8,128)(2,1)S(1)}, bf16[2,128,256]{2,1,0:T(8,128)(2,1)S(1)}, u32[]{:S(2)}, u32[]{:S(2)}) collective-permute-start(bf16[2,128,256]{2,1,0:T(8,128)(2,1)S(1)} %get-tuple-element.58), channel_id=1, source_target_pairs={{0,4},{1,5},{2,6},{3,7},{4,0},{5,1},{6,2},{7,3},{8,12},{9,13},{10,... | collective-permute-start | bytes 393224 | tf_op jit(solution)/shard_map/ppermute | solution.py:726
  59.7 7.2 %collective-permute-start.10 = (bf16[2,128,256]{2,1,0:T(8,128)(2,1)S(1)}, bf16[2,128,256]{2,1,0:T(8,128)(2,1)S(1)}, u32[]{:S(2)}, u32[]{:S(2)}) collective-permute-start(bf16[2,128,256]{2,1,0:T(8,128)(2,1)S(1)} %add_convert_fusion.2), channel_id=1, source_target_pairs={{0,1},{1,0},{2,3},{3,2},{4,5},{5,4},{6,7},{7,6},{8,9},{9,8},{10,11... | collective-permute-start | bytes 393224 | tf_op jit(solution)/shard_map/ppermute | solution.py:726
  63.6 6.4 %collective-permute-start.11 = (bf16[2,2,128,128]{3,2,1,0:T(8,128)(2,1)S(1)}, bf16[2,2,128,128]{3,2,1,0:T(8,128)(2,1)S(1)}, u32[]{:S(2)}, u32[]{:S(2)}) collective-permute-start(bf16[2,2,128,128]{3,2,1,0:T(8,128)(2,1)S(1)} %get-tuple-element.62), channel_id=1, source_target_pairs={{0,8},{1,9},{2,10},{3,11},{4,12},{5,13},{6,14},{7,15},{8,0},{9,1},... | collective-permute-start | bytes 393224 | tf_op jit(solution)/shard_map/ppermute | solution.py:749
  64.2 18.3 %collective-permute-start.14 = (bf16[2,128,1024]{2,1,0:T(8,128)(2,1)S(1)}, bf16[2,128,1024]{2,1,0:T(8,128)(2,1)S(1)}, u32[]{:S(2)}, u32[]{:S(2)}) collective-permute-start(bf16[2,128,1024]{2,1,0:T(8,128)(2,1)S(1)} %get-tuple-element.68), channel_id=1, source_target_pairs={{0,8},{1,9},{2,10},{3,11},{4,12},{5,13},{6,14},{7,15},{8,0},{9,1},... | collective-permute-start | bytes 1572872 | tf_op jit(solution)/shard_map/ppermute | solution.py:755
  70.1 6.4 %collective-permute-start.12 = (bf16[2,128,256]{2,1,0:T(8,128)(2,1)S(1)}, bf16[2,128,256]{2,1,0:T(8,128)(2,1)S(1)}, u32[]{:S(2)}, u32[]{:S(2)}) collective-permute-start(bf16[2,128,256]{2,1,0:T(8,128)(2,1)S(1)} %add_convert_fusion.1), channel_id=1, source_target_pairs={{0,2},{1,3},{2,0},{3,1},{4,6},{5,7},{6,4},{7,5},{8,10},{9,11},{10,... | collective-permute-start | bytes 393224 | tf_op jit(solution)/shard_map/ppermute | solution.py:726
  70.8 9.6 %collective-permute-start.15 = (bf16[2,512,128]{2,1,0:T(8,128)(2,1)S(1)}, bf16[2,512,128]{2,1,0:T(8,128)(2,1)S(1)}, u32[]{:S(2)}, u32[]{:S(2)}) collective-permute-start(bf16[2,512,128]{2,1,0:T(8,128)(2,1)S(1)} %get-tuple-element.72), channel_id=1, source_target_pairs={{0,1},{1,0},{2,3},{3,2},{4,5},{5,4},{6,7},{7,6},{8,9},{9,8},{10,11... | collective-permute-start | bytes 786440 | tf_op jit(solution)/shard_map/ppermute | solution.py:755
  70.9 9.5 %collective-permute-start.16 = (bf16[2,512,128]{2,1,0:T(8,128)(2,1)S(1)}, bf16[2,512,128]{2,1,0:T(8,128)(2,1)S(1)}, u32[]{:S(2)}, u32[]{:S(2)}) collective-permute-start(bf16[2,512,128]{2,1,0:T(8,128)(2,1)S(1)} %get-tuple-element.73), channel_id=1, source_target_pairs={{1,2},{2,1},{3,4},{4,3},{5,6},{6,5},{9,10},{10,9},{11,12},{12,11},... | collective-permute-start | bytes 786440 | tf_op jit(solution)/shard_map/ppermute | solution.py:755
  76.6 5.9 %collective-permute-start.13 = (bf16[2,128,256]{2,1,0:T(8,128)(2,1)S(1)}, bf16[2,128,256]{2,1,0:T(8,128)(2,1)S(1)}, u32[]{:S(2)}, u32[]{:S(2)}) collective-permute-start(bf16[2,128,256]{2,1,0:T(8,128)(2,1)S(1)} %add_convert_fusion.part), channel_id=1, source_target_pairs={{0,8},{1,9},{2,10},{3,11},{4,12},{5,13},{6,14},{7,15},{8,0},{9,1},... | collective-permute-start | bytes 393224 | tf_op jit(solution)/shard_map/ppermute | solution.py:726
  (3 other events, 3.2 us)

commit v9 on v8

--- a/solution.py
+++ b/solution.py
@@ -719,7 +719,8 @@
     assert rows & (rows - 1) == 0 and cols & (cols - 1) == 0
     tiles = rows * cols
     flips = [1 << k for k in range(cols.bit_length() - 1)]
-    flips = flips[-1:] + flips[:-1] + [cols << k for k in range(rows.bit_length() - 1)]
+    flips = flips[:1] + flips[1:][-1:] + flips[1:-1]
+    flips = [cols << k for k in range(rows.bit_length() - 1)] + flips
 
     def fetched(block, flip):
         pairs = [(i, i ^ flip) for i in range(sections * tiles)]
@@ -750,7 +751,7 @@
     if flips[1:]:
         pair = exchange(summed(pair), flips[1])
     if corners:
-        pair, corners = lax.optimization_barrier((pair, corners))
+        pair, corners, own = lax.optimization_barrier((pair, corners, own))
         own[len(downs) :] = add_corners(tile_at, own[len(downs) :], corners, names, half)
     added = [lax.ppermute(strip, both, path) for strip, path in zip(own, paths)]
     for flip in flips[2:]:

time: 85.6 us -> 80.3 us (0.938)
  waiting for transfers between devices: 26 us -> 21.4 us
    ppermute x6, waiting for transfers between devices: 16.5 us -> 13.2 us  [fetched(): return lax.ppermute(block, ('depth',) + both, pairs)]
    ppermute x1, waiting for transfers between devices: 3.13 us -> 1.66 us  [shards(): corners = [lax.ppermute(x, both, path) for x, path in zip(corners, paths)]]
    ppermute x6, starting transfers between devices: 8.6 us -> 7.48 us  [fetched(): return lax.ppermute(block, ('depth',) + both, pairs)]
  transfers between devices with their start and end apart: 17 -> 17, of which waited for: 8 -> 9; matrix products, arithmetic and copies ran while one was open for 1% -> 1% of each run, Pallas kernels for 9% -> 10%
where the time goes in v9:
time: 80.3 us; the launch traced here: 79.9 us
  Pallas kernels  28.5 us (35%)
  waiting for transfers between devices  21.4 us (27%)
  starting transfers between devices  21.2 us (26%)
  local copies, waits for them, and re-layouts  6.92 us (9%)
  between operations  1 us (1%)
  other arithmetic  0.9 us (1%)
    pallas_call x1, Pallas kernels, chain(): pl.pallas_call(functools.partial(chain_kernel, group), grid=(count // gro...  14.4 us
    ppermute x6, waiting for transfers between devices, fetched(): return lax.ppermute(block, ('depth',) + both, pairs)  13.2 us
    ppermute x5, starting transfers between devices, shards(): lax.ppermute(strip, both, path)  10.2 us
    ppermute x6, starting transfers between devices, fetched(): return lax.ppermute(block, ('depth',) + both, pairs)  7.48 us
    unnamed x21, local copies, waits for them, and re-layouts  6.83 us
    pallas_call x1, Pallas kernels, scatter(): pl.pallas_call(functools.partial(scatter_kernel, edges, names, half), in_...  3.65 us
    pallas_call x1, Pallas kernels, prepare(): pl.pallas_call(prep_kernel, grid_spec=pltpu.PrefetchScalarGridSpec(num_sc...  3.37 us
    ppermute x3, waiting for transfers between devices, shards(): added = [lax.ppermute(strip, both, path) for strip, path in zip(own, paths)]  3.14 us
  transfers between devices with their start and end apart: 17, of which 9 were waited for; matrix products, arithmetic and copies ran while one was open for 1% of the time, Pallas kernels for 10%

profile of v9, /device:TPU:0, one launch (start us, length us, event | category | flops | bytes accessed | tf_op | source)
XLA Modules:
  0.0 79.9 jit_solution(17883014074997069659)
XLA Ops:
  1.3 1.2 %copy-done.1 = bf16[1,512,1024]{2,1,0:T(8,128)(2,1)S(1)} copy-done((bf16[1,512,1024]{2,1,0:T(8,128)(2,1)S(1)}, bf16[1,512,1024]{2,1,0:T(8,128)(2,1)}, u32[]{:S(2)}) %copy-start.1) | copy-done | bytes 1048600
  2.5 1.2 %copy-done.3 = bf16[1,512,1024]{2,1,0:T(8,128)(2,1)S(1)} copy-done((bf16[1,512,1024]{2,1,0:T(8,128)(2,1)S(1)}, bf16[1,512,1024]{2,1,0:T(8,128)(2,1)}, u32[]{:S(2)}) %copy-start.3) | copy-done | bytes 1048600
  3.7 1.5 %pack.1 = (bf16[2,128,1024]{2,1,0:T(8,128)(2,1)S(1)}, bf16[2,512,128]{2,1,0:T(8,128)(2,1)}, bf16[2,512,128]{2,1,0:T(8,128)(2,1)}, bf16[2,128,128]{2,1,0:T(8,128)(2,1)}, bf16[2,128,128]{2,1,0:T(8,128)(2,1)}) custom-call(s32[4]{0:T(128)S(1)} %get-tuple-element.86.offsets, bf16[1,512,1024]{2,1,0:T(8,128)(2,1)S(1)} %copy-done.1, bf16[1,512,1024]{2,1,0:T(8,128)(2,1)S(1)} %copy-done.3), custom_call_target="tpu_custom_call" | custom-call | tf_op jit(solution)/shard_map/pack/pallas_call | solution.py:185
  5.2 3.0 %collective-permute-start = (bf16[2,128,1024]{2,1,0:T(8,128)(2,1)S(1)}, bf16[2,128,1024]{2,1,0:T(8,128)(2,1)S(1)}, u32[]{:S(2)}, u32[]{:S(2)}) collective-permute-start(bf16[2,128,1024]{2,1,0:T(8,128)(2,1)S(1)} %get-tuple-element.42.after), channel_id=1, source_target_pairs={{0,8},{1,9},{2,10},{3,11},{4,12},{5,13},{6,14},{7,15},{8,0},{9,1},... | collective-permute-start | bytes 1572872 | tf_op jit(solution)/shard_map/ppermute | solution.py:707
  8.2 1.5 %collective-permute-start.1 = (bf16[2,512,128]{2,1,0:T(8,128)(2,1)}, bf16[2,512,128]{2,1,0:T(8,128)(2,1)S(1)}, u32[]{:S(2)}, u32[]{:S(2)}) collective-permute-start(bf16[2,512,128]{2,1,0:T(8,128)(2,1)} %get-tuple-element.45), channel_id=1, source_target_pairs={{0,1},{1,0},{2,3},{3,2},{4,5},{5,4},{6,7},{7,6},{8,9},{9,8},{10,11... | collective-permute-start | bytes 786440 | tf_op jit(solution)/shard_map/ppermute | solution.py:707
  9.8 1.4 %collective-permute-start.2 = (bf16[2,512,128]{2,1,0:T(8,128)(2,1)}, bf16[2,512,128]{2,1,0:T(8,128)(2,1)}, u32[]{:S(2)}, u32[]{:S(2)}) collective-permute-start(bf16[2,512,128]{2,1,0:T(8,128)(2,1)} %get-tuple-element.46), channel_id=1, source_target_pairs={{1,2},{2,1},{3,4},{4,3},{5,6},{6,5},{9,10},{10,9},{11,12},{12,11},... | collective-permute-start | bytes 786440 | tf_op jit(solution)/shard_map/ppermute | solution.py:707
  11.1 3.6 %collective-permute-start.3 = (bf16[2,128,128]{2,1,0:T(8,128)(2,1)}, bf16[2,128,128]{2,1,0:T(8,128)(2,1)S(1)}, u32[]{:S(2)}, u32[]{:S(2)}) collective-permute-start(bf16[2,128,128]{2,1,0:T(8,128)(2,1)} %get-tuple-element.47), channel_id=1, source_target_pairs={{0,9},{1,8},{2,11},{3,10},{4,13},{5,12},{6,15},{7,14},{8,1},{9,0},... | collective-permute-start | bytes 196616 | tf_op jit(solution)/shard_map/ppermute | solution.py:707
  16.4 1.6 %copy-done = f32[1,1,4,2,256,256]{5,4,3,2,1,0:T(8,128)S(1)} copy-done((f32[1,1,4,2,256,256]{5,4,3,2,1,0:T(8,128)S(1)}, f32[1,1,4,2,256,256]{5,4,3,2,1,0:T(8,128)}, u32[]{:S(2)}) %copy-start) | copy-done | bytes 2097176
  18.9 1.0 %copy-done.7 = f32[2,256,256]{2,1,0:T(8,128)S(1)} copy-done((f32[2,256,256]{2,1,0:T(8,128)S(1)}, f32[2,256,256]{2,1,0:T(8,128)}, u32[]{:S(2)}) %copy-start.7) | copy-done | bytes 524312
  19.9 3.4 %prepare.1 = (f32[2,256,256]{2,1,0:T(8,128)S(1)}, f32[4,256,256]{2,1,0:T(8,128)S(1)}, f32[4,2,256,256]{3,2,1,0:T(8,128)S(1)}) custom-call(s32[16]{0:T(128)S(1)} %reshape.13.places, s32[4]{0:T(128)S(1)} %add_add_fusion.offsets, bf16[2,128,1024]{2,1,0:T(8,128)(2,1)S(1)} %get-tuple-element.42.after, f32[2,256,256]{2,1,0:T(8,128)S(1)} %copy-done.7, ...), custom_call_target="tpu_custom_call" | custom-call | tf_op jit(solution)/shard_map/prepare/pallas_call | solution.py:109
  23.8 2.4 %gather.1 = (bf16[4,2,256,256]{3,2,1,0:T(8,128)(2,1)S(1)}, bf16[4,2,256,256]{3,2,1,0:T(8,128)(2,1)S(1)}) custom-call(s32[16]{0:T(128)S(1)} %reshape.13.places, s32[4]{0:T(128)S(1)} %add_add_fusion.offsets, bf16[1,512,1024]{2,1,0:T(8,128)(2,1)S(1)} %copy-done.2, bf16[1,512,1024]{2,1,0:T(8,128)(2,1)S(1)} %copy-done.4, ...), custom_call_target="tpu_custom_call" | custom-call | tf_op jit(solution)/shard_map/gather/pallas_call | solution.py:270
  26.3 2.6 %collective-permute-done.5.theirs = bf16[4,2,256,256]{3,2,1,0:T(8,128)(2,1)S(1)} collective-permute-done((bf16[4,2,256,256]{3,2,1,0:T(8,128)(2,1)S(1)}, bf16[4,2,256,256]{3,2,1,0:T(8,128)(2,1)S(1)}, u32[]{:S(2)}, u32[]{:S(2)}) %collective-permute-start.5) | collective-permute-done | bytes 1048608 | tf_op jit(solution)/shard_map/ppermute | solution.py:713
  28.9 14.4 %chain.1 = (bf16[4,2,256,256]{3,2,1,0:T(8,128)(2,1)S(1)}, bf16[4,2,256,256]{3,2,1,0:T(8,128)(2,1)S(1)}, bf16[2,128,256]{2,1,0:T(8,128)(2,1)S(1)}, bf16[2,128,256]{2,1,0:T(8,128)(2,1)S(1)}) custom-call(s32[16]{0:T(128)S(1)} %reshape.13.places, s32[4]{0:T(128)S(1)} %bitcast.15, s32[4]{0:T(128)S(1)} %add_add_fusion.offsets, ...), custom_call_target="tpu_custom_call" | custom-call | tf_op jit(solution)/shard_map/chain/pallas_call | solution.py:432
  43.6 1.1 %collective-permute-start.9 = (bf16[2,128,256]{2,1,0:T(8,128)(2,1)S(1)}, bf16[2,128,256]{2,1,0:T(8,128)(2,1)S(1)}, u32[]{:S(2)}, u32[]{:S(2)}) collective-permute-start(bf16[2,128,256]{2,1,0:T(8,128)(2,1)S(1)} %get-tuple-element.56), channel_id=1, source_target_pairs={{0,24},{1,25},{2,26},{3,27},{4,28},{5,29},{6,30},{7,31},{8,16},{9,... | collective-permute-start | bytes 393224 | tf_op jit(solution)/shard_map/ppermute | solution.py:727
  46.1 3.7 %scatter.1 = (f32[2,512,1024]{2,1,0:T(8,128)}, f32[2,128,1024]{2,1,0:T(8,128)S(1)}, f32[2,384,128]{2,1,0:T(8,128)S(1)}, f32[2,384,128]{2,1,0:T(8,128)S(1)}, bf16...) custom-call(s32[16]{0:T(128)S(1)} %reshape.13.places, ...), custom_call_target="tpu_custom_call" | custom-call | bytes 8388608 | tf_op jit(solution)/shard_map/scatter/pallas_call | solution.py:548
  49.7 2.4 %collective-permute-done.8 = bf16[2,128,256]{2,1,0:T(8,128)(2,1)S(1)} collective-permute-done((bf16[2,128,256]{2,1,0:T(8,128)(2,1)S(1)}, bf16[2,128,256]{2,1,0:T(8,128)(2,1)S(1)}, u32[]{:S(2)}, u32[]{:S(2)}) %collective-permute-start.8) | collective-permute-done | bytes 131104 | tf_op jit(solution)/shard_map/ppermute | solution.py:727
  52.3 4.9 %collective-permute-start.10 = (bf16[2,128,256]{2,1,0:T(8,128)(2,1)S(1)}, bf16[2,128,256]{2,1,0:T(8,128)(2,1)S(1)}, u32[]{:S(2)}, u32[]{:S(2)}) collective-permute-start(bf16[2,128,256]{2,1,0:T(8,128)(2,1)S(1)} %add_convert_fusion.2), channel_id=1, source_target_pairs={{0,1},{1,0},{2,3},{3,2},{4,5},{5,4},{6,7},{7,6},{8,9},{9,8},{10,11... | collective-permute-start | bytes 393224 | tf_op jit(solution)/shard_map/ppermute | solution.py:727
  57.7 2.8 %collective-permute-done.10 = bf16[2,128,256]{2,1,0:T(8,128)(2,1)S(1)} collective-permute-done((bf16[2,128,256]{2,1,0:T(8,128)(2,1)S(1)}, bf16[2,128,256]{2,1,0:T(8,128)(2,1)S(1)}, u32[]{:S(2)}, u32[]{:S(2)}) %collective-permute-start.10) | collective-permute-done | bytes 131104 | tf_op jit(solution)/shard_map/ppermute | solution.py:727
  60.4 1.7 %collective-permute-done.11.refs_0_ = bf16[2,2,128,128]{3,2,1,0:T(8,128)(2,1)S(1)} collective-permute-done((bf16[2,2,128,128]{3,2,1,0:T(8,128)(2,1)S(1)}, bf16[2,2,128,128]{3,2,1,0:T(8,128)(2,1)S(1)}, u32[]{:S(2)}, u32[]{:S(2)}) %collective-permute-start.11) | collective-permute-done | bytes 131104 | tf_op jit(solution)/shard_map/ppermute | solution.py:750
  63.5 1.5 %collective-permute-start.15 = (bf16[2,512,128]{2,1,0:T(8,128)(2,1)S(1)}, bf16[2,512,128]{2,1,0:T(8,128)(2,1)S(1)}, u32[]{:S(2)}, u32[]{:S(2)}) collective-permute-start(bf16[2,512,128]{2,1,0:T(8,128)(2,1)S(1)} %get-tuple-element.78), channel_id=1, source_target_pairs={{0,1},{1,0},{2,3},{3,2},{4,5},{5,4},{6,7},{7,6},{8,9},{9,8},{10,11... | collective-permute-start | bytes 786440 | tf_op jit(solution)/shard_map/ppermute | solution.py:756
  65.7 4.7 %collective-permute-done.12 = bf16[2,128,256]{2,1,0:T(8,128)(2,1)S(1)} collective-permute-done((bf16[2,128,256]{2,1,0:T(8,128)(2,1)S(1)}, bf16[2,128,256]{2,1,0:T(8,128)(2,1)S(1)}, u32[]{:S(2)}, u32[]{:S(2)}) %collective-permute-start.12) | collective-permute-done | bytes 131104 | tf_op jit(solution)/shard_map/ppermute | solution.py:727
  70.6 3.1 %collective-permute-done.15.rest_4_ = bf16[2,512,128]{2,1,0:T(8,128)(2,1)S(1)} collective-permute-done((bf16[2,512,128]{2,1,0:T(8,128)(2,1)S(1)}, bf16[2,512,128]{2,1,0:T(8,128)(2,1)S(1)}, u32[]{:S(2)}, u32[]{:S(2)}) %collective-permute-start.15) | collective-permute-done | bytes 262176 | tf_op jit(solution)/shard_map/ppermute | solution.py:756
  73.8 3.3 %collective-permute-done.13.other = bf16[2,128,256]{2,1,0:T(8,128)(2,1)S(1)} collective-permute-done((bf16[2,128,256]{2,1,0:T(8,128)(2,1)S(1)}, bf16[2,128,256]{2,1,0:T(8,128)(2,1)S(1)}, u32[]{:S(2)}, u32[]{:S(2)}) %collective-permute-start.13) | collective-permute-done | bytes 131104 | tf_op jit(solution)/shard_map/ppermute | solution.py:727
  77.1 2.6 %borders.1 = (f32[2,512,1024]{2,1,0:T(8,128)}, f32[2,128,256]{2,1,0:T(8,128)}) custom-call(s32[4]{0:T(128)S(1)} %pad_add_fusion.folds, f32[2,512,1024]{2,1,0:T(8,128)} %get-tuple-element.54.tile_in, bf16[2,128,256]{2,1,0:T(8,128)(2,1)S(1)} %add_convert_fusion.part, ...), custom_call_target="tpu_custom_call", output_to_operand_aliasing={{0}: (1, {})} | custom-call | tf_op jit(solution)/shard_map/borders/pallas_call | solution.py:627
  (45 shorter events, 8.2 us)
Async XLA Ops:
  1.3 1.2 %copy-start.1 = (bf16[1,512,1024]{2,1,0:T(8,128)(2,1)S(1)}, bf16[1,512,1024]{2,1,0:T(8,128)(2,1)}, u32[]{:S(2)}) copy-start(bf16[1,512,1024]{2,1,0:T(8,128)(2,1)} %tile_re.3) | copy-start | bytes 3145732
  3.7 20.1 %copy-start.2 = (bf16[1,512,1024]{2,1,0:T(8,128)(2,1)S(1)}, bf16[1,512,1024]{2,1,0:T(8,128)(2,1)}, u32[]{:S(2)}) copy-start(bf16[1,512,1024]{2,1,0:T(8,128)(2,1)} %tile_re.3) | copy-start | bytes 3145732
  3.7 20.1 %copy-start.4 = (bf16[1,512,1024]{2,1,0:T(8,128)(2,1)S(1)}, bf16[1,512,1024]{2,1,0:T(8,128)(2,1)}, u32[]{:S(2)}) copy-start(bf16[1,512,1024]{2,1,0:T(8,128)(2,1)} %tile_im.3) | copy-start | bytes 3145732
  5.2 18.6 %collective-permute-start = (bf16[2,128,1024]{2,1,0:T(8,128)(2,1)S(1)}, bf16[2,128,1024]{2,1,0:T(8,128)(2,1)S(1)}, u32[]{:S(2)}, u32[]{:S(2)}) collective-permute-start(bf16[2,128,1024]{2,1,0:T(8,128)(2,1)S(1)} %get-tuple-element.42.after), channel_id=1, source_target_pairs={{0,8},{1,9},{2,10},{3,11},{4,12},{5,13},{6,14},{7,15},{8,0},{9,1},... | collective-permute-start | bytes 1572872 | tf_op jit(solution)/shard_map/ppermute | solution.py:707
  8.2 15.5 %collective-permute-start.1 = (bf16[2,512,128]{2,1,0:T(8,128)(2,1)}, bf16[2,512,128]{2,1,0:T(8,128)(2,1)S(1)}, u32[]{:S(2)}, u32[]{:S(2)}) collective-permute-start(bf16[2,512,128]{2,1,0:T(8,128)(2,1)} %get-tuple-element.45), channel_id=1, source_target_pairs={{0,1},{1,0},{2,3},{3,2},{4,5},{5,4},{6,7},{7,6},{8,9},{9,8},{10,11... | collective-permute-start | bytes 786440 | tf_op jit(solution)/shard_map/ppermute | solution.py:707
  9.8 14.0 %collective-permute-start.2 = (bf16[2,512,128]{2,1,0:T(8,128)(2,1)}, bf16[2,512,128]{2,1,0:T(8,128)(2,1)}, u32[]{:S(2)}, u32[]{:S(2)}) collective-permute-start(bf16[2,512,128]{2,1,0:T(8,128)(2,1)} %get-tuple-element.46), channel_id=1, source_target_pairs={{1,2},{2,1},{3,4},{4,3},{5,6},{6,5},{9,10},{10,9},{11,12},{12,11},... | collective-permute-start | bytes 786440 | tf_op jit(solution)/shard_map/ppermute | solution.py:707
  11.1 12.2 %collective-permute-start.3 = (bf16[2,128,128]{2,1,0:T(8,128)(2,1)}, bf16[2,128,128]{2,1,0:T(8,128)(2,1)S(1)}, u32[]{:S(2)}, u32[]{:S(2)}) collective-permute-start(bf16[2,128,128]{2,1,0:T(8,128)(2,1)} %get-tuple-element.47), channel_id=1, source_target_pairs={{0,9},{1,8},{2,11},{3,10},{4,13},{5,12},{6,15},{7,14},{8,1},{9,0},... | collective-permute-start | bytes 196616 | tf_op jit(solution)/shard_map/ppermute | solution.py:707
  14.7 8.6 %collective-permute-start.4 = (bf16[2,128,128]{2,1,0:T(8,128)(2,1)}, bf16[2,128,128]{2,1,0:T(8,128)(2,1)S(1)}, u32[]{:S(2)}, u32[]{:S(2)}) collective-permute-start(bf16[2,128,128]{2,1,0:T(8,128)(2,1)} %get-tuple-element.48), channel_id=1, source_target_pairs={{1,10},{2,9},{3,12},{4,11},{5,14},{6,13},{9,2},{10,1},{11,4},{12,3... | collective-permute-start | bytes 196616 | tf_op jit(solution)/shard_map/ppermute | solution.py:707
  16.4 1.6 %copy-start = (f32[1,1,4,2,256,256]{5,4,3,2,1,0:T(8,128)S(1)}, f32[1,1,4,2,256,256]{5,4,3,2,1,0:T(8,128)}, u32[]{:S(2)}) copy-start(f32[1,1,4,2,256,256]{5,4,3,2,1,0:T(8,128)} %param.14) | copy-start | bytes 6291460
  19.9 9.0 %copy-start.6 = (bf16[4,2,256,256]{3,2,1,0:T(8,128)(2,1)S(1)}, bf16[4,2,256,256]{3,2,1,0:T(8,128)(2,1)}, u32[]{:S(2)}) copy-start(bf16[4,2,256,256]{3,2,1,0:T(8,128)(2,1)} %constant.46.clone.tables) | copy-start | bytes 3145732
  19.9 9.0 %copy-start.8 = (s32[1,1,4]{2,1,0:T(1,128)S(1)}, s32[1,1,4]{2,1,0:T(1,128)}, u32[]{:S(2)}) copy-start(s32[1,1,4]{2,1,0:T(1,128)} %param.13) | copy-start | bytes 52
  26.2 19.5 %copy-start.9 = (s32[4]{0:T(128)S(1)}, s32[4]{0:T(128)}, u32[]{:S(2)}) copy-start(s32[4]{0:T(128)} %get-tuple-element.87) | copy-start | bytes 52
  26.2 2.7 %collective-permute-start.5 = (bf16[4,2,256,256]{3,2,1,0:T(8,128)(2,1)S(1)}, bf16[4,2,256,256]{3,2,1,0:T(8,128)(2,1)S(1)}, u32[]{:S(2)}, u32[]{:S(2)}) collective-permute-start(bf16[4,2,256,256]{3,2,1,0:T(8,128)(2,1)S(1)} %get-tuple-element.50), channel_id=1, source_target_pairs={{0,16},{16,0},{1,17},{17,1},{2,18},{18,2},{3,19},{19,3},{4,20},{20... | collective-permute-start | bytes 3145736 | tf_op jit(solution)/shard_map/ppermute | solution.py:713
  43.3 2.7 %collective-permute-start.6 = (bf16[4,2,256,256]{3,2,1,0:T(8,128)(2,1)S(1)}, bf16[4,2,256,256]{3,2,1,0:T(8,128)(2,1)S(1)}, u32[]{:S(2)}, u32[]{:S(2)}) collective-permute-start(bf16[4,2,256,256]{3,2,1,0:T(8,128)(2,1)S(1)} %get-tuple-element.53), channel_id=1, source_target_pairs={{0,16},{16,0},{1,17},{17,1},{2,18},{18,2},{3,19},{19,3},{4,20},{20... | collective-permute-start | bytes 3145736 | tf_op jit(solution)/shard_map/ppermute | solution.py:717
  43.6 8.6 %collective-permute-start.9 = (bf16[2,128,256]{2,1,0:T(8,128)(2,1)S(1)}, bf16[2,128,256]{2,1,0:T(8,128)(2,1)S(1)}, u32[]{:S(2)}, u32[]{:S(2)}) collective-permute-start(bf16[2,128,256]{2,1,0:T(8,128)(2,1)S(1)} %get-tuple-element.56), channel_id=1, source_target_pairs={{0,24},{1,25},{2,26},{3,27},{4,28},{5,29},{6,30},{7,31},{8,16},{9,... | collective-permute-start | bytes 393224 | tf_op jit(solution)/shard_map/ppermute | solution.py:727
  44.6 7.5 %collective-permute-start.7 = (bf16[2,128,256]{2,1,0:T(8,128)(2,1)S(1)}, bf16[2,128,256]{2,1,0:T(8,128)(2,1)S(1)}, u32[]{:S(2)}, u32[]{:S(2)}) collective-permute-start(bf16[2,128,256]{2,1,0:T(8,128)(2,1)S(1)} %get-tuple-element.56), channel_id=1, source_target_pairs={{0,16},{1,17},{2,18},{3,19},{4,20},{5,21},{6,22},{7,23},{8,24},{9,... | collective-permute-start | bytes 393224 | tf_op jit(solution)/shard_map/ppermute | solution.py:727
  44.8 7.4 %collective-permute-start.8 = (bf16[2,128,256]{2,1,0:T(8,128)(2,1)S(1)}, bf16[2,128,256]{2,1,0:T(8,128)(2,1)S(1)}, u32[]{:S(2)}, u32[]{:S(2)}) collective-permute-start(bf16[2,128,256]{2,1,0:T(8,128)(2,1)S(1)} %get-tuple-element.61), channel_id=1, source_target_pairs={{0,8},{1,9},{2,10},{3,11},{4,12},{5,13},{6,14},{7,15},{8,0},{9,1},... | collective-permute-start | bytes 393224 | tf_op jit(solution)/shard_map/ppermute | solution.py:727
  52.3 8.2 %collective-permute-start.10 = (bf16[2,128,256]{2,1,0:T(8,128)(2,1)S(1)}, bf16[2,128,256]{2,1,0:T(8,128)(2,1)S(1)}, u32[]{:S(2)}, u32[]{:S(2)}) collective-permute-start(bf16[2,128,256]{2,1,0:T(8,128)(2,1)S(1)} %add_convert_fusion.2), channel_id=1, source_target_pairs={{0,1},{1,0},{2,3},{3,2},{4,5},{5,4},{6,7},{7,6},{8,9},{9,8},{10,11... | collective-permute-start | bytes 393224 | tf_op jit(solution)/shard_map/ppermute | solution.py:727
  57.1 5.0 %collective-permute-start.11 = (bf16[2,2,128,128]{3,2,1,0:T(8,128)(2,1)S(1)}, bf16[2,2,128,128]{3,2,1,0:T(8,128)(2,1)S(1)}, u32[]{:S(2)}, u32[]{:S(2)}) collective-permute-start(bf16[2,2,128,128]{3,2,1,0:T(8,128)(2,1)S(1)} %get-tuple-element.65), channel_id=1, source_target_pairs={{0,8},{1,9},{2,10},{3,11},{4,12},{5,13},{6,14},{7,15},{8,0},{9,1},... | collective-permute-start | bytes 393224 | tf_op jit(solution)/shard_map/ppermute | solution.py:750
  62.1 15.0 %collective-permute-start.14 = (bf16[2,128,1024]{2,1,0:T(8,128)(2,1)S(1)}, bf16[2,128,1024]{2,1,0:T(8,128)(2,1)S(1)}, u32[]{:S(2)}, u32[]{:S(2)}) collective-permute-start(bf16[2,128,1024]{2,1,0:T(8,128)(2,1)S(1)} %get-tuple-element.74), channel_id=1, source_target_pairs={{0,8},{1,9},{2,10},{3,11},{4,12},{5,13},{6,14},{7,15},{8,0},{9,1},... | collective-permute-start | bytes 1572872 | tf_op jit(solution)/shard_map/ppermute | solution.py:756
  62.7 7.7 %collective-permute-start.12 = (bf16[2,128,256]{2,1,0:T(8,128)(2,1)S(1)}, bf16[2,128,256]{2,1,0:T(8,128)(2,1)S(1)}, u32[]{:S(2)}, u32[]{:S(2)}) collective-permute-start(bf16[2,128,256]{2,1,0:T(8,128)(2,1)S(1)} %add_convert_fusion.1), channel_id=1, source_target_pairs={{0,4},{1,5},{2,6},{3,7},{4,0},{5,1},{6,2},{7,3},{8,12},{9,13},{10,... | collective-permute-start | bytes 393224 | tf_op jit(solution)/shard_map/ppermute | solution.py:727
  63.5 10.3 %collective-permute-start.15 = (bf16[2,512,128]{2,1,0:T(8,128)(2,1)S(1)}, bf16[2,512,128]{2,1,0:T(8,128)(2,1)S(1)}, u32[]{:S(2)}, u32[]{:S(2)}) collective-permute-start(bf16[2,512,128]{2,1,0:T(8,128)(2,1)S(1)} %get-tuple-element.78), channel_id=1, source_target_pairs={{0,1},{1,0},{2,3},{3,2},{4,5},{5,4},{6,7},{7,6},{8,9},{9,8},{10,11... | collective-permute-start | bytes 786440 | tf_op jit(solution)/shard_map/ppermute | solution.py:756
  65.0 8.8 %collective-permute-start.16 = (bf16[2,512,128]{2,1,0:T(8,128)(2,1)S(1)}, bf16[2,512,128]{2,1,0:T(8,128)(2,1)S(1)}, u32[]{:S(2)}, u32[]{:S(2)}) collective-permute-start(bf16[2,512,128]{2,1,0:T(8,128)(2,1)S(1)} %get-tuple-element.79), channel_id=1, source_target_pairs={{1,2},{2,1},{3,4},{4,3},{5,6},{6,5},{9,10},{10,9},{11,12},{12,11},... | collective-permute-start | bytes 786440 | tf_op jit(solution)/shard_map/ppermute | solution.py:756
  70.4 6.7 %collective-permute-start.13 = (bf16[2,128,256]{2,1,0:T(8,128)(2,1)S(1)}, bf16[2,128,256]{2,1,0:T(8,128)(2,1)S(1)}, u32[]{:S(2)}, u32[]{:S(2)}) collective-permute-start(bf16[2,128,256]{2,1,0:T(8,128)(2,1)S(1)} %add_convert_fusion.part), channel_id=1, source_target_pairs={{0,2},{1,3},{2,0},{3,1},{4,6},{5,7},{6,4},{7,5},{8,10},{9,11},{10,... | collective-permute-start | bytes 393224 | tf_op jit(solution)/shard_map/ppermute | solution.py:727
  (3 other events, 3.2 us)

commit v10 on v9

--- a/solution.py
+++ b/solution.py
@@ -62,37 +62,38 @@
     return jnp.concatenate(parts, axis=1)
 
 
-def prep_kernel(places, offsets, after, probe, *refs):
+def set_order(order):
+    size = order.shape[0]
+    half = size // 2
+    source = lax.broadcasted_iota(jnp.int32, (size, size), 0)
+    target = lax.broadcasted_iota(jnp.int32, (size, size), 1)
+    chosen = source == 2 * (target % half) + target // half
+    order[...] = jnp.where(chosen, 1.0, 0.0).astype(bf16)
+
+
+def in_order(parts, at, order):
+    half = order.shape[0] // 2
+    ids = [at + (pl.ds(start, half, stride=2), slice(None)) for start in range(2)]
+    rows = rows_of(*(cols_of(*(part[i] for part in parts)) for i in ids))
+    first, rest = split(rows)
+    second, third = split(rows - first.astype(f32))
+    table = order[...]
+    return jnp.dot(
+        cols_of(first, second, third), rows_of(table, table, table), preferred_element_type=f32
+    )
+
+
+def wave_kernel(places, offsets, after, probe, *refs):
     step = pl.program_id(0)
-    size = probe.shape[-1]
-    half = size // 2
-    blocks = size // LANES
-    phases, frames = refs[:blocks], refs[blocks : 2 * blocks]
-    kern, sorted_frames, waves, order = refs[2 * blocks :]
-
-    def halved(parts, at):
-        ids = [at + (pl.ds(start, half, stride=2), slice(None)) for start in range(2)]
-        return rows_of(*(cols_of(*(part[i] for part in parts)) for i in ids))
-
-    def in_order(rows):
-        first, rest = split(rows)
-        second, third = split(rows - first.astype(f32))
-        table = order[...]
-        return jnp.dot(
-            cols_of(first, second, third), rows_of(table, table, table), preferred_element_type=f32
-        )
+    phases, (kern, waves, order) = refs[:-3], refs[-3:]
 
     @pl.when(step == 0)
     def _():
-        source = lax.broadcasted_iota(jnp.int32, (size, size), 0)
-        target = lax.broadcasted_iota(jnp.int32, (size, size), 1)
-        chosen = source == 2 * (target % half) + target // half
-        order[...] = jnp.where(chosen, 1.0, 0.0).astype(bf16)
-        angles = in_order(halved(phases, ()))
+        set_order(order)
+        angles = in_order(phases, (), order)
         kern[0] = jnp.cos(angles)
         kern[1] = jnp.sin(angles)
 
-    sorted_frames[0] = in_order(halved(frames, (0, 0)))
     at = 2 * step + offsets[offsets.shape[0] - 1]
     down = places[2 * at] % ROWS
     across = places[2 * at + 1] % LANES
@@ -101,13 +102,22 @@
         waves[0, plane] = pltpu.roll(moved, down, axis=0)
 
 
-def prepare(places, offsets, after, probe, phases, frames):
-    count, sections, size = frames.shape[:3]
+def frame_kernel(offsets, after, *refs):
+    frames, (sorted_frames, order) = refs[:-2], refs[-2:]
+
+    @pl.when(pl.program_id(0) == 0)
+    def _():
+        set_order(order)
+
+    sorted_frames[0] = in_order(frames, (0, 0), order)
+
+
+def shifted_waves(places, offsets, after, probe, phases, count):
+    size = phases.shape[-1]
     blocks = size // LANES
-    last = offsets.shape[0] - 1
     full = lambda *shape: pl.BlockSpec(shape, lambda i, p, o: (0,) * len(shape))
     return pl.pallas_call(
-        prep_kernel,
+        wave_kernel,
         grid_spec=pltpu.PrefetchScalarGridSpec(
             num_scalar_prefetch=2,
             grid=(count,),
@@ -118,34 +128,47 @@
                     pl.BlockSpec((size, LANES), lambda i, p, o, b=b: (0, b))
                     for b in range(blocks)
                 ),
-                *(
-                    pl.BlockSpec((1, 1, size, LANES), lambda i, p, o, b=b: (i, o[last], 0, b))
-                    for b in range(blocks)
-                ),
             ],
             out_specs=[
                 full(2, size, size),
-                pl.BlockSpec((1, size, size), lambda i, p, o: (i, 0, 0)),
                 pl.BlockSpec((1, 2, size, size), lambda i, p, o: (i, 0, 0, 0)),
             ],
             scratch_shapes=[pltpu.VMEM((size, size), bf16)],
         ),
         out_shape=[
             jax.ShapeDtypeStruct((2, size, size), f32),
-            jax.ShapeDtypeStruct((count, size, size), f32),
             jax.ShapeDtypeStruct((count, 2, size, size), f32),
         ],
         compiler_params=pltpu.CompilerParams(vmem_limit_bytes=16 * MIB),
         cost_estimate=pl.CostEstimate(flops=0, bytes_accessed=0, transcendentals=0),
-        name="prepare",
-    )(
-        places,
-        offsets,
-        after,
-        probe,
-        *[phases] * blocks,
-        *[frames] * blocks,
-    )
+        name="waves",
+    )(places, offsets, after, probe, *[phases] * blocks)
+
+
+def sorted_intensities(offsets, after, frames):
+    count, sections, size = frames.shape[:3]
+    blocks = size // LANES
+    last = offsets.shape[0] - 1
+    return pl.pallas_call(
+        frame_kernel,
+        grid_spec=pltpu.PrefetchScalarGridSpec(
+            num_scalar_prefetch=1,
+            grid=(count,),
+            in_specs=[
+                ANY,
+                *(
+                    pl.BlockSpec((1, 1, size, LANES), lambda i, o, b=b: (i, o[last], 0, b))
+                    for b in range(blocks)
+                ),
+            ],
+            out_specs=pl.BlockSpec((1, size, size), lambda i, o: (i, 0, 0)),
+            scratch_shapes=[pltpu.VMEM((size, size), bf16)],
+        ),
+        out_shape=jax.ShapeDtypeStruct((count, size, size), f32),
+        compiler_params=pltpu.CompilerParams(vmem_limit_bytes=16 * MIB),
+        cost_estimate=pl.CostEstimate(flops=0, bytes_accessed=0, transcendentals=0),
+        name="frames",
+    )(offsets, after, *[frames] * blocks)
 
 
 def span(key, offsets, names, half, whole):
@@ -705,12 +728,13 @@
     fold_at = numbers(*(tile_at[k] for k in range(len(names))), first_row)
     own = pack(tile_at, object_re, object_im, edges, names, half)
     strips = [lax.ppermute(strip, both, path) for strip, path in zip(own, paths)]
-    kern, sorted_frames, waves = prepare(places, padded_at, own[0], probe, phases, frames)
+    kern, waves = shifted_waves(places, padded_at, own[0], probe, phases, count)
     mine, other = gather(
         places, padded_at, object_re, object_im, waves, edges, names, strips, size
     )
     across_depth = [(i, 1 - i) for i in range(sections)]
     theirs = lax.ppermute(other, "depth", across_depth)
+    sorted_frames = sorted_intensities(padded_at, mine, frames)
     keep, send, own_rows, other_rows = chain(
         places, live_counts, padded_at, kern, mine, theirs, sorted_frames, waves, count
     )

time: 80.3 us -> 79.9 us (level)
  Pallas kernels: 28.5 us -> 30 us
  waiting for transfers between devices: 21.4 us -> 20 us
    ppermute x6, waiting for transfers between devices: 13.2 us -> 9.6 us  [fetched(): return lax.ppermute(block, ('depth',) + both, pairs)]
    ppermute x3, waiting for transfers between devices: 3.14 us -> 5.24 us  [shards(): added = [lax.ppermute(strip, both, path) for strip, path in zip(own, paths)]]
    ppermute x5, waiting for transfers between devices: 0.44 us -> 2.46 us  [shards(): lax.ppermute(strip, both, path)]
    ppermute x1, waiting for transfers between devices: 2.65 us -> 0.73 us  [shards(): theirs = lax.ppermute(other, 'depth', across_depth)]
    pallas_call x1 -> x2, Pallas kernels: 3.37 us -> 4.87 us  [the longest x1 2.97 us: shifted_waves(): pl.pallas_call(wave_kernel, grid_spec=pltpu.PrefetchScalarGridSpec(num_sc...]
    unnamed x21 -> x19, local copies, waits for them, and re-layouts: 6.83 us -> 6.46 us
  transfers between devices with their start and end apart: 17 -> 17, of which waited for: 9 -> 10; matrix products, arithmetic and copies ran while one was open for 1% -> 1% of each run, Pallas kernels for 10% -> 11%
where the time goes in v10:
time: 79.9 us; the launch traced here: 79.6 us
  Pallas kernels  30 us (38%)
  starting transfers between devices  21.7 us (27%)
  waiting for transfers between devices  20 us (25%)
  local copies, waits for them, and re-layouts  6.55 us (8%)
  between operations  1.01 us (1%)
    pallas_call x1, Pallas kernels, chain(): pl.pallas_call(functools.partial(chain_kernel, group), grid=(count // gro...  14.4 us
    ppermute x5, starting transfers between devices, shards(): lax.ppermute(strip, both, path)  10.2 us
    ppermute x6, waiting for transfers between devices, fetched(): return lax.ppermute(block, ('depth',) + both, pairs)  9.6 us
    ppermute x6, starting transfers between devices, fetched(): return lax.ppermute(block, ('depth',) + both, pairs)  8.21 us
    unnamed x19, local copies, waits for them, and re-layouts  6.46 us
    ppermute x3, waiting for transfers between devices, shards(): added = [lax.ppermute(strip, both, path) for strip, path in zip(own, paths)]  5.24 us
    pallas_call x1, Pallas kernels, scatter(): pl.pallas_call(functools.partial(scatter_kernel, edges, names, half), in_...  3.46 us
    pallas_call x1, Pallas kernels, shifted_waves(): pl.pallas_call(wave_kernel, grid_spec=pltpu.PrefetchScalarGridSpec(num_sc...  2.97 us
  transfers between devices with their start and end apart: 17, of which 10 were waited for; matrix products, arithmetic and copies ran while one was open for 1% of the time, Pallas kernels for 11%

profile of v10, /device:TPU:0, one launch (start us, length us, event | category | flops | bytes accessed | tf_op | source)
XLA Modules:
  0.0 79.6 jit_solution(12801939721778399747)
XLA Ops:
  0.7 1.2 %copy-done.1 = bf16[1,512,1024]{2,1,0:T(8,128)(2,1)S(1)} copy-done((bf16[1,512,1024]{2,1,0:T(8,128)(2,1)S(1)}, bf16[1,512,1024]{2,1,0:T(8,128)(2,1)}, u32[]{:S(2)}) %copy-start.1) | copy-done | bytes 1048600
  2.0 1.2 %copy-done.3 = bf16[1,512,1024]{2,1,0:T(8,128)(2,1)S(1)} copy-done((bf16[1,512,1024]{2,1,0:T(8,128)(2,1)S(1)}, bf16[1,512,1024]{2,1,0:T(8,128)(2,1)}, u32[]{:S(2)}) %copy-start.3) | copy-done | bytes 1048600
  3.2 1.6 %pack.1 = (bf16[2,128,1024]{2,1,0:T(8,128)(2,1)}, bf16[2,512,128]{2,1,0:T(8,128)(2,1)}, bf16[2,512,128]{2,1,0:T(8,128)(2,1)}, bf16[2,128,128]{2,1,0:T(8,128)(2,1)}, bf16[2,128,128]{2,1,0:T(8,128)(2,1)}) custom-call(s32[4]{0:T(128)S(1)} %get-tuple-element.84.offsets, bf16[1,512,1024]{2,1,0:T(8,128)(2,1)S(1)} %copy-done.1, bf16[1,512,1024]{2,1,0:T(8,128)(2,1)S(1)} %copy-done.3), custom_call_target="tpu_custom_call" | custom-call | tf_op jit(solution)/shard_map/pack/pallas_call | solution.py:208
  4.8 3.0 %collective-permute-start = (bf16[2,128,1024]{2,1,0:T(8,128)(2,1)}, bf16[2,128,1024]{2,1,0:T(8,128)(2,1)}, u32[]{:S(2)}, u32[]{:S(2)}) collective-permute-start(bf16[2,128,1024]{2,1,0:T(8,128)(2,1)} %get-tuple-element.41.after), channel_id=1, source_target_pairs={{0,8},{1,9},{2,10},{3,11},{4,12},{5,13},{6,14},{7,15},{8,0},{9,1},... | collective-permute-start | bytes 1572872 | tf_op jit(solution)/shard_map/ppermute | solution.py:730
  7.8 1.5 %collective-permute-start.1 = (bf16[2,512,128]{2,1,0:T(8,128)(2,1)}, bf16[2,512,128]{2,1,0:T(8,128)(2,1)S(1)}, u32[]{:S(2)}, u32[]{:S(2)}) collective-permute-start(bf16[2,512,128]{2,1,0:T(8,128)(2,1)} %get-tuple-element.44), channel_id=1, source_target_pairs={{0,1},{1,0},{2,3},{3,2},{4,5},{5,4},{6,7},{7,6},{8,9},{9,8},{10,11... | collective-permute-start | bytes 786440 | tf_op jit(solution)/shard_map/ppermute | solution.py:730
  9.3 1.4 %collective-permute-start.2 = (bf16[2,512,128]{2,1,0:T(8,128)(2,1)}, bf16[2,512,128]{2,1,0:T(8,128)(2,1)}, u32[]{:S(2)}, u32[]{:S(2)}) collective-permute-start(bf16[2,512,128]{2,1,0:T(8,128)(2,1)} %get-tuple-element.45), channel_id=1, source_target_pairs={{1,2},{2,1},{3,4},{4,3},{5,6},{6,5},{9,10},{10,9},{11,12},{12,11},... | collective-permute-start | bytes 786440 | tf_op jit(solution)/shard_map/ppermute | solution.py:730
  10.7 3.6 %collective-permute-start.3 = (bf16[2,128,128]{2,1,0:T(8,128)(2,1)}, bf16[2,128,128]{2,1,0:T(8,128)(2,1)S(1)}, u32[]{:S(2)}, u32[]{:S(2)}) collective-permute-start(bf16[2,128,128]{2,1,0:T(8,128)(2,1)} %get-tuple-element.46), channel_id=1, source_target_pairs={{0,9},{1,8},{2,11},{3,10},{4,13},{5,12},{6,15},{7,14},{8,1},{9,0},... | collective-permute-start | bytes 196616 | tf_op jit(solution)/shard_map/ppermute | solution.py:730
  17.9 3.0 %waves.1 = (f32[2,256,256]{2,1,0:T(8,128)S(1)}, f32[4,2,256,256]{3,2,1,0:T(8,128)S(1)}) custom-call(s32[16]{0:T(128)S(1)} %reshape.13.places, s32[4]{0:T(128)S(1)} %add_add_fusion.offsets, bf16[2,128,1024]{2,1,0:T(8,128)(2,1)} %get-tuple-element.41.after, f32[2,256,256]{2,1,0:T(8,128)S(1)} %copy-done.7, f32[256,256]{1,0:T(8,128)S(1)} %copy-done.6, ...), custom_call_target="tpu_custom_call" | custom-call | tf_op jit(solution)/shard_map/waves/pallas_call | solution.py:119
  20.9 1.6 %collective-permute-done.3.rest_3_ = bf16[2,128,128]{2,1,0:T(8,128)(2,1)S(1)} collective-permute-done((bf16[2,128,128]{2,1,0:T(8,128)(2,1)}, bf16[2,128,128]{2,1,0:T(8,128)(2,1)S(1)}, u32[]{:S(2)}, u32[]{:S(2)}) %collective-permute-start.3) | collective-permute-done | bytes 65568 | tf_op jit(solution)/shard_map/ppermute | solution.py:730
  24.6 2.5 %gather.1 = (bf16[4,2,256,256]{3,2,1,0:T(8,128)(2,1)S(1)}, bf16[4,2,256,256]{3,2,1,0:T(8,128)(2,1)S(1)}) custom-call(s32[16]{0:T(128)S(1)} %reshape.13.places, s32[4]{0:T(128)S(1)} %add_add_fusion.offsets, bf16[1,512,1024]{2,1,0:T(8,128)(2,1)S(1)} %copy-done.2, bf16[1,512,1024]{2,1,0:T(8,128)(2,1)S(1)} %copy-done.4, ...), custom_call_target="tpu_custom_call" | custom-call | tf_op jit(solution)/shard_map/gather/pallas_call | solution.py:293
  27.2 1.9 %frames.1 = f32[4,256,256]{2,1,0:T(8,128)S(1)} custom-call(s32[4]{0:T(128)S(1)} %add_add_fusion.offsets, bf16[4,2,256,256]{3,2,1,0:T(8,128)(2,1)S(1)} %get-tuple-element.48.after.mine, f32[4,2,256,256]{3,2,1,0:T(8,128)S(1)} %bitcast.13, f32[4,2,256,256]{3,2,1,0:T(8,128)S(1)} %bitcast.14), custom_call_target="tpu_custom_call" | custom-call | tf_op jit(solution)/shard_map/frames/pallas_call | solution.py:152
  29.8 14.4 %chain.1 = (bf16[4,2,256,256]{3,2,1,0:T(8,128)(2,1)S(1)}, bf16[4,2,256,256]{3,2,1,0:T(8,128)(2,1)S(1)}, bf16[2,128,256]{2,1,0:T(8,128)(2,1)S(1)}, bf16[2,128,256]{2,1,0:T(8,128)(2,1)S(1)}) custom-call(s32[16]{0:T(128)S(1)} %reshape.13.places, s32[4]{0:T(128)S(1)} %bitcast.15, s32[4]{0:T(128)S(1)} %add_add_fusion.offsets, ...), custom_call_target="tpu_custom_call" | custom-call | tf_op jit(solution)/shard_map/chain/pallas_call | solution.py:455
  45.3 1.3 %collective-permute-start.8 = (bf16[2,128,256]{2,1,0:T(8,128)(2,1)S(1)}, bf16[2,128,256]{2,1,0:T(8,128)(2,1)S(1)}, u32[]{:S(2)}, u32[]{:S(2)}) collective-permute-start(bf16[2,128,256]{2,1,0:T(8,128)(2,1)S(1)} %get-tuple-element.59), channel_id=1, source_target_pairs={{0,8},{1,9},{2,10},{3,11},{4,12},{5,13},{6,14},{7,15},{8,0},{9,1},... | collective-permute-start | bytes 393224 | tf_op jit(solution)/shard_map/ppermute | solution.py:751
  46.9 3.5 %scatter.1 = (f32[2,512,1024]{2,1,0:T(8,128)}, f32[2,128,1024]{2,1,0:T(8,128)S(1)}, f32[2,384,128]{2,1,0:T(8,128)S(1)}, f32[2,384,128]{2,1,0:T(8,128)S(1)}, bf16...) custom-call(s32[16]{0:T(128)S(1)} %reshape.13.places, ...), custom_call_target="tpu_custom_call" | custom-call | bytes 8388608 | tf_op jit(solution)/shard_map/scatter/pallas_call | solution.py:571
  50.4 2.6 %collective-permute-done.8 = bf16[2,128,256]{2,1,0:T(8,128)(2,1)S(1)} collective-permute-done((bf16[2,128,256]{2,1,0:T(8,128)(2,1)S(1)}, bf16[2,128,256]{2,1,0:T(8,128)(2,1)S(1)}, u32[]{:S(2)}, u32[]{:S(2)}) %collective-permute-start.8) | collective-permute-done | bytes 131104 | tf_op jit(solution)/shard_map/ppermute | solution.py:751
  53.1 2.9 %collective-permute-start.10 = (bf16[2,128,256]{2,1,0:T(8,128)(2,1)S(1)}, bf16[2,128,256]{2,1,0:T(8,128)(2,1)S(1)}, u32[]{:S(2)}, u32[]{:S(2)}) collective-permute-start(bf16[2,128,256]{2,1,0:T(8,128)(2,1)S(1)} %add_convert_fusion.2), channel_id=1, source_target_pairs={{0,1},{1,0},{2,3},{3,2},{4,5},{5,4},{6,7},{7,6},{8,9},{9,8},{10,11... | collective-permute-start | bytes 393224 | tf_op jit(solution)/shard_map/ppermute | solution.py:751
  56.5 2.8 %collective-permute-done.10 = bf16[2,128,256]{2,1,0:T(8,128)(2,1)S(1)} collective-permute-done((bf16[2,128,256]{2,1,0:T(8,128)(2,1)S(1)}, bf16[2,128,256]{2,1,0:T(8,128)(2,1)S(1)}, u32[]{:S(2)}, u32[]{:S(2)}) %collective-permute-start.10) | collective-permute-done | bytes 131104 | tf_op jit(solution)/shard_map/ppermute | solution.py:751
  59.3 1.7 %collective-permute-done.11.refs_0_ = bf16[2,2,128,128]{3,2,1,0:T(8,128)(2,1)S(1)} collective-permute-done((bf16[2,2,128,128]{3,2,1,0:T(8,128)(2,1)S(1)}, bf16[2,2,128,128]{3,2,1,0:T(8,128)(2,1)S(1)}, u32[]{:S(2)}, u32[]{:S(2)}) %collective-permute-start.11) | collective-permute-done | bytes 131104 | tf_op jit(solution)/shard_map/ppermute | solution.py:774
  61.5 2.2 %collective-permute-start.12 = (bf16[2,128,256]{2,1,0:T(8,128)(2,1)S(1)}, bf16[2,128,256]{2,1,0:T(8,128)(2,1)S(1)}, u32[]{:S(2)}, u32[]{:S(2)}) collective-permute-start(bf16[2,128,256]{2,1,0:T(8,128)(2,1)S(1)} %add_convert_fusion.1), channel_id=1, source_target_pairs={{0,4},{1,5},{2,6},{3,7},{4,0},{5,1},{6,2},{7,3},{8,12},{9,13},{10,... | collective-permute-start | bytes 393224 | tf_op jit(solution)/shard_map/ppermute | solution.py:751
  64.4 1.3 %collective-permute-start.15 = (bf16[2,512,128]{2,1,0:T(8,128)(2,1)S(1)}, bf16[2,512,128]{2,1,0:T(8,128)(2,1)S(1)}, u32[]{:S(2)}, u32[]{:S(2)}) collective-permute-start(bf16[2,512,128]{2,1,0:T(8,128)(2,1)S(1)} %get-tuple-element.76), channel_id=1, source_target_pairs={{0,1},{1,0},{2,3},{3,2},{4,5},{5,4},{6,7},{7,6},{8,9},{9,8},{10,11... | collective-permute-start | bytes 786440 | tf_op jit(solution)/shard_map/ppermute | solution.py:780
  66.3 2.6 %collective-permute-done.12 = bf16[2,128,256]{2,1,0:T(8,128)(2,1)S(1)} collective-permute-done((bf16[2,128,256]{2,1,0:T(8,128)(2,1)S(1)}, bf16[2,128,256]{2,1,0:T(8,128)(2,1)S(1)}, u32[]{:S(2)}, u32[]{:S(2)}) %collective-permute-start.12) | collective-permute-done | bytes 131104 | tf_op jit(solution)/shard_map/ppermute | solution.py:751
  69.9 5.2 %collective-permute-done.15.rest_4_ = bf16[2,512,128]{2,1,0:T(8,128)(2,1)S(1)} collective-permute-done((bf16[2,512,128]{2,1,0:T(8,128)(2,1)S(1)}, bf16[2,512,128]{2,1,0:T(8,128)(2,1)S(1)}, u32[]{:S(2)}, u32[]{:S(2)}) %collective-permute-start.15) | collective-permute-done | bytes 262176 | tf_op jit(solution)/shard_map/ppermute | solution.py:780
  75.2 1.6 %collective-permute-done.13.other = bf16[2,128,256]{2,1,0:T(8,128)(2,1)S(1)} collective-permute-done((bf16[2,128,256]{2,1,0:T(8,128)(2,1)S(1)}, bf16[2,128,256]{2,1,0:T(8,128)(2,1)S(1)}, u32[]{:S(2)}, u32[]{:S(2)}) %collective-permute-start.13) | collective-permute-done | bytes 131104 | tf_op jit(solution)/shard_map/ppermute | solution.py:751
  76.8 2.6 %borders.1 = (f32[2,512,1024]{2,1,0:T(8,128)}, f32[2,128,256]{2,1,0:T(8,128)}) custom-call(s32[4]{0:T(128)S(1)} %pad_add_fusion.folds, f32[2,512,1024]{2,1,0:T(8,128)} %get-tuple-element.52.tile_in, bf16[2,128,256]{2,1,0:T(8,128)(2,1)S(1)} %add_convert_fusion.part, ...), custom_call_target="tpu_custom_call", output_to_operand_aliasing={{0}: (1, {})} | custom-call | tf_op jit(solution)/shard_map/borders/pallas_call | solution.py:650
  (44 shorter events, 11.3 us)
Async XLA Ops:
  0.7 1.2 %copy-start.1 = (bf16[1,512,1024]{2,1,0:T(8,128)(2,1)S(1)}, bf16[1,512,1024]{2,1,0:T(8,128)(2,1)}, u32[]{:S(2)}) copy-start(bf16[1,512,1024]{2,1,0:T(8,128)(2,1)} %tile_re.3) | copy-start | bytes 3145732
  2.0 1.2 %copy-start.3 = (bf16[1,512,1024]{2,1,0:T(8,128)(2,1)S(1)}, bf16[1,512,1024]{2,1,0:T(8,128)(2,1)}, u32[]{:S(2)}) copy-start(bf16[1,512,1024]{2,1,0:T(8,128)(2,1)} %tile_im.3) | copy-start | bytes 3145732
  3.2 20.2 %copy-start.2 = (bf16[1,512,1024]{2,1,0:T(8,128)(2,1)S(1)}, bf16[1,512,1024]{2,1,0:T(8,128)(2,1)}, u32[]{:S(2)}) copy-start(bf16[1,512,1024]{2,1,0:T(8,128)(2,1)} %tile_re.3) | copy-start | bytes 3145732
  3.2 24.0 %copy-start = (f32[1,1,4,2,256,256]{5,4,3,2,1,0:T(8,128)S(1)}, f32[1,1,4,2,256,256]{5,4,3,2,1,0:T(8,128)}, u32[]{:S(2)}) copy-start(f32[1,1,4,2,256,256]{5,4,3,2,1,0:T(8,128)} %param.14) | copy-start | bytes 6291460
  4.8 18.6 %collective-permute-start = (bf16[2,128,1024]{2,1,0:T(8,128)(2,1)}, bf16[2,128,1024]{2,1,0:T(8,128)(2,1)}, u32[]{:S(2)}, u32[]{:S(2)}) collective-permute-start(bf16[2,128,1024]{2,1,0:T(8,128)(2,1)} %get-tuple-element.41.after), channel_id=1, source_target_pairs={{0,8},{1,9},{2,10},{3,11},{4,12},{5,13},{6,14},{7,15},{8,0},{9,1},... | collective-permute-start | bytes 1572872 | tf_op jit(solution)/shard_map/ppermute | solution.py:730
  7.8 15.5 %collective-permute-start.1 = (bf16[2,512,128]{2,1,0:T(8,128)(2,1)}, bf16[2,512,128]{2,1,0:T(8,128)(2,1)S(1)}, u32[]{:S(2)}, u32[]{:S(2)}) collective-permute-start(bf16[2,512,128]{2,1,0:T(8,128)(2,1)} %get-tuple-element.44), channel_id=1, source_target_pairs={{0,1},{1,0},{2,3},{3,2},{4,5},{5,4},{6,7},{7,6},{8,9},{9,8},{10,11... | collective-permute-start | bytes 786440 | tf_op jit(solution)/shard_map/ppermute | solution.py:730
  9.3 14.0 %collective-permute-start.2 = (bf16[2,512,128]{2,1,0:T(8,128)(2,1)}, bf16[2,512,128]{2,1,0:T(8,128)(2,1)}, u32[]{:S(2)}, u32[]{:S(2)}) collective-permute-start(bf16[2,512,128]{2,1,0:T(8,128)(2,1)} %get-tuple-element.45), channel_id=1, source_target_pairs={{1,2},{2,1},{3,4},{4,3},{5,6},{6,5},{9,10},{10,9},{11,12},{12,11},... | collective-permute-start | bytes 786440 | tf_op jit(solution)/shard_map/ppermute | solution.py:730
  10.7 11.8 %collective-permute-start.3 = (bf16[2,128,128]{2,1,0:T(8,128)(2,1)}, bf16[2,128,128]{2,1,0:T(8,128)(2,1)S(1)}, u32[]{:S(2)}, u32[]{:S(2)}) collective-permute-start(bf16[2,128,128]{2,1,0:T(8,128)(2,1)} %get-tuple-element.46), channel_id=1, source_target_pairs={{0,9},{1,8},{2,11},{3,10},{4,13},{5,12},{6,15},{7,14},{8,1},{9,0},... | collective-permute-start | bytes 196616 | tf_op jit(solution)/shard_map/ppermute | solution.py:730
  14.3 8.2 %collective-permute-start.4 = (bf16[2,128,128]{2,1,0:T(8,128)(2,1)}, bf16[2,128,128]{2,1,0:T(8,128)(2,1)S(1)}, u32[]{:S(2)}, u32[]{:S(2)}) collective-permute-start(bf16[2,128,128]{2,1,0:T(8,128)(2,1)} %get-tuple-element.47), channel_id=1, source_target_pairs={{1,10},{2,9},{3,12},{4,11},{5,14},{6,13},{9,2},{10,1},{11,4},{12,3... | collective-permute-start | bytes 196616 | tf_op jit(solution)/shard_map/ppermute | solution.py:730
  23.4 1.2 %copy-start.4 = (bf16[1,512,1024]{2,1,0:T(8,128)(2,1)S(1)}, bf16[1,512,1024]{2,1,0:T(8,128)(2,1)}, u32[]{:S(2)}) copy-start(bf16[1,512,1024]{2,1,0:T(8,128)(2,1)} %tile_im.3) | copy-start | bytes 3145732
  27.1 2.8 %copy-start.5 = (bf16[4,2,256,256]{3,2,1,0:T(8,128)(2,1)S(1)}, bf16[4,2,256,256]{3,2,1,0:T(8,128)(2,1)}, u32[]{:S(2)}) copy-start(bf16[4,2,256,256]{3,2,1,0:T(8,128)(2,1)} %constant.46.clone.tables) | copy-start | bytes 3145732
  27.1 2.7 %copy-start.8 = (s32[1,1,4]{2,1,0:T(1,128)S(1)}, s32[1,1,4]{2,1,0:T(1,128)}, u32[]{:S(2)}) copy-start(s32[1,1,4]{2,1,0:T(1,128)} %param.13) | copy-start | bytes 52
  27.1 2.7 %collective-permute-start.5 = (bf16[4,2,256,256]{3,2,1,0:T(8,128)(2,1)S(1)}, bf16[4,2,256,256]{3,2,1,0:T(8,128)(2,1)S(1)}, u32[]{:S(2)}, u32[]{:S(2)}) collective-permute-start(bf16[4,2,256,256]{3,2,1,0:T(8,128)(2,1)S(1)} %get-tuple-element.49), channel_id=1, source_target_pairs={{0,16},{16,0},{1,17},{17,1},{2,18},{18,2},{3,19},{19,3},{4,20},{20... | collective-permute-start | bytes 3145736 | tf_op jit(solution)/shard_map/ppermute | solution.py:736
  44.2 2.7 %collective-permute-start.6 = (bf16[4,2,256,256]{3,2,1,0:T(8,128)(2,1)S(1)}, bf16[4,2,256,256]{3,2,1,0:T(8,128)(2,1)S(1)}, u32[]{:S(2)}, u32[]{:S(2)}) collective-permute-start(bf16[4,2,256,256]{3,2,1,0:T(8,128)(2,1)S(1)} %get-tuple-element.51), channel_id=1, source_target_pairs={{0,16},{16,0},{1,17},{17,1},{2,18},{18,2},{3,19},{19,3},{4,20},{20... | collective-permute-start | bytes 3145736 | tf_op jit(solution)/shard_map/ppermute | solution.py:741
  44.4 8.6 %collective-permute-start.9 = (bf16[2,128,256]{2,1,0:T(8,128)(2,1)S(1)}, bf16[2,128,256]{2,1,0:T(8,128)(2,1)S(1)}, u32[]{:S(2)}, u32[]{:S(2)}) collective-permute-start(bf16[2,128,256]{2,1,0:T(8,128)(2,1)S(1)} %get-tuple-element.54), channel_id=1, source_target_pairs={{0,24},{1,25},{2,26},{3,27},{4,28},{5,29},{6,30},{7,31},{8,16},{9,... | collective-permute-start | bytes 393224 | tf_op jit(solution)/shard_map/ppermute | solution.py:751
  45.1 7.9 %collective-permute-start.7 = (bf16[2,128,256]{2,1,0:T(8,128)(2,1)S(1)}, bf16[2,128,256]{2,1,0:T(8,128)(2,1)S(1)}, u32[]{:S(2)}, u32[]{:S(2)}) collective-permute-start(bf16[2,128,256]{2,1,0:T(8,128)(2,1)S(1)} %get-tuple-element.54), channel_id=1, source_target_pairs={{0,16},{1,17},{2,18},{3,19},{4,20},{5,21},{6,22},{7,23},{8,24},{9,... | collective-permute-start | bytes 393224 | tf_op jit(solution)/shard_map/ppermute | solution.py:751
  45.3 7.8 %collective-permute-start.8 = (bf16[2,128,256]{2,1,0:T(8,128)(2,1)S(1)}, bf16[2,128,256]{2,1,0:T(8,128)(2,1)S(1)}, u32[]{:S(2)}, u32[]{:S(2)}) collective-permute-start(bf16[2,128,256]{2,1,0:T(8,128)(2,1)S(1)} %get-tuple-element.59), channel_id=1, source_target_pairs={{0,8},{1,9},{2,10},{3,11},{4,12},{5,13},{6,14},{7,15},{8,0},{9,1},... | collective-permute-start | bytes 393224 | tf_op jit(solution)/shard_map/ppermute | solution.py:751
  53.1 6.2 %collective-permute-start.10 = (bf16[2,128,256]{2,1,0:T(8,128)(2,1)S(1)}, bf16[2,128,256]{2,1,0:T(8,128)(2,1)S(1)}, u32[]{:S(2)}, u32[]{:S(2)}) collective-permute-start(bf16[2,128,256]{2,1,0:T(8,128)(2,1)S(1)} %add_convert_fusion.2), channel_id=1, source_target_pairs={{0,1},{1,0},{2,3},{3,2},{4,5},{5,4},{6,7},{7,6},{8,9},{9,8},{10,11... | collective-permute-start | bytes 393224 | tf_op jit(solution)/shard_map/ppermute | solution.py:751
  56.0 5.0 %collective-permute-start.11 = (bf16[2,2,128,128]{3,2,1,0:T(8,128)(2,1)S(1)}, bf16[2,2,128,128]{3,2,1,0:T(8,128)(2,1)S(1)}, u32[]{:S(2)}, u32[]{:S(2)}) collective-permute-start(bf16[2,2,128,128]{3,2,1,0:T(8,128)(2,1)S(1)} %get-tuple-element.63), channel_id=1, source_target_pairs={{0,8},{1,9},{2,10},{3,11},{4,12},{5,13},{6,14},{7,15},{8,0},{9,1},... | collective-permute-start | bytes 393224 | tf_op jit(solution)/shard_map/ppermute | solution.py:774
  61.0 15.8 %collective-permute-start.14 = (bf16[2,128,1024]{2,1,0:T(8,128)(2,1)S(1)}, bf16[2,128,1024]{2,1,0:T(8,128)(2,1)S(1)}, u32[]{:S(2)}, u32[]{:S(2)}) collective-permute-start(bf16[2,128,1024]{2,1,0:T(8,128)(2,1)S(1)} %get-tuple-element.72), channel_id=1, source_target_pairs={{0,8},{1,9},{2,10},{3,11},{4,12},{5,13},{6,14},{7,15},{8,0},{9,1},... | collective-permute-start | bytes 1572872 | tf_op jit(solution)/shard_map/ppermute | solution.py:780
  61.5 7.4 %collective-permute-start.12 = (bf16[2,128,256]{2,1,0:T(8,128)(2,1)S(1)}, bf16[2,128,256]{2,1,0:T(8,128)(2,1)S(1)}, u32[]{:S(2)}, u32[]{:S(2)}) collective-permute-start(bf16[2,128,256]{2,1,0:T(8,128)(2,1)S(1)} %add_convert_fusion.1), channel_id=1, source_target_pairs={{0,4},{1,5},{2,6},{3,7},{4,0},{5,1},{6,2},{7,3},{8,12},{9,13},{10,... | collective-permute-start | bytes 393224 | tf_op jit(solution)/shard_map/ppermute | solution.py:751
  64.4 10.8 %collective-permute-start.15 = (bf16[2,512,128]{2,1,0:T(8,128)(2,1)S(1)}, bf16[2,512,128]{2,1,0:T(8,128)(2,1)S(1)}, u32[]{:S(2)}, u32[]{:S(2)}) collective-permute-start(bf16[2,512,128]{2,1,0:T(8,128)(2,1)S(1)} %get-tuple-element.76), channel_id=1, source_target_pairs={{0,1},{1,0},{2,3},{3,2},{4,5},{5,4},{6,7},{7,6},{8,9},{9,8},{10,11... | collective-permute-start | bytes 786440 | tf_op jit(solution)/shard_map/ppermute | solution.py:780
  65.7 9.5 %collective-permute-start.16 = (bf16[2,512,128]{2,1,0:T(8,128)(2,1)S(1)}, bf16[2,512,128]{2,1,0:T(8,128)(2,1)S(1)}, u32[]{:S(2)}, u32[]{:S(2)}) collective-permute-start(bf16[2,512,128]{2,1,0:T(8,128)(2,1)S(1)} %get-tuple-element.77), channel_id=1, source_target_pairs={{1,2},{2,1},{3,4},{4,3},{5,6},{6,5},{9,10},{10,9},{11,12},{12,11},... | collective-permute-start | bytes 786440 | tf_op jit(solution)/shard_map/ppermute | solution.py:780
  69.0 7.8 %collective-permute-start.13 = (bf16[2,128,256]{2,1,0:T(8,128)(2,1)S(1)}, bf16[2,128,256]{2,1,0:T(8,128)(2,1)S(1)}, u32[]{:S(2)}, u32[]{:S(2)}) collective-permute-start(bf16[2,128,256]{2,1,0:T(8,128)(2,1)S(1)} %add_convert_fusion.part), channel_id=1, source_target_pairs={{0,2},{1,3},{2,0},{3,1},{4,6},{5,7},{6,4},{7,5},{8,10},{9,11},{10,... | collective-permute-start | bytes 393224 | tf_op jit(solution)/shard_map/ppermute | solution.py:751
  (2 other events, 2.0 us)
